TPU v7x, 32 devices: a whole 2x2x4 slice. The times are simulated.
32 devices in a mesh: rep: 4 (over z), ctx: 8 (over y, x, core).
Axes of the slice: x: 2, y: 2, z: 4, core: 2. Of those that a mesh axis runs over, the one named last changes fastest.
Arguments:
- query_rows: bfloat16 [4, 1024, 32, 128], P('rep', 'ctx'), may hold values from -17 to 17
- key_rows: bfloat16 [4, 1024, 4, 128], P('rep', 'ctx'), may hold values from -17 to 17
- value_matrix: bfloat16 [4, 1024, 4, 128], P('rep', 'ctx'), may hold values from -6 to 6
- cotangent: bfloat16 [4, 1024, 32, 128], P('rep', 'ctx'), may hold values from -6 to 6
- rotation: bfloat16 [16, 4, 32, 128], replicated, may hold values from -0.29882812 to 0.29882812
- projection: bfloat16 [16, 4, 32, 128], replicated, may hold values from -0.29882812 to 0.29882812
- shift_bias: float32 [16, 4], replicated, may hold values from -4 to 4
- doc_starts: int32 [4, 1024], P('rep'), may hold values from 0 to 1022, as said below
- tenant_ids: int32 [4, 1024], P('rep'), may hold values from 0 to 15, as said below
Outputs:
- d_queries: bfloat16 [4, 1024, 32, 128], P('rep', 'ctx')
- d_keys: bfloat16 [4, 1024, 4, 128], P('rep', 'ctx')
- d_values: bfloat16 [4, 1024, 4, 128], P('rep', 'ctx')
- grad_rotation: float32 [16, 4, 32, 128], P('rep', None, 'ctx')
- grad_projection: float32 [16, 4, 32, 128], P('rep', None, 'ctx')
Inputs may be any that keep to these rules, and one draw needn't show every extreme that they name: doc_starts[r, i] is the first position of the document holding position i of sequence r; documents are consecutive, each of even length 2 to 256; every sequence begins with one of exactly 256 and ends with one of length 2. `tenant_ids`: the tenant of a position's document: equal for all positions of one document.
All inputs are finite; a program needn't handle non-finite values.
Results may differ from a plain program's by a relative error of at most 0.03.
Values may be sent and summed in bfloat16 or wider, within the bound.
No kernel may reach another device: no remote copies, remote signals or barrier semaphores. Data moves between devices by JAX's collectives and lax.ppermute only.
A program may use at most 128 MiB of HBM per device.

v0:
```python
import jax
import jax.numpy as jnp
from jax import lax
from jax.sharding import PartitionSpec as P

DOC_MAX = 256


far_below = -1e30


def shifted(value, axis, steps):
    count = lax.axis_size(axis)
    first, last = (max(0, -steps), min(count, count - steps))
    return lax.ppermute(value, axis, [(source, source + steps) for source in range(first, last)])


def tenant_terms(hidden, upstream, owners, rotation, projection):
    tenant_count = rotation.shape[0]
    low_rank = rotation.shape[1]
    tenant_mask = (jnp.arange(tenant_count, dtype=jnp.int32)[:, None] == owners[None, :]).astype(
        jnp.float32
    )
    both_maps = jnp.concatenate([projection, rotation], axis=1)
    on_both = jnp.einsum("shd,trhd->trs", hidden, both_maps, preferred_element_type=jnp.float32)
    pulled_all = jnp.einsum("shd,trhd->trs", upstream, rotation, preferred_element_type=jnp.float32)
    local_lift = jnp.sum(on_both[:, :low_rank] * tenant_mask[:, None, :], axis=0) - jnp.sum(
        on_both[:, low_rank:] * tenant_mask[:, None, :], axis=0
    )
    local_pull = jnp.sum(pulled_all * tenant_mask[:, None, :], axis=0)
    return (tenant_mask, local_lift, local_pull)


def tenant_grads(hidden, upstream, owners, tenant_count, lifted_low, pulled_low):
    mask_low = (jnp.arange(tenant_count, dtype=jnp.int32)[:, None] == owners[None, :]).astype(
        jnp.bfloat16
    )
    picked_pull = mask_low[:, None, :] * pulled_low[None]
    picked_lift = mask_low[:, None, :] * lifted_low[None]
    grad_proj = jnp.einsum("trs,shd->trhd", picked_pull, hidden, preferred_element_type=jnp.float32)
    grad_rot = (
        jnp.einsum("trs,shd->trhd", picked_lift, upstream, preferred_element_type=jnp.float32)
        - grad_proj
    )
    return (grad_rot, grad_proj)


def hidden_gradient(upstream, tenant_mask, pulled_low, rotation, projection):
    picked_pull = tenant_mask.astype(jnp.bfloat16)[:, None, :] * pulled_low[None]
    hidden_grad = (
        upstream.astype(jnp.float32)
        + jnp.einsum("trs,trhd->shd", picked_pull, projection, preferred_element_type=jnp.float32)
        - jnp.einsum("trs,trhd->shd", picked_pull, rotation, preferred_element_type=jnp.float32)
    )
    return hidden_grad.astype(jnp.bfloat16)


def group_sum(head_grads, kv_count, group_size):
    rows = head_grads.shape[0]
    rounded = lax.optimization_barrier(head_grads.astype(jnp.bfloat16))
    return (
        rounded.astype(jnp.float32)
        .reshape(rows, kv_count, group_size, head_grads.shape[-1])
        .sum(axis=2)
        .astype(jnp.bfloat16)
    )


def on_device(
    query_rows,
    key_rows,
    value_matrix,
    cotangent,
    rotation,
    projection,
    shift_bias,
    doc_starts,
    tenant_ids,
):
    queries = query_rows[0]
    key_set = key_rows[0]
    value_set = value_matrix[0]
    upstream = cotangent[0]
    starts_all = doc_starts[0]
    owners_all = tenant_ids[0]
    head_count = queries.shape[1]
    kv_count = key_set.shape[1]
    group_size = head_count // kv_count
    head_dim = queries.shape[2]
    tokens_here = queries.shape[0]
    scaling = head_dim ** (-0.5)
    tenant_count = rotation.shape[0]
    reach = (DOC_MAX + tokens_here - 1) // tokens_here
    key_parts = []
    value_parts = []
    for step in range(reach, 0, -1):
        behind_keys, behind_values = shifted((key_set, value_set), "ctx", step)
        key_parts.append(behind_keys)
        value_parts.append(behind_values)
    window_keys = jnp.concatenate(key_parts + [key_set], axis=0)
    window_values = jnp.concatenate(value_parts + [value_set], axis=0)
    row_first = lax.axis_index("ctx") * tokens_here
    starts = lax.dynamic_slice_in_dim(starts_all, row_first, tokens_here, 0)
    owners = lax.dynamic_slice_in_dim(owners_all, row_first, tokens_here, 0)
    query_place = row_first + jnp.arange(tokens_here, dtype=jnp.int32)
    key_place = (
        row_first - reach * tokens_here + jnp.arange((reach + 1) * tokens_here, dtype=jnp.int32)
    )
    allowed = (key_place[None, :] >= starts[:, None]) & (key_place[None, :] <= query_place[:, None])

    def head_scores(query_one, key_one):
        scores = (
            jnp.einsum("qgd,pd->gqp", query_one, key_one, preferred_element_type=jnp.float32)
            * scaling
        )
        return jnp.where(allowed[None], scores, far_below)

    def forward_one(pieces):
        query_one, key_one, value_one = pieces
        scores = head_scores(query_one, key_one)
        row_max = jnp.max(scores, axis=-1)
        weights = jnp.exp(scores - row_max[..., None])
        row_total = jnp.sum(weights, axis=-1)
        weights_low = (weights / row_total[..., None]).astype(jnp.bfloat16)
        hidden_one = jnp.einsum(
            "gqp,pd->qgd", weights_low, value_one, preferred_element_type=jnp.float32
        ).astype(jnp.bfloat16)
        return (hidden_one, row_max, row_total)

    query_heads = jnp.moveaxis(queries.reshape(tokens_here, kv_count, group_size, head_dim), 1, 0)
    key_heads = jnp.moveaxis(window_keys, 1, 0)
    value_heads = jnp.moveaxis(window_values, 1, 0)
    hidden_heads, maxima, totals = lax.map(forward_one, (query_heads, key_heads, value_heads))
    hidden = jnp.moveaxis(hidden_heads, 0, 1).reshape(tokens_here, head_count, head_dim)
    tenant_mask, local_lift, local_pull = tenant_terms(
        hidden, upstream, owners, rotation, projection
    )
    bias_rows = jnp.sum(shift_bias[:, :, None] * tenant_mask[:, None, :], axis=0)
    lifted_low = (local_lift + bias_rows).astype(jnp.bfloat16)
    pulled_low = local_pull.astype(jnp.bfloat16)
    grad_hidden = hidden_gradient(upstream, tenant_mask, pulled_low, rotation, projection)
    head_hidden, head_upstream = (
        lax.all_to_all(hidden, "ctx", split_axis=1, concat_axis=0, tiled=True),
        lax.all_to_all(upstream, "ctx", split_axis=1, concat_axis=0, tiled=True),
    )
    all_lift, all_pull = (
        lax.all_gather(lifted_low, "ctx", axis=1, tiled=True),
        lax.all_gather(pulled_low, "ctx", axis=1, tiled=True),
    )
    grad_rot, grad_proj = tenant_grads(
        head_hidden, head_upstream, owners_all, tenant_count, all_lift, all_pull
    )
    row_delta = jnp.sum(grad_hidden.astype(jnp.float32) * hidden.astype(jnp.float32), axis=-1)
    delta_heads = jnp.moveaxis(row_delta.reshape(tokens_here, kv_count, group_size), 0, 2)
    grad_heads = jnp.moveaxis(
        grad_hidden.reshape(tokens_here, kv_count, group_size, head_dim), 1, 0
    )

    def backward_one(pieces):
        query_one, key_one, value_one, grad_one, delta_one, row_max, row_total = pieces
        scores = head_scores(query_one, key_one)
        weights = jnp.exp(scores - row_max[..., None]) / row_total[..., None]
        weights_low = weights.astype(jnp.bfloat16)
        weight_grad = jnp.einsum(
            "qgd,pd->gqp", grad_one, value_one, preferred_element_type=jnp.float32
        )
        score_grad = (weights * (weight_grad - delta_one[:, :, None])).astype(jnp.bfloat16)
        query_grad = (
            jnp.einsum("gqp,pd->qgd", score_grad, key_one, preferred_element_type=jnp.float32)
            * scaling
        ).astype(jnp.bfloat16)
        key_grad = (
            jnp.einsum("gqp,qgd->pgd", score_grad, query_one, preferred_element_type=jnp.float32)
            * scaling
        )
        value_grad = jnp.einsum(
            "gqp,qgd->pgd", weights_low, grad_one, preferred_element_type=jnp.float32
        )
        return (query_grad, key_grad, value_grad)

    query_grads, key_grads, value_grads = lax.map(
        backward_one, (query_heads, key_heads, value_heads, grad_heads, delta_heads, maxima, totals)
    )
    own_dq = jnp.moveaxis(query_grads, 0, 1).reshape(tokens_here, head_count, head_dim)
    window_dk = jnp.moveaxis(key_grads, 0, 1).reshape(
        (reach + 1) * tokens_here, head_count, head_dim
    )
    window_dv = jnp.moveaxis(value_grads, 0, 1).reshape(
        (reach + 1) * tokens_here, head_count, head_dim
    )
    own_dk = window_dk[reach * tokens_here :]
    own_dv = window_dv[reach * tokens_here :]
    for step in range(1, reach + 1):
        lower = (reach - step) * tokens_here
        back_dk, back_dv = shifted(
            (window_dk[lower : lower + tokens_here], window_dv[lower : lower + tokens_here]),
            "ctx",
            -step,
        )
        own_dk = own_dk + back_dk
        own_dv = own_dv + back_dv
    d_keys = group_sum(own_dk, kv_count, group_size)
    d_values = group_sum(own_dv, kv_count, group_size)
    grad_rotation, grad_projection = (
        lax.psum_scatter(grad_rot, "rep", scatter_dimension=0, tiled=True),
        lax.psum_scatter(grad_proj, "rep", scatter_dimension=0, tiled=True),
    )
    return (own_dq[None], d_keys[None], d_values[None], grad_rotation, grad_projection)


def solution(mesh):
    in_specs = (
        P("rep", "ctx", None, None),
        P("rep", "ctx", None, None),
        P("rep", "ctx", None, None),
        P("rep", "ctx", None, None),
        P(),
        P(),
        P(),
        P("rep", None),
        P("rep", None),
    )
    out_specs = (
        P("rep", "ctx", None, None),
        P("rep", "ctx", None, None),
        P("rep", "ctx", None, None),
        P("rep", None, "ctx", None),
        P("rep", None, "ctx", None),
    )
    return jax.shard_map(
        on_device, mesh=mesh, in_specs=in_specs, out_specs=out_specs, check_vma=False
    )
```

profile of v0, /device:TPU:0, one launch (start us, length us, event | category | flops | bytes accessed | tf_op | source)
XLA Modules:
  0.0 322.0 jit_solution(14141776700585846488)
XLA Ops:
  7.2 1.6 copy.115
  8.8 3.0 collective-permute-start.3
  11.8 4.4 %collective-permute-start.2 = (bf16[128,4,128]{2,0,1:T(8,128)(2,1)}, bf16[128,4,128]{2,0,1:T(8,128)(2,1)}, u32[]{:S(2)}, u32[]{:S(2)}) collective-permute-start(bf16[128,4,128]{2,0,1:T(8,128)(2,1)} %bitcast.199), channel_id=1, source_target_pairs={{0,2},{1,3},{2,4},{3,5},{4,6},{5,7},{8,10},{9,11},{10,12},{11,13},... | collective-permute-start | bytes 393224 | tf_op jit(solution)/shard_map/ppermute | solution.py:15
  16.2 1.6 copy.116
  17.8 4.0 %collective-permute-start.1 = (bf16[128,4,128]{2,0,1:T(8,128)(2,1)}, bf16[128,4,128]{2,0,1:T(8,128)(2,1)}, u32[]{:S(2)}, u32[]{:S(2)}) collective-permute-start(bf16[128,4,128]{2,0,1:T(8,128)(2,1)} %bitcast.200), channel_id=1, source_target_pairs={{0,1},{1,2},{2,3},{3,4},{4,5},{5,6},{6,7},{8,9},{9,10},{10,11},{11... | collective-permute-start | bytes 393224 | tf_op jit(solution)/shard_map/ppermute | solution.py:15
  21.8 2.8 collective-permute-start
  24.5 2.7 copy.52
  27.2 4.4 %all-to-all-start = ((bf16[128,32,128]{0,2,1:T(8,128)(2,1)}), bf16[128,32,128]{0,2,1:T(8,128)(2,1)}, u32[]{:S(2)}, u32[]{:S(2)}) async-start(bf16[128,32,128]{0,2,1:T(8,128)(2,1)} %bitcast.10), calls=%async_computation | async-start | bytes 2097152 | tf_op jit(solution)/shard_map/all_to_all | solution.py:144
  32.3 0.7 fusion.49
  33.7 1.1 copy.59
  34.7 1.1 copy.60
  35.8 1.6 copy.49
  37.4 13.2 %all_gather.7 = bf16[4,1024]{1,0:T(4,128)(2,1)} all-gather(bf16[4,128]{1,0:T(4,128)(2,1)S(1)} %copy-done.15), channel_id=1, replica_groups=mesh['rep'=4,'ctx'=8] {'ctx'}, dimensions={1}, use_global_device_ids=true | all-gather | bytes 9216 | tf_op jit(solution)/shard_map/all_gather | solution.py:148
  50.6 1.9 maximum_bitcast_fusion.1
  52.5 1.1 maximum_bitcast_fusion
  53.5 1.2 broadcast.70.clone
  54.8 13.5 %while.30 = (s32[]{:T(128)}, bf16[4,128,8,128]{1,3,2,0:T(8,128)(2,1)}, f32[4,8,128]{2,1,0:T(8,128)}, f32[4,8,128]{2,1,0:T(8,128)}, bf16[4,384,128]{2,1,0:T(8,128...) while((s32[]{:T(128)}, ...), condition=%wide.region_4.5_spmd.clone, body=%wide.region_1.0_spmd.clone.sunk | while | flops 204748800 | bytes 5579385 | solution.py:133
  55.5 2.0 fusion.110
  58.9 2.0 fusion.110
  62.3 2.0 fusion.110
  65.7 2.0 fusion.110
  68.3 4.3 %multiply_reduce_fusion = (f32[128,32]{0,1:T(8,128)}, bf16[128,32,128]{0,2,1:T(8,128)(2,1)}) fusion(bf16[4,128,8,128]{1,3,2,0:T(8,128)(2,1)} %get-tuple-element.115, bf16[16,4,32,128]{3,2,1,0:T(8,128)(2,1)} %param.17, bf16[4,128]{1,0:T(4,128)(2,1)} %copy-done.14, bf16[16,128]{1,0:T(8,128)(2,1)} %copy-done.10, f32[128,32,128,1]{0,2,3,1:T(8,128)S(1)} %fusion.55, ...), kind=kOutput, calls=%fused_computation.66 | convolution fusion | flops 71331840 | bytes 5788672 | tf_op jit(solution)/shard_map/trs,trhd->shd/dot_general | solution.py:53
  72.6 1.6 copy.57
  74.5 28.2 %while.31 = (s32[]{:T(128)}, bf16[4,128,8,128]{1,3,2,0:T(8,128)(2,1)S(1)}, f32[4,384,8,128]{1,3,2,0:T(8,128)}, f32[4,384,8,128]{1,3,2,0:T(8,128)}, bf16[4,384,12...) while((s32[]{:T(128)}, ...), condition=%wide.region_7.8_spmd.clone, body=%wide.region_6.7_spmd.clone.sunk | while | flops 507265024 | bytes 11972253 | solution.py:181
  74.5 0.7 dynamic-slice_bitcast_fusion.8
  75.2 0.7 dynamic-slice_bitcast_fusion.7
  76.5 1.3 fusion.122
  78.2 1.7 bitcast_dynamic-update-slice_fusion.9
  79.8 1.7 bitcast_dynamic-update-slice_fusion.8
  81.5 0.7 dynamic-slice_bitcast_fusion.8
  82.2 0.7 dynamic-slice_bitcast_fusion.7
  83.6 1.3 fusion.122
  85.2 1.7 bitcast_dynamic-update-slice_fusion.9
  87.0 1.6 bitcast_dynamic-update-slice_fusion.8
  88.6 0.7 dynamic-slice_bitcast_fusion.8
  89.3 0.7 dynamic-slice_bitcast_fusion.7
  90.6 1.3 fusion.122
  92.3 1.6 bitcast_dynamic-update-slice_fusion.9
  93.9 1.7 bitcast_dynamic-update-slice_fusion.8
  95.6 0.7 dynamic-slice_bitcast_fusion.8
  96.3 0.7 dynamic-slice_bitcast_fusion.7
  97.7 1.3 fusion.122
  99.3 1.7 bitcast_dynamic-update-slice_fusion.9
  101.0 1.7 bitcast_dynamic-update-slice_fusion.8
  102.7 5.9 %fusion.82 = (f32[128,4,8,128]{0,3,2,1:T(8,128)S(1)}, f32[128,4,8,128]{0,3,2,1:T(8,128)}, f32[128,4,8,128]{0,3,2,1:T(8,128)}) fusion(f32[384,4,8,128]{0,3,2,1:T(8,128)} %bitcast.245), kind=kLoop, calls=%fused_computation.122 | loop fusion | bytes 12582912 | tf_op jit(solution)/shard_map/slice | solution.py:192
  108.6 1.3 collective-permute-start.7
  109.9 1.3 collective-permute-start.6
  111.2 7.4 %all-to-all-start.1 = ((bf16[128,32,128]{0,2,1:T(8,128)(2,1)}), bf16[128,32,128]{0,2,1:T(8,128)(2,1)S(1)}, u32[]{:S(2)}, u32[]{:S(2)}) async-start(bf16[128,32,128]{0,2,1:T(8,128)(2,1)} %bitcast.24), calls=%async_computation.1 | async-start | bytes 2097152 | tf_op jit(solution)/shard_map/all_to_all | solution.py:143
  118.6 5.9 %fusion.83 = (f32[128,4,8,128]{0,3,2,1:T(8,128)}, f32[128,4,8,128]{0,3,2,1:T(8,128)}, f32[128,4,8,128]{0,3,2,1:T(8,128)}) fusion(f32[384,4,8,128]{0,3,2,1:T(8,128)} %bitcast.246), kind=kLoop, calls=%fused_computation.123 | loop fusion | bytes 12582912 | tf_op jit(solution)/shard_map/slice | solution.py:191
  124.5 1.4 collective-permute-start.5
  125.9 1.3 collective-permute-start.4
  127.2 1.9 convolution_bitcast_fusion
  129.3 131.3 %all_gather.6 = bf16[4,1024]{1,0:T(4,128)(2,1)S(1)} all-gather(bf16[4,128]{1,0:T(4,128)(2,1)S(1)} %add_convert_fusion), channel_id=1, replica_groups=mesh['rep'=4,'ctx'=8] {'ctx'}, dimensions={1}, use_global_device_ids=true | all-gather | bytes 9216 | tf_op jit(solution)/shard_map/all_gather | solution.py:147
  260.6 2.3 copy.64
  262.9 1.3 copy.65
  264.2 1.6 fusion.58
  265.8 2.2 convolution_subtract_fusion
  269.3 1.7 copy.58
  271.0 34.0 %all-reduce.5.cloned.1.call-done = (f32[16,4,4,128]{3,0,2,1:T(8,128)}, f32[16,4,4,128]{3,0,2,1:T(8,128)}) async-done(((f32[16,4,4,128]{3,0,2,1:T(8,128)}, f32[16,4,4,128]{3,0,2,1:T(8,128)}), (f32[16,4,4,128]{3,0,2,1:T(8,128)}, f32[16,4,4,128]{3,0,2,1:T(8,128)})) %all-reduce.5.cloned.1.call-update) | async-done | bytes 262160
  304.9 0.9 constant_dynamic-slice_fusion
  307.1 2.7 fusion.44
  309.9 0.8 copy.67
  310.7 3.4 %fusion.46 = bf16[128,32,128]{0,2,1:T(8,128)(2,1)S(1)} fusion(f32[128,32,128]{0,2,1:T(8,128)} %collective-permute-done.5, f32[128,32,128]{0,2,1:T(8,128)} %collective-permute-done.4, f32[128,4,8,128]{0,3,2,1:T(8,128)} %get-tuple-element.269), kind=kLoop, calls=%fused_computation.62 | loop fusion | flops 1572864 | bytes 7340032 | tf_op jit(solution)/shard_map/convert_element_type | solution.py:60
  314.3 0.8 copy.66
  (98 shorter events, 13.3 us)
Async XLA Ops:
  7.2 26.5 %copy-start = (s32[1,1024]{1,0:T(1,128)S(1)}, s32[1,1024]{1,0:T(1,128)}, u32[]{:S(2)}) copy-start(s32[1,1024]{1,0:T(1,128)} %param.20) | copy-start | bytes 12292
  8.8 41.8 %collective-permute-start.3 = (bf16[128,4,128]{2,0,1:T(8,128)(2,1)}, bf16[128,4,128]{2,0,1:T(8,128)(2,1)}, u32[]{:S(2)}, u32[]{:S(2)}) collective-permute-start(bf16[128,4,128]{2,0,1:T(8,128)(2,1)} %bitcast.199), channel_id=1, source_target_pairs={{0,1},{1,2},{2,3},{3,4},{4,5},{5,6},{6,7},{8,9},{9,10},{10,11},{11... | collective-permute-start | bytes 393224 | tf_op jit(solution)/shard_map/ppermute | solution.py:15
  11.8 38.8 %collective-permute-start.2 = (bf16[128,4,128]{2,0,1:T(8,128)(2,1)}, bf16[128,4,128]{2,0,1:T(8,128)(2,1)}, u32[]{:S(2)}, u32[]{:S(2)}) collective-permute-start(bf16[128,4,128]{2,0,1:T(8,128)(2,1)} %bitcast.199), channel_id=1, source_target_pairs={{0,2},{1,3},{2,4},{3,5},{4,6},{5,7},{8,10},{9,11},{10,12},{11,13},... | collective-permute-start | bytes 393224 | tf_op jit(solution)/shard_map/ppermute | solution.py:15
  17.8 13.8 %copy-start.16 = (s32[1,1024]{1,0:T(1,128)S(1)}, s32[1,1024]{1,0:T(1,128)}, u32[]{:S(2)}) copy-start(s32[1,1024]{1,0:T(1,128)} %param.21) | copy-start | bytes 12292
  17.8 14.5 %copy-start.4 = (bf16[16,4,32,128]{3,2,1,0:T(8,128)(2,1)S(1)}, bf16[16,4,32,128]{3,2,1,0:T(8,128)(2,1)}, u32[]{:S(2)}) copy-start(bf16[16,4,32,128]{3,2,1,0:T(8,128)(2,1)} %param.17) | copy-start | bytes 1572868
  17.8 14.5 %copy-start.6 = (bf16[1,128,32,128]{3,2,1,0:T(8,128)(2,1)S(1)}, bf16[1,128,32,128]{3,2,1,0:T(8,128)(2,1)}, u32[]{:S(2)}) copy-start(bf16[1,128,32,128]{3,2,1,0:T(8,128)(2,1)} %param.16) | copy-start | bytes 3145732
  17.8 34.7 %collective-permute-start.1 = (bf16[128,4,128]{2,0,1:T(8,128)(2,1)}, bf16[128,4,128]{2,0,1:T(8,128)(2,1)}, u32[]{:S(2)}, u32[]{:S(2)}) collective-permute-start(bf16[128,4,128]{2,0,1:T(8,128)(2,1)} %bitcast.200), channel_id=1, source_target_pairs={{0,1},{1,2},{2,3},{3,4},{4,5},{5,6},{6,7},{8,9},{9,10},{10,11},{11... | collective-permute-start | bytes 393224 | tf_op jit(solution)/shard_map/ppermute | solution.py:15
  21.8 30.7 %collective-permute-start = (bf16[128,4,128]{2,0,1:T(8,128)(2,1)}, bf16[128,4,128]{2,0,1:T(8,128)(2,1)}, u32[]{:S(2)}, u32[]{:S(2)}) collective-permute-start(bf16[128,4,128]{2,0,1:T(8,128)(2,1)} %bitcast.200), channel_id=1, source_target_pairs={{0,2},{1,3},{2,4},{3,5},{4,6},{5,7},{8,10},{9,11},{10,12},{11,13},... | collective-permute-start | bytes 393224 | tf_op jit(solution)/shard_map/ppermute | solution.py:15
  27.2 5.8 %copy-start.3 = (bf16[16,4,32,128]{3,2,1,0:T(8,128)(2,1)S(1)}, bf16[16,4,32,128]{3,2,1,0:T(8,128)(2,1)}, u32[]{:S(2)}) copy-start(bf16[16,4,32,128]{3,2,1,0:T(8,128)(2,1)} %param.18) | copy-start | bytes 1572868
  27.2 84.0 %all-to-all-start = ((bf16[128,32,128]{0,2,1:T(8,128)(2,1)}), bf16[128,32,128]{0,2,1:T(8,128)(2,1)}, u32[]{:S(2)}, u32[]{:S(2)}) async-start(bf16[128,32,128]{0,2,1:T(8,128)(2,1)} %bitcast.10), calls=%async_computation | async-start | bytes 2097152 | tf_op jit(solution)/shard_map/all_to_all | solution.py:144
  31.6 1.3 copy-start.12
  31.7 1.9 copy-start.10
  33.0 0.6 copy-start.14
  33.7 3.8 %copy-start.15 = (bf16[4,128]{1,0:T(4,128)(2,1)S(1)}, bf16[4,128]{1,0:T(4,128)(2,1)}, u32[]{:S(2)}) copy-start(bf16[4,128]{1,0:T(4,128)(2,1)} %copy-done.14) | copy-start | bytes 3076
  102.7 5.9 %copy-start.1 = (bf16[4,128,8,128]{1,3,2,0:T(8,128)(2,1)}, bf16[4,128,8,128]{1,3,2,0:T(8,128)(2,1)S(1)}, u32[]{:S(2)}) copy-start(bf16[4,128,8,128]{1,3,2,0:T(8,128)(2,1)S(1)} %get-tuple-element.116) | copy-start | bytes 3145732
  108.6 198.5 %collective-permute-start.7 = (f32[128,32,128]{0,2,1:T(8,128)}, f32[128,32,128]{0,2,1:T(8,128)}, u32[]{:S(2)}, u32[]{:S(2)}) collective-permute-start(f32[128,32,128]{0,2,1:T(8,128)} %bitcast.38), channel_id=1, source_target_pairs={{2,0},{3,1},{4,2},{5,3},{6,4},{7,5},{10,8},{11,9},{12,10},{13,11},... | collective-permute-start | bytes 6291464 | tf_op jit(solution)/shard_map/ppermute | solution.py:15
  109.9 197.2 %collective-permute-start.6 = (f32[128,32,128]{0,2,1:T(8,128)}, f32[128,32,128]{0,2,1:T(8,128)}, u32[]{:S(2)}, u32[]{:S(2)}) collective-permute-start(f32[128,32,128]{0,2,1:T(8,128)} %bitcast.37), channel_id=1, source_target_pairs={{1,0},{2,1},{3,2},{4,3},{5,4},{6,5},{7,6},{9,8},{10,9},{11,10},{12... | collective-permute-start | bytes 6291464 | tf_op jit(solution)/shard_map/ppermute | solution.py:15
  111.2 151.7 %all-to-all-start.1 = ((bf16[128,32,128]{0,2,1:T(8,128)(2,1)}), bf16[128,32,128]{0,2,1:T(8,128)(2,1)S(1)}, u32[]{:S(2)}, u32[]{:S(2)}) async-start(bf16[128,32,128]{0,2,1:T(8,128)(2,1)} %bitcast.24), calls=%async_computation.1 | async-start | bytes 2097152 | tf_op jit(solution)/shard_map/all_to_all | solution.py:143
  118.6 186.4 %all-reduce.5.cloned.1.call-start = ((), (), s32[]{:S(2)}) async-start(), calls=%async_computation.2 | async-start | bytes 524288
  118.6 8.6 %copy-start.7 = (bf16[16,4,32,128]{3,1,2,0:T(4,128)(2,1)S(1)}, bf16[16,4,32,128]{3,1,2,0:T(4,128)(2,1)}, u32[]{:S(2)}) copy-start(bf16[16,4,32,128]{3,1,2,0:T(4,128)(2,1)} %copy.59) | copy-start | bytes 1572868
  118.6 8.6 %copy-start.8 = (bf16[16,4,32,128]{3,1,2,0:T(4,128)(2,1)S(1)}, bf16[16,4,32,128]{3,1,2,0:T(4,128)(2,1)}, u32[]{:S(2)}) copy-start(bf16[16,4,32,128]{3,1,2,0:T(4,128)(2,1)} %copy.60) | copy-start | bytes 1572868
  124.5 4.7 %copy-start.13 = (f32[16,128]{1,0:T(8,128)S(1)}, f32[16,128]{1,0:T(8,128)}, u32[]{:S(2)}) copy-start(f32[16,128]{1,0:T(8,128)} %copy-done.12) | copy-start | bytes 24580
  124.5 4.7 %copy-start.17 = (f32[16,4]{0,1:T(4,128)S(1)}, f32[16,4]{0,1:T(4,128)}, u32[]{:S(2)}) copy-start(f32[16,4]{0,1:T(4,128)} %param.19) | copy-start | bytes 772
  124.5 186.3 %collective-permute-start.5 = (f32[128,32,128]{0,2,1:T(8,128)}, f32[128,32,128]{0,2,1:T(8,128)}, u32[]{:S(2)}, u32[]{:S(2)}) collective-permute-start(f32[128,32,128]{0,2,1:T(8,128)} %bitcast.32), channel_id=1, source_target_pairs={{2,0},{3,1},{4,2},{5,3},{6,4},{7,5},{10,8},{11,9},{12,10},{13,11},... | collective-permute-start | bytes 6291464 | tf_op jit(solution)/shard_map/ppermute | solution.py:15
  125.9 184.8 %collective-permute-start.4 = (f32[128,32,128]{0,2,1:T(8,128)}, f32[128,32,128]{0,2,1:T(8,128)}, u32[]{:S(2)}, u32[]{:S(2)}) collective-permute-start(f32[128,32,128]{0,2,1:T(8,128)} %bitcast.31), channel_id=1, source_target_pairs={{1,0},{2,1},{3,2},{4,3},{5,4},{6,5},{7,6},{9,8},{10,9},{11,10},{12... | collective-permute-start | bytes 6291464 | tf_op jit(solution)/shard_map/ppermute | solution.py:15
  260.6 3.6 %copy-start.9 = (bf16[16,1024]{1,0:T(8,128)(2,1)S(1)}, bf16[16,1024]{1,0:T(8,128)(2,1)}, u32[]{:S(2)}) copy-start(bf16[16,1024]{1,0:T(8,128)(2,1)} %fusion.67) | copy-start | bytes 98308
  260.6 3.6 %copy-start.11 = (bf16[4,1024]{1,0:T(4,128)(2,1)S(1)}, bf16[4,1024]{1,0:T(4,128)(2,1)}, u32[]{:S(2)}) copy-start(bf16[4,1024]{1,0:T(4,128)(2,1)} %all_gather.7) | copy-start | bytes 24580
  262.9 5.2 %copy-start.18 = (u32[32]{0:T(128)S(1)}, u32[32]{0:T(128)}, u32[]{:S(2)}) copy-start(u32[32]{0:T(128)} %constant.77) | copy-start | bytes 388
  264.2 5.1 %copy-start.2 = (bf16[4,128,8,128]{1,3,2,0:T(8,128)(2,1)S(1)}, bf16[4,128,8,128]{1,3,2,0:T(8,128)(2,1)}, u32[]{:S(2)}) copy-start(bf16[4,128,8,128]{1,3,2,0:T(8,128)(2,1)} %copy-done.1) | copy-start | bytes 3145732
  265.8 2.2 copy-start.5
Sparse Core Ops, SparseCore 0:
  268.2 36.7 all-reduce.4
where the time goes:
time: 323 us; the launch traced here: 322 us
  blocking collectives  144 us (45%)
  matrix products  43.1 us (13%)
  local copies, waits for them, and re-layouts  42 us (13%)
  waiting for transfers between devices  34 us (11%)
  starting transfers between devices  31.3 us (10%)
  between operations  15.1 us (5%)
  other arithmetic  11.9 us (4%)
    all_gather x1, blocking collectives, on_device(): lax.all_gather(lifted_low, 'ctx', axis=1, tiled=True)  131 us
    unnamed x2, waiting for transfers between devices  34 us
    ppermute x8, starting transfers between devices, shifted(): lax.ppermute(value, axis, [(source, source + steps) for source in range(f...  19.5 us
    unnamed x50, local copies, waits for them, and re-layouts  13.9 us
    all_gather x1, blocking collectives, on_device(): lax.all_gather(pulled_low, 'ctx', axis=1, tiled=True)  13.2 us
    dot_general x4, matrix products, forward_one(): jnp.einsum('gqp,pd->qgd', weights_low, value_one, preferred_element_type=...  8.15 us
    all_to_all x1, starting transfers between devices, on_device(): lax.all_to_all(hidden, 'ctx', split_axis=1, concat_axis=0, tiled=True)  7.39 us
    dot_general x4, matrix products, backward_one(): jnp.einsum('gqp,qgd->pgd', weights_low, grad_one, preferred_element_type=...  6.69 us
  transfers between devices with their start and end apart: 11, of which 1 were waited for; matrix products, arithmetic and copies ran while one was open for 28% of the time, Pallas kernels for 0%

commit v1 on v0

v1 whole, which is shorter than its diff:
```python
import jax
import jax.numpy as jnp
from jax import lax
from jax.experimental import pallas as pl
from jax.experimental.pallas import tpu as pltpu
from jax.sharding import PartitionSpec as P

DOC_MAX = 256
LOW = jnp.bfloat16
WIDE = jnp.float32
far_below = -1e30


def shifted(value, axis, steps):
    count = lax.axis_size(axis)
    first, last = (max(0, -steps), min(count, count - steps))
    return lax.ppermute(value, axis, [(source, source + steps) for source in range(first, last)])


def dot(left, right, left_dim, right_dim, precision=None):
    return lax.dot_general(
        left, right, (((left_dim,), (right_dim,)), ((), ())),
        precision=precision, preferred_element_type=WIDE,
    )


def group_rows(ref, kv_count, group_size):
    rows, _, dim = ref.shape
    wide = 2 * group_size
    parts = []
    for pair in range(kv_count // 2):
        both = ref[:, pair * wide : (pair + 1) * wide, :].astype(WIDE)
        for half in range(2):
            one = both[:, half * group_size : (half + 1) * group_size, :]
            parts.append(one.reshape(rows * group_size, dim).astype(LOW))
    return parts


def lane_head(shape, group_size):
    return lax.broadcasted_iota(jnp.int32, shape, 1) % group_size


def own_terms(maps_by_rows, owner, tenants, low_rank, group_size):
    lanes = maps_by_rows.shape[1]
    same_head = lax.broadcasted_iota(jnp.int32, (group_size, lanes), 0) == lane_head(
        (group_size, lanes), group_size
    )
    span = low_rank * group_size
    total = jnp.zeros((low_rank, group_size, lanes), WIDE)
    for tenant in range(tenants):
        keep = same_head & (owner == tenant)
        block = maps_by_rows[tenant * span : (tenant + 1) * span].reshape(
            low_rank, group_size, lanes
        )
        total = total + jnp.where(keep[None], block, 0.0)
    rows = jnp.sum(total, axis=1)
    rows = jnp.concatenate([rows, rows], axis=0)
    tiles = lanes // 128
    stacked = jnp.concatenate([rows[:, c * 128 : (c + 1) * 128] for c in range(tiles)], axis=0)
    side = lax.broadcasted_iota(jnp.int32, (128, 128), 0) // group_size
    over = lax.broadcasted_iota(jnp.int32, (128, 128), 1) // group_size
    spread = dot(stacked, (side == over).astype(WIDE), 1, 0, lax.Precision.HIGHEST)
    return jnp.concatenate([spread[c * 8 : (c + 1) * 8] for c in range(tiles)], axis=1)


def pull_kernel(cot_ref, rot_ref, proj_ref, meta_ref, gh_ref, diff_ref, pulled_ref, *, kv, group, tenants, rank):
    owner = meta_ref[1:2, :]
    lanes = owner.shape[1]
    cots = group_rows(cot_ref, kv, group)
    rots = group_rows(rot_ref, kv, group)
    projs = group_rows(proj_ref, kv, group)
    on_rot = dot(jnp.concatenate(rots, axis=1), jnp.concatenate(cots, axis=1), 1, 1)
    pulled = own_terms(on_rot, owner, tenants, rank, group).astype(LOW).astype(WIDE)
    pulled_ref[...] = pulled
    same_head = lax.broadcasted_iota(jnp.int32, (group, lanes), 0) == lane_head((group, lanes), group)
    picked = []
    for tenant in range(tenants):
        keep = same_head & (owner == tenant)
        for k in range(rank):
            picked.append(jnp.where(keep, pulled[k : k + 1], 0.0))
    picked = jnp.concatenate(picked, axis=0).T.astype(LOW)
    for g in range(kv):
        diff = (projs[g].astype(WIDE) - rots[g].astype(WIDE)).astype(LOW)
        diff_ref[g] = diff
        gh_ref[g] = (cots[g].astype(WIDE) + dot(picked, diff, 1, 0)).astype(LOW)


def places(lanes, tokens, group):
    key = lax.broadcasted_iota(jnp.int32, (tokens, lanes), 0)
    query = lax.broadcasted_iota(jnp.int32, (tokens, lanes), 1) // group
    return key, key <= query


def forward_kernel(
    bias_ref, q_ref, two_ref, one_ref, own_ref, cot_ref, diff_ref, meta_ref, pulled_ref,
    weights_ref, part_ref, *, kv, group, tenants, rank, scaling,
):
    tokens = own_ref.shape[1]
    first = meta_ref[0:1, :]
    owner = meta_ref[1:2, :]
    lanes = owner.shape[1]
    key, here = places(lanes, tokens, group)
    fold_bias = jnp.where(jnp.where(here, key, key - 2 * tokens) >= first, 0.0, far_below)
    mid_bias = jnp.where(key - tokens >= first, 0.0, far_below)
    queries = group_rows(q_ref, kv, group)
    hidden = []
    for g in range(kv):
        fold = jnp.where(here, dot(own_ref[g], queries[g], 1, 1), dot(two_ref[g], queries[g], 1, 1))
        fold = fold * scaling + fold_bias
        mid = dot(one_ref[g], queries[g], 1, 1) * scaling + mid_bias
        top = jnp.maximum(jnp.max(fold, axis=0, keepdims=True), jnp.max(mid, axis=0, keepdims=True))
        fold = jnp.exp(fold - top)
        mid = jnp.exp(mid - top)
        total = jnp.sum(fold, axis=0, keepdims=True) + jnp.sum(mid, axis=0, keepdims=True)
        share = 1.0 / total
        fold = fold * share
        mid = mid * share
        weights_ref[g, 0:tokens, :] = fold
        weights_ref[g, tokens : 2 * tokens, :] = mid
        low = jnp.concatenate(
            [jnp.where(here, 0.0, fold).astype(LOW), mid.astype(LOW), jnp.where(here, fold, 0.0).astype(LOW)],
            axis=0,
        )
        values = jnp.concatenate([two_ref[kv + g], one_ref[kv + g], own_ref[kv + g]], axis=0)
        hidden.append(dot(values, low, 0, 0).astype(LOW))
    hidden = jnp.concatenate(hidden, axis=0)
    on_diff = dot(jnp.concatenate([diff_ref[g] for g in range(kv)], axis=1), hidden, 1, 0)
    lifted = own_terms(on_diff, owner, tenants, rank, group)
    row = lax.broadcasted_iota(jnp.int32, (8, lanes), 0)
    shift = jnp.zeros((8, lanes), WIDE)
    for tenant in range(tenants):
        column = jnp.zeros((8, 1), WIDE)
        for k in range(rank):
            column = jnp.where(row[:, 0:1] % rank == k, bias_ref[tenant, k], column)
        shift = jnp.where(owner == tenant, column, shift)
    lifted = (lifted + shift).astype(LOW).astype(WIDE)
    pulled = pulled_ref[...]
    span = tenants * rank
    mine = owner == lax.broadcasted_iota(jnp.int32, (span, lanes), 0) // rank
    lift_rows = jnp.where(mine, jnp.concatenate([lifted] * (span // 8), axis=0), 0.0)
    pull_rows = jnp.where(mine, jnp.concatenate([pulled] * (span // 8), axis=0), 0.0)
    head = lane_head((span, lanes), group)
    lift_all = jnp.concatenate([jnp.where(head == h, lift_rows, 0.0).astype(LOW) for h in range(group)], axis=0)
    pull_all = jnp.concatenate([jnp.where(head == h, pull_rows, 0.0).astype(LOW) for h in range(group)], axis=0)
    on_proj = dot(pull_all, hidden, 1, 1)
    on_rot = dot(lift_all, jnp.concatenate(group_rows(cot_ref, kv, group), axis=1), 1, 0) - on_proj
    dim = q_ref.shape[2]
    for g in range(kv):
        for h in range(group):
            rows, columns = slice(h * span, (h + 1) * span), slice(g * dim, (g + 1) * dim)
            part_ref[g * group + h, 0] = on_rot[rows, columns].astype(LOW)
            part_ref[g * group + h, 1] = on_proj[rows, columns].astype(LOW)


def backward_kernel(
    q_ref, gh_ref, two_ref, one_ref, own_ref, weights_ref, dq_ref, back_two_ref, back_one_ref, back_own_ref,
    *, kv, group, scaling,
):
    tokens = own_ref.shape[1]
    lanes = weights_ref.shape[2]
    dim = q_ref.shape[2]
    _, here = places(lanes, tokens, group)
    queries = group_rows(q_ref, kv, group)
    query_grads = []
    for g in range(kv):
        grads = gh_ref[g]
        fold_weights = weights_ref[g, 0:tokens, :]
        mid_weights = weights_ref[g, tokens : 2 * tokens, :]
        fold = jnp.where(here, dot(own_ref[kv + g], grads, 1, 1), dot(two_ref[kv + g], grads, 1, 1))
        mid = dot(one_ref[kv + g], grads, 1, 1)
        delta = jnp.sum(fold * fold_weights, axis=0, keepdims=True) + jnp.sum(
            mid * mid_weights, axis=0, keepdims=True
        )
        fold = fold_weights * (fold - delta)
        mid = mid_weights * (mid - delta)
        score_grad = jnp.concatenate(
            [jnp.where(here, 0.0, fold).astype(LOW), mid.astype(LOW), jnp.where(here, fold, 0.0).astype(LOW)],
            axis=0,
        )
        low = jnp.concatenate(
            [
                jnp.where(here, 0.0, fold_weights).astype(LOW),
                mid_weights.astype(LOW),
                jnp.where(here, fold_weights, 0.0).astype(LOW),
            ],
            axis=0,
        )
        keys = jnp.concatenate([two_ref[g], one_ref[g], own_ref[g]], axis=0)
        key_grad = dot(score_grad, queries[g], 1, 0) * scaling
        value_grad = dot(low, grads, 1, 0)
        for place, grad in ((g, key_grad), (kv + g, value_grad)):
            back_two_ref[place] = grad[0:tokens].astype(LOW)
            back_one_ref[place] = grad[tokens : 2 * tokens].astype(LOW)
            back_own_ref[place] = grad[2 * tokens :]
        query_grad = dot(keys, score_grad, 0, 0) * scaling
        query_grads.append(query_grad.T.reshape(tokens, group, dim))
        if g % 2 == 1:
            both = jnp.concatenate(query_grads[-2:], axis=1).astype(LOW)
            dq_ref[:, (g - 1) * group : (g + 1) * group, :] = both


def on_device(
    query_rows, key_rows, value_matrix, cotangent, rotation, projection, shift_bias, doc_starts, tenant_ids,
):
    queries = query_rows[0]
    upstream = cotangent[0]
    tokens, heads, dim = queries.shape
    kv = key_rows.shape[2]
    group = heads // kv
    scaling = dim ** (-0.5)
    tenants, rank = rotation.shape[0], rotation.shape[1]
    lanes = tokens * group
    ctx = lax.axis_size("ctx")
    rep = lax.axis_size("rep")
    assert 2 * tokens == DOC_MAX

    own = jnp.moveaxis(jnp.concatenate([key_rows[0], value_matrix[0]], axis=1), 1, 0)
    one = shifted(own, "ctx", 1)
    two = shifted(own, "ctx", 2)

    row_first = lax.axis_index("ctx") * tokens
    starts = lax.dynamic_slice_in_dim(doc_starts[0], row_first, tokens, 0) - row_first
    owners = lax.dynamic_slice_in_dim(tenant_ids[0], row_first, tokens, 0)
    meta = jnp.repeat(jnp.stack([starts, owners]), group, axis=1)
    rot = rotation.reshape(tenants * rank, heads, dim)
    proj = projection.reshape(tenants * rank, heads, dim)
    params = pltpu.CompilerParams(vmem_limit_bytes=50 * 1024 * 1024)
    sizes = dict(kv=kv, group=group)

    def call(body, outs, flops, moved, specs=None, **fixed):
        def run(*operands):
            return pl.pallas_call(
                lambda *refs: body(*refs, **fixed),
                out_shape=[jax.ShapeDtypeStruct(*out) for out in outs],
                in_specs=specs or [pl.BlockSpec(memory_space=pltpu.VMEM)] * len(operands),
                out_specs=[pl.BlockSpec(memory_space=pltpu.VMEM)] * len(outs),
                compiler_params=params,
                name=body.__name__,
                cost_estimate=pl.CostEstimate(flops=flops, bytes_accessed=moved, transcendentals=0),
            )(*operands)

        return run

    grad_hidden, diff, pulled = call(
        pull_kernel,
        [((kv, lanes, dim), LOW), ((kv, tenants * rank * group, dim), LOW), ((8, lanes), WIDE)],
        2 * 2**30, 4 * 2**20, tenants=tenants, rank=rank, **sizes,
    )(upstream, rot, proj, meta)
    weights, part = call(
        forward_kernel,
        [((kv, 2 * tokens, lanes), WIDE), ((heads, 2, tenants * rank, dim), LOW)],
        4 * 2**30, 10 * 2**20,
        [pl.BlockSpec(memory_space=pltpu.SMEM)] + [pl.BlockSpec(memory_space=pltpu.VMEM)] * 8,
        tenants=tenants, rank=rank, scaling=scaling, **sizes,
    )(shift_bias, queries, two, one, own, upstream, diff, meta, pulled)
    gathered = lax.all_to_all(part, "ctx", split_axis=0, concat_axis=0, tiled=True)
    d_queries, back_two, back_one, back_own = call(
        backward_kernel,
        [((tokens, heads, dim), LOW), (own.shape, LOW), (own.shape, LOW), (own.shape, WIDE)],
        4 * 2**30, 10 * 2**20, scaling=scaling, **sizes,
    )(queries, grad_hidden, two, one, own, weights)
    from_one = shifted(back_one, "ctx", -1)
    from_two = shifted(back_two, "ctx", -2)

    here = heads // ctx
    by_heads = gathered.reshape(ctx, here, 2, rep, tenants * rank // rep, dim).astype(WIDE).sum(axis=0)
    by_rep = jnp.moveaxis(by_heads.astype(LOW), 2, 0)
    by_rep = lax.all_to_all(by_rep, "rep", split_axis=0, concat_axis=0, tiled=True)
    summed = by_rep.astype(WIDE).sum(axis=0).reshape(here, 2, tenants // rep, rank, dim)
    grads = jnp.moveaxis(summed, 0, 3)
    back = (back_own + from_one.astype(WIDE) + from_two.astype(WIDE)).astype(LOW)
    d_keys = jnp.moveaxis(back[:kv], 0, 1)
    d_values = jnp.moveaxis(back[kv:], 0, 1)
    return (d_queries[None], d_keys[None], d_values[None], grads[0], grads[1])


def solution(mesh):
    rows = P("rep", "ctx", None, None)
    in_specs = (rows, rows, rows, rows, P(), P(), P(), P("rep", None), P("rep", None))
    tenant_rows = P("rep", None, "ctx", None)
    out_specs = (rows, rows, rows, tenant_rows, tenant_rows)
    return jax.shard_map(
        on_device, mesh=mesh, in_specs=in_specs, out_specs=out_specs, check_vma=False
    )
```

time: 323 us -> 65.2 us (0.20)
  blocking collectives: 144 us -> 0 us
  matrix products: 43.1 us -> 0 us
  local copies, waits for them, and re-layouts: 42 us -> 8.24 us
  Pallas kernels: 0 us -> 16.7 us
  waiting for transfers between devices: 34 us -> 18.2 us
  between operations: 15.1 us -> 0.78 us
  starting transfers between devices: 31.3 us -> 18.5 us
  other arithmetic: 11.9 us -> 2.23 us
    all_gather x2 -> x0, blocking collectives: 144 us -> none  [the longest x1 131 us: on_device(): lax.all_gather(lifted_low, 'ctx', axis=1, tiled=True)]
    dot_general x34 -> x0, matrix products: 43.1 us -> none  [the longest x4 8.15 us: forward_one(): jnp.einsum('gqp,pd->qgd', weights_low, value_one, preferred_element_type=...]
    unnamed x2 -> x0, waiting for transfers between devices: 34 us -> none
    pallas_call x0 -> x3, Pallas kernels: none -> 16.7 us  [run(): pl.pallas_call(lambda *refs: body(*refs, **fixed), out_shape=[jax.ShapeDt...]
    ppermute x8 -> x4, waiting for transfers between devices: 0.02 us -> 13.8 us  [shifted(): lax.ppermute(value, axis, [(source, source + steps) for source in range(f...]
    slice x3 -> x0, local copies, waits for them, and re-layouts: 11.7 us -> none  [the longest x1 5.86 us: on_device(): own_dk = window_dk[reach * tokens_here:]]
    ppermute x8 -> x4, starting transfers between devices: 19.5 us -> 9.35 us  [shifted(): lax.ppermute(value, axis, [(source, source + steps) for source in range(f...]
    unnamed x50 -> x11, local copies, waits for them, and re-layouts: 13.9 us -> 5.58 us
  transfers between devices with their start and end apart: 11 -> 6, of which waited for: 1 -> 3; matrix products, arithmetic and copies ran while one was open for 28% -> 5% of each run, Pallas kernels for 0% -> 14%
where the time goes in v1:
time: 65.2 us; the launch traced here: 64.6 us
  starting transfers between devices  18.5 us (28%)
  waiting for transfers between devices  18.2 us (28%)
  Pallas kernels  16.7 us (26%)
  local copies, waits for them, and re-layouts  8.24 us (13%)
  other arithmetic  2.23 us (3%)
  between operations  0.78 us (1%)
    pallas_call x3, Pallas kernels, run(): pl.pallas_call(lambda *refs: body(*refs, **fixed), out_shape=[jax.ShapeDt...  16.7 us
    ppermute x4, waiting for transfers between devices, shifted(): lax.ppermute(value, axis, [(source, source + steps) for source in range(f...  13.8 us
    ppermute x4, starting transfers between devices, shifted(): lax.ppermute(value, axis, [(source, source + steps) for source in range(f...  9.35 us
    unnamed x11, local copies, waits for them, and re-layouts  5.58 us
    all_to_all x1, starting transfers between devices, on_device(): lax.all_to_all(by_rep, 'rep', split_axis=0, concat_axis=0, tiled=True)  4.87 us
    all_to_all x1, waiting for transfers between devices, on_device(): lax.all_to_all(by_rep, 'rep', split_axis=0, concat_axis=0, tiled=True)  4.38 us
    all_to_all x1, starting transfers between devices, on_device(): lax.all_to_all(part, 'ctx', split_axis=0, concat_axis=0, tiled=True)  4.23 us
    reduce_sum x1, other arithmetic, on_device(): gathered.reshape(ctx, here, 2, rep, tenants * rank // rep, dim).astype(WIDE)  1.41 us
  transfers between devices with their start and end apart: 6, of which 3 were waited for; matrix products, arithmetic and copies ran while one was open for 5% of the time, Pallas kernels for 14%

profile of v1, /device:TPU:0, one launch (start us, length us, event | category | flops | bytes accessed | tf_op | source)
XLA Modules:
  0.0 64.6 jit_solution(14992863161849999199)
XLA Ops:
  0.6 0.0 copy-start.1
  0.6 1.1 %copy_bitcast_fusion = (bf16[128,4,128]{2,0,1:T(8,128)(2,1)S(1)}, bf16[128,4,128]{2,0,1:T(8,128)(2,1)S(1)}) fusion(bf16[1,128,4,128]{3,2,1,0:T(4,128)(2,1)} %param.11, bf16[1,128,4,128]{3,2,1,0:T(4,128)(2,1)} %param.10), kind=kLoop, calls=%fused_computation.5 | loop fusion | bytes 524288 | tf_op jit(solution)/shard_map/squeeze | solution.py:217
  1.8 2.4 %collective-permute-start.1 = (bf16[8,128,128]{2,1,0:T(8,128)(2,1)S(1)}, bf16[8,128,128]{2,1,0:T(8,128)(2,1)S(1)}, u32[]{:S(2)}, u32[]{:S(2)}) collective-permute-start(bf16[8,128,128]{2,1,0:T(8,128)(2,1)S(1)} %maximum_bitcast_fusion.refs_4_), channel_id=1, source_target_pairs={{0,1},{1,2},{2,3},{3,4},{4,5},{5,6},{6,7},{8,9},{9,10},{10,11},{11... | collective-permute-start | bytes 786440 | tf_op jit(solution)/shard_map/ppermute | solution.py:17
  4.2 4.4 %collective-permute-start = (bf16[8,128,128]{2,1,0:T(8,128)(2,1)S(1)}, bf16[8,128,128]{2,1,0:T(8,128)(2,1)S(1)}, u32[]{:S(2)}, u32[]{:S(2)}) collective-permute-start(bf16[8,128,128]{2,1,0:T(8,128)(2,1)S(1)} %maximum_bitcast_fusion.refs_4_), channel_id=1, source_target_pairs={{0,2},{1,3},{2,4},{3,5},{4,6},{5,7},{8,10},{9,11},{10,12},{11,13},... | collective-permute-start | bytes 786440 | tf_op jit(solution)/shard_map/ppermute | solution.py:17
  8.6 0.8 %copy.31.refs_0_ = f32[16,4]{1,0:T(8,128)S(1)} copy(f32[16,4]{0,1:T(4,128)} %param.15) | data formatting | bytes 512 | tf_op args[6]
  9.3 0.7 %dynamic-slice_subtract_fusion = (s32[1,128]{1,0:T(1,128)S(1)}, s32[1,128]{1,0:T(1,128)S(1)}) fusion(s32[1,1024]{1,0:T(1,128)} %param.16, s32[]{:T(128)S(6)} %select_n.4, s32[]{:T(128)S(6)} %mul.3, s32[1,1024]{1,0:T(1,128)} %param.17), kind=kLoop, calls=%fused_computation.11 | loop fusion | flops 128 | bytes 2056 | tf_op jit(solution)/shard_map/sub | solution.py:222
  10.0 0.1 broadcast_in_dim.12
  10.1 0.1 reshape.30.refs_3_.refs_7_
  10.2 0.0 copy-start
  10.2 1.2 %copy-done = bf16[1,128,32,128]{3,2,1,0:T(8,128)(2,1)S(1)} copy-done((bf16[1,128,32,128]{3,2,1,0:T(8,128)(2,1)S(1)}, bf16[1,128,32,128]{3,2,1,0:T(8,128)(2,1)}, u32[]{:S(2)}) %copy-start) | copy-done | bytes 1048600
  11.5 0.0 copy-start.2
  11.5 1.0 %copy-done.2 = bf16[16,4,32,128]{3,2,1,0:T(8,128)(2,1)S(1)} copy-done((bf16[16,4,32,128]{3,2,1,0:T(8,128)(2,1)S(1)}, bf16[16,4,32,128]{3,2,1,0:T(8,128)(2,1)}, u32[]{:S(2)}) %copy-start.2) | copy-done | bytes 524312
  12.5 0.0 copy-start.3
  12.5 1.0 %copy-done.3 = bf16[16,4,32,128]{3,2,1,0:T(8,128)(2,1)S(1)} copy-done((bf16[16,4,32,128]{3,2,1,0:T(8,128)(2,1)S(1)}, bf16[16,4,32,128]{3,2,1,0:T(8,128)(2,1)}, u32[]{:S(2)}) %copy-start.3) | copy-done | bytes 524312
  13.5 2.3 %pull_kernel.1 = (bf16[4,1024,128]{2,1,0:T(8,128)(2,1)S(1)}, bf16[4,512,128]{2,1,0:T(8,128)(2,1)S(1)}, f32[8,1024]{1,0:T(8,128)S(1)}) custom-call(bf16[128,32,128]{2,1,0:T(8,128)(2,1)S(1)} %bitcast.30, bf16[64,32,128]{2,1,0:T(8,128)(2,1)S(1)} %bitcast.33, bf16[64,32,128]{2,1,0:T(8,128)(2,1)S(1)} %bitcast.34, s32[2,1024]{1,0:T(2,128)S(1)} %reshape.30.refs_3_.refs_7_), custom_call_target="tpu_custom_call" | custom-call | flops 2147483648 | bytes 4194304 | tf_op jit(solution)/shard_map/pull_kernel/pallas_call | solution.py:232
  15.8 0.0 collective-permute-done.1.refs_3_
  15.9 0.0 collective-permute-done.refs_2_
  15.9 0.0 copy-done.1
  15.9 7.4 %forward_kernel.1 = (f32[4,256,1024]{2,1,0:T(8,128)}, bf16[32,2,64,128]{3,2,1,0:T(8,128)(2,1)}) custom-call(f32[16,4]{1,0:T(8,128)S(1)} %copy.31.refs_0_, bf16[128,32,128]{2,1,0:T(8,128)(2,1)S(1)} %bitcast.31, bf16[8,128,128]{2,1,0:T(8,128)(2,1)S(1)} %collective-permute-done.refs_2_, bf16[8,128,128]{2,1,0:T(8,128)(2,1)S(1)} %collective-permute-done.1.refs_3_, ...), custom_call_target="tpu_custom_call" | custom-call | flops 4294967296 | bytes 10485760 | tf_op jit(solution)/shard_map/forward_kernel/pallas_call | solution.py:232
  23.3 4.2 %all-to-all-start = ((bf16[32,2,64,128]{3,2,1,0:T(8,128)(2,1)}), bf16[32,2,64,128]{3,2,1,0:T(8,128)(2,1)}, u32[]{:S(2)}, u32[]{:S(2)}) async-start(bf16[32,2,64,128]{3,2,1,0:T(8,128)(2,1)} %get-tuple-element.22), calls=%async_computation | async-start | bytes 2097152 | tf_op jit(solution)/shard_map/all_to_all | solution.py:256
  27.6 7.0 %backward_kernel.1 = (bf16[128,32,128]{2,1,0:T(8,128)(2,1)}, bf16[8,128,128]{2,1,0:T(8,128)(2,1)S(1)}, bf16[8,128,128]{2,1,0:T(8,128)(2,1)S(1)}, f32[8,128,128]{2,1,0:T(8,128)S(1)}) custom-call(bf16[128,32,128]{2,1,0:T(8,128)(2,1)S(1)} %bitcast.32, bf16[4,1024,128]{2,1,0:T(8,128)(2,1)S(1)} %get-tuple-element.14.refs_1_, ...), custom_call_target="tpu_custom_call" | custom-call | flops 4294967296 | bytes 10485760 | tf_op jit(solution)/shard_map/backward_kernel/pallas_call | solution.py:232
  34.5 1.3 %collective-permute-start.2 = (bf16[8,128,128]{2,1,0:T(8,128)(2,1)S(1)}, bf16[8,128,128]{2,1,0:T(8,128)(2,1)S(1)}, u32[]{:S(2)}, u32[]{:S(2)}) collective-permute-start(bf16[8,128,128]{2,1,0:T(8,128)(2,1)S(1)} %get-tuple-element.20), channel_id=1, source_target_pairs={{1,0},{2,1},{3,2},{4,3},{5,4},{6,5},{7,6},{9,8},{10,9},{11,10},{12... | collective-permute-start | bytes 786440 | tf_op jit(solution)/shard_map/ppermute | solution.py:17
  35.8 1.3 %collective-permute-start.3 = (bf16[8,128,128]{2,1,0:T(8,128)(2,1)S(1)}, bf16[8,128,128]{2,1,0:T(8,128)(2,1)S(1)}, u32[]{:S(2)}, u32[]{:S(2)}) collective-permute-start(bf16[8,128,128]{2,1,0:T(8,128)(2,1)S(1)} %get-tuple-element.21), channel_id=1, source_target_pairs={{2,0},{3,1},{4,2},{5,3},{6,4},{7,5},{10,8},{11,9},{12,10},{13,11},... | collective-permute-start | bytes 786440 | tf_op jit(solution)/shard_map/ppermute | solution.py:17
  37.1 1.6 %collective-permute-done.2 = bf16[8,128,128]{2,1,0:T(8,128)(2,1)S(1)} collective-permute-done((bf16[8,128,128]{2,1,0:T(8,128)(2,1)S(1)}, bf16[8,128,128]{2,1,0:T(8,128)(2,1)S(1)}, u32[]{:S(2)}, u32[]{:S(2)}) %collective-permute-start.2) | collective-permute-done | bytes 262176 | tf_op jit(solution)/shard_map/ppermute | solution.py:17
  38.7 12.2 %collective-permute-done.3 = bf16[8,128,128]{2,1,0:T(8,128)(2,1)S(1)} collective-permute-done((bf16[8,128,128]{2,1,0:T(8,128)(2,1)S(1)}, bf16[8,128,128]{2,1,0:T(8,128)(2,1)S(1)}, u32[]{:S(2)}, u32[]{:S(2)}) %collective-permute-start.3) | collective-permute-done | bytes 262176 | tf_op jit(solution)/shard_map/ppermute | solution.py:17
  50.9 0.1 add_convert_fusion
  51.0 0.0 all-to-all-done
  51.0 1.4 %reduce_sum.21 = bf16[4,2,4,16,128]{4,3,2,1,0:T(8,128)(2,1)S(1)} reduce(bf16[8,4,2,4,16,128]{5,4,3,2,1,0:T(8,128)(2,1)} %bitcast.12, bf16[]{:T(256)} %constant.14.clone.1), dimensions={0}, to_apply=%region_0.0 | reduce | flops 458752 | bytes 1179650 | tf_op jit(solution)/shard_map/reduce_sum | solution.py:266
  52.4 0.7 %copy.32 = bf16[4,4,2,16,128]{4,3,2,1,0:T(8,128)(2,1)} copy(bf16[4,4,2,16,128]{4,3,0,2,1:T(8,128)(2,1)S(1)} %bitcast.35) | data formatting | bytes 262144 | tf_op jit(solution)/shard_map/transpose | solution.py:267
  53.1 4.9 %all-to-all-start.1 = ((bf16[4,4,2,16,128]{4,3,2,1,0:T(8,128)(2,1)}), bf16[4,4,2,16,128]{4,3,2,1,0:T(8,128)(2,1)S(1)}, u32[]{:S(2)}, u32[]{:S(2)}) async-start(bf16[4,4,2,16,128]{4,3,2,1,0:T(8,128)(2,1)} %copy.32), calls=%async_computation.1 | async-start | bytes 262144 | tf_op jit(solution)/shard_map/all_to_all | solution.py:268
  58.0 0.8 %copy.35 = bf16[1,128,4,128]{3,2,1,0:T(4,128)(2,1)} copy(bf16[1,128,4,128]{3,1,2,0:T(8,128)(2,1)S(1)} %get-tuple-element.43) | data formatting | bytes 262144
  58.8 0.8 %copy.34 = bf16[1,128,4,128]{3,2,1,0:T(4,128)(2,1)} copy(bf16[1,128,4,128]{3,1,2,0:T(8,128)(2,1)S(1)} %get-tuple-element.44) | data formatting | bytes 262144
  59.5 4.4 %all-to-all-done.1 = bf16[4,4,2,16,128]{4,3,2,1,0:T(8,128)(2,1)S(1)} async-done(((bf16[4,4,2,16,128]{4,3,2,1,0:T(8,128)(2,1)}), bf16[4,4,2,16,128]{4,3,2,1,0:T(8,128)(2,1)S(1)}, u32[]{:S(2)}, u32[]{:S(2)}) %all-to-all-start.1) | async-done | bytes 131104 | tf_op jit(solution)/shard_map/all_to_all | solution.py:268
  64.0 0.6 slice_bitcast_fusion.2
  (5 shorter events, 0.1 us)
Async XLA Ops:
  0.6 15.2 %copy-start.1 = (bf16[1,128,32,128]{3,2,1,0:T(8,128)(2,1)S(1)}, bf16[1,128,32,128]{3,2,1,0:T(8,128)(2,1)}, u32[]{:S(2)}) copy-start(bf16[1,128,32,128]{3,2,1,0:T(8,128)(2,1)} %param.9) | copy-start | bytes 3145732
  1.8 14.1 %collective-permute-start.1 = (bf16[8,128,128]{2,1,0:T(8,128)(2,1)S(1)}, bf16[8,128,128]{2,1,0:T(8,128)(2,1)S(1)}, u32[]{:S(2)}, u32[]{:S(2)}) collective-permute-start(bf16[8,128,128]{2,1,0:T(8,128)(2,1)S(1)} %maximum_bitcast_fusion.refs_4_), channel_id=1, source_target_pairs={{0,1},{1,2},{2,3},{3,4},{4,5},{5,6},{6,7},{8,9},{9,10},{10,11},{11... | collective-permute-start | bytes 786440 | tf_op jit(solution)/shard_map/ppermute | solution.py:17
  4.2 11.7 %collective-permute-start = (bf16[8,128,128]{2,1,0:T(8,128)(2,1)S(1)}, bf16[8,128,128]{2,1,0:T(8,128)(2,1)S(1)}, u32[]{:S(2)}, u32[]{:S(2)}) collective-permute-start(bf16[8,128,128]{2,1,0:T(8,128)(2,1)S(1)} %maximum_bitcast_fusion.refs_4_), channel_id=1, source_target_pairs={{0,2},{1,3},{2,4},{3,5},{4,6},{5,7},{8,10},{9,11},{10,12},{11,13},... | collective-permute-start | bytes 786440 | tf_op jit(solution)/shard_map/ppermute | solution.py:17
  10.2 1.2 %copy-start = (bf16[1,128,32,128]{3,2,1,0:T(8,128)(2,1)S(1)}, bf16[1,128,32,128]{3,2,1,0:T(8,128)(2,1)}, u32[]{:S(2)}) copy-start(bf16[1,128,32,128]{3,2,1,0:T(8,128)(2,1)} %param.12) | copy-start | bytes 3145732
  11.5 1.0 %copy-start.2 = (bf16[16,4,32,128]{3,2,1,0:T(8,128)(2,1)S(1)}, bf16[16,4,32,128]{3,2,1,0:T(8,128)(2,1)}, u32[]{:S(2)}) copy-start(bf16[16,4,32,128]{3,2,1,0:T(8,128)(2,1)} %param.13) | copy-start | bytes 1572868
  12.5 1.0 %copy-start.3 = (bf16[16,4,32,128]{3,2,1,0:T(8,128)(2,1)S(1)}, bf16[16,4,32,128]{3,2,1,0:T(8,128)(2,1)}, u32[]{:S(2)}) copy-start(bf16[16,4,32,128]{3,2,1,0:T(8,128)(2,1)} %param.14) | copy-start | bytes 1572868
  23.3 27.7 %all-to-all-start = ((bf16[32,2,64,128]{3,2,1,0:T(8,128)(2,1)}), bf16[32,2,64,128]{3,2,1,0:T(8,128)(2,1)}, u32[]{:S(2)}, u32[]{:S(2)}) async-start(bf16[32,2,64,128]{3,2,1,0:T(8,128)(2,1)} %get-tuple-element.22), calls=%async_computation | async-start | bytes 2097152 | tf_op jit(solution)/shard_map/all_to_all | solution.py:256
  34.5 4.2 %collective-permute-start.2 = (bf16[8,128,128]{2,1,0:T(8,128)(2,1)S(1)}, bf16[8,128,128]{2,1,0:T(8,128)(2,1)S(1)}, u32[]{:S(2)}, u32[]{:S(2)}) collective-permute-start(bf16[8,128,128]{2,1,0:T(8,128)(2,1)S(1)} %get-tuple-element.20), channel_id=1, source_target_pairs={{1,0},{2,1},{3,2},{4,3},{5,4},{6,5},{7,6},{9,8},{10,9},{11,10},{12... | collective-permute-start | bytes 786440 | tf_op jit(solution)/shard_map/ppermute | solution.py:17
  35.8 15.1 %collective-permute-start.3 = (bf16[8,128,128]{2,1,0:T(8,128)(2,1)S(1)}, bf16[8,128,128]{2,1,0:T(8,128)(2,1)S(1)}, u32[]{:S(2)}, u32[]{:S(2)}) collective-permute-start(bf16[8,128,128]{2,1,0:T(8,128)(2,1)S(1)} %get-tuple-element.21), channel_id=1, source_target_pairs={{2,0},{3,1},{4,2},{5,3},{6,4},{7,5},{10,8},{11,9},{12,10},{13,11},... | collective-permute-start | bytes 786440 | tf_op jit(solution)/shard_map/ppermute | solution.py:17
  53.1 10.8 %all-to-all-start.1 = ((bf16[4,4,2,16,128]{4,3,2,1,0:T(8,128)(2,1)}), bf16[4,4,2,16,128]{4,3,2,1,0:T(8,128)(2,1)S(1)}, u32[]{:S(2)}, u32[]{:S(2)}) async-start(bf16[4,4,2,16,128]{4,3,2,1,0:T(8,128)(2,1)} %copy.32), calls=%async_computation.1 | async-start | bytes 262144 | tf_op jit(solution)/shard_map/all_to_all | solution.py:268

commit v2 on v1

--- a/solution.py
+++ b/solution.py
@@ -63,12 +63,36 @@
     return jnp.concatenate([spread[c * 8 : (c + 1) * 8] for c in range(tiles)], axis=1)
 
 
-def pull_kernel(cot_ref, rot_ref, proj_ref, meta_ref, gh_ref, diff_ref, pulled_ref, *, kv, group, tenants, rank):
-    owner = meta_ref[1:2, :]
-    lanes = owner.shape[1]
+def pull_kernel(
+    starts_ref, owners_ref, cot_hbm, rot_hbm, proj_hbm, cots_ref, gh_ref, diff_ref, pulled_ref, meta_ref,
+    cot_ref, rot_ref, proj_ref, sems, *, kv, group, tenants, rank,
+):
+    copies = [
+        pltpu.make_async_copy(source, target, sems.at[at])
+        for at, (source, target) in enumerate(
+            ((cot_hbm, cot_ref), (rot_hbm, rot_ref), (proj_hbm, proj_ref))
+        )
+    ]
+    for copy in copies:
+        copy.start()
+    lanes = meta_ref.shape[1]
+    tokens = lanes // group
+    row_first = lax.axis_index("ctx") * tokens
+    mine = pl.ds(pl.multiple_of(row_first, tokens), tokens)
+    row = lax.broadcasted_iota(jnp.int32, (8, tokens), 0)
+    both = jnp.where(row == 0, starts_ref[:, mine] - row_first, owners_ref[:, mine]).astype(WIDE)
+    repeat = lax.broadcasted_iota(jnp.int32, (tokens, lanes), 0) == (
+        lax.broadcasted_iota(jnp.int32, (tokens, lanes), 1) // group
+    )
+    meta = dot(both, repeat.astype(WIDE), 1, 0, lax.Precision.HIGHEST).astype(jnp.int32)
+    meta_ref[...] = meta
+    owner = meta[1:2, :]
+    copies[0].wait()
     cots = group_rows(cot_ref, kv, group)
+    for g in range(kv):
+        cots_ref[g] = cots[g]
+    copies[1].wait()
     rots = group_rows(rot_ref, kv, group)
-    projs = group_rows(proj_ref, kv, group)
     on_rot = dot(jnp.concatenate(rots, axis=1), jnp.concatenate(cots, axis=1), 1, 1)
     pulled = own_terms(on_rot, owner, tenants, rank, group).astype(LOW).astype(WIDE)
     pulled_ref[...] = pulled
@@ -79,6 +103,8 @@
         for k in range(rank):
             picked.append(jnp.where(keep, pulled[k : k + 1], 0.0))
     picked = jnp.concatenate(picked, axis=0).T.astype(LOW)
+    copies[2].wait()
+    projs = group_rows(proj_ref, kv, group)
     for g in range(kv):
         diff = (projs[g].astype(WIDE) - rots[g].astype(WIDE)).astype(LOW)
         diff_ref[g] = diff
@@ -92,8 +118,8 @@
 
 
 def forward_kernel(
-    bias_ref, q_ref, two_ref, one_ref, own_ref, cot_ref, diff_ref, meta_ref, pulled_ref,
-    weights_ref, part_ref, *, kv, group, tenants, rank, scaling,
+    bias_ref, q_ref, two_ref, one_ref, own_ref, cots_ref, diff_ref, meta_ref, pulled_ref,
+    weights_ref, part_ref, *, kv, group, tenants, rank, scaling, rep, owned,
 ):
     tokens = own_ref.shape[1]
     first = meta_ref[0:1, :]
@@ -126,13 +152,9 @@
     hidden = jnp.concatenate(hidden, axis=0)
     on_diff = dot(jnp.concatenate([diff_ref[g] for g in range(kv)], axis=1), hidden, 1, 0)
     lifted = own_terms(on_diff, owner, tenants, rank, group)
-    row = lax.broadcasted_iota(jnp.int32, (8, lanes), 0)
-    shift = jnp.zeros((8, lanes), WIDE)
-    for tenant in range(tenants):
-        column = jnp.zeros((8, 1), WIDE)
-        for k in range(rank):
-            column = jnp.where(row[:, 0:1] % rank == k, bias_ref[tenant, k], column)
-        shift = jnp.where(owner == tenant, column, shift)
+    one_hot = (owner == lax.broadcasted_iota(jnp.int32, (tenants, lanes), 0)).astype(WIDE)
+    bias = jnp.concatenate([bias_ref[...]] * (8 // rank), axis=0)
+    shift = dot(bias, one_hot, 1, 0, lax.Precision.HIGHEST)
     lifted = (lifted + shift).astype(LOW).astype(WIDE)
     pulled = pulled_ref[...]
     span = tenants * rank
@@ -143,13 +165,16 @@
     lift_all = jnp.concatenate([jnp.where(head == h, lift_rows, 0.0).astype(LOW) for h in range(group)], axis=0)
     pull_all = jnp.concatenate([jnp.where(head == h, pull_rows, 0.0).astype(LOW) for h in range(group)], axis=0)
     on_proj = dot(pull_all, hidden, 1, 1)
-    on_rot = dot(lift_all, jnp.concatenate(group_rows(cot_ref, kv, group), axis=1), 1, 0) - on_proj
+    on_rot = dot(lift_all, jnp.concatenate([cots_ref[g] for g in range(kv)], axis=1), 1, 0) - on_proj
     dim = q_ref.shape[2]
     for g in range(kv):
         for h in range(group):
-            rows, columns = slice(h * span, (h + 1) * span), slice(g * dim, (g + 1) * dim)
-            part_ref[g * group + h, 0] = on_rot[rows, columns].astype(LOW)
-            part_ref[g * group + h, 1] = on_proj[rows, columns].astype(LOW)
+            device, place = (g * group + h) // owned, (g * group + h) % owned
+            columns = slice(g * dim, (g + 1) * dim)
+            for r in range(rep):
+                rows = slice(h * span + r * span // rep, h * span + (r + 1) * span // rep)
+                part_ref[device, r, place, 0] = on_rot[rows, columns].astype(LOW)
+                part_ref[device, r, place, 1] = on_proj[rows, columns].astype(LOW)
 
 
 def backward_kernel(
@@ -218,41 +243,49 @@
     one = shifted(own, "ctx", 1)
     two = shifted(own, "ctx", 2)
 
-    row_first = lax.axis_index("ctx") * tokens
-    starts = lax.dynamic_slice_in_dim(doc_starts[0], row_first, tokens, 0) - row_first
-    owners = lax.dynamic_slice_in_dim(tenant_ids[0], row_first, tokens, 0)
-    meta = jnp.repeat(jnp.stack([starts, owners]), group, axis=1)
     rot = rotation.reshape(tenants * rank, heads, dim)
     proj = projection.reshape(tenants * rank, heads, dim)
-    params = pltpu.CompilerParams(vmem_limit_bytes=50 * 1024 * 1024)
     sizes = dict(kv=kv, group=group)
-
-    def call(body, outs, flops, moved, specs=None, **fixed):
+    vmem = pl.BlockSpec(memory_space=pltpu.VMEM)
+    hbm = pl.BlockSpec(memory_space=pltpu.HBM)
+
+    def call(body, outs, flops, moved, specs=None, scratch=(), limit=24, **fixed):
         def run(*operands):
             return pl.pallas_call(
                 lambda *refs: body(*refs, **fixed),
                 out_shape=[jax.ShapeDtypeStruct(*out) for out in outs],
-                in_specs=specs or [pl.BlockSpec(memory_space=pltpu.VMEM)] * len(operands),
-                out_specs=[pl.BlockSpec(memory_space=pltpu.VMEM)] * len(outs),
-                compiler_params=params,
+                in_specs=specs or [vmem] * len(operands),
+                out_specs=[vmem] * len(outs),
+                scratch_shapes=scratch,
+                compiler_params=pltpu.CompilerParams(vmem_limit_bytes=limit * 2**20),
                 name=body.__name__,
                 cost_estimate=pl.CostEstimate(flops=flops, bytes_accessed=moved, transcendentals=0),
             )(*operands)
 
         return run
 
-    grad_hidden, diff, pulled = call(
+    span = tenants * rank
+    in_kernel = rep if span // rep % 16 == 0 else 1
+    cots, grad_hidden, diff, pulled, meta = call(
         pull_kernel,
-        [((kv, lanes, dim), LOW), ((kv, tenants * rank * group, dim), LOW), ((8, lanes), WIDE)],
-        2 * 2**30, 4 * 2**20, tenants=tenants, rank=rank, **sizes,
-    )(upstream, rot, proj, meta)
+        [
+            ((kv, lanes, dim), LOW), ((kv, lanes, dim), LOW), ((kv, span * group, dim), LOW),
+            ((8, lanes), WIDE), ((8, lanes), jnp.int32),
+        ],
+        2 * 2**30, 4 * 2**20, [vmem, vmem, hbm, hbm, hbm],
+        [
+            pltpu.VMEM((tokens, heads, dim), LOW), pltpu.VMEM((span, heads, dim), LOW),
+            pltpu.VMEM((span, heads, dim), LOW), pltpu.SemaphoreType.DMA((3,)),
+        ],
+        limit=53, tenants=tenants, rank=rank, **sizes,
+    )(doc_starts, tenant_ids, upstream, rot, proj)
+    here = heads // ctx
     weights, part = call(
         forward_kernel,
-        [((kv, 2 * tokens, lanes), WIDE), ((heads, 2, tenants * rank, dim), LOW)],
+        [((kv, 2 * tokens, lanes), WIDE), ((ctx, in_kernel, here, 2, span // in_kernel, dim), LOW)],
         4 * 2**30, 10 * 2**20,
-        [pl.BlockSpec(memory_space=pltpu.SMEM)] + [pl.BlockSpec(memory_space=pltpu.VMEM)] * 8,
-        tenants=tenants, rank=rank, scaling=scaling, **sizes,
-    )(shift_bias, queries, two, one, own, upstream, diff, meta, pulled)
+        tenants=tenants, rank=rank, scaling=scaling, rep=in_kernel, owned=here, **sizes,
+    )(shift_bias.T, queries, two, one, own, cots, diff, meta, pulled)
     gathered = lax.all_to_all(part, "ctx", split_axis=0, concat_axis=0, tiled=True)
     d_queries, back_two, back_one, back_own = call(
         backward_kernel,
@@ -262,9 +295,10 @@
     from_one = shifted(back_one, "ctx", -1)
     from_two = shifted(back_two, "ctx", -2)
 
-    here = heads // ctx
-    by_heads = gathered.reshape(ctx, here, 2, rep, tenants * rank // rep, dim).astype(WIDE).sum(axis=0)
-    by_rep = jnp.moveaxis(by_heads.astype(LOW), 2, 0)
+    by_rep = gathered.astype(WIDE).sum(axis=0).astype(LOW)
+    if in_kernel == 1:
+        by_rep = jnp.moveaxis(by_rep.reshape(here, 2, rep, span // rep, dim), 2, 0)
+    from_one, from_two, _ = lax.optimization_barrier((from_one, from_two, by_rep))
     by_rep = lax.all_to_all(by_rep, "rep", split_axis=0, concat_axis=0, tiled=True)
     summed = by_rep.astype(WIDE).sum(axis=0).reshape(here, 2, tenants // rep, rank, dim)
     grads = jnp.moveaxis(summed, 0, 3)

time: 65.2 us -> 58.9 us (0.903)
  waiting for transfers between devices: 18.2 us -> 9.18 us
  local copies, waits for them, and re-layouts: 8.24 us -> 11.2 us
  Pallas kernels: 16.7 us -> 15.8 us
    ppermute x4, waiting for transfers between devices: 13.8 us -> 0.68 us  [shifted(): lax.ppermute(value, axis, [(source, source + steps) for source in range(f...]
    all_to_all x1, waiting for transfers between devices: 0.01 us -> 4.71 us  [on_device(): lax.all_to_all(part, 'ctx', split_axis=0, concat_axis=0, tiled=True)]
    unnamed x11 -> x18, local copies, waits for them, and re-layouts: 5.58 us -> 9.5 us
    pallas_call x3, Pallas kernels: 16.7 us -> 15.8 us  [run(): pl.pallas_call(lambda *refs: body(*refs, **fixed), out_shape=[jax.ShapeDt...]
    sub x1 -> x0, other arithmetic: 0.67 us -> none  [on_device(): lax.dynamic_slice_in_dim(doc_starts[0], row_first, tokens, 0) - row_first]
    transpose x1 -> x0, local copies, waits for them, and re-layouts: 0.66 us -> none  [on_device(): by_rep = jnp.moveaxis(by_heads.astype(LOW), 2, 0)]
    reduce_sum x1, other arithmetic: 1.41 us -> 2.06 us  [on_device(): by_rep = gathered.astype(WIDE).sum(axis=0).astype(LOW)]
  transfers between devices with their start and end apart: 6 -> 6, of which waited for: 3 -> 4; matrix products, arithmetic and copies ran while one was open for 5% -> 6% of each run, Pallas kernels for 14% -> 17%
where the time goes in v2:
time: 58.9 us; the launch traced here: 58.3 us
  starting transfers between devices  19.1 us (32%)
  Pallas kernels  15.8 us (27%)
  local copies, waits for them, and re-layouts  11.2 us (19%)
  waiting for transfers between devices  9.18 us (16%)
  other arithmetic  2.2 us (4%)
  between operations  0.75 us (1%)
    pallas_call x3, Pallas kernels, run(): pl.pallas_call(lambda *refs: body(*refs, **fixed), out_shape=[jax.ShapeDt...  15.8 us
    unnamed x18, local copies, waits for them, and re-layouts  9.5 us
    ppermute x4, starting transfers between devices, shifted(): lax.ppermute(value, axis, [(source, source + steps) for source in range(f...  9.48 us
    all_to_all x1, starting transfers between devices, on_device(): lax.all_to_all(by_rep, 'rep', split_axis=0, concat_axis=0, tiled=True)  4.87 us
    all_to_all x1, starting transfers between devices, on_device(): lax.all_to_all(part, 'ctx', split_axis=0, concat_axis=0, tiled=True)  4.79 us
    all_to_all x1, waiting for transfers between devices, on_device(): lax.all_to_all(part, 'ctx', split_axis=0, concat_axis=0, tiled=True)  4.71 us
    all_to_all x1, waiting for transfers between devices, on_device(): lax.all_to_all(by_rep, 'rep', split_axis=0, concat_axis=0, tiled=True)  3.79 us
    reduce_sum x1, other arithmetic, on_device(): by_rep = gathered.astype(WIDE).sum(axis=0).astype(LOW)  2.06 us
  transfers between devices with their start and end apart: 6, of which 4 were waited for; matrix products, arithmetic and copies ran while one was open for 6% of the time, Pallas kernels for 17%

profile of v2, /device:TPU:0, one launch (start us, length us, event | category | flops | bytes accessed | tf_op | source)
XLA Modules:
  0.0 58.3 jit_solution(13000818312798692375)
XLA Ops:
  0.6 1.0 %copy_bitcast_fusion = (bf16[128,4,128]{2,0,1:T(8,128)(2,1)S(1)}, bf16[128,4,128]{2,0,1:T(8,128)(2,1)S(1)}) fusion(bf16[1,128,4,128]{3,2,1,0:T(4,128)(2,1)} %param.11, bf16[1,128,4,128]{3,2,1,0:T(4,128)(2,1)} %param.10), kind=kLoop, calls=%fused_computation.5 | loop fusion | bytes 524288 | tf_op jit(solution)/shard_map/squeeze | solution.py:242
  1.6 0.0 copy-start.3
  1.7 0.0 copy-start
  1.7 2.5 %collective-permute-start.1 = (bf16[8,128,128]{2,1,0:T(8,128)(2,1)S(1)}, bf16[8,128,128]{2,1,0:T(8,128)(2,1)S(1)}, u32[]{:S(2)}, u32[]{:S(2)}) collective-permute-start(bf16[8,128,128]{2,1,0:T(8,128)(2,1)S(1)} %maximum_bitcast_fusion.refs_4_), channel_id=1, source_target_pairs={{0,1},{1,2},{2,3},{3,4},{4,5},{5,6},{6,7},{8,9},{9,10},{10,11},{11... | collective-permute-start | bytes 786440 | tf_op jit(solution)/shard_map/ppermute | solution.py:17
  4.2 4.4 %collective-permute-start = (bf16[8,128,128]{2,1,0:T(8,128)(2,1)S(1)}, bf16[8,128,128]{2,1,0:T(8,128)(2,1)S(1)}, u32[]{:S(2)}, u32[]{:S(2)}) collective-permute-start(bf16[8,128,128]{2,1,0:T(8,128)(2,1)S(1)} %maximum_bitcast_fusion.refs_4_), channel_id=1, source_target_pairs={{0,2},{1,3},{2,4},{3,5},{4,6},{5,7},{8,10},{9,11},{10,12},{11,13},... | collective-permute-start | bytes 786440 | tf_op jit(solution)/shard_map/ppermute | solution.py:17
  8.6 0.0 copy-start.1
  8.6 0.7 %copy-done.1 = s32[1,1024]{1,0:T(1,128)S(1)} copy-done((s32[1,1024]{1,0:T(1,128)S(1)}, s32[1,1024]{1,0:T(1,128)}, u32[]{:S(2)}) %copy-start.1) | copy-done | bytes 4120
  9.3 0.0 copy-start.2
  9.3 0.7 %copy-done.2 = s32[1,1024]{1,0:T(1,128)S(1)} copy-done((s32[1,1024]{1,0:T(1,128)S(1)}, s32[1,1024]{1,0:T(1,128)}, u32[]{:S(2)}) %copy-start.2) | copy-done | bytes 4120
  10.0 5.1 %pull_kernel.1 = (bf16[4,1024,128]{2,1,0:T(8,128)(2,1)}, bf16[4,1024,128]{2,1,0:T(8,128)(2,1)}, bf16[4,512,128]{2,1,0:T(8,128)(2,1)S(1)}, f32[8,1024]{1,0:T(8,128)S(1)}, s32[8,1024]{1,0:T(8,128)S(1)}) custom-call(s32[1,1024]{1,0:T(1,128)S(1)} %copy-done.1, s32[1,1024]{1,0:T(1,128)S(1)} %copy-done.2, bf16[128,32,128]{2,1,0:T(8,128)(2,1)} %bitcast.33, ...), custom_call_target="tpu_custom_call" | custom-call | flops 2147483648 | bytes 4194304 | tf_op jit(solution)/shard_map/pull_kernel/pallas_call | solution.py:254
  15.1 0.0 collective-permute-done.1.refs_3_
  15.1 0.2 collective-permute-done.refs_2_
  15.3 0.0 copy-done.3
  15.3 0.0 copy-done
  15.3 0.0 copy-start.7
  15.3 1.2 %copy-done.7 = bf16[4,1024,128]{2,1,0:T(8,128)(2,1)S(1)} copy-done((bf16[4,1024,128]{2,1,0:T(8,128)(2,1)S(1)}, bf16[4,1024,128]{2,1,0:T(8,128)(2,1)}, u32[]{:S(2)}) %copy-start.7) | copy-done | bytes 1048600
  16.5 5.9 %forward_kernel.1 = (f32[4,256,1024]{2,1,0:T(8,128)S(1)}, bf16[8,4,4,2,16,128]{5,4,3,2,1,0:T(8,128)(2,1)}) custom-call(f32[4,16]{1,0:T(4,128)S(1)} %bitcast.30, bf16[128,32,128]{2,1,0:T(8,128)(2,1)S(1)} %bitcast.28, bf16[8,128,128]{2,1,0:T(8,128)(2,1)S(1)} %collective-permute-done.refs_2_, bf16[8,128,128]{2,1,0:T(8,128)(2,1)S(1)} %collective-permute-done.1.refs_3_, ...), custom_call_target="tpu_custom_call" | custom-call | flops 4294967296 | bytes 10485760 | tf_op jit(solution)/shard_map/forward_kernel/pallas_call | solution.py:254
  22.4 0.0 copy-start.4
  22.4 2.0 %copy-done.4 = f32[4,256,1024]{2,1,0:T(8,128)} copy-done((f32[4,256,1024]{2,1,0:T(8,128)}, f32[4,256,1024]{2,1,0:T(8,128)S(1)}, u32[]{:S(2)}) %copy-start.4) | copy-done | bytes 4194328
  24.4 4.8 %all-to-all-start = ((bf16[8,4,4,2,16,128]{5,4,3,2,1,0:T(8,128)(2,1)}), bf16[8,4,4,2,16,128]{5,4,3,2,1,0:T(8,128)(2,1)}, u32[]{:S(2)}, u32[]{:S(2)}) async-start(bf16[8,4,4,2,16,128]{5,4,3,2,1,0:T(8,128)(2,1)} %get-tuple-element.28), calls=%async_computation | async-start | bytes 2097152 | tf_op jit(solution)/shard_map/all_to_all | solution.py:289
  29.2 0.0 copy-start.5
  29.2 2.2 %copy-done.5 = f32[4,256,1024]{2,1,0:T(8,128)S(1)} copy-done((f32[4,256,1024]{2,1,0:T(8,128)S(1)}, f32[4,256,1024]{2,1,0:T(8,128)}, u32[]{:S(2)}) %copy-start.5) | copy-done | bytes 4194328
  31.4 0.0 copy-start.6
  31.4 1.2 %copy-done.6 = bf16[4,1024,128]{2,1,0:T(8,128)(2,1)S(1)} copy-done((bf16[4,1024,128]{2,1,0:T(8,128)(2,1)S(1)}, bf16[4,1024,128]{2,1,0:T(8,128)(2,1)}, u32[]{:S(2)}) %copy-start.6) | copy-done | bytes 1048600
  32.6 4.8 %backward_kernel.1 = (bf16[128,32,128]{2,1,0:T(8,128)(2,1)}, bf16[8,128,128]{2,1,0:T(8,128)(2,1)S(1)}, bf16[8,128,128]{2,1,0:T(8,128)(2,1)S(1)}, f32[8,128,128]{2,1,0:T(8,128)S(1)}) custom-call(bf16[128,32,128]{2,1,0:T(8,128)(2,1)S(1)} %bitcast.29, bf16[4,1024,128]{2,1,0:T(8,128)(2,1)S(1)} %copy-done.6, ...), custom_call_target="tpu_custom_call" | custom-call | flops 4294967296 | bytes 10485760 | tf_op jit(solution)/shard_map/backward_kernel/pallas_call | solution.py:254
  37.4 1.3 %collective-permute-start.2 = (bf16[8,128,128]{2,1,0:T(8,128)(2,1)S(1)}, bf16[8,128,128]{2,1,0:T(8,128)(2,1)S(1)}, u32[]{:S(2)}, u32[]{:S(2)}) collective-permute-start(bf16[8,128,128]{2,1,0:T(8,128)(2,1)S(1)} %get-tuple-element.26), channel_id=1, source_target_pairs={{1,0},{2,1},{3,2},{4,3},{5,4},{6,5},{7,6},{9,8},{10,9},{11,10},{12... | collective-permute-start | bytes 786440 | tf_op jit(solution)/shard_map/ppermute | solution.py:17
  38.7 1.3 %collective-permute-start.3 = (bf16[8,128,128]{2,1,0:T(8,128)(2,1)S(1)}, bf16[8,128,128]{2,1,0:T(8,128)(2,1)S(1)}, u32[]{:S(2)}, u32[]{:S(2)}) collective-permute-start(bf16[8,128,128]{2,1,0:T(8,128)(2,1)S(1)} %get-tuple-element.27), channel_id=1, source_target_pairs={{2,0},{3,1},{4,2},{5,3},{6,4},{7,5},{10,8},{11,9},{12,10},{13,11},... | collective-permute-start | bytes 786440 | tf_op jit(solution)/shard_map/ppermute | solution.py:17
  40.0 4.7 %all-to-all-done = bf16[8,4,4,2,16,128]{5,4,3,2,1,0:T(8,128)(2,1)} async-done(((bf16[8,4,4,2,16,128]{5,4,3,2,1,0:T(8,128)(2,1)}), bf16[8,4,4,2,16,128]{5,4,3,2,1,0:T(8,128)(2,1)}, u32[]{:S(2)}, u32[]{:S(2)}) %all-to-all-start) | async-done | bytes 1048608 | tf_op jit(solution)/shard_map/all_to_all | solution.py:289
  44.7 2.1 %reduce_sum.21 = bf16[4,4,2,16,128]{4,3,2,1,0:T(8,128)(2,1)} reduce(bf16[8,4,4,2,16,128]{5,4,3,2,1,0:T(8,128)(2,1)} %all-to-all-done, bf16[]{:T(256)} %constant.2.clone.1), dimensions={0}, to_apply=%region_0.0 | reduce | flops 458752 | bytes 1179650 | tf_op jit(solution)/shard_map/reduce_sum | solution.py:298
  46.8 4.9 %all-to-all-start.1 = ((bf16[4,4,2,16,128]{4,3,2,1,0:T(8,128)(2,1)}), bf16[4,4,2,16,128]{4,3,2,1,0:T(8,128)(2,1)S(1)}, u32[]{:S(2)}, u32[]{:S(2)}) async-start(bf16[4,4,2,16,128]{4,3,2,1,0:T(8,128)(2,1)} %reduce_sum.21), calls=%async_computation.1 | async-start | bytes 262144 | tf_op jit(solution)/shard_map/all_to_all | solution.py:302
  51.6 0.0 collective-permute-done.2
  51.7 0.5 collective-permute-done.3
  52.1 0.1 add_convert_fusion
  52.3 0.8 %copy.22 = bf16[1,128,4,128]{3,2,1,0:T(4,128)(2,1)} copy(bf16[1,128,4,128]{3,1,2,0:T(8,128)(2,1)S(1)} %get-tuple-element.41) | data formatting | bytes 262144
  53.0 0.8 %copy.21 = bf16[1,128,4,128]{3,2,1,0:T(4,128)(2,1)} copy(bf16[1,128,4,128]{3,1,2,0:T(8,128)(2,1)S(1)} %get-tuple-element.42) | data formatting | bytes 262144
  53.8 3.8 %all-to-all-done.1 = bf16[4,4,2,16,128]{4,3,2,1,0:T(8,128)(2,1)S(1)} async-done(((bf16[4,4,2,16,128]{4,3,2,1,0:T(8,128)(2,1)}), bf16[4,4,2,16,128]{4,3,2,1,0:T(8,128)(2,1)S(1)}, u32[]{:S(2)}, u32[]{:S(2)}) %all-to-all-start.1) | async-done | bytes 131104 | tf_op jit(solution)/shard_map/all_to_all | solution.py:302
  57.6 0.6 %slice_bitcast_fusion.2 = (f32[4,4,4,128]{3,2,1,0:T(4,128)}, f32[4,4,4,128]{3,2,1,0:T(4,128)}) fusion(f32[2,4,4,4,128]{4,3,2,1,0:T(4,128)S(1)} %bitcast.32), kind=kLoop, calls=%fused_computation.8 | loop fusion | bytes 131072 | tf_op jit(solution)/shard_map/squeeze | solution.py:308
  (4 shorter events, 0.1 us)
Async XLA Ops:
  1.6 13.6 %copy-start.3 = (f32[16,4]{0,1:T(4,128)S(1)}, f32[16,4]{0,1:T(4,128)}, u32[]{:S(2)}) copy-start(f32[16,4]{0,1:T(4,128)} %param.15) | copy-start | bytes 772
  1.7 13.6 %copy-start = (bf16[1,128,32,128]{3,2,1,0:T(8,128)(2,1)S(1)}, bf16[1,128,32,128]{3,2,1,0:T(8,128)(2,1)}, u32[]{:S(2)}) copy-start(bf16[1,128,32,128]{3,2,1,0:T(8,128)(2,1)} %param.9) | copy-start | bytes 3145732
  1.7 13.4 %collective-permute-start.1 = (bf16[8,128,128]{2,1,0:T(8,128)(2,1)S(1)}, bf16[8,128,128]{2,1,0:T(8,128)(2,1)S(1)}, u32[]{:S(2)}, u32[]{:S(2)}) collective-permute-start(bf16[8,128,128]{2,1,0:T(8,128)(2,1)S(1)} %maximum_bitcast_fusion.refs_4_), channel_id=1, source_target_pairs={{0,1},{1,2},{2,3},{3,4},{4,5},{5,6},{6,7},{8,9},{9,10},{10,11},{11... | collective-permute-start | bytes 786440 | tf_op jit(solution)/shard_map/ppermute | solution.py:17
  4.2 11.1 %collective-permute-start = (bf16[8,128,128]{2,1,0:T(8,128)(2,1)S(1)}, bf16[8,128,128]{2,1,0:T(8,128)(2,1)S(1)}, u32[]{:S(2)}, u32[]{:S(2)}) collective-permute-start(bf16[8,128,128]{2,1,0:T(8,128)(2,1)S(1)} %maximum_bitcast_fusion.refs_4_), channel_id=1, source_target_pairs={{0,2},{1,3},{2,4},{3,5},{4,6},{5,7},{8,10},{9,11},{10,12},{11,13},... | collective-permute-start | bytes 786440 | tf_op jit(solution)/shard_map/ppermute | solution.py:17
  8.6 0.7 %copy-start.1 = (s32[1,1024]{1,0:T(1,128)S(1)}, s32[1,1024]{1,0:T(1,128)}, u32[]{:S(2)}) copy-start(s32[1,1024]{1,0:T(1,128)} %refs_0_.1) | copy-start | bytes 12292
  9.3 0.7 %copy-start.2 = (s32[1,1024]{1,0:T(1,128)S(1)}, s32[1,1024]{1,0:T(1,128)}, u32[]{:S(2)}) copy-start(s32[1,1024]{1,0:T(1,128)} %refs_1_.1) | copy-start | bytes 12292
  15.3 1.2 %copy-start.7 = (bf16[4,1024,128]{2,1,0:T(8,128)(2,1)S(1)}, bf16[4,1024,128]{2,1,0:T(8,128)(2,1)}, u32[]{:S(2)}) copy-start(bf16[4,1024,128]{2,1,0:T(8,128)(2,1)} %get-tuple-element.19.refs_5_) | copy-start | bytes 3145732
  22.4 2.0 %copy-start.4 = (f32[4,256,1024]{2,1,0:T(8,128)}, f32[4,256,1024]{2,1,0:T(8,128)S(1)}, u32[]{:S(2)}) copy-start(f32[4,256,1024]{2,1,0:T(8,128)S(1)} %get-tuple-element.23.refs_5_) | copy-start | bytes 12582916
  24.4 20.3 %all-to-all-start = ((bf16[8,4,4,2,16,128]{5,4,3,2,1,0:T(8,128)(2,1)}), bf16[8,4,4,2,16,128]{5,4,3,2,1,0:T(8,128)(2,1)}, u32[]{:S(2)}, u32[]{:S(2)}) async-start(bf16[8,4,4,2,16,128]{5,4,3,2,1,0:T(8,128)(2,1)} %get-tuple-element.28), calls=%async_computation | async-start | bytes 2097152 | tf_op jit(solution)/shard_map/all_to_all | solution.py:289
  29.2 2.2 %copy-start.5 = (f32[4,256,1024]{2,1,0:T(8,128)S(1)}, f32[4,256,1024]{2,1,0:T(8,128)}, u32[]{:S(2)}) copy-start(f32[4,256,1024]{2,1,0:T(8,128)} %copy-done.4) | copy-start | bytes 12582916
  31.4 1.2 %copy-start.6 = (bf16[4,1024,128]{2,1,0:T(8,128)(2,1)S(1)}, bf16[4,1024,128]{2,1,0:T(8,128)(2,1)}, u32[]{:S(2)}) copy-start(bf16[4,1024,128]{2,1,0:T(8,128)(2,1)} %get-tuple-element.18.refs_1_) | copy-start | bytes 3145732
  37.4 14.2 %collective-permute-start.2 = (bf16[8,128,128]{2,1,0:T(8,128)(2,1)S(1)}, bf16[8,128,128]{2,1,0:T(8,128)(2,1)S(1)}, u32[]{:S(2)}, u32[]{:S(2)}) collective-permute-start(bf16[8,128,128]{2,1,0:T(8,128)(2,1)S(1)} %get-tuple-element.26), channel_id=1, source_target_pairs={{1,0},{2,1},{3,2},{4,3},{5,4},{6,5},{7,6},{9,8},{10,9},{11,10},{12... | collective-permute-start | bytes 786440 | tf_op jit(solution)/shard_map/ppermute | solution.py:17
  38.7 13.4 %collective-permute-start.3 = (bf16[8,128,128]{2,1,0:T(8,128)(2,1)S(1)}, bf16[8,128,128]{2,1,0:T(8,128)(2,1)S(1)}, u32[]{:S(2)}, u32[]{:S(2)}) collective-permute-start(bf16[8,128,128]{2,1,0:T(8,128)(2,1)S(1)} %get-tuple-element.27), channel_id=1, source_target_pairs={{2,0},{3,1},{4,2},{5,3},{6,4},{7,5},{10,8},{11,9},{12,10},{13,11},... | collective-permute-start | bytes 786440 | tf_op jit(solution)/shard_map/ppermute | solution.py:17
  46.8 10.8 %all-to-all-start.1 = ((bf16[4,4,2,16,128]{4,3,2,1,0:T(8,128)(2,1)}), bf16[4,4,2,16,128]{4,3,2,1,0:T(8,128)(2,1)S(1)}, u32[]{:S(2)}, u32[]{:S(2)}) async-start(bf16[4,4,2,16,128]{4,3,2,1,0:T(8,128)(2,1)} %reduce_sum.21), calls=%async_computation.1 | async-start | bytes 262144 | tf_op jit(solution)/shard_map/all_to_all | solution.py:302

commit v3 on v2

--- a/solution.py
+++ b/solution.py
@@ -15,6 +15,24 @@
     count = lax.axis_size(axis)
     first, last = (max(0, -steps), min(count, count - steps))
     return lax.ppermute(value, axis, [(source, source + steps) for source in range(first, last)])
+
+
+def exchanged(value, axis, bit):
+    count = lax.axis_size(axis)
+    return lax.ppermute(value, axis, [(source, source ^ bit) for source in range(count)])
+
+
+def halved(keep, axis, bit):
+    half = keep.shape[0] // 2
+    other = exchanged(keep[half:], axis, bit)
+    return keep[:half].astype(WIDE) + other.astype(WIDE)
+
+
+def reversed_bits(value, bits):
+    result = 0 * value
+    for bit in range(bits):
+        result = result + ((value >> bit) & 1) * (1 << (bits - 1 - bit))
+    return result
 
 
 def dot(left, right, left_dim, right_dim, precision=None):
@@ -64,17 +82,21 @@
 
 
 def pull_kernel(
-    starts_ref, owners_ref, cot_hbm, rot_hbm, proj_hbm, cots_ref, gh_ref, diff_ref, pulled_ref, meta_ref,
-    cot_ref, rot_ref, proj_ref, sems, *, kv, group, tenants, rank,
+    starts_hbm, owners_hbm, cot_hbm, rot_hbm, proj_hbm, gh_ref, diff_ref, pulled_ref, meta_ref,
+    starts_ref, owners_ref, cot_ref, rot_ref, proj_ref, sems, *, kv, group, tenants, rank,
 ):
+    pairs = (
+        (starts_hbm, starts_ref), (owners_hbm, owners_ref), (cot_hbm, cot_ref),
+        (rot_hbm, rot_ref), (proj_hbm, proj_ref),
+    )
     copies = [
         pltpu.make_async_copy(source, target, sems.at[at])
-        for at, (source, target) in enumerate(
-            ((cot_hbm, cot_ref), (rot_hbm, rot_ref), (proj_hbm, proj_ref))
-        )
+        for at, (source, target) in enumerate(pairs)
     ]
     for copy in copies:
         copy.start()
+    copies[0].wait()
+    copies[1].wait()
     lanes = meta_ref.shape[1]
     tokens = lanes // group
     row_first = lax.axis_index("ctx") * tokens
@@ -87,11 +109,9 @@
     meta = dot(both, repeat.astype(WIDE), 1, 0, lax.Precision.HIGHEST).astype(jnp.int32)
     meta_ref[...] = meta
     owner = meta[1:2, :]
-    copies[0].wait()
+    copies[2].wait()
     cots = group_rows(cot_ref, kv, group)
-    for g in range(kv):
-        cots_ref[g] = cots[g]
-    copies[1].wait()
+    copies[3].wait()
     rots = group_rows(rot_ref, kv, group)
     on_rot = dot(jnp.concatenate(rots, axis=1), jnp.concatenate(cots, axis=1), 1, 1)
     pulled = own_terms(on_rot, owner, tenants, rank, group).astype(LOW).astype(WIDE)
@@ -103,7 +123,7 @@
         for k in range(rank):
             picked.append(jnp.where(keep, pulled[k : k + 1], 0.0))
     picked = jnp.concatenate(picked, axis=0).T.astype(LOW)
-    copies[2].wait()
+    copies[4].wait()
     projs = group_rows(proj_ref, kv, group)
     for g in range(kv):
         diff = (projs[g].astype(WIDE) - rots[g].astype(WIDE)).astype(LOW)
@@ -118,9 +138,11 @@
 
 
 def forward_kernel(
-    bias_ref, q_ref, two_ref, one_ref, own_ref, cots_ref, diff_ref, meta_ref, pulled_ref,
-    weights_ref, part_ref, *, kv, group, tenants, rank, scaling, rep, owned,
+    bias_ref, q_ref, two_ref, one_ref, own_ref, cot_hbm, diff_ref, meta_ref, pulled_ref,
+    weights_ref, send_ref, keep_ref, cot_ref, sem, *, kv, group, tenants, rank, scaling, owned,
 ):
+    fetch = pltpu.make_async_copy(cot_hbm, cot_ref, sem)
+    fetch.start()
     tokens = own_ref.shape[1]
     first = meta_ref[0:1, :]
     owner = meta_ref[1:2, :]
@@ -157,24 +179,35 @@
     shift = dot(bias, one_hot, 1, 0, lax.Precision.HIGHEST)
     lifted = (lifted + shift).astype(LOW).astype(WIDE)
     pulled = pulled_ref[...]
+    ctx, rep = lax.axis_size("ctx"), lax.axis_size("rep")
+    me, layer = lax.axis_index("ctx"), lax.axis_index("rep")
+    per_group = group // owned
     span = tenants * rank
-    mine = owner == lax.broadcasted_iota(jnp.int32, (span, lanes), 0) // rank
+    tenant_row = lax.broadcasted_iota(jnp.int32, (span, lanes), 0) // rank
+    mine = owner == (tenant_row ^ (layer * (tenants // rep)))
     lift_rows = jnp.where(mine, jnp.concatenate([lifted] * (span // 8), axis=0), 0.0)
     pull_rows = jnp.where(mine, jnp.concatenate([pulled] * (span // 8), axis=0), 0.0)
-    head = lane_head((span, lanes), group)
-    lift_all = jnp.concatenate([jnp.where(head == h, lift_rows, 0.0).astype(LOW) for h in range(group)], axis=0)
-    pull_all = jnp.concatenate([jnp.where(head == h, pull_rows, 0.0).astype(LOW) for h in range(group)], axis=0)
+    slot = lane_head((span, lanes), group) ^ ((me % per_group) * owned)
+    lift_all = jnp.concatenate([jnp.where(slot == h, lift_rows, 0.0).astype(LOW) for h in range(group)], axis=0)
+    pull_all = jnp.concatenate([jnp.where(slot == h, pull_rows, 0.0).astype(LOW) for h in range(group)], axis=0)
     on_proj = dot(pull_all, hidden, 1, 1)
-    on_rot = dot(lift_all, jnp.concatenate([cots_ref[g] for g in range(kv)], axis=1), 1, 0) - on_proj
+    fetch.wait()
+    on_rot = dot(lift_all, jnp.concatenate(group_rows(cot_ref, kv, group), axis=1), 1, 0) - on_proj
     dim = q_ref.shape[2]
+    here_rows = span // rep
+    bits = ctx.bit_length() - 1
     for g in range(kv):
-        for h in range(group):
-            device, place = (g * group + h) // owned, (g * group + h) % owned
-            columns = slice(g * dim, (g + 1) * dim)
+        columns = slice(g * dim, (g + 1) * dim)
+        for low in range(per_group):
+            device = (g ^ (me // per_group)) * per_group + low
+            place = reversed_bits(device >> 1, bits - 1)
+            into = send_ref if low % 2 else keep_ref
             for r in range(rep):
-                rows = slice(h * span + r * span // rep, h * span + (r + 1) * span // rep)
-                part_ref[device, r, place, 0] = on_rot[rows, columns].astype(LOW)
-                part_ref[device, r, place, 1] = on_proj[rows, columns].astype(LOW)
+                pieces = []
+                for h in range(low * owned, (low + 1) * owned):
+                    rows = slice(h * span + r * here_rows, h * span + (r + 1) * here_rows)
+                    pieces += [on_rot[rows, columns], on_proj[rows, columns]]
+                into[place, reversed_bits(r, rep.bit_length() - 1)] = jnp.concatenate(pieces, axis=0).astype(LOW)
 
 
 def backward_kernel(
@@ -265,28 +298,31 @@
         return run
 
     span = tenants * rank
-    in_kernel = rep if span // rep % 16 == 0 else 1
-    cots, grad_hidden, diff, pulled, meta = call(
+    here = heads // ctx
+    rows = here * 2 * span // rep
+    grad_hidden, diff, pulled, meta = call(
         pull_kernel,
         [
-            ((kv, lanes, dim), LOW), ((kv, lanes, dim), LOW), ((kv, span * group, dim), LOW),
+            ((kv, lanes, dim), LOW), ((kv, span * group, dim), LOW),
             ((8, lanes), WIDE), ((8, lanes), jnp.int32),
         ],
-        2 * 2**30, 4 * 2**20, [vmem, vmem, hbm, hbm, hbm],
+        2 * 2**30, 4 * 2**20, [hbm] * 5,
         [
+            pltpu.VMEM(doc_starts.shape, jnp.int32), pltpu.VMEM(tenant_ids.shape, jnp.int32),
             pltpu.VMEM((tokens, heads, dim), LOW), pltpu.VMEM((span, heads, dim), LOW),
-            pltpu.VMEM((span, heads, dim), LOW), pltpu.SemaphoreType.DMA((3,)),
+            pltpu.VMEM((span, heads, dim), LOW), pltpu.SemaphoreType.DMA((5,)),
         ],
         limit=53, tenants=tenants, rank=rank, **sizes,
     )(doc_starts, tenant_ids, upstream, rot, proj)
-    here = heads // ctx
-    weights, part = call(
+    weights, send, keep = call(
         forward_kernel,
-        [((kv, 2 * tokens, lanes), WIDE), ((ctx, in_kernel, here, 2, span // in_kernel, dim), LOW)],
-        4 * 2**30, 10 * 2**20,
-        tenants=tenants, rank=rank, scaling=scaling, rep=in_kernel, owned=here, **sizes,
-    )(shift_bias.T, queries, two, one, own, cots, diff, meta, pulled)
-    gathered = lax.all_to_all(part, "ctx", split_axis=0, concat_axis=0, tiled=True)
+        [((kv, 2 * tokens, lanes), WIDE)] + [((ctx // 2, rep, rows, dim), LOW)] * 2,
+        4 * 2**30, 10 * 2**20, [vmem] * 5 + [hbm] + [vmem] * 3,
+        [pltpu.VMEM((tokens, heads, dim), LOW), pltpu.SemaphoreType.DMA],
+        tenants=tenants, rank=rank, scaling=scaling, owned=here, **sizes,
+    )(shift_bias.T, queries, two, one, own, upstream, diff, meta, pulled)
+    part = (keep.astype(WIDE) + exchanged(send, "ctx", 1).astype(WIDE)).astype(LOW)
+    weights, part = lax.optimization_barrier((weights, part))
     d_queries, back_two, back_one, back_own = call(
         backward_kernel,
         [((tokens, heads, dim), LOW), (own.shape, LOW), (own.shape, LOW), (own.shape, WIDE)],
@@ -295,13 +331,19 @@
     from_one = shifted(back_one, "ctx", -1)
     from_two = shifted(back_two, "ctx", -2)
 
-    by_rep = gathered.astype(WIDE).sum(axis=0).astype(LOW)
-    if in_kernel == 1:
-        by_rep = jnp.moveaxis(by_rep.reshape(here, 2, rep, span // rep, dim), 2, 0)
-    from_one, from_two, _ = lax.optimization_barrier((from_one, from_two, by_rep))
-    by_rep = lax.all_to_all(by_rep, "rep", split_axis=0, concat_axis=0, tiled=True)
-    summed = by_rep.astype(WIDE).sum(axis=0).reshape(here, 2, tenants // rep, rank, dim)
-    grads = jnp.moveaxis(summed, 0, 3)
+    bit = 2
+    while bit < ctx:
+        part = halved(part, "ctx", bit).astype(LOW)
+        bit *= 2
+    part = part[0]
+    bit = 1
+    while bit < rep:
+        part = part.astype(LOW)
+        if 2 * bit == rep:
+            from_one, from_two, _ = lax.optimization_barrier((from_one, from_two, part))
+        part = halved(part, "rep", bit)
+        bit *= 2
+    grads = jnp.moveaxis(part.astype(WIDE).reshape(here, 2, tenants // rep, rank, dim), 0, 3)
     back = (back_own + from_one.astype(WIDE) + from_two.astype(WIDE)).astype(LOW)
     d_keys = jnp.moveaxis(back[:kv], 0, 1)
     d_values = jnp.moveaxis(back[kv:], 0, 1)

time: 58.9 us -> 59.9 us (1.017)
  waiting for transfers between devices: 9.18 us -> 19.6 us
  local copies, waits for them, and re-layouts: 11.2 us -> 4.65 us
  other arithmetic: 2.2 us -> 0.4 us
  Pallas kernels: 15.8 us -> 15 us
    ppermute x0 -> x5, waiting for transfers between devices: none -> 11.6 us  [exchanged(): lax.ppermute(value, axis, [(source, source ^ bit) for source in range(cou...]
    ppermute x0 -> x5, starting transfers between devices: none -> 10 us  [exchanged(): lax.ppermute(value, axis, [(source, source ^ bit) for source in range(cou...]
    all_to_all x2 -> x0, starting transfers between devices: 9.66 us -> none  [the longest x1 4.87 us: on_device(): lax.all_to_all(by_rep, 'rep', split_axis=0, concat_axis=0, tiled=True)]
    all_to_all x2 -> x0, waiting for transfers between devices: 8.51 us -> none  [the longest x1 4.71 us: on_device(): lax.all_to_all(part, 'ctx', split_axis=0, concat_axis=0, tiled=True)]
    ppermute x4, waiting for transfers between devices: 0.68 us -> 8.06 us  [shifted(): lax.ppermute(value, axis, [(source, source + steps) for source in range(f...]
    unnamed x18 -> x14, local copies, waits for them, and re-layouts: 9.5 us -> 2.91 us
    reduce_sum x2 -> x0, other arithmetic: 2.08 us -> none  [the longest x1 2.06 us: on_device(): by_rep = gathered.astype(WIDE).sum(axis=0).astype(LOW)]
    pallas_call x3, Pallas kernels: 15.8 us -> 15 us  [run(): pl.pallas_call(lambda *refs: body(*refs, **fixed), out_shape=[jax.ShapeDt...]
  transfers between devices with their start and end apart: 6 -> 9, of which waited for: 4 -> 4; matrix products, arithmetic and copies ran while one was open for 6% -> 3% of each run, Pallas kernels for 17% -> 16%
where the time goes in v3:
time: 59.9 us; the launch traced here: 59.6 us
  waiting for transfers between devices  19.6 us (33%)
  starting transfers between devices  19.1 us (32%)
  Pallas kernels  15 us (25%)
  local copies, waits for them, and re-layouts  4.65 us (8%)
  between operations  0.86 us (1%)
    pallas_call x3, Pallas kernels, run(): pl.pallas_call(lambda *refs: body(*refs, **fixed), out_shape=[jax.ShapeDt...  15 us
    ppermute x5, waiting for transfers between devices, exchanged(): lax.ppermute(value, axis, [(source, source ^ bit) for source in range(cou...  11.6 us
    ppermute x5, starting transfers between devices, exchanged(): lax.ppermute(value, axis, [(source, source ^ bit) for source in range(cou...  10 us
    ppermute x4, starting transfers between devices, shifted(): lax.ppermute(value, axis, [(source, source + steps) for source in range(f...  9.04 us
    ppermute x4, waiting for transfers between devices, shifted(): lax.ppermute(value, axis, [(source, source + steps) for source in range(f...  8.06 us
    unnamed x14, local copies, waits for them, and re-layouts  2.91 us
  transfers between devices with their start and end apart: 9, of which 4 were waited for; matrix products, arithmetic and copies ran while one was open for 3% of the time, Pallas kernels for 16%

profile of v3, /device:TPU:0, one launch (start us, length us, event | category | flops | bytes accessed | tf_op | source)
XLA Modules:
  0.0 59.6 jit_solution(15799065488588345371)
XLA Ops:
  0.6 1.0 %copy_bitcast_fusion = (bf16[128,4,128]{2,0,1:T(8,128)(2,1)S(1)}, bf16[128,4,128]{2,0,1:T(8,128)(2,1)S(1)}) fusion(bf16[1,128,4,128]{3,2,1,0:T(4,128)(2,1)} %param.11, bf16[1,128,4,128]{3,2,1,0:T(4,128)(2,1)} %param.10), kind=kLoop, calls=%fused_computation.9 | loop fusion | bytes 524288 | tf_op jit(solution)/shard_map/squeeze | solution.py:275
  1.6 0.0 copy-start.4
  1.7 0.0 copy-start
  1.7 0.0 copy-start.1
  1.7 5.0 %collective-permute-start = (bf16[8,128,128]{2,1,0:T(8,128)(2,1)S(1)}, bf16[8,128,128]{2,1,0:T(8,128)(2,1)S(1)}, u32[]{:S(2)}, u32[]{:S(2)}) collective-permute-start(bf16[8,128,128]{2,1,0:T(8,128)(2,1)S(1)} %maximum_bitcast_fusion.refs_4_), channel_id=1, source_target_pairs={{0,2},{1,3},{2,4},{3,5},{4,6},{5,7},{8,10},{9,11},{10,12},{11,13},... | collective-permute-start | bytes 786440 | tf_op jit(solution)/shard_map/ppermute | solution.py:17
  6.7 1.5 %collective-permute-start.1 = (bf16[8,128,128]{2,1,0:T(8,128)(2,1)S(1)}, bf16[8,128,128]{2,1,0:T(8,128)(2,1)S(1)}, u32[]{:S(2)}, u32[]{:S(2)}) collective-permute-start(bf16[8,128,128]{2,1,0:T(8,128)(2,1)S(1)} %maximum_bitcast_fusion.refs_4_), channel_id=1, source_target_pairs={{0,1},{1,2},{2,3},{3,4},{4,5},{5,6},{6,7},{8,9},{9,10},{10,11},{11... | collective-permute-start | bytes 786440 | tf_op jit(solution)/shard_map/ppermute | solution.py:17
  8.2 0.0 copy-start.2
  8.2 0.7 %copy-done.2 = s32[1,1024]{1,0:T(1,128)S(1)} copy-done((s32[1,1024]{1,0:T(1,128)S(1)}, s32[1,1024]{1,0:T(1,128)}, u32[]{:S(2)}) %copy-start.2) | copy-done | bytes 4120
  8.9 0.0 copy-start.3
  8.9 0.7 %copy-done.3 = s32[1,1024]{1,0:T(1,128)S(1)} copy-done((s32[1,1024]{1,0:T(1,128)S(1)}, s32[1,1024]{1,0:T(1,128)}, u32[]{:S(2)}) %copy-start.3) | copy-done | bytes 4120
  9.6 4.9 %pull_kernel.1 = (bf16[4,1024,128]{2,1,0:T(8,128)(2,1)}, bf16[4,512,128]{2,1,0:T(8,128)(2,1)S(1)}, f32[8,1024]{1,0:T(8,128)S(1)}, s32[8,1024]{1,0:T(8,128)S(1)}) custom-call(s32[1,1024]{1,0:T(1,128)S(1)} %copy-done.2, s32[1,1024]{1,0:T(1,128)S(1)} %copy-done.3, bf16[128,32,128]{2,1,0:T(8,128)(2,1)} %bitcast.35, bf16[64,32,128]{2,1,0:T(8,128)(2,1)} %bitcast.42, ...), custom_call_target="tpu_custom_call" | custom-call | flops 2147483648 | bytes 4194304 | tf_op jit(solution)/shard_map/pull_kernel/pallas_call | solution.py:287
  14.5 0.0 collective-permute-done.refs_2_
  14.5 0.0 collective-permute-done.1.refs_3_
  14.5 0.0 copy-done.4
  14.6 0.0 copy-done
  14.6 0.0 copy-done.1
  14.6 0.0 copy-start.5
  14.6 5.2 %forward_kernel.1 = (f32[4,256,1024]{2,1,0:T(8,128)S(1)}, bf16[4,4,128,128]{3,2,1,0:T(8,128)(2,1)S(1)}, bf16[4,4,128,128]{3,2,1,0:T(8,128)(2,1)S(1)}) custom-call(f32[4,16]{1,0:T(4,128)S(1)} %bitcast.39, bf16[128,32,128]{2,1,0:T(8,128)(2,1)S(1)} %bitcast.37, bf16[8,128,128]{2,1,0:T(8,128)(2,1)S(1)} %collective-permute-done.refs_2_, ...), custom_call_target="tpu_custom_call" | custom-call | flops 4294967296 | bytes 10485760 | tf_op jit(solution)/shard_map/forward_kernel/pallas_call | solution.py:287
  19.8 2.1 %collective-permute-start.2 = (bf16[4,4,128,128]{3,2,1,0:T(8,128)(2,1)S(1)}, bf16[4,4,128,128]{3,2,1,0:T(8,128)(2,1)S(1)}, u32[]{:S(2)}, u32[]{:S(2)}) collective-permute-start(bf16[4,4,128,128]{3,2,1,0:T(8,128)(2,1)S(1)} %get-tuple-element.26), channel_id=1, source_target_pairs={{0,1},{1,0},{2,3},{3,2},{4,5},{5,4},{6,7},{7,6},{8,9},{9,8},{10,11... | collective-permute-start | bytes 1572872 | tf_op jit(solution)/shard_map/ppermute | solution.py:22
  21.9 1.5 %collective-permute-done.2 = bf16[4,4,128,128]{3,2,1,0:T(8,128)(2,1)S(1)} collective-permute-done((bf16[4,4,128,128]{3,2,1,0:T(8,128)(2,1)S(1)}, bf16[4,4,128,128]{3,2,1,0:T(8,128)(2,1)S(1)}, u32[]{:S(2)}, u32[]{:S(2)}) %collective-permute-start.2) | collective-permute-done | bytes 524320 | tf_op jit(solution)/shard_map/ppermute | solution.py:22
  23.5 0.1 add_convert_fusion
  23.6 1.6 %collective-permute-start.5 = (bf16[2,4,128,128]{3,2,1,0:T(8,128)(2,1)S(1)}, bf16[2,4,128,128]{3,2,1,0:T(8,128)(2,1)S(1)}, u32[]{:S(2)}, u32[]{:S(2)}) collective-permute-start(bf16[2,4,128,128]{3,2,1,0:T(8,128)(2,1)S(1)} %slice.41), channel_id=1, source_target_pairs={{0,2},{1,3},{2,0},{3,1},{4,6},{5,7},{6,4},{7,5},{8,10},{9,11},{10,... | collective-permute-start | bytes 786440 | tf_op jit(solution)/shard_map/ppermute | solution.py:22
  25.2 7.1 %collective-permute-done.5 = bf16[2,4,128,128]{3,2,1,0:T(8,128)(2,1)S(1)} collective-permute-done((bf16[2,4,128,128]{3,2,1,0:T(8,128)(2,1)S(1)}, bf16[2,4,128,128]{3,2,1,0:T(8,128)(2,1)S(1)}, u32[]{:S(2)}, u32[]{:S(2)}) %collective-permute-start.5) | collective-permute-done | bytes 262176 | tf_op jit(solution)/shard_map/ppermute | solution.py:22
  32.3 0.1 add_convert_fusion.2
  32.4 2.1 %collective-permute-start.6 = (bf16[1,4,128,128]{3,2,1,0:T(8,128)(2,1)S(1)}, bf16[1,4,128,128]{3,2,1,0:T(8,128)(2,1)S(1)}, u32[]{:S(2)}, u32[]{:S(2)}) collective-permute-start(bf16[1,4,128,128]{3,2,1,0:T(8,128)(2,1)S(1)} %slice.54), channel_id=1, source_target_pairs={{0,4},{1,5},{2,6},{3,7},{4,0},{5,1},{6,2},{7,3},{8,12},{9,13},{10,... | collective-permute-start | bytes 393224 | tf_op jit(solution)/shard_map/ppermute | solution.py:22
  34.4 3.0 %collective-permute-done.6 = bf16[1,4,128,128]{3,2,1,0:T(8,128)(2,1)S(1)} collective-permute-done((bf16[1,4,128,128]{3,2,1,0:T(8,128)(2,1)S(1)}, bf16[1,4,128,128]{3,2,1,0:T(8,128)(2,1)S(1)}, u32[]{:S(2)}, u32[]{:S(2)}) %collective-permute-start.6) | collective-permute-done | bytes 131104 | tf_op jit(solution)/shard_map/ppermute | solution.py:22
  37.5 1.6 %collective-permute-start.7 = (bf16[2,128,128]{2,1,0:T(8,128)(2,1)S(1)}, bf16[2,128,128]{2,1,0:T(8,128)(2,1)S(1)}, u32[]{:S(2)}, u32[]{:S(2)}) collective-permute-start(bf16[2,128,128]{2,1,0:T(8,128)(2,1)S(1)} %slice_bitcast_fusion.2), channel_id=1, source_target_pairs={{0,8},{8,0},{16,24},{24,16},{1,9},{9,1},{17,25},{25,17},{2,10},{10... | collective-permute-start | bytes 196616 | tf_op jit(solution)/shard_map/ppermute | solution.py:22
  39.1 0.0 copy-done.5
  39.1 4.8 %backward_kernel.1 = (bf16[128,32,128]{2,1,0:T(8,128)(2,1)}, bf16[8,128,128]{2,1,0:T(8,128)(2,1)S(1)}, bf16[8,128,128]{2,1,0:T(8,128)(2,1)S(1)}, f32[8,128,128]{2,1,0:T(8,128)S(1)}) custom-call(bf16[128,32,128]{2,1,0:T(8,128)(2,1)S(1)} %bitcast.38, bf16[4,1024,128]{2,1,0:T(8,128)(2,1)S(1)} %copy-done.5, ...), custom_call_target="tpu_custom_call" | custom-call | flops 4294967296 | bytes 10485760 | tf_op jit(solution)/shard_map/backward_kernel/pallas_call | solution.py:287
  43.9 1.3 %collective-permute-start.3 = (bf16[8,128,128]{2,1,0:T(8,128)(2,1)S(1)}, bf16[8,128,128]{2,1,0:T(8,128)(2,1)S(1)}, u32[]{:S(2)}, u32[]{:S(2)}) collective-permute-start(bf16[8,128,128]{2,1,0:T(8,128)(2,1)S(1)} %get-tuple-element.30), channel_id=1, source_target_pairs={{1,0},{2,1},{3,2},{4,3},{5,4},{6,5},{7,6},{9,8},{10,9},{11,10},{12... | collective-permute-start | bytes 786440 | tf_op jit(solution)/shard_map/ppermute | solution.py:17
  45.2 1.3 %collective-permute-start.4 = (bf16[8,128,128]{2,1,0:T(8,128)(2,1)S(1)}, bf16[8,128,128]{2,1,0:T(8,128)(2,1)S(1)}, u32[]{:S(2)}, u32[]{:S(2)}) collective-permute-start(bf16[8,128,128]{2,1,0:T(8,128)(2,1)S(1)} %get-tuple-element.31), channel_id=1, source_target_pairs={{2,0},{3,1},{4,2},{5,3},{6,4},{7,5},{10,8},{11,9},{12,10},{13,11},... | collective-permute-start | bytes 786440 | tf_op jit(solution)/shard_map/ppermute | solution.py:17
  46.5 0.0 collective-permute-done.7
  46.6 2.7 %collective-permute-start.8 = (bf16[1,128,128]{2,1,0:T(8,128)(2,1)S(1)}, bf16[1,128,128]{2,1,0:T(8,128)(2,1)S(1)}, u32[]{:S(2)}, u32[]{:S(2)}) collective-permute-start(bf16[1,128,128]{2,1,0:T(8,128)(2,1)S(1)} %slice.60), channel_id=1, source_target_pairs={{0,16},{8,24},{16,0},{24,8},{1,17},{9,25},{17,1},{25,9},{2,18},{10... | collective-permute-start | bytes 98312 | tf_op jit(solution)/shard_map/ppermute | solution.py:22
  49.2 0.0 collective-permute-done.3
  49.2 8.1 %collective-permute-done.4 = bf16[8,128,128]{2,1,0:T(8,128)(2,1)S(1)} collective-permute-done((bf16[8,128,128]{2,1,0:T(8,128)(2,1)S(1)}, bf16[8,128,128]{2,1,0:T(8,128)(2,1)S(1)}, u32[]{:S(2)}, u32[]{:S(2)}) %collective-permute-start.4) | collective-permute-done | bytes 262176 | tf_op jit(solution)/shard_map/ppermute | solution.py:17
  57.3 0.1 add_convert_fusion.1
  57.4 0.8 %copy.17 = bf16[1,128,4,128]{3,2,1,0:T(4,128)(2,1)} copy(bf16[1,128,4,128]{3,1,2,0:T(8,128)(2,1)S(1)} %get-tuple-element.41) | data formatting | bytes 262144
  58.2 0.8 %copy.18 = bf16[1,128,4,128]{3,2,1,0:T(4,128)(2,1)} copy(bf16[1,128,4,128]{3,1,2,0:T(8,128)(2,1)S(1)} %get-tuple-element.40) | data formatting | bytes 262144
  58.9 0.0 collective-permute-done.8
  59.0 0.6 %slice_bitcast_fusion.4 = (f32[4,4,4,128]{3,2,1,0:T(4,128)}, f32[4,4,4,128]{3,2,1,0:T(4,128)}) fusion(f32[2,4,4,4,128]{4,3,2,1,0:T(4,128)S(1)} %bitcast.40), kind=kLoop, calls=%fused_computation.15 | loop fusion | bytes 131072 | tf_op jit(solution)/shard_map/squeeze | solution.py:350
  (10 shorter events, 0.2 us)
Async XLA Ops:
  1.6 12.9 %copy-start.4 = (f32[16,4]{0,1:T(4,128)S(1)}, f32[16,4]{0,1:T(4,128)}, u32[]{:S(2)}) copy-start(f32[16,4]{0,1:T(4,128)} %param.15) | copy-start | bytes 772
  1.7 12.9 %copy-start = (bf16[1,128,32,128]{3,2,1,0:T(8,128)(2,1)S(1)}, bf16[1,128,32,128]{3,2,1,0:T(8,128)(2,1)}, u32[]{:S(2)}) copy-start(bf16[1,128,32,128]{3,2,1,0:T(8,128)(2,1)} %param.12) | copy-start | bytes 3145732
  1.7 12.9 %copy-start.1 = (bf16[1,128,32,128]{3,2,1,0:T(8,128)(2,1)S(1)}, bf16[1,128,32,128]{3,2,1,0:T(8,128)(2,1)}, u32[]{:S(2)}) copy-start(bf16[1,128,32,128]{3,2,1,0:T(8,128)(2,1)} %param.9) | copy-start | bytes 3145732
  1.7 12.8 %collective-permute-start = (bf16[8,128,128]{2,1,0:T(8,128)(2,1)S(1)}, bf16[8,128,128]{2,1,0:T(8,128)(2,1)S(1)}, u32[]{:S(2)}, u32[]{:S(2)}) collective-permute-start(bf16[8,128,128]{2,1,0:T(8,128)(2,1)S(1)} %maximum_bitcast_fusion.refs_4_), channel_id=1, source_target_pairs={{0,2},{1,3},{2,4},{3,5},{4,6},{5,7},{8,10},{9,11},{10,12},{11,13},... | collective-permute-start | bytes 786440 | tf_op jit(solution)/shard_map/ppermute | solution.py:17
  6.7 7.8 %collective-permute-start.1 = (bf16[8,128,128]{2,1,0:T(8,128)(2,1)S(1)}, bf16[8,128,128]{2,1,0:T(8,128)(2,1)S(1)}, u32[]{:S(2)}, u32[]{:S(2)}) collective-permute-start(bf16[8,128,128]{2,1,0:T(8,128)(2,1)S(1)} %maximum_bitcast_fusion.refs_4_), channel_id=1, source_target_pairs={{0,1},{1,2},{2,3},{3,4},{4,5},{5,6},{6,7},{8,9},{9,10},{10,11},{11... | collective-permute-start | bytes 786440 | tf_op jit(solution)/shard_map/ppermute | solution.py:17
  8.2 0.7 %copy-start.2 = (s32[1,1024]{1,0:T(1,128)S(1)}, s32[1,1024]{1,0:T(1,128)}, u32[]{:S(2)}) copy-start(s32[1,1024]{1,0:T(1,128)} %refs_0_.1) | copy-start | bytes 12292
  8.9 0.7 %copy-start.3 = (s32[1,1024]{1,0:T(1,128)S(1)}, s32[1,1024]{1,0:T(1,128)}, u32[]{:S(2)}) copy-start(s32[1,1024]{1,0:T(1,128)} %refs_1_.1) | copy-start | bytes 12292
  14.6 24.5 %copy-start.5 = (bf16[4,1024,128]{2,1,0:T(8,128)(2,1)S(1)}, bf16[4,1024,128]{2,1,0:T(8,128)(2,1)}, u32[]{:S(2)}) copy-start(bf16[4,1024,128]{2,1,0:T(8,128)(2,1)} %get-tuple-element.20.refs_1_) | copy-start | bytes 3145732
  19.8 3.6 %collective-permute-start.2 = (bf16[4,4,128,128]{3,2,1,0:T(8,128)(2,1)S(1)}, bf16[4,4,128,128]{3,2,1,0:T(8,128)(2,1)S(1)}, u32[]{:S(2)}, u32[]{:S(2)}) collective-permute-start(bf16[4,4,128,128]{3,2,1,0:T(8,128)(2,1)S(1)} %get-tuple-element.26), channel_id=1, source_target_pairs={{0,1},{1,0},{2,3},{3,2},{4,5},{5,4},{6,7},{7,6},{8,9},{9,8},{10,11... | collective-permute-start | bytes 1572872 | tf_op jit(solution)/shard_map/ppermute | solution.py:22
  23.6 8.7 %collective-permute-start.5 = (bf16[2,4,128,128]{3,2,1,0:T(8,128)(2,1)S(1)}, bf16[2,4,128,128]{3,2,1,0:T(8,128)(2,1)S(1)}, u32[]{:S(2)}, u32[]{:S(2)}) collective-permute-start(bf16[2,4,128,128]{3,2,1,0:T(8,128)(2,1)S(1)} %slice.41), channel_id=1, source_target_pairs={{0,2},{1,3},{2,0},{3,1},{4,6},{5,7},{6,4},{7,5},{8,10},{9,11},{10,... | collective-permute-start | bytes 786440 | tf_op jit(solution)/shard_map/ppermute | solution.py:22
  32.4 5.0 %collective-permute-start.6 = (bf16[1,4,128,128]{3,2,1,0:T(8,128)(2,1)S(1)}, bf16[1,4,128,128]{3,2,1,0:T(8,128)(2,1)S(1)}, u32[]{:S(2)}, u32[]{:S(2)}) collective-permute-start(bf16[1,4,128,128]{3,2,1,0:T(8,128)(2,1)S(1)} %slice.54), channel_id=1, source_target_pairs={{0,4},{1,5},{2,6},{3,7},{4,0},{5,1},{6,2},{7,3},{8,12},{9,13},{10,... | collective-permute-start | bytes 393224 | tf_op jit(solution)/shard_map/ppermute | solution.py:22
  37.5 9.0 %collective-permute-start.7 = (bf16[2,128,128]{2,1,0:T(8,128)(2,1)S(1)}, bf16[2,128,128]{2,1,0:T(8,128)(2,1)S(1)}, u32[]{:S(2)}, u32[]{:S(2)}) collective-permute-start(bf16[2,128,128]{2,1,0:T(8,128)(2,1)S(1)} %slice_bitcast_fusion.2), channel_id=1, source_target_pairs={{0,8},{8,0},{16,24},{24,16},{1,9},{9,1},{17,25},{25,17},{2,10},{10... | collective-permute-start | bytes 196616 | tf_op jit(solution)/shard_map/ppermute | solution.py:22
  43.9 5.3 %collective-permute-start.3 = (bf16[8,128,128]{2,1,0:T(8,128)(2,1)S(1)}, bf16[8,128,128]{2,1,0:T(8,128)(2,1)S(1)}, u32[]{:S(2)}, u32[]{:S(2)}) collective-permute-start(bf16[8,128,128]{2,1,0:T(8,128)(2,1)S(1)} %get-tuple-element.30), channel_id=1, source_target_pairs={{1,0},{2,1},{3,2},{4,3},{5,4},{6,5},{7,6},{9,8},{10,9},{11,10},{12... | collective-permute-start | bytes 786440 | tf_op jit(solution)/shard_map/ppermute | solution.py:17
  45.2 12.1 %collective-permute-start.4 = (bf16[8,128,128]{2,1,0:T(8,128)(2,1)S(1)}, bf16[8,128,128]{2,1,0:T(8,128)(2,1)S(1)}, u32[]{:S(2)}, u32[]{:S(2)}) collective-permute-start(bf16[8,128,128]{2,1,0:T(8,128)(2,1)S(1)} %get-tuple-element.31), channel_id=1, source_target_pairs={{2,0},{3,1},{4,2},{5,3},{6,4},{7,5},{10,8},{11,9},{12,10},{13,11},... | collective-permute-start | bytes 786440 | tf_op jit(solution)/shard_map/ppermute | solution.py:17
  46.6 12.4 %collective-permute-start.8 = (bf16[1,128,128]{2,1,0:T(8,128)(2,1)S(1)}, bf16[1,128,128]{2,1,0:T(8,128)(2,1)S(1)}, u32[]{:S(2)}, u32[]{:S(2)}) collective-permute-start(bf16[1,128,128]{2,1,0:T(8,128)(2,1)S(1)} %slice.60), channel_id=1, source_target_pairs={{0,16},{8,24},{16,0},{24,8},{1,17},{9,25},{17,1},{25,9},{2,18},{10... | collective-permute-start | bytes 98312 | tf_op jit(solution)/shard_map/ppermute | solution.py:22

commit v4 on v3

--- a/solution.py
+++ b/solution.py
@@ -22,9 +22,11 @@
     return lax.ppermute(value, axis, [(source, source ^ bit) for source in range(count)])
 
 
-def halved(keep, axis, bit):
+def halved(keep, axis, bit, beside=None):
     half = keep.shape[0] // 2
     other = exchanged(keep[half:], axis, bit)
+    if beside is not None:
+        other, _ = lax.optimization_barrier((other, beside))
     return keep[:half].astype(WIDE) + other.astype(WIDE)
 
 
@@ -333,14 +335,13 @@
 
     bit = 2
     while bit < ctx:
-        part = halved(part, "ctx", bit).astype(LOW)
+        part = halved(part, "ctx", bit, back_own if bit == 2 else None).astype(LOW)
         bit *= 2
     part = part[0]
+    from_one, from_two, _ = lax.optimization_barrier((from_one, from_two, part))
     bit = 1
     while bit < rep:
         part = part.astype(LOW)
-        if 2 * bit == rep:
-            from_one, from_two, _ = lax.optimization_barrier((from_one, from_two, part))
         part = halved(part, "rep", bit)
         bit *= 2
     grads = jnp.moveaxis(part.astype(WIDE).reshape(here, 2, tenants // rep, rank, dim), 0, 3)

time: 59.9 us -> 55.4 us (0.925)
  the two profiles are of different devices: /device:TPU:0 before, /device:TPU:26 now
where the time goes in v4:
time: 55.4 us; the launch traced here: 55.1 us
  waiting for transfers between devices  20.1 us (36%)
  Pallas kernels  15 us (27%)
  starting transfers between devices  14.1 us (25%)
  local copies, waits for them, and re-layouts  4.65 us (8%)
  between operations  0.83 us (1%)
    pallas_call x3, Pallas kernels, run(): pl.pallas_call(lambda *refs: body(*refs, **fixed), out_shape=[jax.ShapeDt...  15 us
    ppermute x5, waiting for transfers between devices, exchanged(): lax.ppermute(value, axis, [(source, source ^ bit) for source in range(cou...  11.4 us
    ppermute x4, starting transfers between devices, shifted(): lax.ppermute(value, axis, [(source, source + steps) for source in range(f...  10.5 us
    ppermute x4, waiting for transfers between devices, shifted(): lax.ppermute(value, axis, [(source, source + steps) for source in range(f...  8.68 us
    ppermute x5, starting transfers between devices, exchanged(): lax.ppermute(value, axis, [(source, source ^ bit) for source in range(cou...  3.61 us
    unnamed x14, local copies, waits for them, and re-layouts  2.91 us
  transfers between devices with their start and end apart: 9, of which 7 were waited for; matrix products, arithmetic and copies ran while one was open for 3% of the time, Pallas kernels for 18%

profile of v4, /device:TPU:26, one launch (start us, length us, event | category | flops | bytes accessed | tf_op | source)
XLA Modules:
  0.0 55.1 jit_solution(3219936248694585056)
XLA Ops:
  0.6 1.0 %copy_bitcast_fusion = (bf16[128,4,128]{2,0,1:T(8,128)(2,1)S(1)}, bf16[128,4,128]{2,0,1:T(8,128)(2,1)S(1)}) fusion(bf16[1,128,4,128]{3,2,1,0:T(4,128)(2,1)} %param.11, bf16[1,128,4,128]{3,2,1,0:T(4,128)(2,1)} %param.10), kind=kLoop, calls=%fused_computation.9 | loop fusion | bytes 524288 | tf_op jit(solution)/shard_map/squeeze | solution.py:277
  1.6 0.0 copy-start.4
  1.7 0.0 copy-start
  1.7 0.0 copy-start.1
  1.7 2.1 %collective-permute-start.1 = (bf16[8,128,128]{2,1,0:T(8,128)(2,1)S(1)}, bf16[8,128,128]{2,1,0:T(8,128)(2,1)S(1)}, u32[]{:S(2)}, u32[]{:S(2)}) collective-permute-start(bf16[8,128,128]{2,1,0:T(8,128)(2,1)S(1)} %maximum_bitcast_fusion.refs_4_), channel_id=1, source_target_pairs={{0,1},{1,2},{2,3},{3,4},{4,5},{5,6},{6,7},{8,9},{9,10},{10,11},{11... | collective-permute-start | bytes 786440 | tf_op jit(solution)/shard_map/ppermute | solution.py:17
  3.8 3.4 %collective-permute-start = (bf16[8,128,128]{2,1,0:T(8,128)(2,1)S(1)}, bf16[8,128,128]{2,1,0:T(8,128)(2,1)S(1)}, u32[]{:S(2)}, u32[]{:S(2)}) collective-permute-start(bf16[8,128,128]{2,1,0:T(8,128)(2,1)S(1)} %maximum_bitcast_fusion.refs_4_), channel_id=1, source_target_pairs={{0,2},{1,3},{2,4},{3,5},{4,6},{5,7},{8,10},{9,11},{10,12},{11,13},... | collective-permute-start | bytes 786440 | tf_op jit(solution)/shard_map/ppermute | solution.py:17
  7.2 0.0 copy-start.2
  7.2 0.7 %copy-done.2 = s32[1,1024]{1,0:T(1,128)S(1)} copy-done((s32[1,1024]{1,0:T(1,128)S(1)}, s32[1,1024]{1,0:T(1,128)}, u32[]{:S(2)}) %copy-start.2) | copy-done | bytes 4120
  7.9 0.0 copy-start.3
  7.9 0.7 %copy-done.3 = s32[1,1024]{1,0:T(1,128)S(1)} copy-done((s32[1,1024]{1,0:T(1,128)S(1)}, s32[1,1024]{1,0:T(1,128)}, u32[]{:S(2)}) %copy-start.3) | copy-done | bytes 4120
  8.6 5.0 %pull_kernel.1 = (bf16[4,1024,128]{2,1,0:T(8,128)(2,1)}, bf16[4,512,128]{2,1,0:T(8,128)(2,1)S(1)}, f32[8,1024]{1,0:T(8,128)S(1)}, s32[8,1024]{1,0:T(8,128)S(1)}) custom-call(s32[1,1024]{1,0:T(1,128)S(1)} %copy-done.2, s32[1,1024]{1,0:T(1,128)S(1)} %copy-done.3, bf16[128,32,128]{2,1,0:T(8,128)(2,1)} %bitcast.35, bf16[64,32,128]{2,1,0:T(8,128)(2,1)} %bitcast.42, ...), custom_call_target="tpu_custom_call" | custom-call | flops 2147483648 | bytes 4194304 | tf_op jit(solution)/shard_map/pull_kernel/pallas_call | solution.py:289
  13.5 0.0 collective-permute-done.1.refs_3_
  13.5 1.3 %collective-permute-done.refs_2_ = bf16[8,128,128]{2,1,0:T(8,128)(2,1)S(1)} collective-permute-done((bf16[8,128,128]{2,1,0:T(8,128)(2,1)S(1)}, bf16[8,128,128]{2,1,0:T(8,128)(2,1)S(1)}, u32[]{:S(2)}, u32[]{:S(2)}) %collective-permute-start) | collective-permute-done | bytes 262176 | tf_op jit(solution)/shard_map/ppermute | solution.py:17
  14.8 0.0 copy-done.4
  14.8 0.0 copy-done
  14.8 0.0 copy-done.1
  14.8 0.0 copy-start.5
  14.8 5.2 %forward_kernel.1 = (f32[4,256,1024]{2,1,0:T(8,128)S(1)}, bf16[4,4,128,128]{3,2,1,0:T(8,128)(2,1)S(1)}, bf16[4,4,128,128]{3,2,1,0:T(8,128)(2,1)S(1)}) custom-call(f32[4,16]{1,0:T(4,128)S(1)} %bitcast.39, bf16[128,32,128]{2,1,0:T(8,128)(2,1)S(1)} %bitcast.37, bf16[8,128,128]{2,1,0:T(8,128)(2,1)S(1)} %collective-permute-done.refs_2_, ...), custom_call_target="tpu_custom_call" | custom-call | flops 4294967296 | bytes 10485760 | tf_op jit(solution)/shard_map/forward_kernel/pallas_call | solution.py:289
  20.1 0.2 collective-permute-start.2
  20.3 1.8 %collective-permute-done.2 = bf16[4,4,128,128]{3,2,1,0:T(8,128)(2,1)S(1)} collective-permute-done((bf16[4,4,128,128]{3,2,1,0:T(8,128)(2,1)S(1)}, bf16[4,4,128,128]{3,2,1,0:T(8,128)(2,1)S(1)}, u32[]{:S(2)}, u32[]{:S(2)}) %collective-permute-start.2) | collective-permute-done | bytes 524320 | tf_op jit(solution)/shard_map/ppermute | solution.py:22
  22.1 0.1 add_convert_fusion
  22.2 0.3 collective-permute-start.5
  22.5 0.0 copy-done.5
  22.5 4.8 %backward_kernel.1 = (bf16[128,32,128]{2,1,0:T(8,128)(2,1)}, bf16[8,128,128]{2,1,0:T(8,128)(2,1)S(1)}, bf16[8,128,128]{2,1,0:T(8,128)(2,1)S(1)}, f32[8,128,128]{2,1,0:T(8,128)S(1)}) custom-call(bf16[128,32,128]{2,1,0:T(8,128)(2,1)S(1)} %bitcast.38, bf16[4,1024,128]{2,1,0:T(8,128)(2,1)S(1)} %copy-done.5, ...), custom_call_target="tpu_custom_call" | custom-call | flops 4294967296 | bytes 10485760 | tf_op jit(solution)/shard_map/backward_kernel/pallas_call | solution.py:289
  27.3 3.2 %collective-permute-start.3 = (bf16[8,128,128]{2,1,0:T(8,128)(2,1)S(1)}, bf16[8,128,128]{2,1,0:T(8,128)(2,1)S(1)}, u32[]{:S(2)}, u32[]{:S(2)}) collective-permute-start(bf16[8,128,128]{2,1,0:T(8,128)(2,1)S(1)} %get-tuple-element.31), channel_id=1, source_target_pairs={{1,0},{2,1},{3,2},{4,3},{5,4},{6,5},{7,6},{9,8},{10,9},{11,10},{12... | collective-permute-start | bytes 786440 | tf_op jit(solution)/shard_map/ppermute | solution.py:17
  30.5 1.9 %collective-permute-start.4 = (bf16[8,128,128]{2,1,0:T(8,128)(2,1)S(1)}, bf16[8,128,128]{2,1,0:T(8,128)(2,1)S(1)}, u32[]{:S(2)}, u32[]{:S(2)}) collective-permute-start(bf16[8,128,128]{2,1,0:T(8,128)(2,1)S(1)} %get-tuple-element.32), channel_id=1, source_target_pairs={{2,0},{3,1},{4,2},{5,3},{6,4},{7,5},{10,8},{11,9},{12,10},{13,11},... | collective-permute-start | bytes 786440 | tf_op jit(solution)/shard_map/ppermute | solution.py:17
  32.4 0.0 collective-permute-done.5
  32.4 0.1 add_convert_fusion.1
  32.5 2.2 %collective-permute-start.6 = (bf16[1,4,128,128]{3,2,1,0:T(8,128)(2,1)S(1)}, bf16[1,4,128,128]{3,2,1,0:T(8,128)(2,1)S(1)}, u32[]{:S(2)}, u32[]{:S(2)}) collective-permute-start(bf16[1,4,128,128]{3,2,1,0:T(8,128)(2,1)S(1)} %slice.56), channel_id=1, source_target_pairs={{0,4},{1,5},{2,6},{3,7},{4,0},{5,1},{6,2},{7,3},{8,12},{9,13},{10,... | collective-permute-start | bytes 393224 | tf_op jit(solution)/shard_map/ppermute | solution.py:22
  34.8 0.4 collective-permute-done.3
  35.1 7.0 %collective-permute-done.4 = bf16[8,128,128]{2,1,0:T(8,128)(2,1)S(1)} collective-permute-done((bf16[8,128,128]{2,1,0:T(8,128)(2,1)S(1)}, bf16[8,128,128]{2,1,0:T(8,128)(2,1)S(1)}, u32[]{:S(2)}, u32[]{:S(2)}) %collective-permute-start.4) | collective-permute-done | bytes 262176 | tf_op jit(solution)/shard_map/ppermute | solution.py:17
  42.1 2.7 %collective-permute-done.6 = bf16[1,4,128,128]{3,2,1,0:T(8,128)(2,1)S(1)} collective-permute-done((bf16[1,4,128,128]{3,2,1,0:T(8,128)(2,1)S(1)}, bf16[1,4,128,128]{3,2,1,0:T(8,128)(2,1)S(1)}, u32[]{:S(2)}, u32[]{:S(2)}) %collective-permute-start.6) | collective-permute-done | bytes 131104 | tf_op jit(solution)/shard_map/ppermute | solution.py:22
  44.9 0.5 collective-permute-start.7
  45.4 0.1 add_convert_fusion.2
  45.5 3.7 %collective-permute-done.7 = bf16[2,128,128]{2,1,0:T(8,128)(2,1)S(1)} collective-permute-done((bf16[2,128,128]{2,1,0:T(8,128)(2,1)S(1)}, bf16[2,128,128]{2,1,0:T(8,128)(2,1)S(1)}, u32[]{:S(2)}, u32[]{:S(2)}) %collective-permute-start.7) | collective-permute-done | bytes 65568 | tf_op jit(solution)/shard_map/ppermute | solution.py:22
  49.3 0.4 collective-permute-start.8
  49.7 0.8 %copy.18 = bf16[1,128,4,128]{3,2,1,0:T(4,128)(2,1)} copy(bf16[1,128,4,128]{3,1,2,0:T(8,128)(2,1)S(1)} %get-tuple-element.42) | data formatting | bytes 262144
  50.4 0.8 %copy.17 = bf16[1,128,4,128]{3,2,1,0:T(4,128)(2,1)} copy(bf16[1,128,4,128]{3,1,2,0:T(8,128)(2,1)S(1)} %get-tuple-element.43) | data formatting | bytes 262144
  51.2 3.2 %collective-permute-done.8 = bf16[1,128,128]{2,1,0:T(8,128)(2,1)S(1)} collective-permute-done((bf16[1,128,128]{2,1,0:T(8,128)(2,1)S(1)}, bf16[1,128,128]{2,1,0:T(8,128)(2,1)S(1)}, u32[]{:S(2)}, u32[]{:S(2)}) %collective-permute-start.8) | collective-permute-done | bytes 32800 | tf_op jit(solution)/shard_map/ppermute | solution.py:22
  54.4 0.6 %slice_bitcast_fusion.4 = (f32[4,4,4,128]{3,2,1,0:T(4,128)}, f32[4,4,4,128]{3,2,1,0:T(4,128)}) fusion(f32[2,4,4,4,128]{4,3,2,1,0:T(4,128)S(1)} %bitcast.40), kind=kLoop, calls=%fused_computation.15 | loop fusion | bytes 131072 | tf_op jit(solution)/shard_map/squeeze | solution.py:351
  (10 shorter events, 0.2 us)
Async XLA Ops:
  1.6 13.2 %copy-start.4 = (f32[16,4]{0,1:T(4,128)S(1)}, f32[16,4]{0,1:T(4,128)}, u32[]{:S(2)}) copy-start(f32[16,4]{0,1:T(4,128)} %param.15) | copy-start | bytes 772
  1.7 13.2 %copy-start = (bf16[1,128,32,128]{3,2,1,0:T(8,128)(2,1)S(1)}, bf16[1,128,32,128]{3,2,1,0:T(8,128)(2,1)}, u32[]{:S(2)}) copy-start(bf16[1,128,32,128]{3,2,1,0:T(8,128)(2,1)} %param.12) | copy-start | bytes 3145732
  1.7 13.2 %copy-start.1 = (bf16[1,128,32,128]{3,2,1,0:T(8,128)(2,1)S(1)}, bf16[1,128,32,128]{3,2,1,0:T(8,128)(2,1)}, u32[]{:S(2)}) copy-start(bf16[1,128,32,128]{3,2,1,0:T(8,128)(2,1)} %param.9) | copy-start | bytes 3145732
  1.7 11.8 %collective-permute-start.1 = (bf16[8,128,128]{2,1,0:T(8,128)(2,1)S(1)}, bf16[8,128,128]{2,1,0:T(8,128)(2,1)S(1)}, u32[]{:S(2)}, u32[]{:S(2)}) collective-permute-start(bf16[8,128,128]{2,1,0:T(8,128)(2,1)S(1)} %maximum_bitcast_fusion.refs_4_), channel_id=1, source_target_pairs={{0,1},{1,2},{2,3},{3,4},{4,5},{5,6},{6,7},{8,9},{9,10},{10,11},{11... | collective-permute-start | bytes 786440 | tf_op jit(solution)/shard_map/ppermute | solution.py:17
  3.8 11.1 %collective-permute-start = (bf16[8,128,128]{2,1,0:T(8,128)(2,1)S(1)}, bf16[8,128,128]{2,1,0:T(8,128)(2,1)S(1)}, u32[]{:S(2)}, u32[]{:S(2)}) collective-permute-start(bf16[8,128,128]{2,1,0:T(8,128)(2,1)S(1)} %maximum_bitcast_fusion.refs_4_), channel_id=1, source_target_pairs={{0,2},{1,3},{2,4},{3,5},{4,6},{5,7},{8,10},{9,11},{10,12},{11,13},... | collective-permute-start | bytes 786440 | tf_op jit(solution)/shard_map/ppermute | solution.py:17
  7.2 0.7 %copy-start.2 = (s32[1,1024]{1,0:T(1,128)S(1)}, s32[1,1024]{1,0:T(1,128)}, u32[]{:S(2)}) copy-start(s32[1,1024]{1,0:T(1,128)} %refs_0_.1) | copy-start | bytes 12292
  7.9 0.7 %copy-start.3 = (s32[1,1024]{1,0:T(1,128)S(1)}, s32[1,1024]{1,0:T(1,128)}, u32[]{:S(2)}) copy-start(s32[1,1024]{1,0:T(1,128)} %refs_1_.1) | copy-start | bytes 12292
  14.8 7.7 %copy-start.5 = (bf16[4,1024,128]{2,1,0:T(8,128)(2,1)S(1)}, bf16[4,1024,128]{2,1,0:T(8,128)(2,1)}, u32[]{:S(2)}) copy-start(bf16[4,1024,128]{2,1,0:T(8,128)(2,1)} %get-tuple-element.21.refs_1_) | copy-start | bytes 3145732
  20.1 2.0 %collective-permute-start.2 = (bf16[4,4,128,128]{3,2,1,0:T(8,128)(2,1)S(1)}, bf16[4,4,128,128]{3,2,1,0:T(8,128)(2,1)S(1)}, u32[]{:S(2)}, u32[]{:S(2)}) collective-permute-start(bf16[4,4,128,128]{3,2,1,0:T(8,128)(2,1)S(1)} %get-tuple-element.27), channel_id=1, source_target_pairs={{0,1},{1,0},{2,3},{3,2},{4,5},{5,4},{6,7},{7,6},{8,9},{9,8},{10,11... | collective-permute-start | bytes 1572872 | tf_op jit(solution)/shard_map/ppermute | solution.py:22
  22.2 10.2 %collective-permute-start.5 = (bf16[2,4,128,128]{3,2,1,0:T(8,128)(2,1)S(1)}, bf16[2,4,128,128]{3,2,1,0:T(8,128)(2,1)S(1)}, u32[]{:S(2)}, u32[]{:S(2)}) collective-permute-start(bf16[2,4,128,128]{3,2,1,0:T(8,128)(2,1)S(1)} %slice.43), channel_id=1, source_target_pairs={{0,2},{1,3},{2,0},{3,1},{4,6},{5,7},{6,4},{7,5},{8,10},{9,11},{10,... | collective-permute-start | bytes 786440 | tf_op jit(solution)/shard_map/ppermute | solution.py:22
  27.3 7.8 %collective-permute-start.3 = (bf16[8,128,128]{2,1,0:T(8,128)(2,1)S(1)}, bf16[8,128,128]{2,1,0:T(8,128)(2,1)S(1)}, u32[]{:S(2)}, u32[]{:S(2)}) collective-permute-start(bf16[8,128,128]{2,1,0:T(8,128)(2,1)S(1)} %get-tuple-element.31), channel_id=1, source_target_pairs={{1,0},{2,1},{3,2},{4,3},{5,4},{6,5},{7,6},{9,8},{10,9},{11,10},{12... | collective-permute-start | bytes 786440 | tf_op jit(solution)/shard_map/ppermute | solution.py:17
  30.5 11.6 %collective-permute-start.4 = (bf16[8,128,128]{2,1,0:T(8,128)(2,1)S(1)}, bf16[8,128,128]{2,1,0:T(8,128)(2,1)S(1)}, u32[]{:S(2)}, u32[]{:S(2)}) collective-permute-start(bf16[8,128,128]{2,1,0:T(8,128)(2,1)S(1)} %get-tuple-element.32), channel_id=1, source_target_pairs={{2,0},{3,1},{4,2},{5,3},{6,4},{7,5},{10,8},{11,9},{12,10},{13,11},... | collective-permute-start | bytes 786440 | tf_op jit(solution)/shard_map/ppermute | solution.py:17
  32.5 12.3 %collective-permute-start.6 = (bf16[1,4,128,128]{3,2,1,0:T(8,128)(2,1)S(1)}, bf16[1,4,128,128]{3,2,1,0:T(8,128)(2,1)S(1)}, u32[]{:S(2)}, u32[]{:S(2)}) collective-permute-start(bf16[1,4,128,128]{3,2,1,0:T(8,128)(2,1)S(1)} %slice.56), channel_id=1, source_target_pairs={{0,4},{1,5},{2,6},{3,7},{4,0},{5,1},{6,2},{7,3},{8,12},{9,13},{10,... | collective-permute-start | bytes 393224 | tf_op jit(solution)/shard_map/ppermute | solution.py:22
  44.9 4.3 %collective-permute-start.7 = (bf16[2,128,128]{2,1,0:T(8,128)(2,1)S(1)}, bf16[2,128,128]{2,1,0:T(8,128)(2,1)S(1)}, u32[]{:S(2)}, u32[]{:S(2)}) collective-permute-start(bf16[2,128,128]{2,1,0:T(8,128)(2,1)S(1)} %slice_bitcast_fusion.2), channel_id=1, source_target_pairs={{0,8},{8,0},{16,24},{24,16},{1,9},{9,1},{17,25},{25,17},{2,10},{10... | collective-permute-start | bytes 196616 | tf_op jit(solution)/shard_map/ppermute | solution.py:22
  49.3 5.1 %collective-permute-start.8 = (bf16[1,128,128]{2,1,0:T(8,128)(2,1)S(1)}, bf16[1,128,128]{2,1,0:T(8,128)(2,1)S(1)}, u32[]{:S(2)}, u32[]{:S(2)}) collective-permute-start(bf16[1,128,128]{2,1,0:T(8,128)(2,1)S(1)} %slice.60), channel_id=1, source_target_pairs={{0,16},{8,24},{16,0},{24,8},{1,17},{9,25},{17,1},{25,9},{2,18},{10... | collective-permute-start | bytes 98312 | tf_op jit(solution)/shard_map/ppermute | solution.py:22

commit v5 on v3

--- a/solution.py
+++ b/solution.py
@@ -1,5 +1,8 @@
+import itertools
+
 import jax
 import jax.numpy as jnp
+import numpy as np
 from jax import lax
 from jax.experimental import pallas as pl
 from jax.experimental.pallas import tpu as pltpu
@@ -13,26 +16,49 @@
 
 def shifted(value, axis, steps):
     count = lax.axis_size(axis)
-    first, last = (max(0, -steps), min(count, count - steps))
-    return lax.ppermute(value, axis, [(source, source + steps) for source in range(first, last)])
-
-
-def exchanged(value, axis, bit):
-    count = lax.axis_size(axis)
-    return lax.ppermute(value, axis, [(source, source ^ bit) for source in range(count)])
-
-
-def halved(keep, axis, bit):
-    half = keep.shape[0] // 2
-    other = exchanged(keep[half:], axis, bit)
-    return keep[:half].astype(WIDE) + other.astype(WIDE)
-
-
-def reversed_bits(value, bits):
-    result = 0 * value
-    for bit in range(bits):
-        result = result + ((value >> bit) & 1) * (1 << (bits - 1 - bit))
-    return result
+    return lax.ppermute(value, axis, [(source, (source + steps) % count) for source in range(count)])
+
+
+def exchanged(value, bits):
+    axes = tuple(bits)
+    shape = [lax.axis_size(axis) for axis in axes]
+    pairs = []
+    for source in np.ndindex(*shape):
+        target = [at ^ bits[axis] for at, axis in zip(source, axes)]
+        pairs.append((np.ravel_multi_index(source, shape), np.ravel_multi_index(target, shape)))
+    return lax.ppermute(value, axes, [(int(source), int(target)) for source, target in pairs])
+
+
+def reduce_groups():
+    ctx, rep = lax.axis_size("ctx"), lax.axis_size("rep")
+    over_ctx = [{"ctx": 1 << at} for at in range(ctx.bit_length() - 2, 0, -1)]
+    over_rep = [{"rep": 1 << at} for at in range(rep.bit_length() - 1)]
+    return [
+        [pair for pair in pairs if pair] for pairs in itertools.zip_longest(over_ctx, over_rep)
+    ]
+
+
+def reduce_place(index):
+    place = 0
+    for bits in itertools.chain(*reduce_groups()):
+        for axis, bit in bits.items():
+            place = 2 * place + (index[axis] // bit) % 2
+    return place
+
+
+def scattered(part, group, beside=None):
+    count = 1 << len(group)
+    size = part.shape[0] // count
+    others = []
+    for j in range(1, count):
+        bits = {}
+        for at, pair in enumerate(reversed(group)):
+            if (j >> at) & 1:
+                bits.update(pair)
+        others.append(exchanged(part[j * size : (j + 1) * size], bits))
+    if beside is not None:
+        others = lax.optimization_barrier((others, beside))[0]
+    return part[:size].astype(WIDE) + sum(other.astype(WIDE) for other in others)
 
 
 def dot(left, right, left_dim, right_dim, precision=None):
@@ -195,19 +221,17 @@
     on_rot = dot(lift_all, jnp.concatenate(group_rows(cot_ref, kv, group), axis=1), 1, 0) - on_proj
     dim = q_ref.shape[2]
     here_rows = span // rep
-    bits = ctx.bit_length() - 1
     for g in range(kv):
         columns = slice(g * dim, (g + 1) * dim)
         for low in range(per_group):
             device = (g ^ (me // per_group)) * per_group + low
-            place = reversed_bits(device >> 1, bits - 1)
             into = send_ref if low % 2 else keep_ref
             for r in range(rep):
                 pieces = []
                 for h in range(low * owned, (low + 1) * owned):
                     rows = slice(h * span + r * here_rows, h * span + (r + 1) * here_rows)
                     pieces += [on_rot[rows, columns], on_proj[rows, columns]]
-                into[place, reversed_bits(r, rep.bit_length() - 1)] = jnp.concatenate(pieces, axis=0).astype(LOW)
+                into[reduce_place(dict(ctx=device, rep=r))] = jnp.concatenate(pieces, axis=0).astype(LOW)
 
 
 def backward_kernel(
@@ -273,7 +297,7 @@
     assert 2 * tokens == DOC_MAX
 
     own = jnp.moveaxis(jnp.concatenate([key_rows[0], value_matrix[0]], axis=1), 1, 0)
-    one = shifted(own, "ctx", 1)
+    even = lax.axis_index("ctx") % 2 == 0
     two = shifted(own, "ctx", 2)
 
     rot = rotation.reshape(tenants * rank, heads, dim)
@@ -314,37 +338,31 @@
         ],
         limit=53, tenants=tenants, rank=rank, **sizes,
     )(doc_starts, tenant_ids, upstream, rot, proj)
+    two, meta = lax.optimization_barrier((two, meta))
+    one = exchanged(jnp.where(even, own, two), {"ctx": 1})
     weights, send, keep = call(
         forward_kernel,
-        [((kv, 2 * tokens, lanes), WIDE)] + [((ctx // 2, rep, rows, dim), LOW)] * 2,
+        [((kv, 2 * tokens, lanes), WIDE)] + [((ctx * rep // 2, rows, dim), LOW)] * 2,
         4 * 2**30, 10 * 2**20, [vmem] * 5 + [hbm] + [vmem] * 3,
         [pltpu.VMEM((tokens, heads, dim), LOW), pltpu.SemaphoreType.DMA],
         tenants=tenants, rank=rank, scaling=scaling, owned=here, **sizes,
     )(shift_bias.T, queries, two, one, own, upstream, diff, meta, pulled)
-    part = (keep.astype(WIDE) + exchanged(send, "ctx", 1).astype(WIDE)).astype(LOW)
+    part = (keep.astype(WIDE) + exchanged(send, {"ctx": 1}).astype(WIDE)).astype(LOW)
     weights, part = lax.optimization_barrier((weights, part))
     d_queries, back_two, back_one, back_own = call(
         backward_kernel,
         [((tokens, heads, dim), LOW), (own.shape, LOW), (own.shape, LOW), (own.shape, WIDE)],
         4 * 2**30, 10 * 2**20, scaling=scaling, **sizes,
     )(queries, grad_hidden, two, one, own, weights)
-    from_one = shifted(back_one, "ctx", -1)
-    from_two = shifted(back_two, "ctx", -2)
-
-    bit = 2
-    while bit < ctx:
-        part = halved(part, "ctx", bit).astype(LOW)
-        bit *= 2
-    part = part[0]
-    bit = 1
-    while bit < rep:
-        part = part.astype(LOW)
-        if 2 * bit == rep:
-            from_one, from_two, _ = lax.optimization_barrier((from_one, from_two, part))
-        part = halved(part, "rep", bit)
-        bit *= 2
-    grads = jnp.moveaxis(part.astype(WIDE).reshape(here, 2, tenants // rep, rank, dim), 0, 3)
-    back = (back_own + from_one.astype(WIDE) + from_two.astype(WIDE)).astype(LOW)
+    from_mate = exchanged(back_one, {"ctx": 1}).astype(WIDE)
+    onward = back_two.astype(WIDE) + jnp.where(even, 0.0, from_mate)
+    from_two = shifted(onward.astype(LOW), "ctx", -2)
+
+    for at, group_bits in enumerate(reduce_groups()):
+        part = scattered(part.astype(LOW), group_bits, back_own if at == 0 else None)
+    grads = jnp.moveaxis(part.reshape(here, 2, tenants // rep, rank, dim), 0, 3)
+    back = back_own + from_two.astype(WIDE) + jnp.where(even, from_mate, 0.0)
+    back = back.astype(LOW)
     d_keys = jnp.moveaxis(back[:kv], 0, 1)
     d_values = jnp.moveaxis(back[kv:], 0, 1)
     return (d_queries[None], d_keys[None], d_values[None], grads[0], grads[1])

time: 59.9 us -> 45.5 us (0.76)
  waiting for transfers between devices: 19.6 us -> 11.5 us
  starting transfers between devices: 19.1 us -> 12.8 us
    ppermute x9 -> x11, waiting for transfers between devices: 19.6 us -> 11.5 us  [the longest x9 6.98 us: exchanged(): lax.ppermute(value, axes, [(int(source), int(target)) for source, target...]
    ppermute x9 -> x11, starting transfers between devices: 19.1 us -> 12.8 us  [the longest x9 8.28 us: exchanged(): lax.ppermute(value, axes, [(int(source), int(target)) for source, target...]
  transfers between devices with their start and end apart: 9 -> 11, of which waited for: 4 -> 7; matrix products, arithmetic and copies ran while one was open for 3% -> 2% of each run, Pallas kernels for 16% -> 22%
where the time goes in v5:
time: 45.5 us; the launch traced here: 45.3 us
  Pallas kernels  15.1 us (33%)
  starting transfers between devices  12.8 us (28%)
  waiting for transfers between devices  11.5 us (25%)
  local copies, waits for them, and re-layouts  4.65 us (10%)
  between operations  0.75 us (2%)
  other arithmetic  0.49 us (1%)
    pallas_call x3, Pallas kernels, run(): pl.pallas_call(lambda *refs: body(*refs, **fixed), out_shape=[jax.ShapeDt...  15.1 us
    ppermute x9, starting transfers between devices, exchanged(): lax.ppermute(value, axes, [(int(source), int(target)) for source, target...  8.28 us
    ppermute x9, waiting for transfers between devices, exchanged(): lax.ppermute(value, axes, [(int(source), int(target)) for source, target...  6.98 us
    ppermute x2, waiting for transfers between devices, shifted(): lax.ppermute(value, axis, [(source, (source + steps) % count) for source...  4.53 us
    ppermute x2, starting transfers between devices, shifted(): lax.ppermute(value, axis, [(source, (source + steps) % count) for source...  4.51 us
    unnamed x14, local copies, waits for them, and re-layouts  2.91 us
    squeeze x1, local copies, waits for them, and re-layouts, on_device(): value_matrix[0]  1 us
  transfers between devices with their start and end apart: 11, of which 7 were waited for; matrix products, arithmetic and copies ran while one was open for 2% of the time, Pallas kernels for 22%

profile of v5, /device:TPU:0, one launch (start us, length us, event | category | flops | bytes accessed | tf_op | source)
XLA Modules:
  0.0 45.3 jit_solution(15821185763461380097)
XLA Ops:
  0.6 1.0 %copy_bitcast_fusion = (bf16[128,4,128]{2,0,1:T(8,128)(2,1)S(1)}, bf16[128,4,128]{2,0,1:T(8,128)(2,1)S(1)}) fusion(bf16[1,128,4,128]{3,2,1,0:T(4,128)(2,1)} %param.11, bf16[1,128,4,128]{3,2,1,0:T(4,128)(2,1)} %param.10), kind=kLoop, calls=%fused_computation.12 | loop fusion | bytes 524288 | tf_op jit(solution)/shard_map/squeeze | solution.py:299
  1.7 3.0 %collective-permute-start = (bf16[8,128,128]{2,1,0:T(8,128)(2,1)S(1)}, bf16[8,128,128]{2,1,0:T(8,128)(2,1)S(1)}, u32[]{:S(2)}, u32[]{:S(2)}) collective-permute-start(bf16[8,128,128]{2,1,0:T(8,128)(2,1)S(1)} %maximum_bitcast_fusion.refs_4_), channel_id=1, source_target_pairs={{0,2},{1,3},{2,4},{3,5},{4,6},{5,7},{6,0},{7,1},{8,10},{9,11},{10,... | collective-permute-start | bytes 786440 | tf_op jit(solution)/shard_map/ppermute | solution.py:19
  4.7 0.0 copy-start.2
  4.7 0.7 %copy-done.2 = s32[1,1024]{1,0:T(1,128)S(1)} copy-done((s32[1,1024]{1,0:T(1,128)S(1)}, s32[1,1024]{1,0:T(1,128)}, u32[]{:S(2)}) %copy-start.2) | copy-done | bytes 4120
  5.4 0.0 copy-start.3
  5.4 0.7 %copy-done.3 = s32[1,1024]{1,0:T(1,128)S(1)} copy-done((s32[1,1024]{1,0:T(1,128)S(1)}, s32[1,1024]{1,0:T(1,128)}, u32[]{:S(2)}) %copy-start.3) | copy-done | bytes 4120
  6.0 0.0 copy-start
  6.0 0.0 copy-start.1
  6.0 0.0 copy-start.4
  6.0 5.1 %pull_kernel.1 = (bf16[4,1024,128]{2,1,0:T(8,128)(2,1)}, bf16[4,512,128]{2,1,0:T(8,128)(2,1)S(1)}, f32[8,1024]{1,0:T(8,128)S(1)}, s32[8,1024]{1,0:T(8,128)S(1)}) custom-call(s32[1,1024]{1,0:T(1,128)S(1)} %copy-done.2, s32[1,1024]{1,0:T(1,128)S(1)} %copy-done.3, bf16[128,32,128]{2,1,0:T(8,128)(2,1)} %bitcast.30, bf16[64,32,128]{2,1,0:T(8,128)(2,1)} %bitcast.37, ...), custom_call_target="tpu_custom_call" | custom-call | flops 2147483648 | bytes 4194304 | tf_op jit(solution)/shard_map/pull_kernel/pallas_call | solution.py:311
  11.1 0.8 %collective-permute-done.refs_2_ = bf16[8,128,128]{2,1,0:T(8,128)(2,1)S(1)} collective-permute-done((bf16[8,128,128]{2,1,0:T(8,128)(2,1)S(1)}, bf16[8,128,128]{2,1,0:T(8,128)(2,1)S(1)}, u32[]{:S(2)}, u32[]{:S(2)}) %collective-permute-start) | collective-permute-done | bytes 262176 | tf_op jit(solution)/shard_map/ppermute | solution.py:19
  12.0 0.1 collective-permute-start.1
  12.0 1.5 %collective-permute-done.1.refs_3_ = bf16[8,128,128]{2,1,0:T(8,128)(2,1)S(1)} collective-permute-done((bf16[8,128,128]{2,1,0:T(8,128)(2,1)S(1)}, bf16[8,128,128]{2,1,0:T(8,128)(2,1)S(1)}, u32[]{:S(2)}, u32[]{:S(2)}) %collective-permute-start.1) | collective-permute-done | bytes 262176 | tf_op jit(solution)/shard_map/ppermute | solution.py:29
  13.6 0.0 copy-done
  13.6 0.0 copy-done.1
  13.6 0.0 copy-done.4
  13.6 0.0 copy-start.5
  13.6 5.2 %forward_kernel.1 = (f32[4,256,1024]{2,1,0:T(8,128)S(1)}, bf16[16,128,128]{2,1,0:T(8,128)(2,1)S(1)}, bf16[16,128,128]{2,1,0:T(8,128)(2,1)S(1)}) custom-call(f32[4,16]{1,0:T(4,128)S(1)} %bitcast.34, bf16[128,32,128]{2,1,0:T(8,128)(2,1)S(1)} %bitcast.32, bf16[8,128,128]{2,1,0:T(8,128)(2,1)S(1)} %collective-permute-done.refs_2_, ...), custom_call_target="tpu_custom_call" | custom-call | flops 4294967296 | bytes 10485760 | tf_op jit(solution)/shard_map/forward_kernel/pallas_call | solution.py:311
  18.8 0.2 collective-permute-start.2
  19.0 1.8 %collective-permute-done.2 = bf16[16,128,128]{2,1,0:T(8,128)(2,1)S(1)} collective-permute-done((bf16[16,128,128]{2,1,0:T(8,128)(2,1)S(1)}, bf16[16,128,128]{2,1,0:T(8,128)(2,1)S(1)}, u32[]{:S(2)}, u32[]{:S(2)}) %collective-permute-start.2) | collective-permute-done | bytes 524320 | tf_op jit(solution)/shard_map/ppermute | solution.py:29
  20.8 0.1 add_convert_fusion
  21.0 2.8 %collective-permute-start.7 = (bf16[4,128,128]{2,1,0:T(8,128)(2,1)S(1)}, bf16[4,128,128]{2,1,0:T(8,128)(2,1)S(1)}, u32[]{:S(2)}, u32[]{:S(2)}) collective-permute-start(bf16[4,128,128]{2,1,0:T(8,128)(2,1)S(1)} %get-tuple-element.46), channel_id=1, source_target_pairs={{0,12},{1,13},{2,14},{3,15},{4,8},{5,9},{6,10},{7,11},{8,4},{9,5},... | collective-permute-start | bytes 393224 | tf_op jit(solution)/shard_map/ppermute | solution.py:29
  23.8 0.5 %collective-permute-start.6 = (bf16[4,128,128]{2,1,0:T(8,128)(2,1)S(1)}, bf16[4,128,128]{2,1,0:T(8,128)(2,1)S(1)}, u32[]{:S(2)}, u32[]{:S(2)}) collective-permute-start(bf16[4,128,128]{2,1,0:T(8,128)(2,1)S(1)} %get-tuple-element.47), channel_id=1, source_target_pairs={{0,4},{1,5},{2,6},{3,7},{4,0},{5,1},{6,2},{7,3},{8,12},{9,13},{10,... | collective-permute-start | bytes 393224 | tf_op jit(solution)/shard_map/ppermute | solution.py:29
  24.3 0.3 collective-permute-start.5
  24.5 0.0 copy-done.5
  24.5 4.8 %backward_kernel.1 = (bf16[128,32,128]{2,1,0:T(8,128)(2,1)}, bf16[8,128,128]{2,1,0:T(8,128)(2,1)S(1)}, bf16[8,128,128]{2,1,0:T(8,128)(2,1)S(1)}, f32[8,128,128]{2,1,0:T(8,128)S(1)}) custom-call(bf16[128,32,128]{2,1,0:T(8,128)(2,1)S(1)} %bitcast.33, bf16[4,1024,128]{2,1,0:T(8,128)(2,1)S(1)} %copy-done.5, ...), custom_call_target="tpu_custom_call" | custom-call | flops 4294967296 | bytes 10485760 | tf_op jit(solution)/shard_map/backward_kernel/pallas_call | solution.py:311
  29.3 0.0 collective-permute-start.3
  29.3 0.0 collective-permute-done.7
  29.3 1.0 %collective-permute-done.6 = bf16[4,128,128]{2,1,0:T(8,128)(2,1)S(1)} collective-permute-done((bf16[4,128,128]{2,1,0:T(8,128)(2,1)S(1)}, bf16[4,128,128]{2,1,0:T(8,128)(2,1)S(1)}, u32[]{:S(2)}, u32[]{:S(2)}) %collective-permute-start.6) | collective-permute-done | bytes 131104 | tf_op jit(solution)/shard_map/ppermute | solution.py:29
  30.4 0.2 collective-permute-done.5
  30.6 0.1 add_convert_fusion.1
  30.7 2.7 %collective-permute-start.8 = (bf16[1,128,128]{2,1,0:T(8,128)(2,1)S(1)}, bf16[1,128,128]{2,1,0:T(8,128)(2,1)S(1)}, u32[]{:S(2)}, u32[]{:S(2)}) collective-permute-start(bf16[1,128,128]{2,1,0:T(8,128)(2,1)S(1)} %get-tuple-element.51), channel_id=1, source_target_pairs={{0,16},{8,24},{16,0},{24,8},{1,17},{9,25},{17,1},{25,9},{2,18},{10... | collective-permute-start | bytes 98312 | tf_op jit(solution)/shard_map/ppermute | solution.py:29
  33.3 0.4 collective-permute-start.10
  33.7 1.4 %collective-permute-start.9 = (bf16[1,128,128]{2,1,0:T(8,128)(2,1)S(1)}, bf16[1,128,128]{2,1,0:T(8,128)(2,1)S(1)}, u32[]{:S(2)}, u32[]{:S(2)}) collective-permute-start(bf16[1,128,128]{2,1,0:T(8,128)(2,1)S(1)} %get-tuple-element.53), channel_id=1, source_target_pairs={{0,2},{1,3},{2,0},{3,1},{4,6},{5,7},{6,4},{7,5},{8,10},{9,11},{10,... | collective-permute-start | bytes 98312 | tf_op jit(solution)/shard_map/ppermute | solution.py:29
  35.1 0.0 collective-permute-done.3
  35.1 0.1 fusion.1
  35.2 1.5 %collective-permute-start.4 = (bf16[8,128,128]{2,1,0:T(8,128)(2,1)S(1)}, bf16[8,128,128]{2,1,0:T(8,128)(2,1)S(1)}, u32[]{:S(2)}, u32[]{:S(2)}) collective-permute-start(bf16[8,128,128]{2,1,0:T(8,128)(2,1)S(1)} %fusion.1), channel_id=1, source_target_pairs={{0,6},{1,7},{2,0},{3,1},{4,2},{5,3},{6,4},{7,5},{8,14},{9,15},{10,... | collective-permute-start | bytes 786440 | tf_op jit(solution)/shard_map/ppermute | solution.py:19
  36.7 0.0 collective-permute-done.8
  36.7 2.5 %collective-permute-done.10 = bf16[1,128,128]{2,1,0:T(8,128)(2,1)S(1)} collective-permute-done((bf16[1,128,128]{2,1,0:T(8,128)(2,1)S(1)}, bf16[1,128,128]{2,1,0:T(8,128)(2,1)S(1)}, u32[]{:S(2)}, u32[]{:S(2)}) %collective-permute-start.10) | collective-permute-done | bytes 32800 | tf_op jit(solution)/shard_map/ppermute | solution.py:29
  39.2 0.0 collective-permute-done.9
  39.3 0.6 %slice_bitcast_fusion.2 = (f32[4,4,4,128]{3,2,1,0:T(4,128)}, f32[4,4,4,128]{3,2,1,0:T(4,128)}) fusion(f32[2,4,4,4,128]{4,3,2,1,0:T(4,128)S(1)} %bitcast.36), kind=kLoop, calls=%fused_computation.16 | loop fusion | bytes 131072 | tf_op jit(solution)/shard_map/squeeze | solution.py:368
  39.9 3.8 %collective-permute-done.4 = bf16[8,128,128]{2,1,0:T(8,128)(2,1)S(1)} collective-permute-done((bf16[8,128,128]{2,1,0:T(8,128)(2,1)S(1)}, bf16[8,128,128]{2,1,0:T(8,128)(2,1)S(1)}, u32[]{:S(2)}, u32[]{:S(2)}) %collective-permute-start.4) | collective-permute-done | bytes 262176 | tf_op jit(solution)/shard_map/ppermute | solution.py:19
  43.6 0.1 fusion.3
  43.8 0.8 %copy.18 = bf16[1,128,4,128]{3,2,1,0:T(4,128)(2,1)} copy(bf16[1,128,4,128]{3,1,2,0:T(8,128)(2,1)S(1)} %get-tuple-element.49) | data formatting | bytes 262144
  44.5 0.8 %copy.17 = bf16[1,128,4,128]{3,2,1,0:T(4,128)(2,1)} copy(bf16[1,128,4,128]{3,1,2,0:T(8,128)(2,1)S(1)} %get-tuple-element.50) | data formatting | bytes 262144
  (7 shorter events, 0.2 us)
Async XLA Ops:
  1.7 10.3 %collective-permute-start = (bf16[8,128,128]{2,1,0:T(8,128)(2,1)S(1)}, bf16[8,128,128]{2,1,0:T(8,128)(2,1)S(1)}, u32[]{:S(2)}, u32[]{:S(2)}) collective-permute-start(bf16[8,128,128]{2,1,0:T(8,128)(2,1)S(1)} %maximum_bitcast_fusion.refs_4_), channel_id=1, source_target_pairs={{0,2},{1,3},{2,4},{3,5},{4,6},{5,7},{6,0},{7,1},{8,10},{9,11},{10,... | collective-permute-start | bytes 786440 | tf_op jit(solution)/shard_map/ppermute | solution.py:19
  4.7 0.7 %copy-start.2 = (s32[1,1024]{1,0:T(1,128)S(1)}, s32[1,1024]{1,0:T(1,128)}, u32[]{:S(2)}) copy-start(s32[1,1024]{1,0:T(1,128)} %refs_0_.1) | copy-start | bytes 12292
  5.4 0.7 %copy-start.3 = (s32[1,1024]{1,0:T(1,128)S(1)}, s32[1,1024]{1,0:T(1,128)}, u32[]{:S(2)}) copy-start(s32[1,1024]{1,0:T(1,128)} %refs_1_.1) | copy-start | bytes 12292
  6.0 7.5 %copy-start = (bf16[1,128,32,128]{3,2,1,0:T(8,128)(2,1)S(1)}, bf16[1,128,32,128]{3,2,1,0:T(8,128)(2,1)}, u32[]{:S(2)}) copy-start(bf16[1,128,32,128]{3,2,1,0:T(8,128)(2,1)} %param.12) | copy-start | bytes 3145732
  6.0 7.5 %copy-start.1 = (bf16[1,128,32,128]{3,2,1,0:T(8,128)(2,1)S(1)}, bf16[1,128,32,128]{3,2,1,0:T(8,128)(2,1)}, u32[]{:S(2)}) copy-start(bf16[1,128,32,128]{3,2,1,0:T(8,128)(2,1)} %param.9) | copy-start | bytes 3145732
  6.0 7.5 %copy-start.4 = (f32[16,4]{0,1:T(4,128)S(1)}, f32[16,4]{0,1:T(4,128)}, u32[]{:S(2)}) copy-start(f32[16,4]{0,1:T(4,128)} %param.15) | copy-start | bytes 772
  12.0 1.6 %collective-permute-start.1 = (bf16[8,128,128]{2,1,0:T(8,128)(2,1)S(1)}, bf16[8,128,128]{2,1,0:T(8,128)(2,1)S(1)}, u32[]{:S(2)}, u32[]{:S(2)}) collective-permute-start(bf16[8,128,128]{2,1,0:T(8,128)(2,1)S(1)} %broadcast_select_fusion), channel_id=1, source_target_pairs={{0,1},{1,0},{2,3},{3,2},{4,5},{5,4},{6,7},{7,6},{8,9},{9,8},{10,11... | collective-permute-start | bytes 786440 | tf_op jit(solution)/shard_map/ppermute | solution.py:29
  13.6 11.0 %copy-start.5 = (bf16[4,1024,128]{2,1,0:T(8,128)(2,1)S(1)}, bf16[4,1024,128]{2,1,0:T(8,128)(2,1)}, u32[]{:S(2)}) copy-start(bf16[4,1024,128]{2,1,0:T(8,128)(2,1)} %get-tuple-element.23.refs_1_) | copy-start | bytes 3145732
  18.8 2.0 %collective-permute-start.2 = (bf16[16,128,128]{2,1,0:T(8,128)(2,1)S(1)}, bf16[16,128,128]{2,1,0:T(8,128)(2,1)S(1)}, u32[]{:S(2)}, u32[]{:S(2)}) collective-permute-start(bf16[16,128,128]{2,1,0:T(8,128)(2,1)S(1)} %get-tuple-element.31), channel_id=1, source_target_pairs={{0,1},{1,0},{2,3},{3,2},{4,5},{5,4},{6,7},{7,6},{8,9},{9,8},{10,11... | collective-permute-start | bytes 1572872 | tf_op jit(solution)/shard_map/ppermute | solution.py:29
  21.0 8.4 %collective-permute-start.7 = (bf16[4,128,128]{2,1,0:T(8,128)(2,1)S(1)}, bf16[4,128,128]{2,1,0:T(8,128)(2,1)S(1)}, u32[]{:S(2)}, u32[]{:S(2)}) collective-permute-start(bf16[4,128,128]{2,1,0:T(8,128)(2,1)S(1)} %get-tuple-element.46), channel_id=1, source_target_pairs={{0,12},{1,13},{2,14},{3,15},{4,8},{5,9},{6,10},{7,11},{8,4},{9,5},... | collective-permute-start | bytes 393224 | tf_op jit(solution)/shard_map/ppermute | solution.py:29
  23.8 6.6 %collective-permute-start.6 = (bf16[4,128,128]{2,1,0:T(8,128)(2,1)S(1)}, bf16[4,128,128]{2,1,0:T(8,128)(2,1)S(1)}, u32[]{:S(2)}, u32[]{:S(2)}) collective-permute-start(bf16[4,128,128]{2,1,0:T(8,128)(2,1)S(1)} %get-tuple-element.47), channel_id=1, source_target_pairs={{0,4},{1,5},{2,6},{3,7},{4,0},{5,1},{6,2},{7,3},{8,12},{9,13},{10,... | collective-permute-start | bytes 393224 | tf_op jit(solution)/shard_map/ppermute | solution.py:29
  24.3 6.3 %collective-permute-start.5 = (bf16[4,128,128]{2,1,0:T(8,128)(2,1)S(1)}, bf16[4,128,128]{2,1,0:T(8,128)(2,1)S(1)}, u32[]{:S(2)}, u32[]{:S(2)}) collective-permute-start(bf16[4,128,128]{2,1,0:T(8,128)(2,1)S(1)} %get-tuple-element.48), channel_id=1, source_target_pairs={{0,8},{8,0},{16,24},{24,16},{1,9},{9,1},{17,25},{25,17},{2,10},{10... | collective-permute-start | bytes 393224 | tf_op jit(solution)/shard_map/ppermute | solution.py:29
  29.3 5.8 %collective-permute-start.3 = (bf16[8,128,128]{2,1,0:T(8,128)(2,1)S(1)}, bf16[8,128,128]{2,1,0:T(8,128)(2,1)S(1)}, u32[]{:S(2)}, u32[]{:S(2)}) collective-permute-start(bf16[8,128,128]{2,1,0:T(8,128)(2,1)S(1)} %get-tuple-element.36), channel_id=1, source_target_pairs={{0,1},{1,0},{2,3},{3,2},{4,5},{5,4},{6,7},{7,6},{8,9},{9,8},{10,11... | collective-permute-start | bytes 786440 | tf_op jit(solution)/shard_map/ppermute | solution.py:29
  30.7 6.1 %collective-permute-start.8 = (bf16[1,128,128]{2,1,0:T(8,128)(2,1)S(1)}, bf16[1,128,128]{2,1,0:T(8,128)(2,1)S(1)}, u32[]{:S(2)}, u32[]{:S(2)}) collective-permute-start(bf16[1,128,128]{2,1,0:T(8,128)(2,1)S(1)} %get-tuple-element.51), channel_id=1, source_target_pairs={{0,16},{8,24},{16,0},{24,8},{1,17},{9,25},{17,1},{25,9},{2,18},{10... | collective-permute-start | bytes 98312 | tf_op jit(solution)/shard_map/ppermute | solution.py:29
  33.3 5.9 %collective-permute-start.10 = (bf16[1,128,128]{2,1,0:T(8,128)(2,1)S(1)}, bf16[1,128,128]{2,1,0:T(8,128)(2,1)S(1)}, u32[]{:S(2)}, u32[]{:S(2)}) collective-permute-start(bf16[1,128,128]{2,1,0:T(8,128)(2,1)S(1)} %get-tuple-element.52), channel_id=1, source_target_pairs={{0,18},{1,19},{2,16},{3,17},{4,22},{5,23},{6,20},{7,21},{8,26},{9,... | collective-permute-start | bytes 98312 | tf_op jit(solution)/shard_map/ppermute | solution.py:29
  33.7 5.5 %collective-permute-start.9 = (bf16[1,128,128]{2,1,0:T(8,128)(2,1)S(1)}, bf16[1,128,128]{2,1,0:T(8,128)(2,1)S(1)}, u32[]{:S(2)}, u32[]{:S(2)}) collective-permute-start(bf16[1,128,128]{2,1,0:T(8,128)(2,1)S(1)} %get-tuple-element.53), channel_id=1, source_target_pairs={{0,2},{1,3},{2,0},{3,1},{4,6},{5,7},{6,4},{7,5},{8,10},{9,11},{10,... | collective-permute-start | bytes 98312 | tf_op jit(solution)/shard_map/ppermute | solution.py:29
  35.2 8.4 %collective-permute-start.4 = (bf16[8,128,128]{2,1,0:T(8,128)(2,1)S(1)}, bf16[8,128,128]{2,1,0:T(8,128)(2,1)S(1)}, u32[]{:S(2)}, u32[]{:S(2)}) collective-permute-start(bf16[8,128,128]{2,1,0:T(8,128)(2,1)S(1)} %fusion.1), channel_id=1, source_target_pairs={{0,6},{1,7},{2,0},{3,1},{4,2},{5,3},{6,4},{7,5},{8,14},{9,15},{10,... | collective-permute-start | bytes 786440 | tf_op jit(solution)/shard_map/ppermute | solution.py:19

commit v6 on v5

--- a/solution.py
+++ b/solution.py
@@ -58,7 +58,7 @@
         others.append(exchanged(part[j * size : (j + 1) * size], bits))
     if beside is not None:
         others = lax.optimization_barrier((others, beside))[0]
-    return part[:size].astype(WIDE) + sum(other.astype(WIDE) for other in others)
+    return part[:size], others
 
 
 def dot(left, right, left_dim, right_dim, precision=None):
@@ -281,6 +281,26 @@
             dq_ref[:, (g - 1) * group : (g + 1) * group, :] = both
 
 
+def grads_kernel(part_ref, *refs, owned):
+    total = part_ref[0].astype(WIDE)
+    for other_ref in refs[:-2]:
+        total = total + other_ref[0].astype(WIDE)
+    size = refs[-1].shape[0]
+    for place in range(owned):
+        for at in range(2):
+            row = (2 * place + at) * size
+            refs[at - 2][:, place, :] = total[row : row + size]
+
+
+def halo_kernel(own_ref, mate_ref, two_ref, keys_ref, values_ref, wide_keys, wide_values, *, kv):
+    even = (lax.axis_index("ctx") % 2 == 0).astype(WIDE)
+    for at, (wide, out) in enumerate(((wide_keys, keys_ref), (wide_values, values_ref))):
+        for m in range(kv):
+            place = at * kv + m
+            wide[:, m, :] = own_ref[place] + two_ref[place].astype(WIDE) + even * mate_ref[place].astype(WIDE)
+        out[...] = wide[...].astype(LOW)
+
+
 def on_device(
     query_rows, key_rows, value_matrix, cotangent, rotation, projection, shift_bias, doc_starts, tenant_ids,
 ):
@@ -354,17 +374,29 @@
         [((tokens, heads, dim), LOW), (own.shape, LOW), (own.shape, LOW), (own.shape, WIDE)],
         4 * 2**30, 10 * 2**20, scaling=scaling, **sizes,
     )(queries, grad_hidden, two, one, own, weights)
-    from_mate = exchanged(back_one, {"ctx": 1}).astype(WIDE)
-    onward = back_two.astype(WIDE) + jnp.where(even, 0.0, from_mate)
-    from_two = shifted(onward.astype(LOW), "ctx", -2)
-
-    for at, group_bits in enumerate(reduce_groups()):
-        part = scattered(part.astype(LOW), group_bits, back_own if at == 0 else None)
-    grads = jnp.moveaxis(part.reshape(here, 2, tenants // rep, rank, dim), 0, 3)
-    back = back_own + from_two.astype(WIDE) + jnp.where(even, from_mate, 0.0)
-    back = back.astype(LOW)
-    d_keys = jnp.moveaxis(back[:kv], 0, 1)
-    d_values = jnp.moveaxis(back[kv:], 0, 1)
+    from_mate = exchanged(back_one, {"ctx": 1})
+    onward = back_two.astype(WIDE) + jnp.where(even, 0.0, from_mate.astype(WIDE))
+    onward = onward.astype(LOW)
+
+    groups = reduce_groups()
+    for at, group_bits in enumerate(groups):
+        beside = back_own if at == 0 else None
+        if at == len(groups) - 1:
+            part, onward = lax.optimization_barrier((part, onward))
+            from_two = shifted(onward, "ctx", -2)
+            beside = from_two
+        part, others = scattered(part, group_bits, beside)
+        if at < len(groups) - 1:
+            part = part.astype(WIDE) + sum(other.astype(WIDE) for other in others)
+            part = part.astype(LOW)
+    grads = call(
+        grads_kernel, [((span // rep, here, dim), WIDE)] * 2, 2**18, 2**18, owned=here,
+    )(part, *others)
+    grads = [grad.reshape(tenants // rep, rank, here, dim) for grad in grads]
+    d_keys, d_values = call(
+        halo_kernel, [((tokens, kv, dim), LOW)] * 2, 2**20, 2**20,
+        scratch=[pltpu.VMEM((tokens, kv, dim), WIDE)] * 2, kv=kv,
+    )(back_own, from_mate, from_two)
     return (d_queries[None], d_keys[None], d_values[None], grads[0], grads[1])
 
 

time: 45.5 us -> 43.7 us (0.960)
  local copies, waits for them, and re-layouts: 4.65 us -> 2.43 us
  Pallas kernels: 15.1 us -> 16.9 us
  waiting for transfers between devices: 11.5 us -> 10 us
    ppermute x2, waiting for transfers between devices: 4.53 us -> 0.78 us  [shifted(): lax.ppermute(value, axis, [(source, (source + steps) % count) for source...]
    ppermute x9, waiting for transfers between devices: 6.98 us -> 9.23 us  [exchanged(): lax.ppermute(value, axes, [(int(source), int(target)) for source, target...]
    pallas_call x3 -> x5, Pallas kernels: 15.1 us -> 16.9 us  [run(): pl.pallas_call(lambda *refs: body(*refs, **fixed), out_shape=[jax.ShapeDt...]
    unnamed x14 -> x12, local copies, waits for them, and re-layouts: 2.91 us -> 1.39 us
    squeeze x1 -> x0, local copies, waits for them, and re-layouts: 0.63 us -> none  [on_device(): return (d_queries[None], d_keys[None], d_values[None], grads[0], grads[1])]
  transfers between devices with their start and end apart: 11 -> 11, of which waited for: 7 -> 9; matrix products, arithmetic and copies ran while one was open for 2% -> 0% of each run, Pallas kernels for 22% -> 23%
where the time goes in v6:
time: 43.7 us; the launch traced here: 43.5 us
  Pallas kernels  16.9 us (39%)
  starting transfers between devices  13.1 us (30%)
  waiting for transfers between devices  10 us (23%)
  local copies, waits for them, and re-layouts  2.43 us (6%)
  between operations  0.72 us (2%)
    pallas_call x5, Pallas kernels, run(): pl.pallas_call(lambda *refs: body(*refs, **fixed), out_shape=[jax.ShapeDt...  16.9 us
    ppermute x9, waiting for transfers between devices, exchanged(): lax.ppermute(value, axes, [(int(source), int(target)) for source, target...  9.23 us
    ppermute x9, starting transfers between devices, exchanged(): lax.ppermute(value, axes, [(int(source), int(target)) for source, target...  8.28 us
    ppermute x2, starting transfers between devices, shifted(): lax.ppermute(value, axis, [(source, (source + steps) % count) for source...  4.78 us
    unnamed x12, local copies, waits for them, and re-layouts  1.39 us
    squeeze x1, local copies, waits for them, and re-layouts, on_device(): value_matrix[0]  1 us
  transfers between devices with their start and end apart: 11, of which 9 were waited for; matrix products, arithmetic and copies ran while one was open for 0% of the time, Pallas kernels for 23%

profile of v6, /device:TPU:0, one launch (start us, length us, event | category | flops | bytes accessed | tf_op | source)
XLA Modules:
  0.0 43.5 jit_solution(18367080582207199769)
XLA Ops:
  0.6 1.0 %copy_bitcast_fusion = (bf16[128,4,128]{2,0,1:T(8,128)(2,1)S(1)}, bf16[128,4,128]{2,0,1:T(8,128)(2,1)S(1)}) fusion(bf16[1,128,4,128]{3,2,1,0:T(4,128)(2,1)} %param.11, bf16[1,128,4,128]{3,2,1,0:T(4,128)(2,1)} %param.10), kind=kLoop, calls=%fused_computation.5 | loop fusion | bytes 524288 | tf_op jit(solution)/shard_map/squeeze | solution.py:319
  1.7 3.0 %collective-permute-start = (bf16[8,128,128]{2,1,0:T(8,128)(2,1)S(1)}, bf16[8,128,128]{2,1,0:T(8,128)(2,1)S(1)}, u32[]{:S(2)}, u32[]{:S(2)}) collective-permute-start(bf16[8,128,128]{2,1,0:T(8,128)(2,1)S(1)} %maximum_bitcast_fusion.refs_4_), channel_id=1, source_target_pairs={{0,2},{1,3},{2,4},{3,5},{4,6},{5,7},{6,0},{7,1},{8,10},{9,11},{10,... | collective-permute-start | bytes 786440 | tf_op jit(solution)/shard_map/ppermute | solution.py:19
  4.7 0.0 copy-start.2
  4.7 0.7 %copy-done.2 = s32[1,1024]{1,0:T(1,128)S(1)} copy-done((s32[1,1024]{1,0:T(1,128)S(1)}, s32[1,1024]{1,0:T(1,128)}, u32[]{:S(2)}) %copy-start.2) | copy-done | bytes 4120
  5.4 0.0 copy-start.3
  5.4 0.7 %copy-done.3 = s32[1,1024]{1,0:T(1,128)S(1)} copy-done((s32[1,1024]{1,0:T(1,128)S(1)}, s32[1,1024]{1,0:T(1,128)}, u32[]{:S(2)}) %copy-start.3) | copy-done | bytes 4120
  6.0 0.0 copy-start
  6.0 0.0 copy-start.1
  6.0 0.0 copy-start.4
  6.0 5.1 %pull_kernel.1 = (bf16[4,1024,128]{2,1,0:T(8,128)(2,1)}, bf16[4,512,128]{2,1,0:T(8,128)(2,1)S(1)}, f32[8,1024]{1,0:T(8,128)S(1)}, s32[8,1024]{1,0:T(8,128)S(1)}) custom-call(s32[1,1024]{1,0:T(1,128)S(1)} %copy-done.2, s32[1,1024]{1,0:T(1,128)S(1)} %copy-done.3, bf16[128,32,128]{2,1,0:T(8,128)(2,1)} %bitcast.18, bf16[64,32,128]{2,1,0:T(8,128)(2,1)} %bitcast.23, ...), custom_call_target="tpu_custom_call" | custom-call | flops 2147483648 | bytes 4194304 | tf_op jit(solution)/shard_map/pull_kernel/pallas_call | solution.py:331
  11.1 0.8 %collective-permute-done.refs_2_ = bf16[8,128,128]{2,1,0:T(8,128)(2,1)S(1)} collective-permute-done((bf16[8,128,128]{2,1,0:T(8,128)(2,1)S(1)}, bf16[8,128,128]{2,1,0:T(8,128)(2,1)S(1)}, u32[]{:S(2)}, u32[]{:S(2)}) %collective-permute-start) | collective-permute-done | bytes 262176 | tf_op jit(solution)/shard_map/ppermute | solution.py:19
  12.0 0.1 collective-permute-start.1
  12.0 1.5 %collective-permute-done.1.refs_3_ = bf16[8,128,128]{2,1,0:T(8,128)(2,1)S(1)} collective-permute-done((bf16[8,128,128]{2,1,0:T(8,128)(2,1)S(1)}, bf16[8,128,128]{2,1,0:T(8,128)(2,1)S(1)}, u32[]{:S(2)}, u32[]{:S(2)}) %collective-permute-start.1) | collective-permute-done | bytes 262176 | tf_op jit(solution)/shard_map/ppermute | solution.py:29
  13.6 0.0 copy-done
  13.6 0.0 copy-done.1
  13.6 0.0 copy-done.4
  13.6 0.0 copy-start.5
  13.6 5.2 %forward_kernel.1 = (f32[4,256,1024]{2,1,0:T(8,128)S(1)}, bf16[16,128,128]{2,1,0:T(8,128)(2,1)S(1)}, bf16[16,128,128]{2,1,0:T(8,128)(2,1)S(1)}) custom-call(f32[4,16]{1,0:T(4,128)S(1)} %bitcast.22, bf16[128,32,128]{2,1,0:T(8,128)(2,1)S(1)} %bitcast.20, bf16[8,128,128]{2,1,0:T(8,128)(2,1)S(1)} %collective-permute-done.refs_2_, ...), custom_call_target="tpu_custom_call" | custom-call | flops 4294967296 | bytes 10485760 | tf_op jit(solution)/shard_map/forward_kernel/pallas_call | solution.py:331
  18.8 0.2 collective-permute-start.2
  19.0 1.8 %collective-permute-done.2 = bf16[16,128,128]{2,1,0:T(8,128)(2,1)S(1)} collective-permute-done((bf16[16,128,128]{2,1,0:T(8,128)(2,1)S(1)}, bf16[16,128,128]{2,1,0:T(8,128)(2,1)S(1)}, u32[]{:S(2)}, u32[]{:S(2)}) %collective-permute-start.2) | collective-permute-done | bytes 524320 | tf_op jit(solution)/shard_map/ppermute | solution.py:29
  20.8 0.1 add_convert_fusion
  21.0 2.8 %collective-permute-start.6 = (bf16[4,128,128]{2,1,0:T(8,128)(2,1)S(1)}, bf16[4,128,128]{2,1,0:T(8,128)(2,1)S(1)}, u32[]{:S(2)}, u32[]{:S(2)}) collective-permute-start(bf16[4,128,128]{2,1,0:T(8,128)(2,1)S(1)} %get-tuple-element.59), channel_id=1, source_target_pairs={{0,12},{1,13},{2,14},{3,15},{4,8},{5,9},{6,10},{7,11},{8,4},{9,5},... | collective-permute-start | bytes 393224 | tf_op jit(solution)/shard_map/ppermute | solution.py:29
  23.8 0.5 %collective-permute-start.5 = (bf16[4,128,128]{2,1,0:T(8,128)(2,1)S(1)}, bf16[4,128,128]{2,1,0:T(8,128)(2,1)S(1)}, u32[]{:S(2)}, u32[]{:S(2)}) collective-permute-start(bf16[4,128,128]{2,1,0:T(8,128)(2,1)S(1)} %get-tuple-element.60), channel_id=1, source_target_pairs={{0,4},{1,5},{2,6},{3,7},{4,0},{5,1},{6,2},{7,3},{8,12},{9,13},{10,... | collective-permute-start | bytes 393224 | tf_op jit(solution)/shard_map/ppermute | solution.py:29
  24.3 0.3 collective-permute-start.4
  24.5 0.0 copy-done.5
  24.5 4.8 %backward_kernel.1 = (bf16[128,32,128]{2,1,0:T(8,128)(2,1)}, bf16[8,128,128]{2,1,0:T(8,128)(2,1)S(1)}, bf16[8,128,128]{2,1,0:T(8,128)(2,1)S(1)}, f32[8,128,128]{2,1,0:T(8,128)S(1)}) custom-call(bf16[128,32,128]{2,1,0:T(8,128)(2,1)S(1)} %bitcast.21, bf16[4,1024,128]{2,1,0:T(8,128)(2,1)S(1)} %copy-done.5, ...), custom_call_target="tpu_custom_call" | custom-call | flops 4294967296 | bytes 10485760 | tf_op jit(solution)/shard_map/backward_kernel/pallas_call | solution.py:331
  29.3 0.0 collective-permute-start.3
  29.3 0.0 collective-permute-done.6
  29.3 1.0 %collective-permute-done.5 = bf16[4,128,128]{2,1,0:T(8,128)(2,1)S(1)} collective-permute-done((bf16[4,128,128]{2,1,0:T(8,128)(2,1)S(1)}, bf16[4,128,128]{2,1,0:T(8,128)(2,1)S(1)}, u32[]{:S(2)}, u32[]{:S(2)}) %collective-permute-start.5) | collective-permute-done | bytes 131104 | tf_op jit(solution)/shard_map/ppermute | solution.py:29
  30.4 0.2 collective-permute-done.4
  30.6 0.1 add_convert_fusion.2
  30.6 0.2 collective-permute-done.3.refs_1_
  30.9 0.1 add_convert_fusion.1
  31.0 1.8 %collective-permute-start.7 = (bf16[8,128,128]{2,1,0:T(8,128)(2,1)S(1)}, bf16[8,128,128]{2,1,0:T(8,128)(2,1)S(1)}, u32[]{:S(2)}, u32[]{:S(2)}) collective-permute-start(bf16[8,128,128]{2,1,0:T(8,128)(2,1)S(1)} %add_convert_fusion.1), channel_id=1, source_target_pairs={{0,6},{1,7},{2,0},{3,1},{4,2},{5,3},{6,4},{7,5},{8,14},{9,15},{10,... | collective-permute-start | bytes 786440 | tf_op jit(solution)/shard_map/ppermute | solution.py:19
  32.8 2.6 %collective-permute-start.10 = (bf16[1,128,128]{2,1,0:T(8,128)(2,1)S(1)}, bf16[1,128,128]{2,1,0:T(8,128)(2,1)S(1)}, u32[]{:S(2)}, u32[]{:S(2)}) collective-permute-start(bf16[1,128,128]{2,1,0:T(8,128)(2,1)S(1)} %get-tuple-element.62), channel_id=1, source_target_pairs={{0,18},{1,19},{2,16},{3,17},{4,22},{5,23},{6,20},{7,21},{8,26},{9,... | collective-permute-start | bytes 98312 | tf_op jit(solution)/shard_map/ppermute | solution.py:29
  35.3 1.6 %collective-permute-start.9 = (bf16[1,128,128]{2,1,0:T(8,128)(2,1)S(1)}, bf16[1,128,128]{2,1,0:T(8,128)(2,1)S(1)}, u32[]{:S(2)}, u32[]{:S(2)}) collective-permute-start(bf16[1,128,128]{2,1,0:T(8,128)(2,1)S(1)} %get-tuple-element.63), channel_id=1, source_target_pairs={{0,2},{1,3},{2,0},{3,1},{4,6},{5,7},{6,4},{7,5},{8,10},{9,11},{10,... | collective-permute-start | bytes 98312 | tf_op jit(solution)/shard_map/ppermute | solution.py:29
  36.9 0.3 collective-permute-start.8
  37.2 1.7 %collective-permute-done.10.refs_3_ = bf16[1,128,128]{2,1,0:T(8,128)(2,1)S(1)} collective-permute-done((bf16[1,128,128]{2,1,0:T(8,128)(2,1)S(1)}, bf16[1,128,128]{2,1,0:T(8,128)(2,1)S(1)}, u32[]{:S(2)}, u32[]{:S(2)}) %collective-permute-start.10) | collective-permute-done | bytes 32800 | tf_op jit(solution)/shard_map/ppermute | solution.py:29
  38.9 1.9 %collective-permute-done.9.refs_2_ = bf16[1,128,128]{2,1,0:T(8,128)(2,1)S(1)} collective-permute-done((bf16[1,128,128]{2,1,0:T(8,128)(2,1)S(1)}, bf16[1,128,128]{2,1,0:T(8,128)(2,1)S(1)}, u32[]{:S(2)}, u32[]{:S(2)}) %collective-permute-start.9) | collective-permute-done | bytes 32800 | tf_op jit(solution)/shard_map/ppermute | solution.py:29
  40.8 0.9 %collective-permute-done.8.refs_1_ = bf16[1,128,128]{2,1,0:T(8,128)(2,1)S(1)} collective-permute-done((bf16[1,128,128]{2,1,0:T(8,128)(2,1)S(1)}, bf16[1,128,128]{2,1,0:T(8,128)(2,1)S(1)}, u32[]{:S(2)}, u32[]{:S(2)}) %collective-permute-start.8) | collective-permute-done | bytes 32800 | tf_op jit(solution)/shard_map/ppermute | solution.py:29
  41.7 0.0 collective-permute-done.7.refs_2_
  41.7 0.7 %grads_kernel.1 = (f32[16,4,128]{2,1,0:T(4,128)}, f32[16,4,128]{2,1,0:T(4,128)}) custom-call(bf16[1,128,128]{2,1,0:T(8,128)(2,1)S(1)} %get-tuple-element.65.refs_0_, bf16[1,128,128]{2,1,0:T(8,128)(2,1)S(1)} %collective-permute-done.8.refs_1_, bf16[1,128,128]{2,1,0:T(8,128)(2,1)S(1)} %collective-permute-done.9.refs_2_, ...), custom_call_target="tpu_custom_call" | custom-call | flops 262144 | bytes 262144 | tf_op jit(solution)/shard_map/grads_kernel/pallas_call | solution.py:331
  42.4 1.1 %halo_kernel.1 = (bf16[128,4,128]{2,1,0:T(4,128)(2,1)}, bf16[128,4,128]{2,1,0:T(4,128)(2,1)}) custom-call(f32[8,128,128]{2,1,0:T(8,128)S(1)} %get-tuple-element.43.refs_0_, bf16[8,128,128]{2,1,0:T(8,128)(2,1)S(1)} %collective-permute-done.3.refs_1_, bf16[8,128,128]{2,1,0:T(8,128)(2,1)S(1)} %collective-permute-done.7.refs_2_), custom_call_target="tpu_custom_call" | custom-call | flops 1048576 | bytes 1048576 | tf_op jit(solution)/shard_map/halo_kernel/pallas_call | solution.py:331
  (4 shorter events, 0.1 us)
Async XLA Ops:
  1.7 10.3 %collective-permute-start = (bf16[8,128,128]{2,1,0:T(8,128)(2,1)S(1)}, bf16[8,128,128]{2,1,0:T(8,128)(2,1)S(1)}, u32[]{:S(2)}, u32[]{:S(2)}) collective-permute-start(bf16[8,128,128]{2,1,0:T(8,128)(2,1)S(1)} %maximum_bitcast_fusion.refs_4_), channel_id=1, source_target_pairs={{0,2},{1,3},{2,4},{3,5},{4,6},{5,7},{6,0},{7,1},{8,10},{9,11},{10,... | collective-permute-start | bytes 786440 | tf_op jit(solution)/shard_map/ppermute | solution.py:19
  4.7 0.7 %copy-start.2 = (s32[1,1024]{1,0:T(1,128)S(1)}, s32[1,1024]{1,0:T(1,128)}, u32[]{:S(2)}) copy-start(s32[1,1024]{1,0:T(1,128)} %refs_0_.1) | copy-start | bytes 12292
  5.4 0.7 %copy-start.3 = (s32[1,1024]{1,0:T(1,128)S(1)}, s32[1,1024]{1,0:T(1,128)}, u32[]{:S(2)}) copy-start(s32[1,1024]{1,0:T(1,128)} %refs_1_.1) | copy-start | bytes 12292
  6.0 7.5 %copy-start = (bf16[1,128,32,128]{3,2,1,0:T(8,128)(2,1)S(1)}, bf16[1,128,32,128]{3,2,1,0:T(8,128)(2,1)}, u32[]{:S(2)}) copy-start(bf16[1,128,32,128]{3,2,1,0:T(8,128)(2,1)} %param.12) | copy-start | bytes 3145732
  6.0 7.5 %copy-start.1 = (bf16[1,128,32,128]{3,2,1,0:T(8,128)(2,1)S(1)}, bf16[1,128,32,128]{3,2,1,0:T(8,128)(2,1)}, u32[]{:S(2)}) copy-start(bf16[1,128,32,128]{3,2,1,0:T(8,128)(2,1)} %param.9) | copy-start | bytes 3145732
  6.0 7.5 %copy-start.4 = (f32[16,4]{0,1:T(4,128)S(1)}, f32[16,4]{0,1:T(4,128)}, u32[]{:S(2)}) copy-start(f32[16,4]{0,1:T(4,128)} %param.15) | copy-start | bytes 772
  12.0 1.6 %collective-permute-start.1 = (bf16[8,128,128]{2,1,0:T(8,128)(2,1)S(1)}, bf16[8,128,128]{2,1,0:T(8,128)(2,1)S(1)}, u32[]{:S(2)}, u32[]{:S(2)}) collective-permute-start(bf16[8,128,128]{2,1,0:T(8,128)(2,1)S(1)} %broadcast_select_fusion), channel_id=1, source_target_pairs={{0,1},{1,0},{2,3},{3,2},{4,5},{5,4},{6,7},{7,6},{8,9},{9,8},{10,11... | collective-permute-start | bytes 786440 | tf_op jit(solution)/shard_map/ppermute | solution.py:29
  13.6 11.0 %copy-start.5 = (bf16[4,1024,128]{2,1,0:T(8,128)(2,1)S(1)}, bf16[4,1024,128]{2,1,0:T(8,128)(2,1)}, u32[]{:S(2)}) copy-start(bf16[4,1024,128]{2,1,0:T(8,128)(2,1)} %get-tuple-element.32.refs_1_) | copy-start | bytes 3145732
  18.8 2.0 %collective-permute-start.2 = (bf16[16,128,128]{2,1,0:T(8,128)(2,1)S(1)}, bf16[16,128,128]{2,1,0:T(8,128)(2,1)S(1)}, u32[]{:S(2)}, u32[]{:S(2)}) collective-permute-start(bf16[16,128,128]{2,1,0:T(8,128)(2,1)S(1)} %get-tuple-element.40), channel_id=1, source_target_pairs={{0,1},{1,0},{2,3},{3,2},{4,5},{5,4},{6,7},{7,6},{8,9},{9,8},{10,11... | collective-permute-start | bytes 1572872 | tf_op jit(solution)/shard_map/ppermute | solution.py:29
  21.0 8.4 %collective-permute-start.6 = (bf16[4,128,128]{2,1,0:T(8,128)(2,1)S(1)}, bf16[4,128,128]{2,1,0:T(8,128)(2,1)S(1)}, u32[]{:S(2)}, u32[]{:S(2)}) collective-permute-start(bf16[4,128,128]{2,1,0:T(8,128)(2,1)S(1)} %get-tuple-element.59), channel_id=1, source_target_pairs={{0,12},{1,13},{2,14},{3,15},{4,8},{5,9},{6,10},{7,11},{8,4},{9,5},... | collective-permute-start | bytes 393224 | tf_op jit(solution)/shard_map/ppermute | solution.py:29
  23.8 6.6 %collective-permute-start.5 = (bf16[4,128,128]{2,1,0:T(8,128)(2,1)S(1)}, bf16[4,128,128]{2,1,0:T(8,128)(2,1)S(1)}, u32[]{:S(2)}, u32[]{:S(2)}) collective-permute-start(bf16[4,128,128]{2,1,0:T(8,128)(2,1)S(1)} %get-tuple-element.60), channel_id=1, source_target_pairs={{0,4},{1,5},{2,6},{3,7},{4,0},{5,1},{6,2},{7,3},{8,12},{9,13},{10,... | collective-permute-start | bytes 393224 | tf_op jit(solution)/shard_map/ppermute | solution.py:29
  24.3 6.3 %collective-permute-start.4 = (bf16[4,128,128]{2,1,0:T(8,128)(2,1)S(1)}, bf16[4,128,128]{2,1,0:T(8,128)(2,1)S(1)}, u32[]{:S(2)}, u32[]{:S(2)}) collective-permute-start(bf16[4,128,128]{2,1,0:T(8,128)(2,1)S(1)} %get-tuple-element.61), channel_id=1, source_target_pairs={{0,8},{8,0},{16,24},{24,16},{1,9},{9,1},{17,25},{25,17},{2,10},{10... | collective-permute-start | bytes 393224 | tf_op jit(solution)/shard_map/ppermute | solution.py:29
  29.3 1.5 %collective-permute-start.3 = (bf16[8,128,128]{2,1,0:T(8,128)(2,1)S(1)}, bf16[8,128,128]{2,1,0:T(8,128)(2,1)S(1)}, u32[]{:S(2)}, u32[]{:S(2)}) collective-permute-start(bf16[8,128,128]{2,1,0:T(8,128)(2,1)S(1)} %get-tuple-element.44), channel_id=1, source_target_pairs={{0,1},{1,0},{2,3},{3,2},{4,5},{5,4},{6,7},{7,6},{8,9},{9,8},{10,11... | collective-permute-start | bytes 786440 | tf_op jit(solution)/shard_map/ppermute | solution.py:29
  31.0 10.7 %collective-permute-start.7 = (bf16[8,128,128]{2,1,0:T(8,128)(2,1)S(1)}, bf16[8,128,128]{2,1,0:T(8,128)(2,1)S(1)}, u32[]{:S(2)}, u32[]{:S(2)}) collective-permute-start(bf16[8,128,128]{2,1,0:T(8,128)(2,1)S(1)} %add_convert_fusion.1), channel_id=1, source_target_pairs={{0,6},{1,7},{2,0},{3,1},{4,2},{5,3},{6,4},{7,5},{8,14},{9,15},{10,... | collective-permute-start | bytes 786440 | tf_op jit(solution)/shard_map/ppermute | solution.py:19
  32.8 6.1 %collective-permute-start.10 = (bf16[1,128,128]{2,1,0:T(8,128)(2,1)S(1)}, bf16[1,128,128]{2,1,0:T(8,128)(2,1)S(1)}, u32[]{:S(2)}, u32[]{:S(2)}) collective-permute-start(bf16[1,128,128]{2,1,0:T(8,128)(2,1)S(1)} %get-tuple-element.62), channel_id=1, source_target_pairs={{0,18},{1,19},{2,16},{3,17},{4,22},{5,23},{6,20},{7,21},{8,26},{9,... | collective-permute-start | bytes 98312 | tf_op jit(solution)/shard_map/ppermute | solution.py:29
  35.3 5.4 %collective-permute-start.9 = (bf16[1,128,128]{2,1,0:T(8,128)(2,1)S(1)}, bf16[1,128,128]{2,1,0:T(8,128)(2,1)S(1)}, u32[]{:S(2)}, u32[]{:S(2)}) collective-permute-start(bf16[1,128,128]{2,1,0:T(8,128)(2,1)S(1)} %get-tuple-element.63), channel_id=1, source_target_pairs={{0,2},{1,3},{2,0},{3,1},{4,6},{5,7},{6,4},{7,5},{8,10},{9,11},{10,... | collective-permute-start | bytes 98312 | tf_op jit(solution)/shard_map/ppermute | solution.py:29
  36.9 4.8 %collective-permute-start.8 = (bf16[1,128,128]{2,1,0:T(8,128)(2,1)S(1)}, bf16[1,128,128]{2,1,0:T(8,128)(2,1)S(1)}, u32[]{:S(2)}, u32[]{:S(2)}) collective-permute-start(bf16[1,128,128]{2,1,0:T(8,128)(2,1)S(1)} %get-tuple-element.64), channel_id=1, source_target_pairs={{0,16},{8,24},{16,0},{24,8},{1,17},{9,25},{17,1},{25,9},{2,18},{10... | collective-permute-start | bytes 98312 | tf_op jit(solution)/shard_map/ppermute | solution.py:29

commit v7 on v6

--- a/solution.py
+++ b/solution.py
@@ -107,22 +107,7 @@
     return jnp.concatenate([spread[c * 8 : (c + 1) * 8] for c in range(tiles)], axis=1)
 
 
-def pull_kernel(
-    starts_hbm, owners_hbm, cot_hbm, rot_hbm, proj_hbm, gh_ref, diff_ref, pulled_ref, meta_ref,
-    starts_ref, owners_ref, cot_ref, rot_ref, proj_ref, sems, *, kv, group, tenants, rank,
-):
-    pairs = (
-        (starts_hbm, starts_ref), (owners_hbm, owners_ref), (cot_hbm, cot_ref),
-        (rot_hbm, rot_ref), (proj_hbm, proj_ref),
-    )
-    copies = [
-        pltpu.make_async_copy(source, target, sems.at[at])
-        for at, (source, target) in enumerate(pairs)
-    ]
-    for copy in copies:
-        copy.start()
-    copies[0].wait()
-    copies[1].wait()
+def place_kernel(starts_ref, owners_ref, meta_ref, bias_ref, *, group):
     lanes = meta_ref.shape[1]
     tokens = lanes // group
     row_first = lax.axis_index("ctx") * tokens
@@ -134,14 +119,40 @@
     )
     meta = dot(both, repeat.astype(WIDE), 1, 0, lax.Precision.HIGHEST).astype(jnp.int32)
     meta_ref[...] = meta
-    owner = meta[1:2, :]
-    copies[2].wait()
+    first = meta[0:1, :]
+    key, here = places(lanes, tokens, group)
+    bias_ref[0] = jnp.where(jnp.where(here, key, key - 2 * tokens) >= first, 0.0, far_below)
+    bias_ref[1] = jnp.where(key - tokens >= first, 0.0, far_below)
+
+
+def slots_of(lanes, group, owned):
+    per_group = group // owned
+    head = lane_head((1, lanes), group)
+    return head ^ ((lax.axis_index("ctx") % per_group) * owned)
+
+
+def tenants_of(lanes, tenants, rank):
+    row = lax.broadcasted_iota(jnp.int32, (tenants * rank, lanes), 0) // rank
+    return row ^ (lax.axis_index("rep") * (tenants // lax.axis_size("rep")))
+
+
+def picked_rows(rows, owner, slots, tenants, rank, group):
+    lanes = owner.shape[1]
+    mine = owner == tenants_of(lanes, tenants, rank)
+    rows = jnp.where(mine, jnp.concatenate([rows] * (tenants * rank // 8), axis=0), 0.0)
+    return [jnp.where(slots == h, rows, 0.0).astype(LOW) for h in range(group)]
+
+
+def pull_kernel(
+    meta_ref, cot_ref, rot_ref, proj_ref, q_ref, gh_ref, diff_ref, cots_ref, queries_ref, pull_ref,
+    *, kv, group, tenants, rank, owned,
+):
+    lanes = meta_ref.shape[1]
+    owner = meta_ref[1:2, :]
     cots = group_rows(cot_ref, kv, group)
-    copies[3].wait()
     rots = group_rows(rot_ref, kv, group)
     on_rot = dot(jnp.concatenate(rots, axis=1), jnp.concatenate(cots, axis=1), 1, 1)
     pulled = own_terms(on_rot, owner, tenants, rank, group).astype(LOW).astype(WIDE)
-    pulled_ref[...] = pulled
     same_head = lax.broadcasted_iota(jnp.int32, (group, lanes), 0) == lane_head((group, lanes), group)
     picked = []
     for tenant in range(tenants):
@@ -149,12 +160,18 @@
         for k in range(rank):
             picked.append(jnp.where(keep, pulled[k : k + 1], 0.0))
     picked = jnp.concatenate(picked, axis=0).T.astype(LOW)
-    copies[4].wait()
     projs = group_rows(proj_ref, kv, group)
     for g in range(kv):
         diff = (projs[g].astype(WIDE) - rots[g].astype(WIDE)).astype(LOW)
         diff_ref[g] = diff
         gh_ref[g] = (cots[g].astype(WIDE) + dot(picked, diff, 1, 0)).astype(LOW)
+        cots_ref[g] = cots[g]
+    for g, rows in enumerate(group_rows(q_ref, kv, group)):
+        queries_ref[g] = rows
+    span = tenants * rank
+    slots = slots_of(lanes, group, owned)
+    for h, rows in enumerate(picked_rows(pulled, owner, slots, tenants, rank, group)):
+        pull_ref[h * span : (h + 1) * span, :] = rows
 
 
 def places(lanes, tokens, group):
@@ -164,24 +181,19 @@
 
 
 def forward_kernel(
-    bias_ref, q_ref, two_ref, one_ref, own_ref, cot_hbm, diff_ref, meta_ref, pulled_ref,
-    weights_ref, send_ref, keep_ref, cot_ref, sem, *, kv, group, tenants, rank, scaling, owned,
+    shift_ref, queries_ref, two_ref, one_ref, own_ref, cots_ref, diff_ref, meta_ref, pull_ref, bias_ref,
+    weights_ref, send_ref, keep_ref, *, kv, group, tenants, rank, scaling, owned,
 ):
-    fetch = pltpu.make_async_copy(cot_hbm, cot_ref, sem)
-    fetch.start()
     tokens = own_ref.shape[1]
-    first = meta_ref[0:1, :]
     owner = meta_ref[1:2, :]
     lanes = owner.shape[1]
-    key, here = places(lanes, tokens, group)
-    fold_bias = jnp.where(jnp.where(here, key, key - 2 * tokens) >= first, 0.0, far_below)
-    mid_bias = jnp.where(key - tokens >= first, 0.0, far_below)
-    queries = group_rows(q_ref, kv, group)
+    _, here = places(lanes, tokens, group)
     hidden = []
     for g in range(kv):
-        fold = jnp.where(here, dot(own_ref[g], queries[g], 1, 1), dot(two_ref[g], queries[g], 1, 1))
-        fold = fold * scaling + fold_bias
-        mid = dot(one_ref[g], queries[g], 1, 1) * scaling + mid_bias
+        queries = queries_ref[g]
+        fold = jnp.where(here, dot(own_ref[g], queries, 1, 1), dot(two_ref[g], queries, 1, 1))
+        fold = fold * scaling + bias_ref[0]
+        mid = dot(one_ref[g], queries, 1, 1) * scaling + bias_ref[1]
         top = jnp.maximum(jnp.max(fold, axis=0, keepdims=True), jnp.max(mid, axis=0, keepdims=True))
         fold = jnp.exp(fold - top)
         mid = jnp.exp(mid - top)
@@ -201,25 +213,18 @@
     on_diff = dot(jnp.concatenate([diff_ref[g] for g in range(kv)], axis=1), hidden, 1, 0)
     lifted = own_terms(on_diff, owner, tenants, rank, group)
     one_hot = (owner == lax.broadcasted_iota(jnp.int32, (tenants, lanes), 0)).astype(WIDE)
-    bias = jnp.concatenate([bias_ref[...]] * (8 // rank), axis=0)
+    bias = jnp.concatenate([shift_ref[...]] * (8 // rank), axis=0)
     shift = dot(bias, one_hot, 1, 0, lax.Precision.HIGHEST)
     lifted = (lifted + shift).astype(LOW).astype(WIDE)
-    pulled = pulled_ref[...]
-    ctx, rep = lax.axis_size("ctx"), lax.axis_size("rep")
-    me, layer = lax.axis_index("ctx"), lax.axis_index("rep")
+    rep = lax.axis_size("rep")
+    me = lax.axis_index("ctx")
     per_group = group // owned
     span = tenants * rank
-    tenant_row = lax.broadcasted_iota(jnp.int32, (span, lanes), 0) // rank
-    mine = owner == (tenant_row ^ (layer * (tenants // rep)))
-    lift_rows = jnp.where(mine, jnp.concatenate([lifted] * (span // 8), axis=0), 0.0)
-    pull_rows = jnp.where(mine, jnp.concatenate([pulled] * (span // 8), axis=0), 0.0)
-    slot = lane_head((span, lanes), group) ^ ((me % per_group) * owned)
-    lift_all = jnp.concatenate([jnp.where(slot == h, lift_rows, 0.0).astype(LOW) for h in range(group)], axis=0)
-    pull_all = jnp.concatenate([jnp.where(slot == h, pull_rows, 0.0).astype(LOW) for h in range(group)], axis=0)
-    on_proj = dot(pull_all, hidden, 1, 1)
-    fetch.wait()
-    on_rot = dot(lift_all, jnp.concatenate(group_rows(cot_ref, kv, group), axis=1), 1, 0) - on_proj
-    dim = q_ref.shape[2]
+    slots = slots_of(lanes, group, owned)
+    lift_all = jnp.concatenate(picked_rows(lifted, owner, slots, tenants, rank, group), axis=0)
+    on_proj = dot(pull_ref[...], hidden, 1, 1)
+    on_rot = dot(lift_all, jnp.concatenate([cots_ref[g] for g in range(kv)], axis=1), 1, 0) - on_proj
+    dim = two_ref.shape[2]
     here_rows = span // rep
     for g in range(kv):
         columns = slice(g * dim, (g + 1) * dim)
@@ -235,14 +240,13 @@
 
 
 def backward_kernel(
-    q_ref, gh_ref, two_ref, one_ref, own_ref, weights_ref, dq_ref, back_two_ref, back_one_ref, back_own_ref,
+    queries_ref, gh_ref, two_ref, one_ref, own_ref, weights_ref, dq_ref, back_two_ref, back_one_ref, back_own_ref,
     *, kv, group, scaling,
 ):
     tokens = own_ref.shape[1]
     lanes = weights_ref.shape[2]
-    dim = q_ref.shape[2]
+    dim = queries_ref.shape[2]
     _, here = places(lanes, tokens, group)
-    queries = group_rows(q_ref, kv, group)
     query_grads = []
     for g in range(kv):
         grads = gh_ref[g]
@@ -268,7 +272,7 @@
             axis=0,
         )
         keys = jnp.concatenate([two_ref[g], one_ref[g], own_ref[g]], axis=0)
-        key_grad = dot(score_grad, queries[g], 1, 0) * scaling
+        key_grad = dot(score_grad, queries_ref[g], 1, 0) * scaling
         value_grad = dot(low, grads, 1, 0)
         for place, grad in ((g, key_grad), (kv + g, value_grad)):
             back_two_ref[place] = grad[0:tokens].astype(LOW)
@@ -292,13 +296,15 @@
             refs[at - 2][:, place, :] = total[row : row + size]
 
 
-def halo_kernel(own_ref, mate_ref, two_ref, keys_ref, values_ref, wide_keys, wide_values, *, kv):
+def halo_kernel(own_ref, mate_ref, two_ref, keys_ref, values_ref, wide_ref, *, kv):
+    tokens = own_ref.shape[1]
     even = (lax.axis_index("ctx") % 2 == 0).astype(WIDE)
-    for at, (wide, out) in enumerate(((wide_keys, keys_ref), (wide_values, values_ref))):
+    for at, out in enumerate((keys_ref, values_ref)):
         for m in range(kv):
             place = at * kv + m
-            wide[:, m, :] = own_ref[place] + two_ref[place].astype(WIDE) + even * mate_ref[place].astype(WIDE)
-        out[...] = wide[...].astype(LOW)
+            total = own_ref[place] + two_ref[place].astype(WIDE) + even * mate_ref[place].astype(WIDE)
+            wide_ref[at, pl.ds(m, tokens, stride=kv), :] = total
+        out[...] = wide_ref[at].astype(LOW)
 
 
 def on_device(
@@ -316,15 +322,11 @@
     rep = lax.axis_size("rep")
     assert 2 * tokens == DOC_MAX
 
-    own = jnp.moveaxis(jnp.concatenate([key_rows[0], value_matrix[0]], axis=1), 1, 0)
-    even = lax.axis_index("ctx") % 2 == 0
-    two = shifted(own, "ctx", 2)
 
     rot = rotation.reshape(tenants * rank, heads, dim)
     proj = projection.reshape(tenants * rank, heads, dim)
     sizes = dict(kv=kv, group=group)
     vmem = pl.BlockSpec(memory_space=pltpu.VMEM)
-    hbm = pl.BlockSpec(memory_space=pltpu.HBM)
 
     def call(body, outs, flops, moved, specs=None, scratch=(), limit=24, **fixed):
         def run(*operands):
@@ -344,29 +346,29 @@
     span = tenants * rank
     here = heads // ctx
     rows = here * 2 * span // rep
-    grad_hidden, diff, pulled, meta = call(
+    own = jnp.moveaxis(jnp.concatenate([key_rows[0], value_matrix[0]], axis=1), 1, 0)
+    even = lax.axis_index("ctx") % 2 == 0
+    two = shifted(own, "ctx", 2)
+    meta, biases = call(
+        place_kernel, [((8, lanes), jnp.int32), ((2, tokens, lanes), WIDE)], 8 * 2**30, 2**20,
+        group=group,
+    )(doc_starts, tenant_ids)
+    grad_hidden, diff, cots, queries, pull = call(
         pull_kernel,
         [
-            ((kv, lanes, dim), LOW), ((kv, span * group, dim), LOW),
-            ((8, lanes), WIDE), ((8, lanes), jnp.int32),
+            ((kv, lanes, dim), LOW), ((kv, span * group, dim), LOW), ((kv, lanes, dim), LOW),
+            ((kv, lanes, dim), LOW), ((span * group, lanes), LOW),
         ],
-        2 * 2**30, 4 * 2**20, [hbm] * 5,
-        [
-            pltpu.VMEM(doc_starts.shape, jnp.int32), pltpu.VMEM(tenant_ids.shape, jnp.int32),
-            pltpu.VMEM((tokens, heads, dim), LOW), pltpu.VMEM((span, heads, dim), LOW),
-            pltpu.VMEM((span, heads, dim), LOW), pltpu.SemaphoreType.DMA((5,)),
-        ],
-        limit=53, tenants=tenants, rank=rank, **sizes,
-    )(doc_starts, tenant_ids, upstream, rot, proj)
-    two, meta = lax.optimization_barrier((two, meta))
+        2 * 2**30, 4 * 2**20, tenants=tenants, rank=rank, owned=here, **sizes,
+    )(meta, upstream, rot, proj, queries)
+    two, pull = lax.optimization_barrier((two, pull))
     one = exchanged(jnp.where(even, own, two), {"ctx": 1})
     weights, send, keep = call(
         forward_kernel,
         [((kv, 2 * tokens, lanes), WIDE)] + [((ctx * rep // 2, rows, dim), LOW)] * 2,
-        4 * 2**30, 10 * 2**20, [vmem] * 5 + [hbm] + [vmem] * 3,
-        [pltpu.VMEM((tokens, heads, dim), LOW), pltpu.SemaphoreType.DMA],
+        4 * 2**30, 10 * 2**20,
         tenants=tenants, rank=rank, scaling=scaling, owned=here, **sizes,
-    )(shift_bias.T, queries, two, one, own, upstream, diff, meta, pulled)
+    )(shift_bias.T, queries, two, one, own, cots, diff, meta, pull, biases)
     part = (keep.astype(WIDE) + exchanged(send, {"ctx": 1}).astype(WIDE)).astype(LOW)
     weights, part = lax.optimization_barrier((weights, part))
     d_queries, back_two, back_one, back_own = call(
@@ -394,10 +396,11 @@
     )(part, *others)
     grads = [grad.reshape(tenants // rep, rank, here, dim) for grad in grads]
     d_keys, d_values = call(
-        halo_kernel, [((tokens, kv, dim), LOW)] * 2, 2**20, 2**20,
-        scratch=[pltpu.VMEM((tokens, kv, dim), WIDE)] * 2, kv=kv,
+        halo_kernel, [((tokens * kv, dim), LOW)] * 2, 2**20, 2**20,
+        scratch=[pltpu.VMEM((2, tokens * kv, dim), WIDE)], kv=kv,
     )(back_own, from_mate, from_two)
-    return (d_queries[None], d_keys[None], d_values[None], grads[0], grads[1])
+    d_keys, d_values = (grad.reshape(key_rows.shape) for grad in (d_keys, d_values))
+    return (d_queries[None], d_keys, d_values, grads[0], grads[1])
 
 
 def solution(mesh):

time: 43.7 us -> 43.3 us (level)
  Pallas kernels: 16.9 us -> 14.5 us
  local copies, waits for them, and re-layouts: 2.43 us -> 4.44 us
    pallas_call x5 -> x6, Pallas kernels: 16.9 us -> 14.5 us  [run(): pl.pallas_call(lambda *refs: body(*refs, **fixed), out_shape=[jax.ShapeDt...]
    unnamed x12 -> x18, local copies, waits for them, and re-layouts: 1.39 us -> 3.4 us
  transfers between devices with their start and end apart: 11 -> 11, of which waited for: 9 -> 9; matrix products, arithmetic and copies ran while one was open for 0% -> 0% of each run, Pallas kernels for 23% -> 19%
where the time goes in v7:
time: 43.3 us; the launch traced here: 43.1 us
  Pallas kernels  14.5 us (33%)
  starting transfers between devices  13.1 us (30%)
  waiting for transfers between devices  9.95 us (23%)
  local copies, waits for them, and re-layouts  4.44 us (10%)
  between operations  0.76 us (2%)
    pallas_call x6, Pallas kernels, run(): pl.pallas_call(lambda *refs: body(*refs, **fixed), out_shape=[jax.ShapeDt...  14.5 us
    ppermute x9, waiting for transfers between devices, exchanged(): lax.ppermute(value, axes, [(int(source), int(target)) for source, target...  9.23 us
    ppermute x9, starting transfers between devices, exchanged(): lax.ppermute(value, axes, [(int(source), int(target)) for source, target...  8.28 us
    ppermute x2, starting transfers between devices, shifted(): lax.ppermute(value, axis, [(source, (source + steps) % count) for source...  4.78 us
    unnamed x18, local copies, waits for them, and re-layouts  3.4 us
    squeeze x1, local copies, waits for them, and re-layouts, on_device(): value_matrix[0]  1 us
  transfers between devices with their start and end apart: 11, of which 9 were waited for; matrix products, arithmetic and copies ran while one was open for 0% of the time, Pallas kernels for 19%

profile of v7, /device:TPU:0, one launch (start us, length us, event | category | flops | bytes accessed | tf_op | source)
XLA Modules:
  0.0 43.1 jit_solution(3147590982963230358)
XLA Ops:
  0.6 1.0 %copy_bitcast_fusion = (bf16[128,4,128]{2,0,1:T(8,128)(2,1)S(1)}, bf16[128,4,128]{2,0,1:T(8,128)(2,1)S(1)}) fusion(bf16[1,128,4,128]{3,2,1,0:T(4,128)(2,1)} %param.11, bf16[1,128,4,128]{3,2,1,0:T(4,128)(2,1)} %param.10), kind=kLoop, calls=%fused_computation.5 | loop fusion | bytes 524288 | tf_op jit(solution)/shard_map/squeeze | solution.py:349
  1.7 0.0 copy-start
  1.7 0.0 copy-start.1
  1.7 0.0 copy-start.2
  1.7 3.0 %collective-permute-start = (bf16[8,128,128]{2,1,0:T(8,128)(2,1)S(1)}, bf16[8,128,128]{2,1,0:T(8,128)(2,1)S(1)}, u32[]{:S(2)}, u32[]{:S(2)}) collective-permute-start(bf16[8,128,128]{2,1,0:T(8,128)(2,1)S(1)} %maximum_bitcast_fusion.refs_4_), channel_id=1, source_target_pairs={{0,2},{1,3},{2,4},{3,5},{4,6},{5,7},{6,0},{7,1},{8,10},{9,11},{10,... | collective-permute-start | bytes 786440 | tf_op jit(solution)/shard_map/ppermute | solution.py:19
  4.7 0.0 copy-start.4
  4.7 0.7 %copy-done.4 = s32[1,1024]{1,0:T(1,128)S(1)} copy-done((s32[1,1024]{1,0:T(1,128)S(1)}, s32[1,1024]{1,0:T(1,128)}, u32[]{:S(2)}) %copy-start.4) | copy-done | bytes 4120
  5.4 0.0 copy-start.5
  5.4 0.7 %copy-done.5 = s32[1,1024]{1,0:T(1,128)S(1)} copy-done((s32[1,1024]{1,0:T(1,128)S(1)}, s32[1,1024]{1,0:T(1,128)}, u32[]{:S(2)}) %copy-start.5) | copy-done | bytes 4120
  6.1 0.3 place_kernel.1
  6.4 0.0 copy-start.7
  6.4 1.0 %copy-done.7 = f32[2,128,1024]{2,1,0:T(8,128)} copy-done((f32[2,128,1024]{2,1,0:T(8,128)}, f32[2,128,1024]{2,1,0:T(8,128)S(1)}, u32[]{:S(2)}) %copy-start.7) | copy-done | bytes 1048600
  7.4 0.0 copy-done
  7.4 0.0 copy-done.1
  7.4 0.0 copy-done.2
  7.4 0.0 copy-start.3
  7.4 1.0 %copy-done.3 = bf16[16,4,32,128]{3,2,1,0:T(8,128)(2,1)S(1)} copy-done((bf16[16,4,32,128]{3,2,1,0:T(8,128)(2,1)S(1)}, bf16[16,4,32,128]{3,2,1,0:T(8,128)(2,1)}, u32[]{:S(2)}) %copy-start.3) | copy-done | bytes 524312
  8.5 0.0 copy-start.6
  8.5 0.0 copy-start.8
  8.5 2.8 %pull_kernel.1 = (bf16[4,1024,128]{2,1,0:T(8,128)(2,1)S(1)}, bf16[4,512,128]{2,1,0:T(8,128)(2,1)S(1)}, bf16[4,1024,128]{2,1,0:T(8,128)(2,1)S(1)}, bf16[4,1024,128]{2,1,0:T(8,128)(2,1)S(1)}, bf16[512,1024]{1,0:T(8,128)(2,1)S(1)}) custom-call(s32[8,1024]{1,0:T(8,128)S(1)} %get-tuple-element.35.refs_0_.refs_7_, bf16[128,32,128]{2,1,0:T(8,128)(2,1)S(1)} %bitcast.18, ...), custom_call_target="tpu_custom_call" | custom-call | flops 2147483648 | bytes 4194304 | tf_op jit(solution)/shard_map/pull_kernel/pallas_call | solution.py:333
  11.2 0.7 %collective-permute-done.refs_2_ = bf16[8,128,128]{2,1,0:T(8,128)(2,1)S(1)} collective-permute-done((bf16[8,128,128]{2,1,0:T(8,128)(2,1)S(1)}, bf16[8,128,128]{2,1,0:T(8,128)(2,1)S(1)}, u32[]{:S(2)}, u32[]{:S(2)}) %collective-permute-start) | collective-permute-done | bytes 262176 | tf_op jit(solution)/shard_map/ppermute | solution.py:19
  12.0 0.1 collective-permute-start.1
  12.1 1.5 %collective-permute-done.1.refs_3_ = bf16[8,128,128]{2,1,0:T(8,128)(2,1)S(1)} collective-permute-done((bf16[8,128,128]{2,1,0:T(8,128)(2,1)S(1)}, bf16[8,128,128]{2,1,0:T(8,128)(2,1)S(1)}, u32[]{:S(2)}, u32[]{:S(2)}) %collective-permute-start.1) | collective-permute-done | bytes 262176 | tf_op jit(solution)/shard_map/ppermute | solution.py:29
  13.6 0.0 copy-done.6
  13.6 0.0 copy-done.8
  13.6 4.9 %forward_kernel.1 = (f32[4,256,1024]{2,1,0:T(8,128)S(1)}, bf16[16,128,128]{2,1,0:T(8,128)(2,1)S(1)}, bf16[16,128,128]{2,1,0:T(8,128)(2,1)S(1)}) custom-call(f32[4,16]{1,0:T(4,128)S(1)} %bitcast.22, bf16[4,1024,128]{2,1,0:T(8,128)(2,1)S(1)} %get-tuple-element.36.refs_1_.refs_0_, bf16[8,128,128]{2,1,0:T(8,128)(2,1)S(1)} %collective-permute-done.refs_2_, ...), custom_call_target="tpu_custom_call" | custom-call | flops 4294967296 | bytes 10485760 | tf_op jit(solution)/shard_map/forward_kernel/pallas_call | solution.py:333
  18.6 0.2 collective-permute-start.2
  18.8 1.8 %collective-permute-done.2 = bf16[16,128,128]{2,1,0:T(8,128)(2,1)S(1)} collective-permute-done((bf16[16,128,128]{2,1,0:T(8,128)(2,1)S(1)}, bf16[16,128,128]{2,1,0:T(8,128)(2,1)S(1)}, u32[]{:S(2)}, u32[]{:S(2)}) %collective-permute-start.2) | collective-permute-done | bytes 524320 | tf_op jit(solution)/shard_map/ppermute | solution.py:29
  20.5 0.1 add_convert_fusion
  20.7 2.8 %collective-permute-start.6 = (bf16[4,128,128]{2,1,0:T(8,128)(2,1)S(1)}, bf16[4,128,128]{2,1,0:T(8,128)(2,1)S(1)}, u32[]{:S(2)}, u32[]{:S(2)}) collective-permute-start(bf16[4,128,128]{2,1,0:T(8,128)(2,1)S(1)} %get-tuple-element.65), channel_id=1, source_target_pairs={{0,12},{1,13},{2,14},{3,15},{4,8},{5,9},{6,10},{7,11},{8,4},{9,5},... | collective-permute-start | bytes 393224 | tf_op jit(solution)/shard_map/ppermute | solution.py:29
  23.5 0.5 %collective-permute-start.5 = (bf16[4,128,128]{2,1,0:T(8,128)(2,1)S(1)}, bf16[4,128,128]{2,1,0:T(8,128)(2,1)S(1)}, u32[]{:S(2)}, u32[]{:S(2)}) collective-permute-start(bf16[4,128,128]{2,1,0:T(8,128)(2,1)S(1)} %get-tuple-element.66), channel_id=1, source_target_pairs={{0,4},{1,5},{2,6},{3,7},{4,0},{5,1},{6,2},{7,3},{8,12},{9,13},{10,... | collective-permute-start | bytes 393224 | tf_op jit(solution)/shard_map/ppermute | solution.py:29
  24.0 0.3 collective-permute-start.4
  24.3 5.0 %backward_kernel.1 = (bf16[128,32,128]{2,1,0:T(8,128)(2,1)}, bf16[8,128,128]{2,1,0:T(8,128)(2,1)S(1)}, bf16[8,128,128]{2,1,0:T(8,128)(2,1)S(1)}, f32[8,128,128]{2,1,0:T(8,128)S(1)}) custom-call(bf16[4,1024,128]{2,1,0:T(8,128)(2,1)S(1)} %get-tuple-element.36.refs_1_.refs_0_, bf16[4,1024,128]{2,1,0:T(8,128)(2,1)S(1)} %get-tuple-element.37.refs_1_, ...), custom_call_target="tpu_custom_call" | custom-call | flops 4294967296 | bytes 10485760 | tf_op jit(solution)/shard_map/backward_kernel/pallas_call | solution.py:333
  29.2 0.0 collective-permute-start.3
  29.2 0.0 collective-permute-done.6
  29.2 0.9 %collective-permute-done.5 = bf16[4,128,128]{2,1,0:T(8,128)(2,1)S(1)} collective-permute-done((bf16[4,128,128]{2,1,0:T(8,128)(2,1)S(1)}, bf16[4,128,128]{2,1,0:T(8,128)(2,1)S(1)}, u32[]{:S(2)}, u32[]{:S(2)}) %collective-permute-start.5) | collective-permute-done | bytes 131104 | tf_op jit(solution)/shard_map/ppermute | solution.py:29
  30.1 0.2 collective-permute-done.4
  30.3 0.1 add_convert_fusion.2
  30.4 0.4 collective-permute-done.3.refs_1_
  30.8 0.1 add_convert_fusion.1
  30.9 1.8 %collective-permute-start.7 = (bf16[8,128,128]{2,1,0:T(8,128)(2,1)S(1)}, bf16[8,128,128]{2,1,0:T(8,128)(2,1)S(1)}, u32[]{:S(2)}, u32[]{:S(2)}) collective-permute-start(bf16[8,128,128]{2,1,0:T(8,128)(2,1)S(1)} %add_convert_fusion.1), channel_id=1, source_target_pairs={{0,6},{1,7},{2,0},{3,1},{4,2},{5,3},{6,4},{7,5},{8,14},{9,15},{10,... | collective-permute-start | bytes 786440 | tf_op jit(solution)/shard_map/ppermute | solution.py:19
  32.7 2.6 %collective-permute-start.10 = (bf16[1,128,128]{2,1,0:T(8,128)(2,1)S(1)}, bf16[1,128,128]{2,1,0:T(8,128)(2,1)S(1)}, u32[]{:S(2)}, u32[]{:S(2)}) collective-permute-start(bf16[1,128,128]{2,1,0:T(8,128)(2,1)S(1)} %get-tuple-element.68), channel_id=1, source_target_pairs={{0,18},{1,19},{2,16},{3,17},{4,22},{5,23},{6,20},{7,21},{8,26},{9,... | collective-permute-start | bytes 98312 | tf_op jit(solution)/shard_map/ppermute | solution.py:29
  35.2 1.6 %collective-permute-start.9 = (bf16[1,128,128]{2,1,0:T(8,128)(2,1)S(1)}, bf16[1,128,128]{2,1,0:T(8,128)(2,1)S(1)}, u32[]{:S(2)}, u32[]{:S(2)}) collective-permute-start(bf16[1,128,128]{2,1,0:T(8,128)(2,1)S(1)} %get-tuple-element.69), channel_id=1, source_target_pairs={{0,2},{1,3},{2,0},{3,1},{4,6},{5,7},{6,4},{7,5},{8,10},{9,11},{10,... | collective-permute-start | bytes 98312 | tf_op jit(solution)/shard_map/ppermute | solution.py:29
  36.8 0.3 collective-permute-start.8
  37.1 1.7 %collective-permute-done.10.refs_3_ = bf16[1,128,128]{2,1,0:T(8,128)(2,1)S(1)} collective-permute-done((bf16[1,128,128]{2,1,0:T(8,128)(2,1)S(1)}, bf16[1,128,128]{2,1,0:T(8,128)(2,1)S(1)}, u32[]{:S(2)}, u32[]{:S(2)}) %collective-permute-start.10) | collective-permute-done | bytes 32800 | tf_op jit(solution)/shard_map/ppermute | solution.py:29
  38.8 1.9 %collective-permute-done.9.refs_2_ = bf16[1,128,128]{2,1,0:T(8,128)(2,1)S(1)} collective-permute-done((bf16[1,128,128]{2,1,0:T(8,128)(2,1)S(1)}, bf16[1,128,128]{2,1,0:T(8,128)(2,1)S(1)}, u32[]{:S(2)}, u32[]{:S(2)}) %collective-permute-start.9) | collective-permute-done | bytes 32800 | tf_op jit(solution)/shard_map/ppermute | solution.py:29
  40.7 0.9 %collective-permute-done.8.refs_1_ = bf16[1,128,128]{2,1,0:T(8,128)(2,1)S(1)} collective-permute-done((bf16[1,128,128]{2,1,0:T(8,128)(2,1)S(1)}, bf16[1,128,128]{2,1,0:T(8,128)(2,1)S(1)}, u32[]{:S(2)}, u32[]{:S(2)}) %collective-permute-start.8) | collective-permute-done | bytes 32800 | tf_op jit(solution)/shard_map/ppermute | solution.py:29
  41.6 0.0 collective-permute-done.7.refs_2_
  41.6 0.7 %grads_kernel.1 = (f32[16,4,128]{2,1,0:T(4,128)}, f32[16,4,128]{2,1,0:T(4,128)}) custom-call(bf16[1,128,128]{2,1,0:T(8,128)(2,1)S(1)} %get-tuple-element.71.refs_0_, bf16[1,128,128]{2,1,0:T(8,128)(2,1)S(1)} %collective-permute-done.8.refs_1_, bf16[1,128,128]{2,1,0:T(8,128)(2,1)S(1)} %collective-permute-done.9.refs_2_, ...), custom_call_target="tpu_custom_call" | custom-call | flops 262144 | bytes 262144 | tf_op jit(solution)/shard_map/grads_kernel/pallas_call | solution.py:333
  42.3 0.8 %halo_kernel.1 = (bf16[512,128]{1,0:T(8,128)(2,1)}, bf16[512,128]{1,0:T(8,128)(2,1)}) custom-call(f32[8,128,128]{2,1,0:T(8,128)S(1)} %get-tuple-element.49.refs_0_, bf16[8,128,128]{2,1,0:T(8,128)(2,1)S(1)} %collective-permute-done.3.refs_1_, bf16[8,128,128]{2,1,0:T(8,128)(2,1)S(1)} %collective-permute-done.7.refs_2_), custom_call_target="tpu_custom_call" | custom-call | flops 1048576 | bytes 1048576 | tf_op jit(solution)/shard_map/halo_kernel/pallas_call | solution.py:333
  (4 shorter events, 0.1 us)
Async XLA Ops:
  1.7 5.7 %copy-start = (bf16[1,128,32,128]{3,2,1,0:T(8,128)(2,1)S(1)}, bf16[1,128,32,128]{3,2,1,0:T(8,128)(2,1)}, u32[]{:S(2)}) copy-start(bf16[1,128,32,128]{3,2,1,0:T(8,128)(2,1)} %param.12) | copy-start | bytes 3145732
  1.7 5.7 %copy-start.1 = (bf16[1,128,32,128]{3,2,1,0:T(8,128)(2,1)S(1)}, bf16[1,128,32,128]{3,2,1,0:T(8,128)(2,1)}, u32[]{:S(2)}) copy-start(bf16[1,128,32,128]{3,2,1,0:T(8,128)(2,1)} %param.9) | copy-start | bytes 3145732
  1.7 5.7 %copy-start.2 = (bf16[16,4,32,128]{3,2,1,0:T(8,128)(2,1)S(1)}, bf16[16,4,32,128]{3,2,1,0:T(8,128)(2,1)}, u32[]{:S(2)}) copy-start(bf16[16,4,32,128]{3,2,1,0:T(8,128)(2,1)} %param.13) | copy-start | bytes 1572868
  1.7 10.3 %collective-permute-start = (bf16[8,128,128]{2,1,0:T(8,128)(2,1)S(1)}, bf16[8,128,128]{2,1,0:T(8,128)(2,1)S(1)}, u32[]{:S(2)}, u32[]{:S(2)}) collective-permute-start(bf16[8,128,128]{2,1,0:T(8,128)(2,1)S(1)} %maximum_bitcast_fusion.refs_4_), channel_id=1, source_target_pairs={{0,2},{1,3},{2,4},{3,5},{4,6},{5,7},{6,0},{7,1},{8,10},{9,11},{10,... | collective-permute-start | bytes 786440 | tf_op jit(solution)/shard_map/ppermute | solution.py:19
  4.7 0.7 %copy-start.4 = (s32[1,1024]{1,0:T(1,128)S(1)}, s32[1,1024]{1,0:T(1,128)}, u32[]{:S(2)}) copy-start(s32[1,1024]{1,0:T(1,128)} %refs_0_.1) | copy-start | bytes 12292
  5.4 0.7 %copy-start.5 = (s32[1,1024]{1,0:T(1,128)S(1)}, s32[1,1024]{1,0:T(1,128)}, u32[]{:S(2)}) copy-start(s32[1,1024]{1,0:T(1,128)} %refs_1_.1) | copy-start | bytes 12292
  6.4 1.0 %copy-start.7 = (f32[2,128,1024]{2,1,0:T(8,128)}, f32[2,128,1024]{2,1,0:T(8,128)S(1)}, u32[]{:S(2)}) copy-start(f32[2,128,1024]{2,1,0:T(8,128)S(1)} %get-tuple-element.43.refs_9_) | copy-start | bytes 3145732
  7.4 1.0 %copy-start.3 = (bf16[16,4,32,128]{3,2,1,0:T(8,128)(2,1)S(1)}, bf16[16,4,32,128]{3,2,1,0:T(8,128)(2,1)}, u32[]{:S(2)}) copy-start(bf16[16,4,32,128]{3,2,1,0:T(8,128)(2,1)} %param.14) | copy-start | bytes 1572868
  8.5 5.2 %copy-start.6 = (f32[16,4]{0,1:T(4,128)S(1)}, f32[16,4]{0,1:T(4,128)}, u32[]{:S(2)}) copy-start(f32[16,4]{0,1:T(4,128)} %param.15) | copy-start | bytes 772
  8.5 5.2 %copy-start.8 = (f32[2,128,1024]{2,1,0:T(8,128)S(1)}, f32[2,128,1024]{2,1,0:T(8,128)}, u32[]{:S(2)}) copy-start(f32[2,128,1024]{2,1,0:T(8,128)} %copy-done.7) | copy-start | bytes 3145732
  12.0 1.6 %collective-permute-start.1 = (bf16[8,128,128]{2,1,0:T(8,128)(2,1)S(1)}, bf16[8,128,128]{2,1,0:T(8,128)(2,1)S(1)}, u32[]{:S(2)}, u32[]{:S(2)}) collective-permute-start(bf16[8,128,128]{2,1,0:T(8,128)(2,1)S(1)} %broadcast_select_fusion), channel_id=1, source_target_pairs={{0,1},{1,0},{2,3},{3,2},{4,5},{5,4},{6,7},{7,6},{8,9},{9,8},{10,11... | collective-permute-start | bytes 786440 | tf_op jit(solution)/shard_map/ppermute | solution.py:29
  18.6 2.0 %collective-permute-start.2 = (bf16[16,128,128]{2,1,0:T(8,128)(2,1)S(1)}, bf16[16,128,128]{2,1,0:T(8,128)(2,1)S(1)}, u32[]{:S(2)}, u32[]{:S(2)}) collective-permute-start(bf16[16,128,128]{2,1,0:T(8,128)(2,1)S(1)} %get-tuple-element.46), channel_id=1, source_target_pairs={{0,1},{1,0},{2,3},{3,2},{4,5},{5,4},{6,7},{7,6},{8,9},{9,8},{10,11... | collective-permute-start | bytes 1572872 | tf_op jit(solution)/shard_map/ppermute | solution.py:29
  20.7 8.5 %collective-permute-start.6 = (bf16[4,128,128]{2,1,0:T(8,128)(2,1)S(1)}, bf16[4,128,128]{2,1,0:T(8,128)(2,1)S(1)}, u32[]{:S(2)}, u32[]{:S(2)}) collective-permute-start(bf16[4,128,128]{2,1,0:T(8,128)(2,1)S(1)} %get-tuple-element.65), channel_id=1, source_target_pairs={{0,12},{1,13},{2,14},{3,15},{4,8},{5,9},{6,10},{7,11},{8,4},{9,5},... | collective-permute-start | bytes 393224 | tf_op jit(solution)/shard_map/ppermute | solution.py:29
  23.5 6.6 %collective-permute-start.5 = (bf16[4,128,128]{2,1,0:T(8,128)(2,1)S(1)}, bf16[4,128,128]{2,1,0:T(8,128)(2,1)S(1)}, u32[]{:S(2)}, u32[]{:S(2)}) collective-permute-start(bf16[4,128,128]{2,1,0:T(8,128)(2,1)S(1)} %get-tuple-element.66), channel_id=1, source_target_pairs={{0,4},{1,5},{2,6},{3,7},{4,0},{5,1},{6,2},{7,3},{8,12},{9,13},{10,... | collective-permute-start | bytes 393224 | tf_op jit(solution)/shard_map/ppermute | solution.py:29
  24.0 6.3 %collective-permute-start.4 = (bf16[4,128,128]{2,1,0:T(8,128)(2,1)S(1)}, bf16[4,128,128]{2,1,0:T(8,128)(2,1)S(1)}, u32[]{:S(2)}, u32[]{:S(2)}) collective-permute-start(bf16[4,128,128]{2,1,0:T(8,128)(2,1)S(1)} %get-tuple-element.67), channel_id=1, source_target_pairs={{0,8},{8,0},{16,24},{24,16},{1,9},{9,1},{17,25},{25,17},{2,10},{10... | collective-permute-start | bytes 393224 | tf_op jit(solution)/shard_map/ppermute | solution.py:29
  29.2 1.5 %collective-permute-start.3 = (bf16[8,128,128]{2,1,0:T(8,128)(2,1)S(1)}, bf16[8,128,128]{2,1,0:T(8,128)(2,1)S(1)}, u32[]{:S(2)}, u32[]{:S(2)}) collective-permute-start(bf16[8,128,128]{2,1,0:T(8,128)(2,1)S(1)} %get-tuple-element.50), channel_id=1, source_target_pairs={{0,1},{1,0},{2,3},{3,2},{4,5},{5,4},{6,7},{7,6},{8,9},{9,8},{10,11... | collective-permute-start | bytes 786440 | tf_op jit(solution)/shard_map/ppermute | solution.py:29
  30.9 10.7 %collective-permute-start.7 = (bf16[8,128,128]{2,1,0:T(8,128)(2,1)S(1)}, bf16[8,128,128]{2,1,0:T(8,128)(2,1)S(1)}, u32[]{:S(2)}, u32[]{:S(2)}) collective-permute-start(bf16[8,128,128]{2,1,0:T(8,128)(2,1)S(1)} %add_convert_fusion.1), channel_id=1, source_target_pairs={{0,6},{1,7},{2,0},{3,1},{4,2},{5,3},{6,4},{7,5},{8,14},{9,15},{10,... | collective-permute-start | bytes 786440 | tf_op jit(solution)/shard_map/ppermute | solution.py:19
  32.7 6.1 %collective-permute-start.10 = (bf16[1,128,128]{2,1,0:T(8,128)(2,1)S(1)}, bf16[1,128,128]{2,1,0:T(8,128)(2,1)S(1)}, u32[]{:S(2)}, u32[]{:S(2)}) collective-permute-start(bf16[1,128,128]{2,1,0:T(8,128)(2,1)S(1)} %get-tuple-element.68), channel_id=1, source_target_pairs={{0,18},{1,19},{2,16},{3,17},{4,22},{5,23},{6,20},{7,21},{8,26},{9,... | collective-permute-start | bytes 98312 | tf_op jit(solution)/shard_map/ppermute | solution.py:29
  35.2 5.4 %collective-permute-start.9 = (bf16[1,128,128]{2,1,0:T(8,128)(2,1)S(1)}, bf16[1,128,128]{2,1,0:T(8,128)(2,1)S(1)}, u32[]{:S(2)}, u32[]{:S(2)}) collective-permute-start(bf16[1,128,128]{2,1,0:T(8,128)(2,1)S(1)} %get-tuple-element.69), channel_id=1, source_target_pairs={{0,2},{1,3},{2,0},{3,1},{4,6},{5,7},{6,4},{7,5},{8,10},{9,11},{10,... | collective-permute-start | bytes 98312 | tf_op jit(solution)/shard_map/ppermute | solution.py:29
  36.8 4.8 %collective-permute-start.8 = (bf16[1,128,128]{2,1,0:T(8,128)(2,1)S(1)}, bf16[1,128,128]{2,1,0:T(8,128)(2,1)S(1)}, u32[]{:S(2)}, u32[]{:S(2)}) collective-permute-start(bf16[1,128,128]{2,1,0:T(8,128)(2,1)S(1)} %get-tuple-element.70), channel_id=1, source_target_pairs={{0,16},{8,24},{16,0},{24,8},{1,17},{9,25},{17,1},{25,9},{2,18},{10... | collective-permute-start | bytes 98312 | tf_op jit(solution)/shard_map/ppermute | solution.py:29

commit v8 on v7

--- a/solution.py
+++ b/solution.py
@@ -12,6 +12,7 @@
 LOW = jnp.bfloat16
 WIDE = jnp.float32
 far_below = -1e30
+PIECE = 256
 
 
 def shifted(value, axis, steps):
@@ -174,6 +175,11 @@
         pull_ref[h * span : (h + 1) * span, :] = rows
 
 
+def here_of(tokens, group, piece):
+    key = lax.broadcasted_iota(jnp.int32, (tokens, PIECE), 0)
+    return key <= lax.broadcasted_iota(jnp.int32, (tokens, PIECE), 1) // group + piece * (PIECE // group)
+
+
 def places(lanes, tokens, group):
     key = lax.broadcasted_iota(jnp.int32, (tokens, lanes), 0)
     query = lax.broadcasted_iota(jnp.int32, (tokens, lanes), 1) // group
@@ -182,34 +188,37 @@
 
 def forward_kernel(
     shift_ref, queries_ref, two_ref, one_ref, own_ref, cots_ref, diff_ref, meta_ref, pull_ref, bias_ref,
-    weights_ref, send_ref, keep_ref, *, kv, group, tenants, rank, scaling, owned,
+    low_ref, send_ref, keep_ref, hidden_ref, *, kv, group, tenants, rank, scaling, owned,
 ):
     tokens = own_ref.shape[1]
+    dim = own_ref.shape[2]
     owner = meta_ref[1:2, :]
     lanes = owner.shape[1]
-    _, here = places(lanes, tokens, group)
-    hidden = []
     for g in range(kv):
-        queries = queries_ref[g]
-        fold = jnp.where(here, dot(own_ref[g], queries, 1, 1), dot(two_ref[g], queries, 1, 1))
-        fold = fold * scaling + bias_ref[0]
-        mid = dot(one_ref[g], queries, 1, 1) * scaling + bias_ref[1]
-        top = jnp.maximum(jnp.max(fold, axis=0, keepdims=True), jnp.max(mid, axis=0, keepdims=True))
-        fold = jnp.exp(fold - top)
-        mid = jnp.exp(mid - top)
-        total = jnp.sum(fold, axis=0, keepdims=True) + jnp.sum(mid, axis=0, keepdims=True)
-        share = 1.0 / total
-        fold = fold * share
-        mid = mid * share
-        weights_ref[g, 0:tokens, :] = fold
-        weights_ref[g, tokens : 2 * tokens, :] = mid
-        low = jnp.concatenate(
-            [jnp.where(here, 0.0, fold).astype(LOW), mid.astype(LOW), jnp.where(here, fold, 0.0).astype(LOW)],
-            axis=0,
-        )
-        values = jnp.concatenate([two_ref[kv + g], one_ref[kv + g], own_ref[kv + g]], axis=0)
-        hidden.append(dot(values, low, 0, 0).astype(LOW))
-    hidden = jnp.concatenate(hidden, axis=0)
+        values = jnp.concatenate([two_ref[kv + g], one_ref[kv + g], own_ref[kv + g]], axis=0).T
+        for piece in range(lanes // PIECE):
+            columns = slice(piece * PIECE, (piece + 1) * PIECE)
+            here = here_of(tokens, group, piece)
+            queries = queries_ref[g, columns, :]
+            fold = jnp.where(here, dot(own_ref[g], queries, 1, 1), dot(two_ref[g], queries, 1, 1))
+            fold = fold * scaling + bias_ref[0, :, columns]
+            mid = dot(one_ref[g], queries, 1, 1) * scaling + bias_ref[1, :, columns]
+            top = jnp.max(jnp.maximum(fold, mid), axis=0, keepdims=True)
+            fold = jnp.exp(fold - top)
+            mid = jnp.exp(mid - top)
+            share = 1.0 / jnp.sum(fold + mid, axis=0, keepdims=True)
+            fold = fold * share
+            low = jnp.concatenate(
+                [
+                    jnp.where(here, 0.0, fold).astype(LOW),
+                    (mid * share).astype(LOW),
+                    jnp.where(here, fold, 0.0).astype(LOW),
+                ],
+                axis=0,
+            )
+            low_ref[g, :, columns] = low
+            hidden_ref[g * dim : (g + 1) * dim, columns] = dot(values, low, 1, 0).astype(LOW)
+    hidden = hidden_ref[...]
     on_diff = dot(jnp.concatenate([diff_ref[g] for g in range(kv)], axis=1), hidden, 1, 0)
     lifted = own_terms(on_diff, owner, tenants, rank, group)
     one_hot = (owner == lax.broadcasted_iota(jnp.int32, (tenants, lanes), 0)).astype(WIDE)
@@ -224,7 +233,6 @@
     lift_all = jnp.concatenate(picked_rows(lifted, owner, slots, tenants, rank, group), axis=0)
     on_proj = dot(pull_ref[...], hidden, 1, 1)
     on_rot = dot(lift_all, jnp.concatenate([cots_ref[g] for g in range(kv)], axis=1), 1, 0) - on_proj
-    dim = two_ref.shape[2]
     here_rows = span // rep
     for g in range(kv):
         columns = slice(g * dim, (g + 1) * dim)
@@ -240,49 +248,42 @@
 
 
 def backward_kernel(
-    queries_ref, gh_ref, two_ref, one_ref, own_ref, weights_ref, dq_ref, back_two_ref, back_one_ref, back_own_ref,
-    *, kv, group, scaling,
+    queries_ref, gh_ref, two_ref, one_ref, own_ref, low_ref, dq_hbm, back_two_ref, back_one_ref, back_own_ref,
+    grad_ref, dq_ref, sems, *, kv, group, scaling,
 ):
-    tokens = own_ref.shape[1]
-    lanes = weights_ref.shape[2]
-    dim = queries_ref.shape[2]
-    _, here = places(lanes, tokens, group)
-    query_grads = []
+    tokens, dim = own_ref.shape[1:]
+    lanes = low_ref.shape[2]
+    rows = PIECE // group
+    windows = [
+        jnp.concatenate([two_ref[place], one_ref[place], own_ref[place]], axis=0) for place in range(2 * kv)
+    ]
+    keys = [window.T for window in windows[:kv]]
+    copies = []
+    for piece in range(lanes // PIECE):
+        columns = slice(piece * PIECE, (piece + 1) * PIECE)
+        here = slice(piece * rows, (piece + 1) * rows)
+        for g in range(kv):
+            weights = low_ref[g, :, columns].astype(WIDE)
+            weight_grad = dot(windows[kv + g], gh_ref[g, columns, :], 1, 1)
+            delta = jnp.sum(weights * weight_grad, axis=0, keepdims=True)
+            score_grad = (weights * (weight_grad - delta)).astype(LOW)
+            grad_ref[g, :, columns] = score_grad
+            query_grad = (dot(keys[g], score_grad, 1, 0) * scaling).T.reshape(rows, group, dim)
+            if g % 2 == 1:
+                both = jnp.concatenate([before, query_grad], axis=1).astype(LOW)
+                dq_ref[here, (g - 1) * group : (g + 1) * group, :] = both
+            before = query_grad
+        copies.append(pltpu.make_async_copy(dq_ref.at[here], dq_hbm.at[here], sems.at[piece]))
+        copies[-1].start()
     for g in range(kv):
-        grads = gh_ref[g]
-        fold_weights = weights_ref[g, 0:tokens, :]
-        mid_weights = weights_ref[g, tokens : 2 * tokens, :]
-        fold = jnp.where(here, dot(own_ref[kv + g], grads, 1, 1), dot(two_ref[kv + g], grads, 1, 1))
-        mid = dot(one_ref[kv + g], grads, 1, 1)
-        delta = jnp.sum(fold * fold_weights, axis=0, keepdims=True) + jnp.sum(
-            mid * mid_weights, axis=0, keepdims=True
-        )
-        fold = fold_weights * (fold - delta)
-        mid = mid_weights * (mid - delta)
-        score_grad = jnp.concatenate(
-            [jnp.where(here, 0.0, fold).astype(LOW), mid.astype(LOW), jnp.where(here, fold, 0.0).astype(LOW)],
-            axis=0,
-        )
-        low = jnp.concatenate(
-            [
-                jnp.where(here, 0.0, fold_weights).astype(LOW),
-                mid_weights.astype(LOW),
-                jnp.where(here, fold_weights, 0.0).astype(LOW),
-            ],
-            axis=0,
-        )
-        keys = jnp.concatenate([two_ref[g], one_ref[g], own_ref[g]], axis=0)
-        key_grad = dot(score_grad, queries_ref[g], 1, 0) * scaling
-        value_grad = dot(low, grads, 1, 0)
+        key_grad = dot(grad_ref[g], queries_ref[g], 1, 0) * scaling
+        value_grad = dot(low_ref[g], gh_ref[g], 1, 0)
         for place, grad in ((g, key_grad), (kv + g, value_grad)):
             back_two_ref[place] = grad[0:tokens].astype(LOW)
             back_one_ref[place] = grad[tokens : 2 * tokens].astype(LOW)
             back_own_ref[place] = grad[2 * tokens :]
-        query_grad = dot(keys, score_grad, 0, 0) * scaling
-        query_grads.append(query_grad.T.reshape(tokens, group, dim))
-        if g % 2 == 1:
-            both = jnp.concatenate(query_grads[-2:], axis=1).astype(LOW)
-            dq_ref[:, (g - 1) * group : (g + 1) * group, :] = both
+    for copy in copies:
+        copy.wait()
 
 
 def grads_kernel(part_ref, *refs, owned):
@@ -328,15 +329,15 @@
     sizes = dict(kv=kv, group=group)
     vmem = pl.BlockSpec(memory_space=pltpu.VMEM)
 
-    def call(body, outs, flops, moved, specs=None, scratch=(), limit=24, **fixed):
+    def call(body, outs, flops, moved, out_specs=None, scratch=(), **fixed):
         def run(*operands):
             return pl.pallas_call(
                 lambda *refs: body(*refs, **fixed),
                 out_shape=[jax.ShapeDtypeStruct(*out) for out in outs],
-                in_specs=specs or [vmem] * len(operands),
-                out_specs=[vmem] * len(outs),
+                in_specs=[vmem] * len(operands),
+                out_specs=out_specs or [vmem] * len(outs),
                 scratch_shapes=scratch,
-                compiler_params=pltpu.CompilerParams(vmem_limit_bytes=limit * 2**20),
+                compiler_params=pltpu.CompilerParams(vmem_limit_bytes=24 * 2**20),
                 name=body.__name__,
                 cost_estimate=pl.CostEstimate(flops=flops, bytes_accessed=moved, transcendentals=0),
             )(*operands)
@@ -363,19 +364,24 @@
     )(meta, upstream, rot, proj, queries)
     two, pull = lax.optimization_barrier((two, pull))
     one = exchanged(jnp.where(even, own, two), {"ctx": 1})
-    weights, send, keep = call(
+    low, send, keep = call(
         forward_kernel,
-        [((kv, 2 * tokens, lanes), WIDE)] + [((ctx * rep // 2, rows, dim), LOW)] * 2,
-        4 * 2**30, 10 * 2**20,
+        [((kv, 3 * tokens, lanes), LOW)] + [((ctx * rep // 2, rows, dim), LOW)] * 2,
+        4 * 2**30, 10 * 2**20, scratch=[pltpu.VMEM((heads // group * dim, lanes), LOW)],
         tenants=tenants, rank=rank, scaling=scaling, owned=here, **sizes,
     )(shift_bias.T, queries, two, one, own, cots, diff, meta, pull, biases)
     part = (keep.astype(WIDE) + exchanged(send, {"ctx": 1}).astype(WIDE)).astype(LOW)
-    weights, part = lax.optimization_barrier((weights, part))
+    low, part = lax.optimization_barrier((low, part))
     d_queries, back_two, back_one, back_own = call(
         backward_kernel,
         [((tokens, heads, dim), LOW), (own.shape, LOW), (own.shape, LOW), (own.shape, WIDE)],
-        4 * 2**30, 10 * 2**20, scaling=scaling, **sizes,
-    )(queries, grad_hidden, two, one, own, weights)
+        4 * 2**30, 10 * 2**20,
+        scratch=[
+            pltpu.VMEM((kv, 3 * tokens, lanes), LOW), pltpu.VMEM((tokens, heads, dim), LOW),
+            pltpu.SemaphoreType.DMA((lanes // PIECE,)),
+        ],
+        out_specs=[pl.BlockSpec(memory_space=pltpu.HBM), vmem, vmem, vmem], scaling=scaling, **sizes,
+    )(queries, grad_hidden, two, one, own, low)
     from_mate = exchanged(back_one, {"ctx": 1})
     onward = back_two.astype(WIDE) + jnp.where(even, 0.0, from_mate.astype(WIDE))
     onward = onward.astype(LOW)

time: 43.3 us -> 49.1 us (1.13)
  Pallas kernels: 14.5 us -> 20.2 us
    pallas_call x6, Pallas kernels: 14.5 us -> 20.2 us  [run(): pl.pallas_call(lambda *refs: body(*refs, **fixed), out_shape=[jax.ShapeDt...]
  transfers between devices with their start and end apart: 11 -> 11, of which waited for: 9 -> 7; matrix products, arithmetic and copies ran while one was open for 0% -> 0% of each run, Pallas kernels for 19% -> 23%
where the time goes in v8:
time: 49.1 us; the launch traced here: 48.9 us
  Pallas kernels  20.2 us (41%)
  starting transfers between devices  13.1 us (27%)
  waiting for transfers between devices  9.92 us (20%)
  local copies, waits for them, and re-layouts  4.44 us (9%)
  between operations  0.8 us (2%)
    pallas_call x6, Pallas kernels, run(): pl.pallas_call(lambda *refs: body(*refs, **fixed), out_shape=[jax.ShapeDt...  20.2 us
    ppermute x9, waiting for transfers between devices, exchanged(): lax.ppermute(value, axes, [(int(source), int(target)) for source, target...  9.2 us
    ppermute x9, starting transfers between devices, exchanged(): lax.ppermute(value, axes, [(int(source), int(target)) for source, target...  8.34 us
    ppermute x2, starting transfers between devices, shifted(): lax.ppermute(value, axis, [(source, (source + steps) % count) for source...  4.78 us
    unnamed x18, local copies, waits for them, and re-layouts  3.4 us
    squeeze x1, local copies, waits for them, and re-layouts, on_device(): value_matrix[0]  1 us
  transfers between devices with their start and end apart: 11, of which 7 were waited for; matrix products, arithmetic and copies ran while one was open for 0% of the time, Pallas kernels for 23%

profile of v8, /device:TPU:0, one launch (start us, length us, event | category | flops | bytes accessed | tf_op | source)
XLA Modules:
  0.0 48.9 jit_solution(17418501378022640579)
XLA Ops:
  0.6 1.0 %copy_bitcast_fusion = (bf16[128,4,128]{2,0,1:T(8,128)(2,1)S(1)}, bf16[128,4,128]{2,0,1:T(8,128)(2,1)S(1)}) fusion(bf16[1,128,4,128]{3,2,1,0:T(4,128)(2,1)} %param.11, bf16[1,128,4,128]{3,2,1,0:T(4,128)(2,1)} %param.10), kind=kLoop, calls=%fused_computation.5 | loop fusion | bytes 524288 | tf_op jit(solution)/shard_map/squeeze | solution.py:350
  1.7 0.0 copy-start
  1.7 0.0 copy-start.1
  1.7 0.0 copy-start.2
  1.7 3.0 %collective-permute-start = (bf16[8,128,128]{2,1,0:T(8,128)(2,1)S(1)}, bf16[8,128,128]{2,1,0:T(8,128)(2,1)S(1)}, u32[]{:S(2)}, u32[]{:S(2)}) collective-permute-start(bf16[8,128,128]{2,1,0:T(8,128)(2,1)S(1)} %maximum_bitcast_fusion.refs_4_), channel_id=1, source_target_pairs={{0,2},{1,3},{2,4},{3,5},{4,6},{5,7},{6,0},{7,1},{8,10},{9,11},{10,... | collective-permute-start | bytes 786440 | tf_op jit(solution)/shard_map/ppermute | solution.py:20
  4.7 0.0 copy-start.4
  4.7 0.7 %copy-done.4 = s32[1,1024]{1,0:T(1,128)S(1)} copy-done((s32[1,1024]{1,0:T(1,128)S(1)}, s32[1,1024]{1,0:T(1,128)}, u32[]{:S(2)}) %copy-start.4) | copy-done | bytes 4120
  5.4 0.0 copy-start.5
  5.4 0.7 %copy-done.5 = s32[1,1024]{1,0:T(1,128)S(1)} copy-done((s32[1,1024]{1,0:T(1,128)S(1)}, s32[1,1024]{1,0:T(1,128)}, u32[]{:S(2)}) %copy-start.5) | copy-done | bytes 4120
  6.1 0.3 place_kernel.1
  6.4 0.0 copy-start.7
  6.4 1.0 %copy-done.7 = f32[2,128,1024]{2,1,0:T(8,128)} copy-done((f32[2,128,1024]{2,1,0:T(8,128)}, f32[2,128,1024]{2,1,0:T(8,128)S(1)}, u32[]{:S(2)}) %copy-start.7) | copy-done | bytes 1048600
  7.4 0.0 copy-done
  7.4 0.0 copy-done.1
  7.4 0.0 copy-done.2
  7.4 0.0 copy-start.3
  7.4 1.0 %copy-done.3 = bf16[16,4,32,128]{3,2,1,0:T(8,128)(2,1)S(1)} copy-done((bf16[16,4,32,128]{3,2,1,0:T(8,128)(2,1)S(1)}, bf16[16,4,32,128]{3,2,1,0:T(8,128)(2,1)}, u32[]{:S(2)}) %copy-start.3) | copy-done | bytes 524312
  8.5 0.0 copy-start.6
  8.5 0.0 copy-start.8
  8.5 2.8 %pull_kernel.1 = (bf16[4,1024,128]{2,1,0:T(8,128)(2,1)S(1)}, bf16[4,512,128]{2,1,0:T(8,128)(2,1)S(1)}, bf16[4,1024,128]{2,1,0:T(8,128)(2,1)S(1)}, bf16[4,1024,128]{2,1,0:T(8,128)(2,1)S(1)}, bf16[512,1024]{1,0:T(8,128)(2,1)S(1)}) custom-call(s32[8,1024]{1,0:T(8,128)S(1)} %get-tuple-element.35.refs_0_.refs_7_, bf16[128,32,128]{2,1,0:T(8,128)(2,1)S(1)} %bitcast.18, ...), custom_call_target="tpu_custom_call" | custom-call | flops 2147483648 | bytes 4194304 | tf_op jit(solution)/shard_map/pull_kernel/pallas_call | solution.py:334
  11.2 0.7 %collective-permute-done.refs_2_ = bf16[8,128,128]{2,1,0:T(8,128)(2,1)S(1)} collective-permute-done((bf16[8,128,128]{2,1,0:T(8,128)(2,1)S(1)}, bf16[8,128,128]{2,1,0:T(8,128)(2,1)S(1)}, u32[]{:S(2)}, u32[]{:S(2)}) %collective-permute-start) | collective-permute-done | bytes 262176 | tf_op jit(solution)/shard_map/ppermute | solution.py:20
  12.0 0.1 collective-permute-start.1
  12.1 1.5 %collective-permute-done.1.refs_3_ = bf16[8,128,128]{2,1,0:T(8,128)(2,1)S(1)} collective-permute-done((bf16[8,128,128]{2,1,0:T(8,128)(2,1)S(1)}, bf16[8,128,128]{2,1,0:T(8,128)(2,1)S(1)}, u32[]{:S(2)}, u32[]{:S(2)}) %collective-permute-start.1) | collective-permute-done | bytes 262176 | tf_op jit(solution)/shard_map/ppermute | solution.py:30
  13.6 0.0 copy-done.6
  13.6 0.0 copy-done.8
  13.6 7.4 %forward_kernel.1 = (bf16[4,384,1024]{2,1,0:T(8,128)(2,1)S(1)}, bf16[16,128,128]{2,1,0:T(8,128)(2,1)S(1)}, bf16[16,128,128]{2,1,0:T(8,128)(2,1)S(1)}) custom-call(f32[4,16]{1,0:T(4,128)S(1)} %bitcast.22, bf16[4,1024,128]{2,1,0:T(8,128)(2,1)S(1)} %get-tuple-element.36.refs_1_.refs_0_, bf16[8,128,128]{2,1,0:T(8,128)(2,1)S(1)} %collective-permute-done.refs_2_, ...), custom_call_target="tpu_custom_call" | custom-call | flops 4294967296 | bytes 10485760 | tf_op jit(solution)/shard_map/forward_kernel/pallas_call | solution.py:334
  21.0 0.2 collective-permute-start.2
  21.2 1.8 %collective-permute-done.2 = bf16[16,128,128]{2,1,0:T(8,128)(2,1)S(1)} collective-permute-done((bf16[16,128,128]{2,1,0:T(8,128)(2,1)S(1)}, bf16[16,128,128]{2,1,0:T(8,128)(2,1)S(1)}, u32[]{:S(2)}, u32[]{:S(2)}) %collective-permute-start.2) | collective-permute-done | bytes 524320 | tf_op jit(solution)/shard_map/ppermute | solution.py:30
  23.0 0.1 add_convert_fusion
  23.2 2.8 %collective-permute-start.6 = (bf16[4,128,128]{2,1,0:T(8,128)(2,1)S(1)}, bf16[4,128,128]{2,1,0:T(8,128)(2,1)S(1)}, u32[]{:S(2)}, u32[]{:S(2)}) collective-permute-start(bf16[4,128,128]{2,1,0:T(8,128)(2,1)S(1)} %get-tuple-element.65), channel_id=1, source_target_pairs={{0,12},{1,13},{2,14},{3,15},{4,8},{5,9},{6,10},{7,11},{8,4},{9,5},... | collective-permute-start | bytes 393224 | tf_op jit(solution)/shard_map/ppermute | solution.py:30
  26.0 0.5 %collective-permute-start.5 = (bf16[4,128,128]{2,1,0:T(8,128)(2,1)S(1)}, bf16[4,128,128]{2,1,0:T(8,128)(2,1)S(1)}, u32[]{:S(2)}, u32[]{:S(2)}) collective-permute-start(bf16[4,128,128]{2,1,0:T(8,128)(2,1)S(1)} %get-tuple-element.66), channel_id=1, source_target_pairs={{0,4},{1,5},{2,6},{3,7},{4,0},{5,1},{6,2},{7,3},{8,12},{9,13},{10,... | collective-permute-start | bytes 393224 | tf_op jit(solution)/shard_map/ppermute | solution.py:30
  26.5 0.3 collective-permute-start.4
  26.7 8.3 %backward_kernel.1 = (bf16[128,32,128]{2,1,0:T(8,128)(2,1)}, bf16[8,128,128]{2,1,0:T(8,128)(2,1)S(1)}, bf16[8,128,128]{2,1,0:T(8,128)(2,1)S(1)}, f32[8,128,128]{2,1,0:T(8,128)S(1)}) custom-call(bf16[4,1024,128]{2,1,0:T(8,128)(2,1)S(1)} %get-tuple-element.36.refs_1_.refs_0_, bf16[4,1024,128]{2,1,0:T(8,128)(2,1)S(1)} %get-tuple-element.37.refs_1_, ...), custom_call_target="tpu_custom_call" | custom-call | flops 4294967296 | bytes 10485760 | tf_op jit(solution)/shard_map/backward_kernel/pallas_call | solution.py:334
  35.0 0.1 collective-permute-start.3
  35.1 0.0 collective-permute-done.6
  35.1 0.0 collective-permute-done.5
  35.1 0.0 collective-permute-done.4
  35.1 0.1 add_convert_fusion.2
  35.2 1.4 %collective-permute-done.3.refs_1_ = bf16[8,128,128]{2,1,0:T(8,128)(2,1)S(1)} collective-permute-done((bf16[8,128,128]{2,1,0:T(8,128)(2,1)S(1)}, bf16[8,128,128]{2,1,0:T(8,128)(2,1)S(1)}, u32[]{:S(2)}, u32[]{:S(2)}) %collective-permute-start.3) | collective-permute-done | bytes 262176 | tf_op jit(solution)/shard_map/ppermute | solution.py:30
  36.6 0.1 add_convert_fusion.1
  36.7 1.8 %collective-permute-start.7 = (bf16[8,128,128]{2,1,0:T(8,128)(2,1)S(1)}, bf16[8,128,128]{2,1,0:T(8,128)(2,1)S(1)}, u32[]{:S(2)}, u32[]{:S(2)}) collective-permute-start(bf16[8,128,128]{2,1,0:T(8,128)(2,1)S(1)} %add_convert_fusion.1), channel_id=1, source_target_pairs={{0,6},{1,7},{2,0},{3,1},{4,2},{5,3},{6,4},{7,5},{8,14},{9,15},{10,... | collective-permute-start | bytes 786440 | tf_op jit(solution)/shard_map/ppermute | solution.py:20
  38.5 2.6 %collective-permute-start.10 = (bf16[1,128,128]{2,1,0:T(8,128)(2,1)S(1)}, bf16[1,128,128]{2,1,0:T(8,128)(2,1)S(1)}, u32[]{:S(2)}, u32[]{:S(2)}) collective-permute-start(bf16[1,128,128]{2,1,0:T(8,128)(2,1)S(1)} %get-tuple-element.68), channel_id=1, source_target_pairs={{0,18},{1,19},{2,16},{3,17},{4,22},{5,23},{6,20},{7,21},{8,26},{9,... | collective-permute-start | bytes 98312 | tf_op jit(solution)/shard_map/ppermute | solution.py:30
  41.1 1.6 %collective-permute-start.9 = (bf16[1,128,128]{2,1,0:T(8,128)(2,1)S(1)}, bf16[1,128,128]{2,1,0:T(8,128)(2,1)S(1)}, u32[]{:S(2)}, u32[]{:S(2)}) collective-permute-start(bf16[1,128,128]{2,1,0:T(8,128)(2,1)S(1)} %get-tuple-element.69), channel_id=1, source_target_pairs={{0,2},{1,3},{2,0},{3,1},{4,6},{5,7},{6,4},{7,5},{8,10},{9,11},{10,... | collective-permute-start | bytes 98312 | tf_op jit(solution)/shard_map/ppermute | solution.py:30
  42.6 0.3 collective-permute-start.8
  42.9 1.7 %collective-permute-done.10.refs_3_ = bf16[1,128,128]{2,1,0:T(8,128)(2,1)S(1)} collective-permute-done((bf16[1,128,128]{2,1,0:T(8,128)(2,1)S(1)}, bf16[1,128,128]{2,1,0:T(8,128)(2,1)S(1)}, u32[]{:S(2)}, u32[]{:S(2)}) %collective-permute-start.10) | collective-permute-done | bytes 32800 | tf_op jit(solution)/shard_map/ppermute | solution.py:30
  44.6 1.9 %collective-permute-done.9.refs_2_ = bf16[1,128,128]{2,1,0:T(8,128)(2,1)S(1)} collective-permute-done((bf16[1,128,128]{2,1,0:T(8,128)(2,1)S(1)}, bf16[1,128,128]{2,1,0:T(8,128)(2,1)S(1)}, u32[]{:S(2)}, u32[]{:S(2)}) %collective-permute-start.9) | collective-permute-done | bytes 32800 | tf_op jit(solution)/shard_map/ppermute | solution.py:30
  46.5 0.9 %collective-permute-done.8.refs_1_ = bf16[1,128,128]{2,1,0:T(8,128)(2,1)S(1)} collective-permute-done((bf16[1,128,128]{2,1,0:T(8,128)(2,1)S(1)}, bf16[1,128,128]{2,1,0:T(8,128)(2,1)S(1)}, u32[]{:S(2)}, u32[]{:S(2)}) %collective-permute-start.8) | collective-permute-done | bytes 32800 | tf_op jit(solution)/shard_map/ppermute | solution.py:30
  47.4 0.0 collective-permute-done.7.refs_2_
  47.4 0.7 %grads_kernel.1 = (f32[16,4,128]{2,1,0:T(4,128)}, f32[16,4,128]{2,1,0:T(4,128)}) custom-call(bf16[1,128,128]{2,1,0:T(8,128)(2,1)S(1)} %get-tuple-element.71.refs_0_, bf16[1,128,128]{2,1,0:T(8,128)(2,1)S(1)} %collective-permute-done.8.refs_1_, bf16[1,128,128]{2,1,0:T(8,128)(2,1)S(1)} %collective-permute-done.9.refs_2_, ...), custom_call_target="tpu_custom_call" | custom-call | flops 262144 | bytes 262144 | tf_op jit(solution)/shard_map/grads_kernel/pallas_call | solution.py:334
  48.1 0.8 %halo_kernel.1 = (bf16[512,128]{1,0:T(8,128)(2,1)}, bf16[512,128]{1,0:T(8,128)(2,1)}) custom-call(f32[8,128,128]{2,1,0:T(8,128)S(1)} %get-tuple-element.49.refs_0_, bf16[8,128,128]{2,1,0:T(8,128)(2,1)S(1)} %collective-permute-done.3.refs_1_, bf16[8,128,128]{2,1,0:T(8,128)(2,1)S(1)} %collective-permute-done.7.refs_2_), custom_call_target="tpu_custom_call" | custom-call | flops 1048576 | bytes 1048576 | tf_op jit(solution)/shard_map/halo_kernel/pallas_call | solution.py:334
  (4 shorter events, 0.1 us)
Async XLA Ops:
  1.7 5.7 %copy-start = (bf16[1,128,32,128]{3,2,1,0:T(8,128)(2,1)S(1)}, bf16[1,128,32,128]{3,2,1,0:T(8,128)(2,1)}, u32[]{:S(2)}) copy-start(bf16[1,128,32,128]{3,2,1,0:T(8,128)(2,1)} %param.12) | copy-start | bytes 3145732
  1.7 5.7 %copy-start.1 = (bf16[1,128,32,128]{3,2,1,0:T(8,128)(2,1)S(1)}, bf16[1,128,32,128]{3,2,1,0:T(8,128)(2,1)}, u32[]{:S(2)}) copy-start(bf16[1,128,32,128]{3,2,1,0:T(8,128)(2,1)} %param.9) | copy-start | bytes 3145732
  1.7 5.7 %copy-start.2 = (bf16[16,4,32,128]{3,2,1,0:T(8,128)(2,1)S(1)}, bf16[16,4,32,128]{3,2,1,0:T(8,128)(2,1)}, u32[]{:S(2)}) copy-start(bf16[16,4,32,128]{3,2,1,0:T(8,128)(2,1)} %param.13) | copy-start | bytes 1572868
  1.7 10.3 %collective-permute-start = (bf16[8,128,128]{2,1,0:T(8,128)(2,1)S(1)}, bf16[8,128,128]{2,1,0:T(8,128)(2,1)S(1)}, u32[]{:S(2)}, u32[]{:S(2)}) collective-permute-start(bf16[8,128,128]{2,1,0:T(8,128)(2,1)S(1)} %maximum_bitcast_fusion.refs_4_), channel_id=1, source_target_pairs={{0,2},{1,3},{2,4},{3,5},{4,6},{5,7},{6,0},{7,1},{8,10},{9,11},{10,... | collective-permute-start | bytes 786440 | tf_op jit(solution)/shard_map/ppermute | solution.py:20
  4.7 0.7 %copy-start.4 = (s32[1,1024]{1,0:T(1,128)S(1)}, s32[1,1024]{1,0:T(1,128)}, u32[]{:S(2)}) copy-start(s32[1,1024]{1,0:T(1,128)} %refs_0_.1) | copy-start | bytes 12292
  5.4 0.7 %copy-start.5 = (s32[1,1024]{1,0:T(1,128)S(1)}, s32[1,1024]{1,0:T(1,128)}, u32[]{:S(2)}) copy-start(s32[1,1024]{1,0:T(1,128)} %refs_1_.1) | copy-start | bytes 12292
  6.4 1.0 %copy-start.7 = (f32[2,128,1024]{2,1,0:T(8,128)}, f32[2,128,1024]{2,1,0:T(8,128)S(1)}, u32[]{:S(2)}) copy-start(f32[2,128,1024]{2,1,0:T(8,128)S(1)} %get-tuple-element.43.refs_9_) | copy-start | bytes 3145732
  7.4 1.0 %copy-start.3 = (bf16[16,4,32,128]{3,2,1,0:T(8,128)(2,1)S(1)}, bf16[16,4,32,128]{3,2,1,0:T(8,128)(2,1)}, u32[]{:S(2)}) copy-start(bf16[16,4,32,128]{3,2,1,0:T(8,128)(2,1)} %param.14) | copy-start | bytes 1572868
  8.5 5.2 %copy-start.6 = (f32[16,4]{0,1:T(4,128)S(1)}, f32[16,4]{0,1:T(4,128)}, u32[]{:S(2)}) copy-start(f32[16,4]{0,1:T(4,128)} %param.15) | copy-start | bytes 772
  8.5 5.2 %copy-start.8 = (f32[2,128,1024]{2,1,0:T(8,128)S(1)}, f32[2,128,1024]{2,1,0:T(8,128)}, u32[]{:S(2)}) copy-start(f32[2,128,1024]{2,1,0:T(8,128)} %copy-done.7) | copy-start | bytes 3145732
  12.0 1.6 %collective-permute-start.1 = (bf16[8,128,128]{2,1,0:T(8,128)(2,1)S(1)}, bf16[8,128,128]{2,1,0:T(8,128)(2,1)S(1)}, u32[]{:S(2)}, u32[]{:S(2)}) collective-permute-start(bf16[8,128,128]{2,1,0:T(8,128)(2,1)S(1)} %broadcast_select_fusion), channel_id=1, source_target_pairs={{0,1},{1,0},{2,3},{3,2},{4,5},{5,4},{6,7},{7,6},{8,9},{9,8},{10,11... | collective-permute-start | bytes 786440 | tf_op jit(solution)/shard_map/ppermute | solution.py:30
  21.0 2.0 %collective-permute-start.2 = (bf16[16,128,128]{2,1,0:T(8,128)(2,1)S(1)}, bf16[16,128,128]{2,1,0:T(8,128)(2,1)S(1)}, u32[]{:S(2)}, u32[]{:S(2)}) collective-permute-start(bf16[16,128,128]{2,1,0:T(8,128)(2,1)S(1)} %get-tuple-element.46), channel_id=1, source_target_pairs={{0,1},{1,0},{2,3},{3,2},{4,5},{5,4},{6,7},{7,6},{8,9},{9,8},{10,11... | collective-permute-start | bytes 1572872 | tf_op jit(solution)/shard_map/ppermute | solution.py:30
  23.2 11.9 %collective-permute-start.6 = (bf16[4,128,128]{2,1,0:T(8,128)(2,1)S(1)}, bf16[4,128,128]{2,1,0:T(8,128)(2,1)S(1)}, u32[]{:S(2)}, u32[]{:S(2)}) collective-permute-start(bf16[4,128,128]{2,1,0:T(8,128)(2,1)S(1)} %get-tuple-element.65), channel_id=1, source_target_pairs={{0,12},{1,13},{2,14},{3,15},{4,8},{5,9},{6,10},{7,11},{8,4},{9,5},... | collective-permute-start | bytes 393224 | tf_op jit(solution)/shard_map/ppermute | solution.py:30
  26.0 9.1 %collective-permute-start.5 = (bf16[4,128,128]{2,1,0:T(8,128)(2,1)S(1)}, bf16[4,128,128]{2,1,0:T(8,128)(2,1)S(1)}, u32[]{:S(2)}, u32[]{:S(2)}) collective-permute-start(bf16[4,128,128]{2,1,0:T(8,128)(2,1)S(1)} %get-tuple-element.66), channel_id=1, source_target_pairs={{0,4},{1,5},{2,6},{3,7},{4,0},{5,1},{6,2},{7,3},{8,12},{9,13},{10,... | collective-permute-start | bytes 393224 | tf_op jit(solution)/shard_map/ppermute | solution.py:30
  26.5 8.6 %collective-permute-start.4 = (bf16[4,128,128]{2,1,0:T(8,128)(2,1)S(1)}, bf16[4,128,128]{2,1,0:T(8,128)(2,1)S(1)}, u32[]{:S(2)}, u32[]{:S(2)}) collective-permute-start(bf16[4,128,128]{2,1,0:T(8,128)(2,1)S(1)} %get-tuple-element.67), channel_id=1, source_target_pairs={{0,8},{8,0},{16,24},{24,16},{1,9},{9,1},{17,25},{25,17},{2,10},{10... | collective-permute-start | bytes 393224 | tf_op jit(solution)/shard_map/ppermute | solution.py:30
  35.0 1.6 %collective-permute-start.3 = (bf16[8,128,128]{2,1,0:T(8,128)(2,1)S(1)}, bf16[8,128,128]{2,1,0:T(8,128)(2,1)S(1)}, u32[]{:S(2)}, u32[]{:S(2)}) collective-permute-start(bf16[8,128,128]{2,1,0:T(8,128)(2,1)S(1)} %get-tuple-element.50), channel_id=1, source_target_pairs={{0,1},{1,0},{2,3},{3,2},{4,5},{5,4},{6,7},{7,6},{8,9},{9,8},{10,11... | collective-permute-start | bytes 786440 | tf_op jit(solution)/shard_map/ppermute | solution.py:30
  36.7 10.7 %collective-permute-start.7 = (bf16[8,128,128]{2,1,0:T(8,128)(2,1)S(1)}, bf16[8,128,128]{2,1,0:T(8,128)(2,1)S(1)}, u32[]{:S(2)}, u32[]{:S(2)}) collective-permute-start(bf16[8,128,128]{2,1,0:T(8,128)(2,1)S(1)} %add_convert_fusion.1), channel_id=1, source_target_pairs={{0,6},{1,7},{2,0},{3,1},{4,2},{5,3},{6,4},{7,5},{8,14},{9,15},{10,... | collective-permute-start | bytes 786440 | tf_op jit(solution)/shard_map/ppermute | solution.py:20
  38.5 6.1 %collective-permute-start.10 = (bf16[1,128,128]{2,1,0:T(8,128)(2,1)S(1)}, bf16[1,128,128]{2,1,0:T(8,128)(2,1)S(1)}, u32[]{:S(2)}, u32[]{:S(2)}) collective-permute-start(bf16[1,128,128]{2,1,0:T(8,128)(2,1)S(1)} %get-tuple-element.68), channel_id=1, source_target_pairs={{0,18},{1,19},{2,16},{3,17},{4,22},{5,23},{6,20},{7,21},{8,26},{9,... | collective-permute-start | bytes 98312 | tf_op jit(solution)/shard_map/ppermute | solution.py:30
  41.1 5.4 %collective-permute-start.9 = (bf16[1,128,128]{2,1,0:T(8,128)(2,1)S(1)}, bf16[1,128,128]{2,1,0:T(8,128)(2,1)S(1)}, u32[]{:S(2)}, u32[]{:S(2)}) collective-permute-start(bf16[1,128,128]{2,1,0:T(8,128)(2,1)S(1)} %get-tuple-element.69), channel_id=1, source_target_pairs={{0,2},{1,3},{2,0},{3,1},{4,6},{5,7},{6,4},{7,5},{8,10},{9,11},{10,... | collective-permute-start | bytes 98312 | tf_op jit(solution)/shard_map/ppermute | solution.py:30
  42.6 4.8 %collective-permute-start.8 = (bf16[1,128,128]{2,1,0:T(8,128)(2,1)S(1)}, bf16[1,128,128]{2,1,0:T(8,128)(2,1)S(1)}, u32[]{:S(2)}, u32[]{:S(2)}) collective-permute-start(bf16[1,128,128]{2,1,0:T(8,128)(2,1)S(1)} %get-tuple-element.70), channel_id=1, source_target_pairs={{0,16},{8,24},{16,0},{24,8},{1,17},{9,25},{17,1},{25,9},{2,18},{10... | collective-permute-start | bytes 98312 | tf_op jit(solution)/shard_map/ppermute | solution.py:30

commit v9 on v8

--- a/solution.py
+++ b/solution.py
@@ -12,7 +12,6 @@
 LOW = jnp.bfloat16
 WIDE = jnp.float32
 far_below = -1e30
-PIECE = 256
 
 
 def shifted(value, axis, steps):
@@ -175,11 +174,6 @@
         pull_ref[h * span : (h + 1) * span, :] = rows
 
 
-def here_of(tokens, group, piece):
-    key = lax.broadcasted_iota(jnp.int32, (tokens, PIECE), 0)
-    return key <= lax.broadcasted_iota(jnp.int32, (tokens, PIECE), 1) // group + piece * (PIECE // group)
-
-
 def places(lanes, tokens, group):
     key = lax.broadcasted_iota(jnp.int32, (tokens, lanes), 0)
     query = lax.broadcasted_iota(jnp.int32, (tokens, lanes), 1) // group
@@ -194,30 +188,29 @@
     dim = own_ref.shape[2]
     owner = meta_ref[1:2, :]
     lanes = owner.shape[1]
+    _, here = places(lanes, tokens, group)
+    windows = [
+        jnp.concatenate([two_ref[place], one_ref[place], own_ref[place]], axis=0) for place in range(2 * kv)
+    ]
+
+    def weigh(scores):
+        fold = jnp.where(here, scores[2 * tokens :], scores[0:tokens]) * scaling + bias_ref[0]
+        mid = scores[tokens : 2 * tokens] * scaling + bias_ref[1]
+        top = jnp.max(jnp.maximum(fold, mid), axis=0, keepdims=True)
+        fold = jnp.exp(fold - top)
+        mid = jnp.exp(mid - top)
+        share = 1.0 / jnp.sum(fold + mid, axis=0, keepdims=True)
+        fold = fold * share
+        pieces = [jnp.where(here, 0.0, fold), mid * share, jnp.where(here, fold, 0.0)]
+        return jnp.concatenate([piece.astype(LOW) for piece in pieces], axis=0)
+
+    scores = dot(windows[0], queries_ref[0], 1, 1)
     for g in range(kv):
-        values = jnp.concatenate([two_ref[kv + g], one_ref[kv + g], own_ref[kv + g]], axis=0).T
-        for piece in range(lanes // PIECE):
-            columns = slice(piece * PIECE, (piece + 1) * PIECE)
-            here = here_of(tokens, group, piece)
-            queries = queries_ref[g, columns, :]
-            fold = jnp.where(here, dot(own_ref[g], queries, 1, 1), dot(two_ref[g], queries, 1, 1))
-            fold = fold * scaling + bias_ref[0, :, columns]
-            mid = dot(one_ref[g], queries, 1, 1) * scaling + bias_ref[1, :, columns]
-            top = jnp.max(jnp.maximum(fold, mid), axis=0, keepdims=True)
-            fold = jnp.exp(fold - top)
-            mid = jnp.exp(mid - top)
-            share = 1.0 / jnp.sum(fold + mid, axis=0, keepdims=True)
-            fold = fold * share
-            low = jnp.concatenate(
-                [
-                    jnp.where(here, 0.0, fold).astype(LOW),
-                    (mid * share).astype(LOW),
-                    jnp.where(here, fold, 0.0).astype(LOW),
-                ],
-                axis=0,
-            )
-            low_ref[g, :, columns] = low
-            hidden_ref[g * dim : (g + 1) * dim, columns] = dot(values, low, 1, 0).astype(LOW)
+        ahead = dot(windows[g + 1], queries_ref[g + 1], 1, 1) if g + 1 < kv else None
+        low = weigh(scores)
+        low_ref[g] = low
+        hidden_ref[g * dim : (g + 1) * dim, :] = dot(windows[kv + g], low, 0, 0).astype(LOW)
+        scores = ahead
     hidden = hidden_ref[...]
     on_diff = dot(jnp.concatenate([diff_ref[g] for g in range(kv)], axis=1), hidden, 1, 0)
     lifted = own_terms(on_diff, owner, tenants, rank, group)
@@ -249,39 +242,33 @@
 
 def backward_kernel(
     queries_ref, gh_ref, two_ref, one_ref, own_ref, low_ref, dq_hbm, back_two_ref, back_one_ref, back_own_ref,
-    grad_ref, dq_ref, sems, *, kv, group, scaling,
+    dq_ref, sems, *, kv, group, scaling,
 ):
     tokens, dim = own_ref.shape[1:]
-    lanes = low_ref.shape[2]
-    rows = PIECE // group
     windows = [
         jnp.concatenate([two_ref[place], one_ref[place], own_ref[place]], axis=0) for place in range(2 * kv)
     ]
-    keys = [window.T for window in windows[:kv]]
     copies = []
-    for piece in range(lanes // PIECE):
-        columns = slice(piece * PIECE, (piece + 1) * PIECE)
-        here = slice(piece * rows, (piece + 1) * rows)
-        for g in range(kv):
-            weights = low_ref[g, :, columns].astype(WIDE)
-            weight_grad = dot(windows[kv + g], gh_ref[g, columns, :], 1, 1)
-            delta = jnp.sum(weights * weight_grad, axis=0, keepdims=True)
-            score_grad = (weights * (weight_grad - delta)).astype(LOW)
-            grad_ref[g, :, columns] = score_grad
-            query_grad = (dot(keys[g], score_grad, 1, 0) * scaling).T.reshape(rows, group, dim)
-            if g % 2 == 1:
-                both = jnp.concatenate([before, query_grad], axis=1).astype(LOW)
-                dq_ref[here, (g - 1) * group : (g + 1) * group, :] = both
-            before = query_grad
-        copies.append(pltpu.make_async_copy(dq_ref.at[here], dq_hbm.at[here], sems.at[piece]))
-        copies[-1].start()
+    weight_grad = dot(windows[kv], gh_ref[0], 1, 1)
     for g in range(kv):
-        key_grad = dot(grad_ref[g], queries_ref[g], 1, 0) * scaling
+        ahead = dot(windows[kv + g + 1], gh_ref[g + 1], 1, 1) if g + 1 < kv else None
+        weights = low_ref[g].astype(WIDE)
+        delta = jnp.sum(weights * weight_grad, axis=0, keepdims=True)
+        score_grad = (weights * (weight_grad - delta)).astype(LOW)
+        query_grad = (dot(windows[g], score_grad, 0, 0) * scaling).T.reshape(tokens, group, dim)
+        if g % 2 == 1:
+            heads = slice((g - 1) * group, (g + 1) * group)
+            dq_ref[:, heads, :] = jnp.concatenate([before, query_grad], axis=1).astype(LOW)
+            copies.append(pltpu.make_async_copy(dq_ref.at[:, heads], dq_hbm.at[:, heads], sems.at[g // 2]))
+            copies[-1].start()
+        before = query_grad
+        key_grad = dot(score_grad, queries_ref[g], 1, 0) * scaling
         value_grad = dot(low_ref[g], gh_ref[g], 1, 0)
         for place, grad in ((g, key_grad), (kv + g, value_grad)):
             back_two_ref[place] = grad[0:tokens].astype(LOW)
             back_one_ref[place] = grad[tokens : 2 * tokens].astype(LOW)
             back_own_ref[place] = grad[2 * tokens :]
+        weight_grad = ahead
     for copy in copies:
         copy.wait()
 
@@ -377,8 +364,7 @@
         [((tokens, heads, dim), LOW), (own.shape, LOW), (own.shape, LOW), (own.shape, WIDE)],
         4 * 2**30, 10 * 2**20,
         scratch=[
-            pltpu.VMEM((kv, 3 * tokens, lanes), LOW), pltpu.VMEM((tokens, heads, dim), LOW),
-            pltpu.SemaphoreType.DMA((lanes // PIECE,)),
+            pltpu.VMEM((tokens, heads, dim), LOW), pltpu.SemaphoreType.DMA((kv // 2,)),
         ],
         out_specs=[pl.BlockSpec(memory_space=pltpu.HBM), vmem, vmem, vmem], scaling=scaling, **sizes,
     )(queries, grad_hidden, two, one, own, low)

time: 49.1 us -> 42.6 us (0.87)
  Pallas kernels: 20.2 us -> 13.7 us
    pallas_call x6, Pallas kernels: 20.2 us -> 13.7 us  [run(): pl.pallas_call(lambda *refs: body(*refs, **fixed), out_shape=[jax.ShapeDt...]
  transfers between devices with their start and end apart: 11 -> 11, of which waited for: 7 -> 9; matrix products, arithmetic and copies ran while one was open for 0% -> 0% of each run, Pallas kernels for 23% -> 18%
where the time goes in v9:
time: 42.6 us; the launch traced here: 42.3 us
  Pallas kernels  13.7 us (32%)
  starting transfers between devices  13.1 us (31%)
  waiting for transfers between devices  9.94 us (23%)
  local copies, waits for them, and re-layouts  4.44 us (10%)
  between operations  0.78 us (2%)
    pallas_call x6, Pallas kernels, run(): pl.pallas_call(lambda *refs: body(*refs, **fixed), out_shape=[jax.ShapeDt...  13.7 us
    ppermute x9, waiting for transfers between devices, exchanged(): lax.ppermute(value, axes, [(int(source), int(target)) for source, target...  9.22 us
    ppermute x9, starting transfers between devices, exchanged(): lax.ppermute(value, axes, [(int(source), int(target)) for source, target...  8.34 us
    ppermute x2, starting transfers between devices, shifted(): lax.ppermute(value, axis, [(source, (source + steps) % count) for source...  4.78 us
    unnamed x18, local copies, waits for them, and re-layouts  3.4 us
    squeeze x1, local copies, waits for them, and re-layouts, on_device(): value_matrix[0]  1 us
  transfers between devices with their start and end apart: 11, of which 9 were waited for; matrix products, arithmetic and copies ran while one was open for 0% of the time, Pallas kernels for 18%

profile of v9, /device:TPU:0, one launch (start us, length us, event | category | flops | bytes accessed | tf_op | source)
XLA Modules:
  0.0 42.3 jit_solution(2563637788586652303)
XLA Ops:
  0.6 1.0 %copy_bitcast_fusion = (bf16[128,4,128]{2,0,1:T(8,128)(2,1)S(1)}, bf16[128,4,128]{2,0,1:T(8,128)(2,1)S(1)}) fusion(bf16[1,128,4,128]{3,2,1,0:T(4,128)(2,1)} %param.11, bf16[1,128,4,128]{3,2,1,0:T(4,128)(2,1)} %param.10), kind=kLoop, calls=%fused_computation.5 | loop fusion | bytes 524288 | tf_op jit(solution)/shard_map/squeeze | solution.py:337
  1.7 0.0 copy-start
  1.7 0.0 copy-start.1
  1.7 0.0 copy-start.2
  1.7 3.0 %collective-permute-start = (bf16[8,128,128]{2,1,0:T(8,128)(2,1)S(1)}, bf16[8,128,128]{2,1,0:T(8,128)(2,1)S(1)}, u32[]{:S(2)}, u32[]{:S(2)}) collective-permute-start(bf16[8,128,128]{2,1,0:T(8,128)(2,1)S(1)} %maximum_bitcast_fusion.refs_4_), channel_id=1, source_target_pairs={{0,2},{1,3},{2,4},{3,5},{4,6},{5,7},{6,0},{7,1},{8,10},{9,11},{10,... | collective-permute-start | bytes 786440 | tf_op jit(solution)/shard_map/ppermute | solution.py:19
  4.7 0.0 copy-start.4
  4.7 0.7 %copy-done.4 = s32[1,1024]{1,0:T(1,128)S(1)} copy-done((s32[1,1024]{1,0:T(1,128)S(1)}, s32[1,1024]{1,0:T(1,128)}, u32[]{:S(2)}) %copy-start.4) | copy-done | bytes 4120
  5.4 0.0 copy-start.5
  5.4 0.7 %copy-done.5 = s32[1,1024]{1,0:T(1,128)S(1)} copy-done((s32[1,1024]{1,0:T(1,128)S(1)}, s32[1,1024]{1,0:T(1,128)}, u32[]{:S(2)}) %copy-start.5) | copy-done | bytes 4120
  6.1 0.3 place_kernel.1
  6.4 0.0 copy-start.7
  6.4 1.0 %copy-done.7 = f32[2,128,1024]{2,1,0:T(8,128)} copy-done((f32[2,128,1024]{2,1,0:T(8,128)}, f32[2,128,1024]{2,1,0:T(8,128)S(1)}, u32[]{:S(2)}) %copy-start.7) | copy-done | bytes 1048600
  7.4 0.0 copy-done
  7.4 0.0 copy-done.1
  7.4 0.0 copy-done.2
  7.4 0.0 copy-start.3
  7.4 1.0 %copy-done.3 = bf16[16,4,32,128]{3,2,1,0:T(8,128)(2,1)S(1)} copy-done((bf16[16,4,32,128]{3,2,1,0:T(8,128)(2,1)S(1)}, bf16[16,4,32,128]{3,2,1,0:T(8,128)(2,1)}, u32[]{:S(2)}) %copy-start.3) | copy-done | bytes 524312
  8.5 0.0 copy-start.6
  8.5 0.0 copy-start.8
  8.5 2.8 %pull_kernel.1 = (bf16[4,1024,128]{2,1,0:T(8,128)(2,1)S(1)}, bf16[4,512,128]{2,1,0:T(8,128)(2,1)S(1)}, bf16[4,1024,128]{2,1,0:T(8,128)(2,1)S(1)}, bf16[4,1024,128]{2,1,0:T(8,128)(2,1)S(1)}, bf16[512,1024]{1,0:T(8,128)(2,1)S(1)}) custom-call(s32[8,1024]{1,0:T(8,128)S(1)} %get-tuple-element.35.refs_0_.refs_7_, bf16[128,32,128]{2,1,0:T(8,128)(2,1)S(1)} %bitcast.18, ...), custom_call_target="tpu_custom_call" | custom-call | flops 2147483648 | bytes 4194304 | tf_op jit(solution)/shard_map/pull_kernel/pallas_call | solution.py:321
  11.2 0.7 %collective-permute-done.refs_2_ = bf16[8,128,128]{2,1,0:T(8,128)(2,1)S(1)} collective-permute-done((bf16[8,128,128]{2,1,0:T(8,128)(2,1)S(1)}, bf16[8,128,128]{2,1,0:T(8,128)(2,1)S(1)}, u32[]{:S(2)}, u32[]{:S(2)}) %collective-permute-start) | collective-permute-done | bytes 262176 | tf_op jit(solution)/shard_map/ppermute | solution.py:19
  12.0 0.1 collective-permute-start.1
  12.1 1.5 %collective-permute-done.1.refs_3_ = bf16[8,128,128]{2,1,0:T(8,128)(2,1)S(1)} collective-permute-done((bf16[8,128,128]{2,1,0:T(8,128)(2,1)S(1)}, bf16[8,128,128]{2,1,0:T(8,128)(2,1)S(1)}, u32[]{:S(2)}, u32[]{:S(2)}) %collective-permute-start.1) | collective-permute-done | bytes 262176 | tf_op jit(solution)/shard_map/ppermute | solution.py:29
  13.6 0.0 copy-done.6
  13.6 0.0 copy-done.8
  13.6 4.4 %forward_kernel.1 = (bf16[4,384,1024]{2,1,0:T(8,128)(2,1)S(1)}, bf16[16,128,128]{2,1,0:T(8,128)(2,1)S(1)}, bf16[16,128,128]{2,1,0:T(8,128)(2,1)S(1)}) custom-call(f32[4,16]{1,0:T(4,128)S(1)} %bitcast.22, bf16[4,1024,128]{2,1,0:T(8,128)(2,1)S(1)} %get-tuple-element.36.refs_1_.refs_0_, bf16[8,128,128]{2,1,0:T(8,128)(2,1)S(1)} %collective-permute-done.refs_2_, ...), custom_call_target="tpu_custom_call" | custom-call | flops 4294967296 | bytes 10485760 | tf_op jit(solution)/shard_map/forward_kernel/pallas_call | solution.py:321
  18.0 0.2 collective-permute-start.2
  18.2 1.8 %collective-permute-done.2 = bf16[16,128,128]{2,1,0:T(8,128)(2,1)S(1)} collective-permute-done((bf16[16,128,128]{2,1,0:T(8,128)(2,1)S(1)}, bf16[16,128,128]{2,1,0:T(8,128)(2,1)S(1)}, u32[]{:S(2)}, u32[]{:S(2)}) %collective-permute-start.2) | collective-permute-done | bytes 524320 | tf_op jit(solution)/shard_map/ppermute | solution.py:29
  20.0 0.1 add_convert_fusion
  20.2 2.8 %collective-permute-start.6 = (bf16[4,128,128]{2,1,0:T(8,128)(2,1)S(1)}, bf16[4,128,128]{2,1,0:T(8,128)(2,1)S(1)}, u32[]{:S(2)}, u32[]{:S(2)}) collective-permute-start(bf16[4,128,128]{2,1,0:T(8,128)(2,1)S(1)} %get-tuple-element.65), channel_id=1, source_target_pairs={{0,12},{1,13},{2,14},{3,15},{4,8},{5,9},{6,10},{7,11},{8,4},{9,5},... | collective-permute-start | bytes 393224 | tf_op jit(solution)/shard_map/ppermute | solution.py:29
  23.0 0.5 %collective-permute-start.5 = (bf16[4,128,128]{2,1,0:T(8,128)(2,1)S(1)}, bf16[4,128,128]{2,1,0:T(8,128)(2,1)S(1)}, u32[]{:S(2)}, u32[]{:S(2)}) collective-permute-start(bf16[4,128,128]{2,1,0:T(8,128)(2,1)S(1)} %get-tuple-element.66), channel_id=1, source_target_pairs={{0,4},{1,5},{2,6},{3,7},{4,0},{5,1},{6,2},{7,3},{8,12},{9,13},{10,... | collective-permute-start | bytes 393224 | tf_op jit(solution)/shard_map/ppermute | solution.py:29
  23.5 0.3 collective-permute-start.4
  23.7 4.7 %backward_kernel.1 = (bf16[128,32,128]{2,1,0:T(8,128)(2,1)}, bf16[8,128,128]{2,1,0:T(8,128)(2,1)S(1)}, bf16[8,128,128]{2,1,0:T(8,128)(2,1)S(1)}, f32[8,128,128]{2,1,0:T(8,128)S(1)}) custom-call(bf16[4,1024,128]{2,1,0:T(8,128)(2,1)S(1)} %get-tuple-element.36.refs_1_.refs_0_, bf16[4,1024,128]{2,1,0:T(8,128)(2,1)S(1)} %get-tuple-element.37.refs_1_, ...), custom_call_target="tpu_custom_call" | custom-call | flops 4294967296 | bytes 10485760 | tf_op jit(solution)/shard_map/backward_kernel/pallas_call | solution.py:321
  28.4 0.1 collective-permute-start.3
  28.5 0.0 collective-permute-done.6
  28.5 1.1 %collective-permute-done.5 = bf16[4,128,128]{2,1,0:T(8,128)(2,1)S(1)} collective-permute-done((bf16[4,128,128]{2,1,0:T(8,128)(2,1)S(1)}, bf16[4,128,128]{2,1,0:T(8,128)(2,1)S(1)}, u32[]{:S(2)}, u32[]{:S(2)}) %collective-permute-start.5) | collective-permute-done | bytes 131104 | tf_op jit(solution)/shard_map/ppermute | solution.py:29
  29.6 0.2 collective-permute-done.4
  29.8 0.1 add_convert_fusion.2
  29.8 0.2 collective-permute-done.3.refs_1_
  30.0 0.1 add_convert_fusion.1
  30.1 1.8 %collective-permute-start.7 = (bf16[8,128,128]{2,1,0:T(8,128)(2,1)S(1)}, bf16[8,128,128]{2,1,0:T(8,128)(2,1)S(1)}, u32[]{:S(2)}, u32[]{:S(2)}) collective-permute-start(bf16[8,128,128]{2,1,0:T(8,128)(2,1)S(1)} %add_convert_fusion.1), channel_id=1, source_target_pairs={{0,6},{1,7},{2,0},{3,1},{4,2},{5,3},{6,4},{7,5},{8,14},{9,15},{10,... | collective-permute-start | bytes 786440 | tf_op jit(solution)/shard_map/ppermute | solution.py:19
  31.9 2.6 %collective-permute-start.10 = (bf16[1,128,128]{2,1,0:T(8,128)(2,1)S(1)}, bf16[1,128,128]{2,1,0:T(8,128)(2,1)S(1)}, u32[]{:S(2)}, u32[]{:S(2)}) collective-permute-start(bf16[1,128,128]{2,1,0:T(8,128)(2,1)S(1)} %get-tuple-element.68), channel_id=1, source_target_pairs={{0,18},{1,19},{2,16},{3,17},{4,22},{5,23},{6,20},{7,21},{8,26},{9,... | collective-permute-start | bytes 98312 | tf_op jit(solution)/shard_map/ppermute | solution.py:29
  34.5 1.6 %collective-permute-start.9 = (bf16[1,128,128]{2,1,0:T(8,128)(2,1)S(1)}, bf16[1,128,128]{2,1,0:T(8,128)(2,1)S(1)}, u32[]{:S(2)}, u32[]{:S(2)}) collective-permute-start(bf16[1,128,128]{2,1,0:T(8,128)(2,1)S(1)} %get-tuple-element.69), channel_id=1, source_target_pairs={{0,2},{1,3},{2,0},{3,1},{4,6},{5,7},{6,4},{7,5},{8,10},{9,11},{10,... | collective-permute-start | bytes 98312 | tf_op jit(solution)/shard_map/ppermute | solution.py:29
  36.1 0.3 collective-permute-start.8
  36.4 1.7 %collective-permute-done.10.refs_3_ = bf16[1,128,128]{2,1,0:T(8,128)(2,1)S(1)} collective-permute-done((bf16[1,128,128]{2,1,0:T(8,128)(2,1)S(1)}, bf16[1,128,128]{2,1,0:T(8,128)(2,1)S(1)}, u32[]{:S(2)}, u32[]{:S(2)}) %collective-permute-start.10) | collective-permute-done | bytes 32800 | tf_op jit(solution)/shard_map/ppermute | solution.py:29
  38.1 1.9 %collective-permute-done.9.refs_2_ = bf16[1,128,128]{2,1,0:T(8,128)(2,1)S(1)} collective-permute-done((bf16[1,128,128]{2,1,0:T(8,128)(2,1)S(1)}, bf16[1,128,128]{2,1,0:T(8,128)(2,1)S(1)}, u32[]{:S(2)}, u32[]{:S(2)}) %collective-permute-start.9) | collective-permute-done | bytes 32800 | tf_op jit(solution)/shard_map/ppermute | solution.py:29
  39.9 0.9 %collective-permute-done.8.refs_1_ = bf16[1,128,128]{2,1,0:T(8,128)(2,1)S(1)} collective-permute-done((bf16[1,128,128]{2,1,0:T(8,128)(2,1)S(1)}, bf16[1,128,128]{2,1,0:T(8,128)(2,1)S(1)}, u32[]{:S(2)}, u32[]{:S(2)}) %collective-permute-start.8) | collective-permute-done | bytes 32800 | tf_op jit(solution)/shard_map/ppermute | solution.py:29
  40.9 0.0 collective-permute-done.7.refs_2_
  40.9 0.7 %grads_kernel.1 = (f32[16,4,128]{2,1,0:T(4,128)}, f32[16,4,128]{2,1,0:T(4,128)}) custom-call(bf16[1,128,128]{2,1,0:T(8,128)(2,1)S(1)} %get-tuple-element.71.refs_0_, bf16[1,128,128]{2,1,0:T(8,128)(2,1)S(1)} %collective-permute-done.8.refs_1_, bf16[1,128,128]{2,1,0:T(8,128)(2,1)S(1)} %collective-permute-done.9.refs_2_, ...), custom_call_target="tpu_custom_call" | custom-call | flops 262144 | bytes 262144 | tf_op jit(solution)/shard_map/grads_kernel/pallas_call | solution.py:321
  41.5 0.8 %halo_kernel.1 = (bf16[512,128]{1,0:T(8,128)(2,1)}, bf16[512,128]{1,0:T(8,128)(2,1)}) custom-call(f32[8,128,128]{2,1,0:T(8,128)S(1)} %get-tuple-element.49.refs_0_, bf16[8,128,128]{2,1,0:T(8,128)(2,1)S(1)} %collective-permute-done.3.refs_1_, bf16[8,128,128]{2,1,0:T(8,128)(2,1)S(1)} %collective-permute-done.7.refs_2_), custom_call_target="tpu_custom_call" | custom-call | flops 1048576 | bytes 1048576 | tf_op jit(solution)/shard_map/halo_kernel/pallas_call | solution.py:321
  (4 shorter events, 0.1 us)
Async XLA Ops:
  1.7 5.7 %copy-start = (bf16[1,128,32,128]{3,2,1,0:T(8,128)(2,1)S(1)}, bf16[1,128,32,128]{3,2,1,0:T(8,128)(2,1)}, u32[]{:S(2)}) copy-start(bf16[1,128,32,128]{3,2,1,0:T(8,128)(2,1)} %param.12) | copy-start | bytes 3145732
  1.7 5.7 %copy-start.1 = (bf16[1,128,32,128]{3,2,1,0:T(8,128)(2,1)S(1)}, bf16[1,128,32,128]{3,2,1,0:T(8,128)(2,1)}, u32[]{:S(2)}) copy-start(bf16[1,128,32,128]{3,2,1,0:T(8,128)(2,1)} %param.9) | copy-start | bytes 3145732
  1.7 5.7 %copy-start.2 = (bf16[16,4,32,128]{3,2,1,0:T(8,128)(2,1)S(1)}, bf16[16,4,32,128]{3,2,1,0:T(8,128)(2,1)}, u32[]{:S(2)}) copy-start(bf16[16,4,32,128]{3,2,1,0:T(8,128)(2,1)} %param.13) | copy-start | bytes 1572868
  1.7 10.3 %collective-permute-start = (bf16[8,128,128]{2,1,0:T(8,128)(2,1)S(1)}, bf16[8,128,128]{2,1,0:T(8,128)(2,1)S(1)}, u32[]{:S(2)}, u32[]{:S(2)}) collective-permute-start(bf16[8,128,128]{2,1,0:T(8,128)(2,1)S(1)} %maximum_bitcast_fusion.refs_4_), channel_id=1, source_target_pairs={{0,2},{1,3},{2,4},{3,5},{4,6},{5,7},{6,0},{7,1},{8,10},{9,11},{10,... | collective-permute-start | bytes 786440 | tf_op jit(solution)/shard_map/ppermute | solution.py:19
  4.7 0.7 %copy-start.4 = (s32[1,1024]{1,0:T(1,128)S(1)}, s32[1,1024]{1,0:T(1,128)}, u32[]{:S(2)}) copy-start(s32[1,1024]{1,0:T(1,128)} %refs_0_.1) | copy-start | bytes 12292
  5.4 0.7 %copy-start.5 = (s32[1,1024]{1,0:T(1,128)S(1)}, s32[1,1024]{1,0:T(1,128)}, u32[]{:S(2)}) copy-start(s32[1,1024]{1,0:T(1,128)} %refs_1_.1) | copy-start | bytes 12292
  6.4 1.0 %copy-start.7 = (f32[2,128,1024]{2,1,0:T(8,128)}, f32[2,128,1024]{2,1,0:T(8,128)S(1)}, u32[]{:S(2)}) copy-start(f32[2,128,1024]{2,1,0:T(8,128)S(1)} %get-tuple-element.43.refs_9_) | copy-start | bytes 3145732
  7.4 1.0 %copy-start.3 = (bf16[16,4,32,128]{3,2,1,0:T(8,128)(2,1)S(1)}, bf16[16,4,32,128]{3,2,1,0:T(8,128)(2,1)}, u32[]{:S(2)}) copy-start(bf16[16,4,32,128]{3,2,1,0:T(8,128)(2,1)} %param.14) | copy-start | bytes 1572868
  8.5 5.2 %copy-start.6 = (f32[16,4]{0,1:T(4,128)S(1)}, f32[16,4]{0,1:T(4,128)}, u32[]{:S(2)}) copy-start(f32[16,4]{0,1:T(4,128)} %param.15) | copy-start | bytes 772
  8.5 5.2 %copy-start.8 = (f32[2,128,1024]{2,1,0:T(8,128)S(1)}, f32[2,128,1024]{2,1,0:T(8,128)}, u32[]{:S(2)}) copy-start(f32[2,128,1024]{2,1,0:T(8,128)} %copy-done.7) | copy-start | bytes 3145732
  12.0 1.6 %collective-permute-start.1 = (bf16[8,128,128]{2,1,0:T(8,128)(2,1)S(1)}, bf16[8,128,128]{2,1,0:T(8,128)(2,1)S(1)}, u32[]{:S(2)}, u32[]{:S(2)}) collective-permute-start(bf16[8,128,128]{2,1,0:T(8,128)(2,1)S(1)} %broadcast_select_fusion), channel_id=1, source_target_pairs={{0,1},{1,0},{2,3},{3,2},{4,5},{5,4},{6,7},{7,6},{8,9},{9,8},{10,11... | collective-permute-start | bytes 786440 | tf_op jit(solution)/shard_map/ppermute | solution.py:29
  18.0 2.0 %collective-permute-start.2 = (bf16[16,128,128]{2,1,0:T(8,128)(2,1)S(1)}, bf16[16,128,128]{2,1,0:T(8,128)(2,1)S(1)}, u32[]{:S(2)}, u32[]{:S(2)}) collective-permute-start(bf16[16,128,128]{2,1,0:T(8,128)(2,1)S(1)} %get-tuple-element.46), channel_id=1, source_target_pairs={{0,1},{1,0},{2,3},{3,2},{4,5},{5,4},{6,7},{7,6},{8,9},{9,8},{10,11... | collective-permute-start | bytes 1572872 | tf_op jit(solution)/shard_map/ppermute | solution.py:29
  20.2 8.3 %collective-permute-start.6 = (bf16[4,128,128]{2,1,0:T(8,128)(2,1)S(1)}, bf16[4,128,128]{2,1,0:T(8,128)(2,1)S(1)}, u32[]{:S(2)}, u32[]{:S(2)}) collective-permute-start(bf16[4,128,128]{2,1,0:T(8,128)(2,1)S(1)} %get-tuple-element.65), channel_id=1, source_target_pairs={{0,12},{1,13},{2,14},{3,15},{4,8},{5,9},{6,10},{7,11},{8,4},{9,5},... | collective-permute-start | bytes 393224 | tf_op jit(solution)/shard_map/ppermute | solution.py:29
  23.0 6.6 %collective-permute-start.5 = (bf16[4,128,128]{2,1,0:T(8,128)(2,1)S(1)}, bf16[4,128,128]{2,1,0:T(8,128)(2,1)S(1)}, u32[]{:S(2)}, u32[]{:S(2)}) collective-permute-start(bf16[4,128,128]{2,1,0:T(8,128)(2,1)S(1)} %get-tuple-element.66), channel_id=1, source_target_pairs={{0,4},{1,5},{2,6},{3,7},{4,0},{5,1},{6,2},{7,3},{8,12},{9,13},{10,... | collective-permute-start | bytes 393224 | tf_op jit(solution)/shard_map/ppermute | solution.py:29
  23.5 6.3 %collective-permute-start.4 = (bf16[4,128,128]{2,1,0:T(8,128)(2,1)S(1)}, bf16[4,128,128]{2,1,0:T(8,128)(2,1)S(1)}, u32[]{:S(2)}, u32[]{:S(2)}) collective-permute-start(bf16[4,128,128]{2,1,0:T(8,128)(2,1)S(1)} %get-tuple-element.67), channel_id=1, source_target_pairs={{0,8},{8,0},{16,24},{24,16},{1,9},{9,1},{17,25},{25,17},{2,10},{10... | collective-permute-start | bytes 393224 | tf_op jit(solution)/shard_map/ppermute | solution.py:29
  28.4 1.6 %collective-permute-start.3 = (bf16[8,128,128]{2,1,0:T(8,128)(2,1)S(1)}, bf16[8,128,128]{2,1,0:T(8,128)(2,1)S(1)}, u32[]{:S(2)}, u32[]{:S(2)}) collective-permute-start(bf16[8,128,128]{2,1,0:T(8,128)(2,1)S(1)} %get-tuple-element.50), channel_id=1, source_target_pairs={{0,1},{1,0},{2,3},{3,2},{4,5},{5,4},{6,7},{7,6},{8,9},{9,8},{10,11... | collective-permute-start | bytes 786440 | tf_op jit(solution)/shard_map/ppermute | solution.py:29
  30.1 10.7 %collective-permute-start.7 = (bf16[8,128,128]{2,1,0:T(8,128)(2,1)S(1)}, bf16[8,128,128]{2,1,0:T(8,128)(2,1)S(1)}, u32[]{:S(2)}, u32[]{:S(2)}) collective-permute-start(bf16[8,128,128]{2,1,0:T(8,128)(2,1)S(1)} %add_convert_fusion.1), channel_id=1, source_target_pairs={{0,6},{1,7},{2,0},{3,1},{4,2},{5,3},{6,4},{7,5},{8,14},{9,15},{10,... | collective-permute-start | bytes 786440 | tf_op jit(solution)/shard_map/ppermute | solution.py:19
  31.9 6.1 %collective-permute-start.10 = (bf16[1,128,128]{2,1,0:T(8,128)(2,1)S(1)}, bf16[1,128,128]{2,1,0:T(8,128)(2,1)S(1)}, u32[]{:S(2)}, u32[]{:S(2)}) collective-permute-start(bf16[1,128,128]{2,1,0:T(8,128)(2,1)S(1)} %get-tuple-element.68), channel_id=1, source_target_pairs={{0,18},{1,19},{2,16},{3,17},{4,22},{5,23},{6,20},{7,21},{8,26},{9,... | collective-permute-start | bytes 98312 | tf_op jit(solution)/shard_map/ppermute | solution.py:29
  34.5 5.4 %collective-permute-start.9 = (bf16[1,128,128]{2,1,0:T(8,128)(2,1)S(1)}, bf16[1,128,128]{2,1,0:T(8,128)(2,1)S(1)}, u32[]{:S(2)}, u32[]{:S(2)}) collective-permute-start(bf16[1,128,128]{2,1,0:T(8,128)(2,1)S(1)} %get-tuple-element.69), channel_id=1, source_target_pairs={{0,2},{1,3},{2,0},{3,1},{4,6},{5,7},{6,4},{7,5},{8,10},{9,11},{10,... | collective-permute-start | bytes 98312 | tf_op jit(solution)/shard_map/ppermute | solution.py:29
  36.1 4.8 %collective-permute-start.8 = (bf16[1,128,128]{2,1,0:T(8,128)(2,1)S(1)}, bf16[1,128,128]{2,1,0:T(8,128)(2,1)S(1)}, u32[]{:S(2)}, u32[]{:S(2)}) collective-permute-start(bf16[1,128,128]{2,1,0:T(8,128)(2,1)S(1)} %get-tuple-element.70), channel_id=1, source_target_pairs={{0,16},{8,24},{16,0},{24,8},{1,17},{9,25},{17,1},{25,9},{2,18},{10... | collective-permute-start | bytes 98312 | tf_op jit(solution)/shard_map/ppermute | solution.py:29

commit v10 on v9

--- a/solution.py
+++ b/solution.py
@@ -31,11 +31,9 @@
 
 def reduce_groups():
     ctx, rep = lax.axis_size("ctx"), lax.axis_size("rep")
-    over_ctx = [{"ctx": 1 << at} for at in range(ctx.bit_length() - 2, 0, -1)]
-    over_rep = [{"rep": 1 << at} for at in range(rep.bit_length() - 1)]
-    return [
-        [pair for pair in pairs if pair] for pairs in itertools.zip_longest(over_ctx, over_rep)
-    ]
+    bits = [{"ctx": 1 << at} for at in range(ctx.bit_length() - 2, 0, -1)]
+    bits += [{"rep": 1 << at} for at in range(rep.bit_length() - 1)]
+    return [bits[at : at + 2] for at in range(0, len(bits), 2)]
 
 
 def reduce_place(index):
@@ -54,7 +52,7 @@
         bits = {}
         for at, pair in enumerate(reversed(group)):
             if (j >> at) & 1:
-                bits.update(pair)
+                bits.update({axis: bits.get(axis, 0) | bit for axis, bit in pair.items()})
         others.append(exchanged(part[j * size : (j + 1) * size], bits))
     if beside is not None:
         others = lax.optimization_barrier((others, beside))[0]
@@ -273,18 +271,18 @@
         copy.wait()
 
 
-def grads_kernel(part_ref, *refs, owned):
+def finish_kernel(
+    own_ref, mate_ref, two_ref, part_ref, *refs, kv, owned,
+):
+    *other_refs, keys_ref, values_ref, rot_ref, proj_ref, wide_ref = refs
     total = part_ref[0].astype(WIDE)
-    for other_ref in refs[:-2]:
+    for other_ref in other_refs:
         total = total + other_ref[0].astype(WIDE)
-    size = refs[-1].shape[0]
+    size = rot_ref.shape[0]
     for place in range(owned):
-        for at in range(2):
+        for at, out in enumerate((rot_ref, proj_ref)):
             row = (2 * place + at) * size
-            refs[at - 2][:, place, :] = total[row : row + size]
-
-
-def halo_kernel(own_ref, mate_ref, two_ref, keys_ref, values_ref, wide_ref, *, kv):
+            out[:, place, :] = total[row : row + size]
     tokens = own_ref.shape[1]
     even = (lax.axis_index("ctx") % 2 == 0).astype(WIDE)
     for at, out in enumerate((keys_ref, values_ref)):
@@ -383,14 +381,11 @@
         if at < len(groups) - 1:
             part = part.astype(WIDE) + sum(other.astype(WIDE) for other in others)
             part = part.astype(LOW)
-    grads = call(
-        grads_kernel, [((span // rep, here, dim), WIDE)] * 2, 2**18, 2**18, owned=here,
-    )(part, *others)
+    d_keys, d_values, *grads = call(
+        finish_kernel, [((tokens * kv, dim), LOW)] * 2 + [((span // rep, here, dim), WIDE)] * 2, 2**20, 2**20,
+        scratch=[pltpu.VMEM((2, tokens * kv, dim), WIDE)], kv=kv, owned=here,
+    )(back_own, from_mate, from_two, part, *others)
     grads = [grad.reshape(tenants // rep, rank, here, dim) for grad in grads]
-    d_keys, d_values = call(
-        halo_kernel, [((tokens * kv, dim), LOW)] * 2, 2**20, 2**20,
-        scratch=[pltpu.VMEM((2, tokens * kv, dim), WIDE)], kv=kv,
-    )(back_own, from_mate, from_two)
     d_keys, d_values = (grad.reshape(key_rows.shape) for grad in (d_keys, d_values))
     return (d_queries[None], d_keys, d_values, grads[0], grads[1])
 

time: 42.6 us -> 41.7 us (0.979)
  Pallas kernels: 13.7 us -> 13.1 us
    pallas_call x6 -> x5, Pallas kernels: 13.7 us -> 13.1 us  [run(): pl.pallas_call(lambda *refs: body(*refs, **fixed), out_shape=[jax.ShapeDt...]
  transfers between devices with their start and end apart: 11 -> 11, of which waited for: 9 -> 9; matrix products, arithmetic and copies ran while one was open for 0% -> 0% of each run, Pallas kernels for 18% -> 19%
where the time goes in v10:
time: 41.7 us; the launch traced here: 41.4 us
  starting transfers between devices  13.1 us (31%)
  Pallas kernels  13.1 us (31%)
  waiting for transfers between devices  9.63 us (23%)
  local copies, waits for them, and re-layouts  4.44 us (11%)
  between operations  0.78 us (2%)
    pallas_call x5, Pallas kernels, run(): pl.pallas_call(lambda *refs: body(*refs, **fixed), out_shape=[jax.ShapeDt...  13.1 us
    ppermute x9, waiting for transfers between devices, exchanged(): lax.ppermute(value, axes, [(int(source), int(target)) for source, target...  8.91 us
    ppermute x9, starting transfers between devices, exchanged(): lax.ppermute(value, axes, [(int(source), int(target)) for source, target...  8.34 us
    ppermute x2, starting transfers between devices, shifted(): lax.ppermute(value, axis, [(source, (source + steps) % count) for source...  4.78 us
    unnamed x18, local copies, waits for them, and re-layouts  3.4 us
    squeeze x1, local copies, waits for them, and re-layouts, on_device(): value_matrix[0]  1 us
  transfers between devices with their start and end apart: 11, of which 9 were waited for; matrix products, arithmetic and copies ran while one was open for 0% of the time, Pallas kernels for 19%

profile of v10, /device:TPU:0, one launch (start us, length us, event | category | flops | bytes accessed | tf_op | source)
XLA Modules:
  0.0 41.4 jit_solution(9667469865589222594)
XLA Ops:
  0.6 1.0 %copy_bitcast_fusion = (bf16[128,4,128]{2,0,1:T(8,128)(2,1)S(1)}, bf16[128,4,128]{2,0,1:T(8,128)(2,1)S(1)}) fusion(bf16[1,128,4,128]{3,2,1,0:T(4,128)(2,1)} %param.11, bf16[1,128,4,128]{3,2,1,0:T(4,128)(2,1)} %param.10), kind=kLoop, calls=%fused_computation.5 | loop fusion | bytes 524288 | tf_op jit(solution)/shard_map/squeeze | solution.py:335
  1.7 0.0 copy-start
  1.7 0.0 copy-start.1
  1.7 0.0 copy-start.2
  1.7 3.0 %collective-permute-start = (bf16[8,128,128]{2,1,0:T(8,128)(2,1)S(1)}, bf16[8,128,128]{2,1,0:T(8,128)(2,1)S(1)}, u32[]{:S(2)}, u32[]{:S(2)}) collective-permute-start(bf16[8,128,128]{2,1,0:T(8,128)(2,1)S(1)} %maximum_bitcast_fusion.refs_4_), channel_id=1, source_target_pairs={{0,2},{1,3},{2,4},{3,5},{4,6},{5,7},{6,0},{7,1},{8,10},{9,11},{10,... | collective-permute-start | bytes 786440 | tf_op jit(solution)/shard_map/ppermute | solution.py:19
  4.7 0.0 copy-start.4
  4.7 0.7 %copy-done.4 = s32[1,1024]{1,0:T(1,128)S(1)} copy-done((s32[1,1024]{1,0:T(1,128)S(1)}, s32[1,1024]{1,0:T(1,128)}, u32[]{:S(2)}) %copy-start.4) | copy-done | bytes 4120
  5.4 0.0 copy-start.5
  5.4 0.7 %copy-done.5 = s32[1,1024]{1,0:T(1,128)S(1)} copy-done((s32[1,1024]{1,0:T(1,128)S(1)}, s32[1,1024]{1,0:T(1,128)}, u32[]{:S(2)}) %copy-start.5) | copy-done | bytes 4120
  6.1 0.3 place_kernel.1
  6.4 0.0 copy-start.7
  6.4 1.0 %copy-done.7 = f32[2,128,1024]{2,1,0:T(8,128)} copy-done((f32[2,128,1024]{2,1,0:T(8,128)}, f32[2,128,1024]{2,1,0:T(8,128)S(1)}, u32[]{:S(2)}) %copy-start.7) | copy-done | bytes 1048600
  7.4 0.0 copy-done
  7.4 0.0 copy-done.1
  7.4 0.0 copy-done.2
  7.4 0.0 copy-start.3
  7.4 1.0 %copy-done.3 = bf16[16,4,32,128]{3,2,1,0:T(8,128)(2,1)S(1)} copy-done((bf16[16,4,32,128]{3,2,1,0:T(8,128)(2,1)S(1)}, bf16[16,4,32,128]{3,2,1,0:T(8,128)(2,1)}, u32[]{:S(2)}) %copy-start.3) | copy-done | bytes 524312
  8.5 0.0 copy-start.6
  8.5 0.0 copy-start.8
  8.5 2.8 %pull_kernel.1 = (bf16[4,1024,128]{2,1,0:T(8,128)(2,1)S(1)}, bf16[4,512,128]{2,1,0:T(8,128)(2,1)S(1)}, bf16[4,1024,128]{2,1,0:T(8,128)(2,1)S(1)}, bf16[4,1024,128]{2,1,0:T(8,128)(2,1)S(1)}, bf16[512,1024]{1,0:T(8,128)(2,1)S(1)}) custom-call(s32[8,1024]{1,0:T(8,128)S(1)} %get-tuple-element.35.refs_0_.refs_7_, bf16[128,32,128]{2,1,0:T(8,128)(2,1)S(1)} %bitcast.18, ...), custom_call_target="tpu_custom_call" | custom-call | flops 2147483648 | bytes 4194304 | tf_op jit(solution)/shard_map/pull_kernel/pallas_call | solution.py:319
  11.2 0.7 %collective-permute-done.refs_2_ = bf16[8,128,128]{2,1,0:T(8,128)(2,1)S(1)} collective-permute-done((bf16[8,128,128]{2,1,0:T(8,128)(2,1)S(1)}, bf16[8,128,128]{2,1,0:T(8,128)(2,1)S(1)}, u32[]{:S(2)}, u32[]{:S(2)}) %collective-permute-start) | collective-permute-done | bytes 262176 | tf_op jit(solution)/shard_map/ppermute | solution.py:19
  12.0 0.1 collective-permute-start.1
  12.1 1.5 %collective-permute-done.1.refs_3_ = bf16[8,128,128]{2,1,0:T(8,128)(2,1)S(1)} collective-permute-done((bf16[8,128,128]{2,1,0:T(8,128)(2,1)S(1)}, bf16[8,128,128]{2,1,0:T(8,128)(2,1)S(1)}, u32[]{:S(2)}, u32[]{:S(2)}) %collective-permute-start.1) | collective-permute-done | bytes 262176 | tf_op jit(solution)/shard_map/ppermute | solution.py:29
  13.6 0.0 copy-done.6
  13.6 0.0 copy-done.8
  13.6 4.4 %forward_kernel.1 = (bf16[4,384,1024]{2,1,0:T(8,128)(2,1)S(1)}, bf16[16,128,128]{2,1,0:T(8,128)(2,1)S(1)}, bf16[16,128,128]{2,1,0:T(8,128)(2,1)S(1)}) custom-call(f32[4,16]{1,0:T(4,128)S(1)} %bitcast.22, bf16[4,1024,128]{2,1,0:T(8,128)(2,1)S(1)} %get-tuple-element.36.refs_1_.refs_0_, bf16[8,128,128]{2,1,0:T(8,128)(2,1)S(1)} %collective-permute-done.refs_2_, ...), custom_call_target="tpu_custom_call" | custom-call | flops 4294967296 | bytes 10485760 | tf_op jit(solution)/shard_map/forward_kernel/pallas_call | solution.py:319
  18.0 0.2 collective-permute-start.2
  18.2 1.8 %collective-permute-done.2 = bf16[16,128,128]{2,1,0:T(8,128)(2,1)S(1)} collective-permute-done((bf16[16,128,128]{2,1,0:T(8,128)(2,1)S(1)}, bf16[16,128,128]{2,1,0:T(8,128)(2,1)S(1)}, u32[]{:S(2)}, u32[]{:S(2)}) %collective-permute-start.2) | collective-permute-done | bytes 524320 | tf_op jit(solution)/shard_map/ppermute | solution.py:29
  20.0 0.1 add_convert_fusion
  20.2 1.8 %collective-permute-start.6 = (bf16[4,128,128]{2,1,0:T(8,128)(2,1)S(1)}, bf16[4,128,128]{2,1,0:T(8,128)(2,1)S(1)}, u32[]{:S(2)}, u32[]{:S(2)}) collective-permute-start(bf16[4,128,128]{2,1,0:T(8,128)(2,1)S(1)} %get-tuple-element.65), channel_id=1, source_target_pairs={{0,6},{1,7},{2,4},{3,5},{4,2},{5,3},{6,0},{7,1},{8,14},{9,15},{10,... | collective-permute-start | bytes 393224 | tf_op jit(solution)/shard_map/ppermute | solution.py:29
  22.0 0.5 %collective-permute-start.5 = (bf16[4,128,128]{2,1,0:T(8,128)(2,1)S(1)}, bf16[4,128,128]{2,1,0:T(8,128)(2,1)S(1)}, u32[]{:S(2)}, u32[]{:S(2)}) collective-permute-start(bf16[4,128,128]{2,1,0:T(8,128)(2,1)S(1)} %get-tuple-element.66), channel_id=1, source_target_pairs={{0,4},{1,5},{2,6},{3,7},{4,0},{5,1},{6,2},{7,3},{8,12},{9,13},{10,... | collective-permute-start | bytes 393224 | tf_op jit(solution)/shard_map/ppermute | solution.py:29
  22.5 1.2 %collective-permute-start.4 = (bf16[4,128,128]{2,1,0:T(8,128)(2,1)S(1)}, bf16[4,128,128]{2,1,0:T(8,128)(2,1)S(1)}, u32[]{:S(2)}, u32[]{:S(2)}) collective-permute-start(bf16[4,128,128]{2,1,0:T(8,128)(2,1)S(1)} %get-tuple-element.67), channel_id=1, source_target_pairs={{0,2},{1,3},{2,0},{3,1},{4,6},{5,7},{6,4},{7,5},{8,10},{9,11},{10,... | collective-permute-start | bytes 393224 | tf_op jit(solution)/shard_map/ppermute | solution.py:29
  23.7 4.7 %backward_kernel.1 = (bf16[128,32,128]{2,1,0:T(8,128)(2,1)}, bf16[8,128,128]{2,1,0:T(8,128)(2,1)S(1)}, bf16[8,128,128]{2,1,0:T(8,128)(2,1)S(1)}, f32[8,128,128]{2,1,0:T(8,128)S(1)}) custom-call(bf16[4,1024,128]{2,1,0:T(8,128)(2,1)S(1)} %get-tuple-element.36.refs_1_.refs_0_, bf16[4,1024,128]{2,1,0:T(8,128)(2,1)S(1)} %get-tuple-element.37.refs_1_, ...), custom_call_target="tpu_custom_call" | custom-call | flops 4294967296 | bytes 10485760 | tf_op jit(solution)/shard_map/backward_kernel/pallas_call | solution.py:319
  28.4 0.1 collective-permute-start.3
  28.5 0.0 collective-permute-done.6
  28.5 1.0 %collective-permute-done.5 = bf16[4,128,128]{2,1,0:T(8,128)(2,1)S(1)} collective-permute-done((bf16[4,128,128]{2,1,0:T(8,128)(2,1)S(1)}, bf16[4,128,128]{2,1,0:T(8,128)(2,1)S(1)}, u32[]{:S(2)}, u32[]{:S(2)}) %collective-permute-start.5) | collective-permute-done | bytes 131104 | tf_op jit(solution)/shard_map/ppermute | solution.py:29
  29.5 0.3 collective-permute-done.4
  29.8 0.1 add_convert_fusion.2
  29.9 0.2 collective-permute-done.3.refs_1_
  30.0 0.1 add_convert_fusion.1
  30.1 1.8 %collective-permute-start.7 = (bf16[8,128,128]{2,1,0:T(8,128)(2,1)S(1)}, bf16[8,128,128]{2,1,0:T(8,128)(2,1)S(1)}, u32[]{:S(2)}, u32[]{:S(2)}) collective-permute-start(bf16[8,128,128]{2,1,0:T(8,128)(2,1)S(1)} %add_convert_fusion.1), channel_id=1, source_target_pairs={{0,6},{1,7},{2,0},{3,1},{4,2},{5,3},{6,4},{7,5},{8,14},{9,15},{10,... | collective-permute-start | bytes 786440 | tf_op jit(solution)/shard_map/ppermute | solution.py:19
  31.9 3.7 %collective-permute-start.10 = (bf16[1,128,128]{2,1,0:T(8,128)(2,1)S(1)}, bf16[1,128,128]{2,1,0:T(8,128)(2,1)S(1)}, u32[]{:S(2)}, u32[]{:S(2)}) collective-permute-start(bf16[1,128,128]{2,1,0:T(8,128)(2,1)S(1)} %get-tuple-element.68), channel_id=1, source_target_pairs={{0,24},{8,16},{16,8},{24,0},{1,25},{9,17},{17,9},{25,1},{2,26},{10... | collective-permute-start | bytes 98312 | tf_op jit(solution)/shard_map/ppermute | solution.py:29
  35.6 0.0 collective-permute-start.9
  35.6 0.8 %collective-permute-start.8 = (bf16[1,128,128]{2,1,0:T(8,128)(2,1)S(1)}, bf16[1,128,128]{2,1,0:T(8,128)(2,1)S(1)}, u32[]{:S(2)}, u32[]{:S(2)}) collective-permute-start(bf16[1,128,128]{2,1,0:T(8,128)(2,1)S(1)} %get-tuple-element.70), channel_id=1, source_target_pairs={{0,16},{8,24},{16,0},{24,8},{1,17},{9,25},{17,1},{25,9},{2,18},{10... | collective-permute-start | bytes 98312 | tf_op jit(solution)/shard_map/ppermute | solution.py:29
  36.4 1.3 %collective-permute-done.10.refs_6_ = bf16[1,128,128]{2,1,0:T(8,128)(2,1)S(1)} collective-permute-done((bf16[1,128,128]{2,1,0:T(8,128)(2,1)S(1)}, bf16[1,128,128]{2,1,0:T(8,128)(2,1)S(1)}, u32[]{:S(2)}, u32[]{:S(2)}) %collective-permute-start.10) | collective-permute-done | bytes 32800 | tf_op jit(solution)/shard_map/ppermute | solution.py:29
  37.7 1.8 %collective-permute-done.9.refs_5_ = bf16[1,128,128]{2,1,0:T(8,128)(2,1)S(1)} collective-permute-done((bf16[1,128,128]{2,1,0:T(8,128)(2,1)S(1)}, bf16[1,128,128]{2,1,0:T(8,128)(2,1)S(1)}, u32[]{:S(2)}, u32[]{:S(2)}) %collective-permute-start.9) | collective-permute-done | bytes 32800 | tf_op jit(solution)/shard_map/ppermute | solution.py:29
  39.5 1.0 %collective-permute-done.8.refs_4_ = bf16[1,128,128]{2,1,0:T(8,128)(2,1)S(1)} collective-permute-done((bf16[1,128,128]{2,1,0:T(8,128)(2,1)S(1)}, bf16[1,128,128]{2,1,0:T(8,128)(2,1)S(1)}, u32[]{:S(2)}, u32[]{:S(2)}) %collective-permute-start.8) | collective-permute-done | bytes 32800 | tf_op jit(solution)/shard_map/ppermute | solution.py:29
  40.6 0.0 collective-permute-done.7.refs_2_
  40.6 0.8 %finish_kernel.1 = (bf16[512,128]{1,0:T(8,128)(2,1)}, bf16[512,128]{1,0:T(8,128)(2,1)}, f32[16,4,128]{2,1,0:T(4,128)}, f32[16,4,128]{2,1,0:T(4,128)}) custom-call(f32[8,128,128]{2,1,0:T(8,128)S(1)} %get-tuple-element.49.refs_0_, bf16[8,128,128]{2,1,0:T(8,128)(2,1)S(1)} %collective-permute-done.3.refs_1_, ...), custom_call_target="tpu_custom_call" | custom-call | flops 1048576 | bytes 1048576 | tf_op jit(solution)/shard_map/finish_kernel/pallas_call | solution.py:319
  (4 shorter events, 0.1 us)
Async XLA Ops:
  1.7 5.7 %copy-start = (bf16[1,128,32,128]{3,2,1,0:T(8,128)(2,1)S(1)}, bf16[1,128,32,128]{3,2,1,0:T(8,128)(2,1)}, u32[]{:S(2)}) copy-start(bf16[1,128,32,128]{3,2,1,0:T(8,128)(2,1)} %param.12) | copy-start | bytes 3145732
  1.7 5.7 %copy-start.1 = (bf16[1,128,32,128]{3,2,1,0:T(8,128)(2,1)S(1)}, bf16[1,128,32,128]{3,2,1,0:T(8,128)(2,1)}, u32[]{:S(2)}) copy-start(bf16[1,128,32,128]{3,2,1,0:T(8,128)(2,1)} %param.9) | copy-start | bytes 3145732
  1.7 5.7 %copy-start.2 = (bf16[16,4,32,128]{3,2,1,0:T(8,128)(2,1)S(1)}, bf16[16,4,32,128]{3,2,1,0:T(8,128)(2,1)}, u32[]{:S(2)}) copy-start(bf16[16,4,32,128]{3,2,1,0:T(8,128)(2,1)} %param.13) | copy-start | bytes 1572868
  1.7 10.3 %collective-permute-start = (bf16[8,128,128]{2,1,0:T(8,128)(2,1)S(1)}, bf16[8,128,128]{2,1,0:T(8,128)(2,1)S(1)}, u32[]{:S(2)}, u32[]{:S(2)}) collective-permute-start(bf16[8,128,128]{2,1,0:T(8,128)(2,1)S(1)} %maximum_bitcast_fusion.refs_4_), channel_id=1, source_target_pairs={{0,2},{1,3},{2,4},{3,5},{4,6},{5,7},{6,0},{7,1},{8,10},{9,11},{10,... | collective-permute-start | bytes 786440 | tf_op jit(solution)/shard_map/ppermute | solution.py:19
  4.7 0.7 %copy-start.4 = (s32[1,1024]{1,0:T(1,128)S(1)}, s32[1,1024]{1,0:T(1,128)}, u32[]{:S(2)}) copy-start(s32[1,1024]{1,0:T(1,128)} %refs_0_.1) | copy-start | bytes 12292
  5.4 0.7 %copy-start.5 = (s32[1,1024]{1,0:T(1,128)S(1)}, s32[1,1024]{1,0:T(1,128)}, u32[]{:S(2)}) copy-start(s32[1,1024]{1,0:T(1,128)} %refs_1_.1) | copy-start | bytes 12292
  6.4 1.0 %copy-start.7 = (f32[2,128,1024]{2,1,0:T(8,128)}, f32[2,128,1024]{2,1,0:T(8,128)S(1)}, u32[]{:S(2)}) copy-start(f32[2,128,1024]{2,1,0:T(8,128)S(1)} %get-tuple-element.43.refs_9_) | copy-start | bytes 3145732
  7.4 1.0 %copy-start.3 = (bf16[16,4,32,128]{3,2,1,0:T(8,128)(2,1)S(1)}, bf16[16,4,32,128]{3,2,1,0:T(8,128)(2,1)}, u32[]{:S(2)}) copy-start(bf16[16,4,32,128]{3,2,1,0:T(8,128)(2,1)} %param.14) | copy-start | bytes 1572868
  8.5 5.2 %copy-start.6 = (f32[16,4]{0,1:T(4,128)S(1)}, f32[16,4]{0,1:T(4,128)}, u32[]{:S(2)}) copy-start(f32[16,4]{0,1:T(4,128)} %param.15) | copy-start | bytes 772
  8.5 5.2 %copy-start.8 = (f32[2,128,1024]{2,1,0:T(8,128)S(1)}, f32[2,128,1024]{2,1,0:T(8,128)}, u32[]{:S(2)}) copy-start(f32[2,128,1024]{2,1,0:T(8,128)} %copy-done.7) | copy-start | bytes 3145732
  12.0 1.6 %collective-permute-start.1 = (bf16[8,128,128]{2,1,0:T(8,128)(2,1)S(1)}, bf16[8,128,128]{2,1,0:T(8,128)(2,1)S(1)}, u32[]{:S(2)}, u32[]{:S(2)}) collective-permute-start(bf16[8,128,128]{2,1,0:T(8,128)(2,1)S(1)} %broadcast_select_fusion), channel_id=1, source_target_pairs={{0,1},{1,0},{2,3},{3,2},{4,5},{5,4},{6,7},{7,6},{8,9},{9,8},{10,11... | collective-permute-start | bytes 786440 | tf_op jit(solution)/shard_map/ppermute | solution.py:29
  18.0 2.0 %collective-permute-start.2 = (bf16[16,128,128]{2,1,0:T(8,128)(2,1)S(1)}, bf16[16,128,128]{2,1,0:T(8,128)(2,1)S(1)}, u32[]{:S(2)}, u32[]{:S(2)}) collective-permute-start(bf16[16,128,128]{2,1,0:T(8,128)(2,1)S(1)} %get-tuple-element.46), channel_id=1, source_target_pairs={{0,1},{1,0},{2,3},{3,2},{4,5},{5,4},{6,7},{7,6},{8,9},{9,8},{10,11... | collective-permute-start | bytes 1572872 | tf_op jit(solution)/shard_map/ppermute | solution.py:29
  20.2 8.3 %collective-permute-start.6 = (bf16[4,128,128]{2,1,0:T(8,128)(2,1)S(1)}, bf16[4,128,128]{2,1,0:T(8,128)(2,1)S(1)}, u32[]{:S(2)}, u32[]{:S(2)}) collective-permute-start(bf16[4,128,128]{2,1,0:T(8,128)(2,1)S(1)} %get-tuple-element.65), channel_id=1, source_target_pairs={{0,6},{1,7},{2,4},{3,5},{4,2},{5,3},{6,0},{7,1},{8,14},{9,15},{10,... | collective-permute-start | bytes 393224 | tf_op jit(solution)/shard_map/ppermute | solution.py:29
  22.0 7.5 %collective-permute-start.5 = (bf16[4,128,128]{2,1,0:T(8,128)(2,1)S(1)}, bf16[4,128,128]{2,1,0:T(8,128)(2,1)S(1)}, u32[]{:S(2)}, u32[]{:S(2)}) collective-permute-start(bf16[4,128,128]{2,1,0:T(8,128)(2,1)S(1)} %get-tuple-element.66), channel_id=1, source_target_pairs={{0,4},{1,5},{2,6},{3,7},{4,0},{5,1},{6,2},{7,3},{8,12},{9,13},{10,... | collective-permute-start | bytes 393224 | tf_op jit(solution)/shard_map/ppermute | solution.py:29
  22.5 7.3 %collective-permute-start.4 = (bf16[4,128,128]{2,1,0:T(8,128)(2,1)S(1)}, bf16[4,128,128]{2,1,0:T(8,128)(2,1)S(1)}, u32[]{:S(2)}, u32[]{:S(2)}) collective-permute-start(bf16[4,128,128]{2,1,0:T(8,128)(2,1)S(1)} %get-tuple-element.67), channel_id=1, source_target_pairs={{0,2},{1,3},{2,0},{3,1},{4,6},{5,7},{6,4},{7,5},{8,10},{9,11},{10,... | collective-permute-start | bytes 393224 | tf_op jit(solution)/shard_map/ppermute | solution.py:29
  28.4 1.6 %collective-permute-start.3 = (bf16[8,128,128]{2,1,0:T(8,128)(2,1)S(1)}, bf16[8,128,128]{2,1,0:T(8,128)(2,1)S(1)}, u32[]{:S(2)}, u32[]{:S(2)}) collective-permute-start(bf16[8,128,128]{2,1,0:T(8,128)(2,1)S(1)} %get-tuple-element.50), channel_id=1, source_target_pairs={{0,1},{1,0},{2,3},{3,2},{4,5},{5,4},{6,7},{7,6},{8,9},{9,8},{10,11... | collective-permute-start | bytes 786440 | tf_op jit(solution)/shard_map/ppermute | solution.py:29
  30.1 10.4 %collective-permute-start.7 = (bf16[8,128,128]{2,1,0:T(8,128)(2,1)S(1)}, bf16[8,128,128]{2,1,0:T(8,128)(2,1)S(1)}, u32[]{:S(2)}, u32[]{:S(2)}) collective-permute-start(bf16[8,128,128]{2,1,0:T(8,128)(2,1)S(1)} %add_convert_fusion.1), channel_id=1, source_target_pairs={{0,6},{1,7},{2,0},{3,1},{4,2},{5,3},{6,4},{7,5},{8,14},{9,15},{10,... | collective-permute-start | bytes 786440 | tf_op jit(solution)/shard_map/ppermute | solution.py:19
  31.9 5.8 %collective-permute-start.10 = (bf16[1,128,128]{2,1,0:T(8,128)(2,1)S(1)}, bf16[1,128,128]{2,1,0:T(8,128)(2,1)S(1)}, u32[]{:S(2)}, u32[]{:S(2)}) collective-permute-start(bf16[1,128,128]{2,1,0:T(8,128)(2,1)S(1)} %get-tuple-element.68), channel_id=1, source_target_pairs={{0,24},{8,16},{16,8},{24,0},{1,25},{9,17},{17,9},{25,1},{2,26},{10... | collective-permute-start | bytes 98312 | tf_op jit(solution)/shard_map/ppermute | solution.py:29
  35.6 3.9 %collective-permute-start.9 = (bf16[1,128,128]{2,1,0:T(8,128)(2,1)S(1)}, bf16[1,128,128]{2,1,0:T(8,128)(2,1)S(1)}, u32[]{:S(2)}, u32[]{:S(2)}) collective-permute-start(bf16[1,128,128]{2,1,0:T(8,128)(2,1)S(1)} %get-tuple-element.69), channel_id=1, source_target_pairs={{0,8},{8,0},{16,24},{24,16},{1,9},{9,1},{17,25},{25,17},{2,10},{10... | collective-permute-start | bytes 98312 | tf_op jit(solution)/shard_map/ppermute | solution.py:29
  35.6 5.0 %collective-permute-start.8 = (bf16[1,128,128]{2,1,0:T(8,128)(2,1)S(1)}, bf16[1,128,128]{2,1,0:T(8,128)(2,1)S(1)}, u32[]{:S(2)}, u32[]{:S(2)}) collective-permute-start(bf16[1,128,128]{2,1,0:T(8,128)(2,1)S(1)} %get-tuple-element.70), channel_id=1, source_target_pairs={{0,16},{8,24},{16,0},{24,8},{1,17},{9,25},{17,1},{25,9},{2,18},{10... | collective-permute-start | bytes 98312 | tf_op jit(solution)/shard_map/ppermute | solution.py:29

commit v11 on v10

--- a/solution.py
+++ b/solution.py
@@ -142,15 +142,32 @@
 
 
 def pull_kernel(
-    meta_ref, cot_ref, rot_ref, proj_ref, q_ref, gh_ref, diff_ref, cots_ref, queries_ref, pull_ref,
+    meta_ref, cot_ref, rot_ref, q_ref, cots_ref, queries_ref, pulled_ref, pull_ref,
     *, kv, group, tenants, rank, owned,
 ):
-    lanes = meta_ref.shape[1]
     owner = meta_ref[1:2, :]
+    lanes = owner.shape[1]
     cots = group_rows(cot_ref, kv, group)
     rots = group_rows(rot_ref, kv, group)
     on_rot = dot(jnp.concatenate(rots, axis=1), jnp.concatenate(cots, axis=1), 1, 1)
     pulled = own_terms(on_rot, owner, tenants, rank, group).astype(LOW).astype(WIDE)
+    pulled_ref[...] = pulled
+    for g, rows in enumerate(group_rows(q_ref, kv, group)):
+        queries_ref[g] = rows
+        cots_ref[g] = cots[g]
+    span = tenants * rank
+    slots = slots_of(lanes, group, owned)
+    for h, rows in enumerate(picked_rows(pulled, owner, slots, tenants, rank, group)):
+        pull_ref[h * span : (h + 1) * span, :] = rows
+
+
+def hidden_grad_kernel(
+    meta_ref, pulled_ref, cots_ref, rot_ref, proj_ref, gh_ref, diff_ref, *, kv, group, tenants, rank,
+):
+    owner = meta_ref[1:2, :]
+    lanes = owner.shape[1]
+    dim = cots_ref.shape[2]
+    pulled = pulled_ref[...]
     same_head = lax.broadcasted_iota(jnp.int32, (group, lanes), 0) == lane_head((group, lanes), group)
     picked = []
     for tenant in range(tenants):
@@ -158,18 +175,13 @@
         for k in range(rank):
             picked.append(jnp.where(keep, pulled[k : k + 1], 0.0))
     picked = jnp.concatenate(picked, axis=0).T.astype(LOW)
+    rots = group_rows(rot_ref, kv, group)
     projs = group_rows(proj_ref, kv, group)
+    diffs = [(proj.astype(WIDE) - rot.astype(WIDE)).astype(LOW) for proj, rot in zip(projs, rots)]
+    steered = dot(picked, jnp.concatenate(diffs, axis=1), 1, 0)
     for g in range(kv):
-        diff = (projs[g].astype(WIDE) - rots[g].astype(WIDE)).astype(LOW)
-        diff_ref[g] = diff
-        gh_ref[g] = (cots[g].astype(WIDE) + dot(picked, diff, 1, 0)).astype(LOW)
-        cots_ref[g] = cots[g]
-    for g, rows in enumerate(group_rows(q_ref, kv, group)):
-        queries_ref[g] = rows
-    span = tenants * rank
-    slots = slots_of(lanes, group, owned)
-    for h, rows in enumerate(picked_rows(pulled, owner, slots, tenants, rank, group)):
-        pull_ref[h * span : (h + 1) * span, :] = rows
+        diff_ref[g] = diffs[g]
+        gh_ref[g] = (cots_ref[g].astype(WIDE) + steered[:, g * dim : (g + 1) * dim]).astype(LOW)
 
 
 def places(lanes, tokens, group):
@@ -178,20 +190,21 @@
     return key, key <= query
 
 
-def forward_kernel(
-    shift_ref, queries_ref, two_ref, one_ref, own_ref, cots_ref, diff_ref, meta_ref, pull_ref, bias_ref,
-    low_ref, send_ref, keep_ref, hidden_ref, *, kv, group, tenants, rank, scaling, owned,
-):
+def window_of(two_ref, one_ref, own_ref, head):
+    return jnp.concatenate([two_ref[head], one_ref[head], own_ref[head]], axis=0)
+
+
+def score_kernel(queries_ref, two_ref, one_ref, own_ref, bias_ref, low_ref, *, group, scaling, first):
     tokens = own_ref.shape[1]
-    dim = own_ref.shape[2]
-    owner = meta_ref[1:2, :]
-    lanes = owner.shape[1]
-    _, here = places(lanes, tokens, group)
-    windows = [
-        jnp.concatenate([two_ref[place], one_ref[place], own_ref[place]], axis=0) for place in range(2 * kv)
-    ]
-
-    def weigh(scores):
+    _, here = places(queries_ref.shape[1], tokens, group)
+    count = low_ref.shape[0]
+
+    def scores_of(at):
+        return dot(window_of(two_ref, one_ref, own_ref, first + at), queries_ref[first + at], 1, 1)
+
+    scores = scores_of(0)
+    for at in range(count):
+        ahead = scores_of(at + 1) if at + 1 < count else None
         fold = jnp.where(here, scores[2 * tokens :], scores[0:tokens]) * scaling + bias_ref[0]
         mid = scores[tokens : 2 * tokens] * scaling + bias_ref[1]
         top = jnp.max(jnp.maximum(fold, mid), axis=0, keepdims=True)
@@ -200,16 +213,22 @@
         share = 1.0 / jnp.sum(fold + mid, axis=0, keepdims=True)
         fold = fold * share
         pieces = [jnp.where(here, 0.0, fold), mid * share, jnp.where(here, fold, 0.0)]
-        return jnp.concatenate([piece.astype(LOW) for piece in pieces], axis=0)
-
-    scores = dot(windows[0], queries_ref[0], 1, 1)
+        low_ref[at] = jnp.concatenate([piece.astype(LOW) for piece in pieces], axis=0)
+        scores = ahead
+
+
+def forward_kernel(
+    shift_ref, near_ref, far_ref, two_ref, one_ref, own_ref, cots_ref, diff_ref, meta_ref, pull_ref,
+    send_ref, keep_ref, *, kv, group, tenants, rank, owned,
+):
+    dim = own_ref.shape[2]
+    owner = meta_ref[1:2, :]
+    lanes = owner.shape[1]
+    hidden = []
     for g in range(kv):
-        ahead = dot(windows[g + 1], queries_ref[g + 1], 1, 1) if g + 1 < kv else None
-        low = weigh(scores)
-        low_ref[g] = low
-        hidden_ref[g * dim : (g + 1) * dim, :] = dot(windows[kv + g], low, 0, 0).astype(LOW)
-        scores = ahead
-    hidden = hidden_ref[...]
+        low = (near_ref if g < kv // 2 else far_ref)[g % (kv // 2)]
+        hidden.append(dot(window_of(two_ref, one_ref, own_ref, g), low, 0, 0).astype(LOW))
+    hidden = jnp.concatenate(hidden, axis=0)
     on_diff = dot(jnp.concatenate([diff_ref[g] for g in range(kv)], axis=1), hidden, 1, 0)
     lifted = own_terms(on_diff, owner, tenants, rank, group)
     one_hot = (owner == lax.broadcasted_iota(jnp.int32, (tenants, lanes), 0)).astype(WIDE)
@@ -239,21 +258,23 @@
 
 
 def backward_kernel(
-    queries_ref, gh_ref, two_ref, one_ref, own_ref, low_ref, dq_hbm, back_two_ref, back_one_ref, back_own_ref,
-    dq_ref, sems, *, kv, group, scaling,
-):
-    tokens, dim = own_ref.shape[1:]
-    windows = [
-        jnp.concatenate([two_ref[place], one_ref[place], own_ref[place]], axis=0) for place in range(2 * kv)
-    ]
+    queries_ref, gh_ref, near_ref, far_ref, two_keys, one_keys, own_keys, two_values, one_values, own_values,
+    dq_hbm, back_two_ref, back_one_ref, back_own_ref, dq_ref, sems, *, kv, group, scaling,
+):
+    tokens, dim = own_keys.shape[1:]
+
+    def weight_grad_of(g):
+        return dot(window_of(two_values, one_values, own_values, g), gh_ref[g], 1, 1)
+
     copies = []
-    weight_grad = dot(windows[kv], gh_ref[0], 1, 1)
+    weight_grad = weight_grad_of(0)
     for g in range(kv):
-        ahead = dot(windows[kv + g + 1], gh_ref[g + 1], 1, 1) if g + 1 < kv else None
-        weights = low_ref[g].astype(WIDE)
+        ahead = weight_grad_of(g + 1) if g + 1 < kv else None
+        low = (near_ref if g < kv // 2 else far_ref)[g % (kv // 2)]
+        weights = low.astype(WIDE)
         delta = jnp.sum(weights * weight_grad, axis=0, keepdims=True)
         score_grad = (weights * (weight_grad - delta)).astype(LOW)
-        query_grad = (dot(windows[g], score_grad, 0, 0) * scaling).T.reshape(tokens, group, dim)
+        query_grad = (dot(window_of(two_keys, one_keys, own_keys, g), score_grad, 0, 0) * scaling).T.reshape(tokens, group, dim)
         if g % 2 == 1:
             heads = slice((g - 1) * group, (g + 1) * group)
             dq_ref[:, heads, :] = jnp.concatenate([before, query_grad], axis=1).astype(LOW)
@@ -261,7 +282,7 @@
             copies[-1].start()
         before = query_grad
         key_grad = dot(score_grad, queries_ref[g], 1, 0) * scaling
-        value_grad = dot(low_ref[g], gh_ref[g], 1, 0)
+        value_grad = dot(low, gh_ref[g], 1, 0)
         for place, grad in ((g, key_grad), (kv + g, value_grad)):
             back_two_ref[place] = grad[0:tokens].astype(LOW)
             back_one_ref[place] = grad[tokens : 2 * tokens].astype(LOW)
@@ -322,7 +343,7 @@
                 in_specs=[vmem] * len(operands),
                 out_specs=out_specs or [vmem] * len(outs),
                 scratch_shapes=scratch,
-                compiler_params=pltpu.CompilerParams(vmem_limit_bytes=24 * 2**20),
+                compiler_params=pltpu.CompilerParams(vmem_limit_bytes=12 * 2**20),
                 name=body.__name__,
                 cost_estimate=pl.CostEstimate(flops=flops, bytes_accessed=moved, transcendentals=0),
             )(*operands)
@@ -332,40 +353,57 @@
     span = tenants * rank
     here = heads // ctx
     rows = here * 2 * span // rep
-    own = jnp.moveaxis(jnp.concatenate([key_rows[0], value_matrix[0]], axis=1), 1, 0)
+    own_keys = lax.optimization_barrier(jnp.moveaxis(key_rows[0], 1, 0))
     even = lax.axis_index("ctx") % 2 == 0
-    two = shifted(own, "ctx", 2)
+    two_keys = shifted(own_keys, "ctx", 2)
     meta, biases = call(
         place_kernel, [((8, lanes), jnp.int32), ((2, tokens, lanes), WIDE)], 8 * 2**30, 2**20,
         group=group,
     )(doc_starts, tenant_ids)
-    grad_hidden, diff, cots, queries, pull = call(
+    own_values, meta = lax.optimization_barrier((jnp.moveaxis(value_matrix[0], 1, 0), meta))
+    two_values = shifted(own_values, "ctx", 2)
+    cots, queries, pulled, pull = call(
         pull_kernel,
-        [
-            ((kv, lanes, dim), LOW), ((kv, span * group, dim), LOW), ((kv, lanes, dim), LOW),
-            ((kv, lanes, dim), LOW), ((span * group, lanes), LOW),
-        ],
-        2 * 2**30, 4 * 2**20, tenants=tenants, rank=rank, owned=here, **sizes,
-    )(meta, upstream, rot, proj, queries)
-    two, pull = lax.optimization_barrier((two, pull))
-    one = exchanged(jnp.where(even, own, two), {"ctx": 1})
-    low, send, keep = call(
-        forward_kernel,
-        [((kv, 3 * tokens, lanes), LOW)] + [((ctx * rep // 2, rows, dim), LOW)] * 2,
-        4 * 2**30, 10 * 2**20, scratch=[pltpu.VMEM((heads // group * dim, lanes), LOW)],
-        tenants=tenants, rank=rank, scaling=scaling, owned=here, **sizes,
-    )(shift_bias.T, queries, two, one, own, cots, diff, meta, pull, biases)
+        [((kv, lanes, dim), LOW), ((kv, lanes, dim), LOW), ((8, lanes), WIDE), ((span * group, lanes), LOW)],
+        2**30, 4 * 2**20, tenants=tenants, rank=rank, owned=here, **sizes,
+    )(meta, upstream, rot, queries)
+    two_keys, pulled = lax.optimization_barrier((two_keys, pulled))
+    one_keys = exchanged(jnp.where(even, own_keys, two_keys), {"ctx": 1})
+    grad_hidden, diff = call(
+        hidden_grad_kernel, [((kv, lanes, dim), LOW), ((kv, span * group, dim), LOW)],
+        2 * 2**30, 4 * 2**20, tenants=tenants, rank=rank, **sizes,
+    )(meta, pulled, cots, rot, proj)
+    one_keys, grad_hidden = lax.optimization_barrier((one_keys, grad_hidden))
+
+    def weights_of(first):
+        return call(
+            score_kernel, [((kv // 2, 3 * tokens, lanes), LOW)], 2 * 2**30, 4 * 2**20,
+            group=group, scaling=scaling, first=first,
+        )(queries, two_keys, one_keys, own_keys, biases)[0]
+
+    near = weights_of(0)
+    two_values, near = lax.optimization_barrier((two_values, near))
+    one_values = exchanged(jnp.where(even, own_values, two_values), {"ctx": 1})
+    far = weights_of(kv // 2)
+    one_values, far = lax.optimization_barrier((one_values, far))
+    send, keep = call(
+        forward_kernel, [((ctx * rep // 2, rows, dim), LOW)] * 2, 4 * 2**30, 10 * 2**20,
+        tenants=tenants, rank=rank, owned=here, **sizes,
+    )(shift_bias.T, near, far, two_values, one_values, own_values, cots, diff, meta, pull)
     part = (keep.astype(WIDE) + exchanged(send, {"ctx": 1}).astype(WIDE)).astype(LOW)
-    low, part = lax.optimization_barrier((low, part))
+    near, part = lax.optimization_barrier((near, part))
+    window = (2 * kv, tokens, dim)
     d_queries, back_two, back_one, back_own = call(
         backward_kernel,
-        [((tokens, heads, dim), LOW), (own.shape, LOW), (own.shape, LOW), (own.shape, WIDE)],
+        [((tokens, heads, dim), LOW), (window, LOW), (window, LOW), (window, WIDE)],
         4 * 2**30, 10 * 2**20,
         scratch=[
             pltpu.VMEM((tokens, heads, dim), LOW), pltpu.SemaphoreType.DMA((kv // 2,)),
         ],
         out_specs=[pl.BlockSpec(memory_space=pltpu.HBM), vmem, vmem, vmem], scaling=scaling, **sizes,
-    )(queries, grad_hidden, two, one, own, low)
+    )(
+        queries, grad_hidden, near, far, two_keys, one_keys, own_keys, two_values, one_values, own_values,
+    )
     from_mate = exchanged(back_one, {"ctx": 1})
     onward = back_two.astype(WIDE) + jnp.where(even, 0.0, from_mate.astype(WIDE))
     onward = onward.astype(LOW)

time: 41.7 us -> 40.7 us (0.976)
  starting transfers between devices: 13.1 us -> 14.8 us
  waiting for transfers between devices: 9.63 us -> 8 us
  local copies, waits for them, and re-layouts: 4.44 us -> 3.36 us
    ppermute x9 -> x10, waiting for transfers between devices: 8.91 us -> 7.71 us  [exchanged(): lax.ppermute(value, axes, [(int(source), int(target)) for source, target...]
    ppermute x2 -> x3, starting transfers between devices: 4.78 us -> 5.98 us  [shifted(): lax.ppermute(value, axis, [(source, (source + steps) % count) for source...]
    squeeze x1 -> x0, local copies, waits for them, and re-layouts: 1 us -> none  [on_device(): value_matrix[0]]
    ppermute x9 -> x10, starting transfers between devices: 8.34 us -> 8.79 us  [exchanged(): lax.ppermute(value, axes, [(int(source), int(target)) for source, target...]
    ppermute x2 -> x3, waiting for transfers between devices: 0.72 us -> 0.29 us  [shifted(): lax.ppermute(value, axis, [(source, (source + steps) % count) for source...]
    pallas_call x5 -> x8, Pallas kernels: 13.1 us -> 13.2 us  [run(): pl.pallas_call(lambda *refs: body(*refs, **fixed), out_shape=[jax.ShapeDt...]
    unnamed x18 -> x22, local copies, waits for them, and re-layouts: 3.4 us -> 3.32 us
  transfers between devices with their start and end apart: 11 -> 13, of which waited for: 9 -> 9; matrix products, arithmetic and copies ran while one was open for 0% -> 0% of each run, Pallas kernels for 19% -> 24%
where the time goes in v11:
time: 40.7 us; the launch traced here: 40.5 us
  starting transfers between devices  14.8 us (36%)
  Pallas kernels  13.2 us (32%)
  waiting for transfers between devices  8 us (20%)
  local copies, waits for them, and re-layouts  3.36 us (8%)
  between operations  0.84 us (2%)
    pallas_call x8, Pallas kernels, run(): pl.pallas_call(lambda *refs: body(*refs, **fixed), out_shape=[jax.ShapeDt...  13.2 us
    ppermute x10, starting transfers between devices, exchanged(): lax.ppermute(value, axes, [(int(source), int(target)) for source, target...  8.79 us
    ppermute x10, waiting for transfers between devices, exchanged(): lax.ppermute(value, axes, [(int(source), int(target)) for source, target...  7.71 us
    ppermute x3, starting transfers between devices, shifted(): lax.ppermute(value, axis, [(source, (source + steps) % count) for source...  5.98 us
    unnamed x22, local copies, waits for them, and re-layouts  3.32 us
  transfers between devices with their start and end apart: 13, of which 9 were waited for; matrix products, arithmetic and copies ran while one was open for 0% of the time, Pallas kernels for 24%

profile of v11, /device:TPU:0, one launch (start us, length us, event | category | flops | bytes accessed | tf_op | source)
XLA Modules:
  0.0 40.5 jit_solution(12000652377529864902)
XLA Ops:
  0.6 0.9 %copy.18 = bf16[1,128,4,128]{3,1,2,0:T(8,128)(2,1)S(1)} copy(bf16[1,128,4,128]{3,2,1,0:T(4,128)(2,1)} %param.10) | data formatting | bytes 262144 | tf_op args[1]
  1.6 0.0 copy-start
  1.6 0.0 copy-start.1
  1.6 0.0 copy-start.2
  1.6 3.0 %collective-permute-start = (bf16[4,128,128]{2,1,0:T(8,128)(2,1)S(1)}, bf16[4,128,128]{2,1,0:T(8,128)(2,1)S(1)}, u32[]{:S(2)}, u32[]{:S(2)}) collective-permute-start(bf16[4,128,128]{2,1,0:T(8,128)(2,1)S(1)} %bitcast.20), channel_id=1, source_target_pairs={{0,2},{1,3},{2,4},{3,5},{4,6},{5,7},{6,0},{7,1},{8,10},{9,11},{10,... | collective-permute-start | bytes 393224 | tf_op jit(solution)/shard_map/ppermute | solution.py:19
  4.6 0.0 copy-start.4
  4.6 0.7 %copy-done.4 = s32[1,1024]{1,0:T(1,128)S(1)} copy-done((s32[1,1024]{1,0:T(1,128)S(1)}, s32[1,1024]{1,0:T(1,128)}, u32[]{:S(2)}) %copy-start.4) | copy-done | bytes 4120
  5.3 0.0 copy-start.5
  5.3 0.7 %copy-done.5 = s32[1,1024]{1,0:T(1,128)S(1)} copy-done((s32[1,1024]{1,0:T(1,128)S(1)}, s32[1,1024]{1,0:T(1,128)}, u32[]{:S(2)}) %copy-start.5) | copy-done | bytes 4120
  6.0 0.0 copy-start.9
  6.0 0.3 place_kernel.1
  6.3 0.0 copy-start.7
  6.3 1.0 %copy-done.7 = f32[2,128,1024]{2,1,0:T(8,128)} copy-done((f32[2,128,1024]{2,1,0:T(8,128)}, f32[2,128,1024]{2,1,0:T(8,128)S(1)}, u32[]{:S(2)}) %copy-start.7) | copy-done | bytes 1048600
  7.3 0.0 copy-done.9
  7.3 1.5 %collective-permute-start.2 = (bf16[4,128,128]{2,1,0:T(8,128)(2,1)S(1)}, bf16[4,128,128]{2,1,0:T(8,128)(2,1)S(1)}, u32[]{:S(2)}, u32[]{:S(2)}) collective-permute-start(bf16[4,128,128]{2,1,0:T(8,128)(2,1)S(1)} %bitcast.25), channel_id=1, source_target_pairs={{0,2},{1,3},{2,4},{3,5},{4,6},{5,7},{6,0},{7,1},{8,10},{9,11},{10,... | collective-permute-start | bytes 393224 | tf_op jit(solution)/shard_map/ppermute | solution.py:19
  8.9 0.0 copy-done
  8.9 0.0 copy-done.1
  8.9 0.0 copy-done.2
  8.9 0.0 copy-start.3
  8.9 1.4 %pull_kernel.1 = (bf16[4,1024,128]{2,1,0:T(8,128)(2,1)S(1)}, bf16[4,1024,128]{2,1,0:T(8,128)(2,1)S(1)}, f32[8,1024]{1,0:T(8,128)S(1)}, bf16[512,1024]{1,0:T(8,128)(2,1)S(1)}) custom-call(s32[8,1024]{1,0:T(8,128)S(1)} %get-tuple-element.44.refs_0_.refs_8_, bf16[128,32,128]{2,1,0:T(8,128)(2,1)S(1)} %bitcast.29, bf16[64,32,128]{2,1,0:T(8,128)(2,1)S(1)} %bitcast.31, ...), custom_call_target="tpu_custom_call" | custom-call | flops 1073741824 | bytes 4194304 | tf_op jit(solution)/shard_map/pull_kernel/pallas_call | solution.py:340
  10.3 0.0 collective-permute-done.refs_1_.refs_4_
  10.3 0.1 collective-permute-start.1
  10.4 0.0 copy-done.3
  10.4 0.0 copy-start.8
  10.4 0.8 %hidden_grad_kernel.1 = (bf16[4,1024,128]{2,1,0:T(8,128)(2,1)S(1)}, bf16[4,512,128]{2,1,0:T(8,128)(2,1)S(1)}) custom-call(s32[8,1024]{1,0:T(8,128)S(1)} %get-tuple-element.44.refs_0_.refs_8_, f32[8,1024]{1,0:T(8,128)S(1)} %get-tuple-element.48.refs_1_, bf16[4,1024,128]{2,1,0:T(8,128)(2,1)S(1)} %get-tuple-element.49.refs_2_.refs_6_, ...), custom_call_target="tpu_custom_call" | custom-call | flops 2147483648 | bytes 4194304 | tf_op jit(solution)/shard_map/hidden_grad_kernel/pallas_call | solution.py:340
  11.2 0.5 %collective-permute-done.1.refs_2_.refs_5_ = bf16[4,128,128]{2,1,0:T(8,128)(2,1)S(1)} collective-permute-done((bf16[4,128,128]{2,1,0:T(8,128)(2,1)S(1)}, bf16[4,128,128]{2,1,0:T(8,128)(2,1)S(1)}, u32[]{:S(2)}, u32[]{:S(2)}) %collective-permute-start.1) | collective-permute-done | bytes 131104 | tf_op jit(solution)/shard_map/ppermute | solution.py:29
  11.7 0.0 copy-done.8
  11.7 1.2 %score_kernel.2.refs_1_.refs_2_ = bf16[2,384,1024]{2,1,0:T(8,128)(2,1)S(1)} custom-call(bf16[4,1024,128]{2,1,0:T(8,128)(2,1)S(1)} %get-tuple-element.45.refs_0_, bf16[4,128,128]{2,1,0:T(8,128)(2,1)S(1)} %collective-permute-done.refs_1_.refs_4_, bf16[4,128,128]{2,1,0:T(8,128)(2,1)S(1)} %collective-permute-done.1.refs_2_.refs_5_, ...), custom_call_target="tpu_custom_call" | custom-call | flops 2147483648 | bytes 4194304 | tf_op jit(solution)/shard_map/score_kernel/pallas_call | solution.py:340
  12.9 0.3 collective-permute-done.2.refs_3_.refs_7_
  13.3 0.0 copy-start.6
  13.3 0.2 collective-permute-start.3
  13.4 1.2 %score_kernel.3.refs_2_.refs_3_ = bf16[2,384,1024]{2,1,0:T(8,128)(2,1)S(1)} custom-call(bf16[4,1024,128]{2,1,0:T(8,128)(2,1)S(1)} %get-tuple-element.45.refs_0_, bf16[4,128,128]{2,1,0:T(8,128)(2,1)S(1)} %collective-permute-done.refs_1_.refs_4_, bf16[4,128,128]{2,1,0:T(8,128)(2,1)S(1)} %collective-permute-done.1.refs_2_.refs_5_, ...), custom_call_target="tpu_custom_call" | custom-call | flops 2147483648 | bytes 4194304 | tf_op jit(solution)/shard_map/score_kernel/pallas_call | solution.py:340
  14.6 0.0 collective-permute-done.3.refs_4_.refs_8_
  14.7 0.0 copy-done.6
  14.7 2.7 %forward_kernel.1 = (bf16[16,128,128]{2,1,0:T(8,128)(2,1)S(1)}, bf16[16,128,128]{2,1,0:T(8,128)(2,1)S(1)}) custom-call(f32[4,16]{1,0:T(4,128)S(1)} %bitcast.34, bf16[2,384,1024]{2,1,0:T(8,128)(2,1)S(1)} %score_kernel.2.refs_1_.refs_2_, bf16[2,384,1024]{2,1,0:T(8,128)(2,1)S(1)} %score_kernel.3.refs_2_.refs_3_, ...), custom_call_target="tpu_custom_call" | custom-call | flops 4294967296 | bytes 10485760 | tf_op jit(solution)/shard_map/forward_kernel/pallas_call | solution.py:340
  17.4 0.4 %collective-permute-start.4 = (bf16[16,128,128]{2,1,0:T(8,128)(2,1)S(1)}, bf16[16,128,128]{2,1,0:T(8,128)(2,1)S(1)}, u32[]{:S(2)}, u32[]{:S(2)}) collective-permute-start(bf16[16,128,128]{2,1,0:T(8,128)(2,1)S(1)} %get-tuple-element.62), channel_id=1, source_target_pairs={{0,1},{1,0},{2,3},{3,2},{4,5},{5,4},{6,7},{7,6},{8,9},{9,8},{10,11... | collective-permute-start | bytes 1572872 | tf_op jit(solution)/shard_map/ppermute | solution.py:29
  17.9 1.5 %collective-permute-done.4 = bf16[16,128,128]{2,1,0:T(8,128)(2,1)S(1)} collective-permute-done((bf16[16,128,128]{2,1,0:T(8,128)(2,1)S(1)}, bf16[16,128,128]{2,1,0:T(8,128)(2,1)S(1)}, u32[]{:S(2)}, u32[]{:S(2)}) %collective-permute-start.4) | collective-permute-done | bytes 524320 | tf_op jit(solution)/shard_map/ppermute | solution.py:29
  19.4 0.1 add_convert_fusion
  19.6 1.5 %collective-permute-start.8 = (bf16[4,128,128]{2,1,0:T(8,128)(2,1)S(1)}, bf16[4,128,128]{2,1,0:T(8,128)(2,1)S(1)}, u32[]{:S(2)}, u32[]{:S(2)}) collective-permute-start(bf16[4,128,128]{2,1,0:T(8,128)(2,1)S(1)} %get-tuple-element.81), channel_id=1, source_target_pairs={{0,6},{1,7},{2,4},{3,5},{4,2},{5,3},{6,0},{7,1},{8,14},{9,15},{10,... | collective-permute-start | bytes 393224 | tf_op jit(solution)/shard_map/ppermute | solution.py:29
  21.1 1.5 %collective-permute-start.7 = (bf16[4,128,128]{2,1,0:T(8,128)(2,1)S(1)}, bf16[4,128,128]{2,1,0:T(8,128)(2,1)S(1)}, u32[]{:S(2)}, u32[]{:S(2)}) collective-permute-start(bf16[4,128,128]{2,1,0:T(8,128)(2,1)S(1)} %get-tuple-element.82), channel_id=1, source_target_pairs={{0,4},{1,5},{2,6},{3,7},{4,0},{5,1},{6,2},{7,3},{8,12},{9,13},{10,... | collective-permute-start | bytes 393224 | tf_op jit(solution)/shard_map/ppermute | solution.py:29
  22.6 0.6 %collective-permute-start.6 = (bf16[4,128,128]{2,1,0:T(8,128)(2,1)S(1)}, bf16[4,128,128]{2,1,0:T(8,128)(2,1)S(1)}, u32[]{:S(2)}, u32[]{:S(2)}) collective-permute-start(bf16[4,128,128]{2,1,0:T(8,128)(2,1)S(1)} %get-tuple-element.83), channel_id=1, source_target_pairs={{0,2},{1,3},{2,0},{3,1},{4,6},{5,7},{6,4},{7,5},{8,10},{9,11},{10,... | collective-permute-start | bytes 393224 | tf_op jit(solution)/shard_map/ppermute | solution.py:29
  23.2 4.7 %backward_kernel.1 = (bf16[128,32,128]{2,1,0:T(8,128)(2,1)}, bf16[8,128,128]{2,1,0:T(8,128)(2,1)S(1)}, bf16[8,128,128]{2,1,0:T(8,128)(2,1)S(1)}, f32[8,128,128]{2,1,0:T(8,128)S(1)}) custom-call(bf16[4,1024,128]{2,1,0:T(8,128)(2,1)S(1)} %get-tuple-element.45.refs_0_, bf16[4,1024,128]{2,1,0:T(8,128)(2,1)S(1)} %get-tuple-element.51.refs_1_, ...), custom_call_target="tpu_custom_call" | custom-call | flops 4294967296 | bytes 10485760 | tf_op jit(solution)/shard_map/backward_kernel/pallas_call | solution.py:340
  27.8 0.1 collective-permute-start.5
  27.9 0.0 collective-permute-done.8
  27.9 1.2 %collective-permute-done.7 = bf16[4,128,128]{2,1,0:T(8,128)(2,1)S(1)} collective-permute-done((bf16[4,128,128]{2,1,0:T(8,128)(2,1)S(1)}, bf16[4,128,128]{2,1,0:T(8,128)(2,1)S(1)}, u32[]{:S(2)}, u32[]{:S(2)}) %collective-permute-start.7) | collective-permute-done | bytes 131104 | tf_op jit(solution)/shard_map/ppermute | solution.py:29
  29.1 0.1 collective-permute-done.6
  29.3 0.1 add_convert_fusion.2
  29.3 0.1 collective-permute-done.5.refs_1_
  29.4 0.1 add_convert_fusion.1
  29.5 1.4 %collective-permute-start.9 = (bf16[8,128,128]{2,1,0:T(8,128)(2,1)S(1)}, bf16[8,128,128]{2,1,0:T(8,128)(2,1)S(1)}, u32[]{:S(2)}, u32[]{:S(2)}) collective-permute-start(bf16[8,128,128]{2,1,0:T(8,128)(2,1)S(1)} %add_convert_fusion.1), channel_id=1, source_target_pairs={{0,6},{1,7},{2,0},{3,1},{4,2},{5,3},{6,4},{7,5},{8,14},{9,15},{10,... | collective-permute-start | bytes 786440 | tf_op jit(solution)/shard_map/ppermute | solution.py:19
  31.0 3.7 %collective-permute-start.12 = (bf16[1,128,128]{2,1,0:T(8,128)(2,1)S(1)}, bf16[1,128,128]{2,1,0:T(8,128)(2,1)S(1)}, u32[]{:S(2)}, u32[]{:S(2)}) collective-permute-start(bf16[1,128,128]{2,1,0:T(8,128)(2,1)S(1)} %get-tuple-element.84), channel_id=1, source_target_pairs={{0,24},{8,16},{16,8},{24,0},{1,25},{9,17},{17,9},{25,1},{2,26},{10... | collective-permute-start | bytes 98312 | tf_op jit(solution)/shard_map/ppermute | solution.py:29
  34.7 0.0 collective-permute-start.11
  34.7 0.8 %collective-permute-start.10 = (bf16[1,128,128]{2,1,0:T(8,128)(2,1)S(1)}, bf16[1,128,128]{2,1,0:T(8,128)(2,1)S(1)}, u32[]{:S(2)}, u32[]{:S(2)}) collective-permute-start(bf16[1,128,128]{2,1,0:T(8,128)(2,1)S(1)} %get-tuple-element.86), channel_id=1, source_target_pairs={{0,16},{8,24},{16,0},{24,8},{1,17},{9,25},{17,1},{25,9},{2,18},{10... | collective-permute-start | bytes 98312 | tf_op jit(solution)/shard_map/ppermute | solution.py:29
  35.5 1.3 %collective-permute-done.12.refs_6_ = bf16[1,128,128]{2,1,0:T(8,128)(2,1)S(1)} collective-permute-done((bf16[1,128,128]{2,1,0:T(8,128)(2,1)S(1)}, bf16[1,128,128]{2,1,0:T(8,128)(2,1)S(1)}, u32[]{:S(2)}, u32[]{:S(2)}) %collective-permute-start.12) | collective-permute-done | bytes 32800 | tf_op jit(solution)/shard_map/ppermute | solution.py:29
  36.8 1.8 %collective-permute-done.11.refs_5_ = bf16[1,128,128]{2,1,0:T(8,128)(2,1)S(1)} collective-permute-done((bf16[1,128,128]{2,1,0:T(8,128)(2,1)S(1)}, bf16[1,128,128]{2,1,0:T(8,128)(2,1)S(1)}, u32[]{:S(2)}, u32[]{:S(2)}) %collective-permute-start.11) | collective-permute-done | bytes 32800 | tf_op jit(solution)/shard_map/ppermute | solution.py:29
  38.6 1.0 %collective-permute-done.10.refs_4_ = bf16[1,128,128]{2,1,0:T(8,128)(2,1)S(1)} collective-permute-done((bf16[1,128,128]{2,1,0:T(8,128)(2,1)S(1)}, bf16[1,128,128]{2,1,0:T(8,128)(2,1)S(1)}, u32[]{:S(2)}, u32[]{:S(2)}) %collective-permute-start.10) | collective-permute-done | bytes 32800 | tf_op jit(solution)/shard_map/ppermute | solution.py:29
  39.6 0.0 collective-permute-done.9.refs_2_
  39.6 0.8 %finish_kernel.1 = (bf16[512,128]{1,0:T(8,128)(2,1)}, bf16[512,128]{1,0:T(8,128)(2,1)}, f32[16,4,128]{2,1,0:T(4,128)}, f32[16,4,128]{2,1,0:T(4,128)}) custom-call(f32[8,128,128]{2,1,0:T(8,128)S(1)} %get-tuple-element.65.refs_0_, bf16[8,128,128]{2,1,0:T(8,128)(2,1)S(1)} %collective-permute-done.5.refs_1_, ...), custom_call_target="tpu_custom_call" | custom-call | flops 1048576 | bytes 1048576 | tf_op jit(solution)/shard_map/finish_kernel/pallas_call | solution.py:340
  (5 shorter events, 0.1 us)
Async XLA Ops:
  1.6 7.3 %copy-start = (bf16[1,128,32,128]{3,2,1,0:T(8,128)(2,1)S(1)}, bf16[1,128,32,128]{3,2,1,0:T(8,128)(2,1)}, u32[]{:S(2)}) copy-start(bf16[1,128,32,128]{3,2,1,0:T(8,128)(2,1)} %param.12) | copy-start | bytes 3145732
  1.6 7.3 %copy-start.1 = (bf16[1,128,32,128]{3,2,1,0:T(8,128)(2,1)S(1)}, bf16[1,128,32,128]{3,2,1,0:T(8,128)(2,1)}, u32[]{:S(2)}) copy-start(bf16[1,128,32,128]{3,2,1,0:T(8,128)(2,1)} %param.9) | copy-start | bytes 3145732
  1.6 7.3 %copy-start.2 = (bf16[16,4,32,128]{3,2,1,0:T(8,128)(2,1)S(1)}, bf16[16,4,32,128]{3,2,1,0:T(8,128)(2,1)}, u32[]{:S(2)}) copy-start(bf16[16,4,32,128]{3,2,1,0:T(8,128)(2,1)} %param.13) | copy-start | bytes 1572868
  1.6 8.7 %collective-permute-start = (bf16[4,128,128]{2,1,0:T(8,128)(2,1)S(1)}, bf16[4,128,128]{2,1,0:T(8,128)(2,1)S(1)}, u32[]{:S(2)}, u32[]{:S(2)}) collective-permute-start(bf16[4,128,128]{2,1,0:T(8,128)(2,1)S(1)} %bitcast.20), channel_id=1, source_target_pairs={{0,2},{1,3},{2,4},{3,5},{4,6},{5,7},{6,0},{7,1},{8,10},{9,11},{10,... | collective-permute-start | bytes 393224 | tf_op jit(solution)/shard_map/ppermute | solution.py:19
  4.6 0.7 %copy-start.4 = (s32[1,1024]{1,0:T(1,128)S(1)}, s32[1,1024]{1,0:T(1,128)}, u32[]{:S(2)}) copy-start(s32[1,1024]{1,0:T(1,128)} %refs_0_.1) | copy-start | bytes 12292
  5.3 0.7 %copy-start.5 = (s32[1,1024]{1,0:T(1,128)S(1)}, s32[1,1024]{1,0:T(1,128)}, u32[]{:S(2)}) copy-start(s32[1,1024]{1,0:T(1,128)} %refs_1_.1) | copy-start | bytes 12292
  6.0 1.3 %copy-start.9 = (bf16[1,128,4,128]{3,2,1,0:T(4,128)(2,1)S(1)}, bf16[1,128,4,128]{3,2,1,0:T(4,128)(2,1)}, u32[]{:S(2)}) copy-start(bf16[1,128,4,128]{3,2,1,0:T(4,128)(2,1)} %param.11) | copy-start | bytes 393220
  6.3 1.0 %copy-start.7 = (f32[2,128,1024]{2,1,0:T(8,128)}, f32[2,128,1024]{2,1,0:T(8,128)S(1)}, u32[]{:S(2)}) copy-start(f32[2,128,1024]{2,1,0:T(8,128)S(1)} %get-tuple-element.54.refs_4_) | copy-start | bytes 3145732
  7.3 5.9 %collective-permute-start.2 = (bf16[4,128,128]{2,1,0:T(8,128)(2,1)S(1)}, bf16[4,128,128]{2,1,0:T(8,128)(2,1)S(1)}, u32[]{:S(2)}, u32[]{:S(2)}) collective-permute-start(bf16[4,128,128]{2,1,0:T(8,128)(2,1)S(1)} %bitcast.25), channel_id=1, source_target_pairs={{0,2},{1,3},{2,4},{3,5},{4,6},{5,7},{6,0},{7,1},{8,10},{9,11},{10,... | collective-permute-start | bytes 393224 | tf_op jit(solution)/shard_map/ppermute | solution.py:19
  8.9 1.5 %copy-start.3 = (bf16[16,4,32,128]{3,2,1,0:T(8,128)(2,1)S(1)}, bf16[16,4,32,128]{3,2,1,0:T(8,128)(2,1)}, u32[]{:S(2)}) copy-start(bf16[16,4,32,128]{3,2,1,0:T(8,128)(2,1)} %param.14) | copy-start | bytes 1572868
  10.3 1.4 %collective-permute-start.1 = (bf16[4,128,128]{2,1,0:T(8,128)(2,1)S(1)}, bf16[4,128,128]{2,1,0:T(8,128)(2,1)S(1)}, u32[]{:S(2)}, u32[]{:S(2)}) collective-permute-start(bf16[4,128,128]{2,1,0:T(8,128)(2,1)S(1)} %broadcast_select_fusion.1), channel_id=1, source_target_pairs={{0,1},{1,0},{2,3},{3,2},{4,5},{5,4},{6,7},{7,6},{8,9},{9,8},{10,11... | collective-permute-start | bytes 393224 | tf_op jit(solution)/shard_map/ppermute | solution.py:29
  10.4 1.3 %copy-start.8 = (f32[2,128,1024]{2,1,0:T(8,128)S(1)}, f32[2,128,1024]{2,1,0:T(8,128)}, u32[]{:S(2)}) copy-start(f32[2,128,1024]{2,1,0:T(8,128)} %copy-done.7) | copy-start | bytes 3145732
  13.3 1.4 %copy-start.6 = (f32[16,4]{0,1:T(4,128)S(1)}, f32[16,4]{0,1:T(4,128)}, u32[]{:S(2)}) copy-start(f32[16,4]{0,1:T(4,128)} %param.15) | copy-start | bytes 772
  13.3 1.4 %collective-permute-start.3 = (bf16[4,128,128]{2,1,0:T(8,128)(2,1)S(1)}, bf16[4,128,128]{2,1,0:T(8,128)(2,1)S(1)}, u32[]{:S(2)}, u32[]{:S(2)}) collective-permute-start(bf16[4,128,128]{2,1,0:T(8,128)(2,1)S(1)} %broadcast_select_fusion), channel_id=1, source_target_pairs={{0,1},{1,0},{2,3},{3,2},{4,5},{5,4},{6,7},{7,6},{8,9},{9,8},{10,11... | collective-permute-start | bytes 393224 | tf_op jit(solution)/shard_map/ppermute | solution.py:29
  17.4 2.0 %collective-permute-start.4 = (bf16[16,128,128]{2,1,0:T(8,128)(2,1)S(1)}, bf16[16,128,128]{2,1,0:T(8,128)(2,1)S(1)}, u32[]{:S(2)}, u32[]{:S(2)}) collective-permute-start(bf16[16,128,128]{2,1,0:T(8,128)(2,1)S(1)} %get-tuple-element.62), channel_id=1, source_target_pairs={{0,1},{1,0},{2,3},{3,2},{4,5},{5,4},{6,7},{7,6},{8,9},{9,8},{10,11... | collective-permute-start | bytes 1572872 | tf_op jit(solution)/shard_map/ppermute | solution.py:29
  19.6 8.3 %collective-permute-start.8 = (bf16[4,128,128]{2,1,0:T(8,128)(2,1)S(1)}, bf16[4,128,128]{2,1,0:T(8,128)(2,1)S(1)}, u32[]{:S(2)}, u32[]{:S(2)}) collective-permute-start(bf16[4,128,128]{2,1,0:T(8,128)(2,1)S(1)} %get-tuple-element.81), channel_id=1, source_target_pairs={{0,6},{1,7},{2,4},{3,5},{4,2},{5,3},{6,0},{7,1},{8,14},{9,15},{10,... | collective-permute-start | bytes 393224 | tf_op jit(solution)/shard_map/ppermute | solution.py:29
  21.1 8.1 %collective-permute-start.7 = (bf16[4,128,128]{2,1,0:T(8,128)(2,1)S(1)}, bf16[4,128,128]{2,1,0:T(8,128)(2,1)S(1)}, u32[]{:S(2)}, u32[]{:S(2)}) collective-permute-start(bf16[4,128,128]{2,1,0:T(8,128)(2,1)S(1)} %get-tuple-element.82), channel_id=1, source_target_pairs={{0,4},{1,5},{2,6},{3,7},{4,0},{5,1},{6,2},{7,3},{8,12},{9,13},{10,... | collective-permute-start | bytes 393224 | tf_op jit(solution)/shard_map/ppermute | solution.py:29
  22.6 6.7 %collective-permute-start.6 = (bf16[4,128,128]{2,1,0:T(8,128)(2,1)S(1)}, bf16[4,128,128]{2,1,0:T(8,128)(2,1)S(1)}, u32[]{:S(2)}, u32[]{:S(2)}) collective-permute-start(bf16[4,128,128]{2,1,0:T(8,128)(2,1)S(1)} %get-tuple-element.83), channel_id=1, source_target_pairs={{0,2},{1,3},{2,0},{3,1},{4,6},{5,7},{6,4},{7,5},{8,10},{9,11},{10,... | collective-permute-start | bytes 393224 | tf_op jit(solution)/shard_map/ppermute | solution.py:29
  27.8 1.6 %collective-permute-start.5 = (bf16[8,128,128]{2,1,0:T(8,128)(2,1)S(1)}, bf16[8,128,128]{2,1,0:T(8,128)(2,1)S(1)}, u32[]{:S(2)}, u32[]{:S(2)}) collective-permute-start(bf16[8,128,128]{2,1,0:T(8,128)(2,1)S(1)} %get-tuple-element.66), channel_id=1, source_target_pairs={{0,1},{1,0},{2,3},{3,2},{4,5},{5,4},{6,7},{7,6},{8,9},{9,8},{10,11... | collective-permute-start | bytes 786440 | tf_op jit(solution)/shard_map/ppermute | solution.py:29
  29.5 10.1 %collective-permute-start.9 = (bf16[8,128,128]{2,1,0:T(8,128)(2,1)S(1)}, bf16[8,128,128]{2,1,0:T(8,128)(2,1)S(1)}, u32[]{:S(2)}, u32[]{:S(2)}) collective-permute-start(bf16[8,128,128]{2,1,0:T(8,128)(2,1)S(1)} %add_convert_fusion.1), channel_id=1, source_target_pairs={{0,6},{1,7},{2,0},{3,1},{4,2},{5,3},{6,4},{7,5},{8,14},{9,15},{10,... | collective-permute-start | bytes 786440 | tf_op jit(solution)/shard_map/ppermute | solution.py:19
  31.0 5.8 %collective-permute-start.12 = (bf16[1,128,128]{2,1,0:T(8,128)(2,1)S(1)}, bf16[1,128,128]{2,1,0:T(8,128)(2,1)S(1)}, u32[]{:S(2)}, u32[]{:S(2)}) collective-permute-start(bf16[1,128,128]{2,1,0:T(8,128)(2,1)S(1)} %get-tuple-element.84), channel_id=1, source_target_pairs={{0,24},{8,16},{16,8},{24,0},{1,25},{9,17},{17,9},{25,1},{2,26},{10... | collective-permute-start | bytes 98312 | tf_op jit(solution)/shard_map/ppermute | solution.py:29
  34.7 3.9 %collective-permute-start.11 = (bf16[1,128,128]{2,1,0:T(8,128)(2,1)S(1)}, bf16[1,128,128]{2,1,0:T(8,128)(2,1)S(1)}, u32[]{:S(2)}, u32[]{:S(2)}) collective-permute-start(bf16[1,128,128]{2,1,0:T(8,128)(2,1)S(1)} %get-tuple-element.85), channel_id=1, source_target_pairs={{0,8},{8,0},{16,24},{24,16},{1,9},{9,1},{17,25},{25,17},{2,10},{10... | collective-permute-start | bytes 98312 | tf_op jit(solution)/shard_map/ppermute | solution.py:29
  34.7 5.0 %collective-permute-start.10 = (bf16[1,128,128]{2,1,0:T(8,128)(2,1)S(1)}, bf16[1,128,128]{2,1,0:T(8,128)(2,1)S(1)}, u32[]{:S(2)}, u32[]{:S(2)}) collective-permute-start(bf16[1,128,128]{2,1,0:T(8,128)(2,1)S(1)} %get-tuple-element.86), channel_id=1, source_target_pairs={{0,16},{8,24},{16,0},{24,8},{1,17},{9,25},{17,1},{25,9},{2,18},{10... | collective-permute-start | bytes 98312 | tf_op jit(solution)/shard_map/ppermute | solution.py:29

commit v12 on v11

--- a/solution.py
+++ b/solution.py
@@ -105,13 +105,13 @@
     return jnp.concatenate([spread[c * 8 : (c + 1) * 8] for c in range(tiles)], axis=1)
 
 
-def place_kernel(starts_ref, owners_ref, meta_ref, bias_ref, *, group):
+def place_kernel(rows_ref, meta_ref, bias_ref, *, group):
     lanes = meta_ref.shape[1]
     tokens = lanes // group
     row_first = lax.axis_index("ctx") * tokens
     mine = pl.ds(pl.multiple_of(row_first, tokens), tokens)
     row = lax.broadcasted_iota(jnp.int32, (8, tokens), 0)
-    both = jnp.where(row == 0, starts_ref[:, mine] - row_first, owners_ref[:, mine]).astype(WIDE)
+    both = jnp.where(row == 0, rows_ref[0:1, mine] - row_first, rows_ref[1:2, mine]).astype(WIDE)
     repeat = lax.broadcasted_iota(jnp.int32, (tokens, lanes), 0) == (
         lax.broadcasted_iota(jnp.int32, (tokens, lanes), 1) // group
     )
@@ -353,13 +353,14 @@
     span = tenants * rank
     here = heads // ctx
     rows = here * 2 * span // rep
+    even = jnp.reshape(lax.axis_index("ctx") % 2 == 0, (1, 1, 1))
+    key_rows, even = lax.optimization_barrier((key_rows, even))
     own_keys = lax.optimization_barrier(jnp.moveaxis(key_rows[0], 1, 0))
-    even = lax.axis_index("ctx") % 2 == 0
     two_keys = shifted(own_keys, "ctx", 2)
     meta, biases = call(
         place_kernel, [((8, lanes), jnp.int32), ((2, tokens, lanes), WIDE)], 8 * 2**30, 2**20,
         group=group,
-    )(doc_starts, tenant_ids)
+    )(jnp.concatenate([doc_starts, tenant_ids], axis=0))
     own_values, meta = lax.optimization_barrier((jnp.moveaxis(value_matrix[0], 1, 0), meta))
     two_values = shifted(own_values, "ctx", 2)
     cots, queries, pulled, pull = call(

time: 40.7 us -> 40.4 us (level)
  local copies, waits for them, and re-layouts: 3.36 us -> 1.52 us
  starting transfers between devices: 14.8 us -> 15.6 us
  other arithmetic: 0.34 us -> 1.05 us
    unnamed x22 -> x13, local copies, waits for them, and re-layouts: 3.32 us -> 0.56 us
    ppermute x3, starting transfers between devices: 5.98 us -> 6.92 us  [shifted(): lax.ppermute(value, axis, [(source, (source + steps) % count) for source...]
    optimization_barrier x0 -> x1, local copies, waits for them, and re-layouts: none -> 0.92 us  [on_device(): key_rows, even = lax.optimization_barrier((key_rows, even))]
    concatenate x0 -> x1, other arithmetic: none -> 0.71 us  [on_device(): jnp.concatenate([doc_starts, tenant_ids], axis=0)]
  transfers between devices with their start and end apart: 13 -> 13, of which waited for: 9 -> 10; matrix products, arithmetic and copies ran while one was open for 0% -> 2% of each run, Pallas kernels for 24% -> 24%
where the time goes in v12:
time: 40.4 us; the launch traced here: 40.1 us
  starting transfers between devices  15.6 us (39%)
  Pallas kernels  13.1 us (32%)
  waiting for transfers between devices  8.04 us (20%)
  local copies, waits for them, and re-layouts  1.52 us (4%)
  other arithmetic  1.05 us (3%)
  between operations  0.85 us (2%)
    pallas_call x8, Pallas kernels, run(): pl.pallas_call(lambda *refs: body(*refs, **fixed), out_shape=[jax.ShapeDt...  13.1 us
    ppermute x10, starting transfers between devices, exchanged(): lax.ppermute(value, axes, [(int(source), int(target)) for source, target...  8.63 us
    ppermute x10, waiting for transfers between devices, exchanged(): lax.ppermute(value, axes, [(int(source), int(target)) for source, target...  7.73 us
    ppermute x3, starting transfers between devices, shifted(): lax.ppermute(value, axis, [(source, (source + steps) % count) for source...  6.92 us
    optimization_barrier x1, local copies, waits for them, and re-layouts, on_device(): key_rows, even = lax.optimization_barrier((key_rows, even))  0.92 us
  transfers between devices with their start and end apart: 13, of which 10 were waited for; matrix products, arithmetic and copies ran while one was open for 2% of the time, Pallas kernels for 24%

profile of v12, /device:TPU:0, one launch (start us, length us, event | category | flops | bytes accessed | tf_op | source)
XLA Modules:
  0.0 40.1 jit_solution(72268835387099962)
XLA Ops:
  0.6 0.9 %copy.18 = bf16[1,128,4,128]{3,1,2,0:T(8,128)(2,1)S(1)} copy(bf16[1,128,4,128]{3,2,1,0:T(4,128)(2,1)} %param.10) | data formatting | bytes 262144 | tf_op jit(solution)/shard_map/optimization_barrier | solution.py:357
  1.6 3.0 %collective-permute-start = (bf16[4,128,128]{2,1,0:T(8,128)(2,1)S(1)}, bf16[4,128,128]{2,1,0:T(8,128)(2,1)S(1)}, u32[]{:S(2)}, u32[]{:S(2)}) collective-permute-start(bf16[4,128,128]{2,1,0:T(8,128)(2,1)S(1)} %bitcast.22), channel_id=1, source_target_pairs={{0,2},{1,3},{2,4},{3,5},{4,6},{5,7},{6,0},{7,1},{8,10},{9,11},{10,... | collective-permute-start | bytes 393224 | tf_op jit(solution)/shard_map/ppermute | solution.py:19
  4.6 0.7 %pad_add_fusion.refs_0_ = s32[2,1024]{1,0:T(2,128)S(1)} fusion(s32[1,1024]{1,0:T(1,128)} %param.17, s32[1,1024]{1,0:T(1,128)} %param.16), kind=kLoop, calls=%fused_computation.7 | loop fusion | flops 2048 | bytes 16384 | tf_op jit(solution)/shard_map/concatenate | solution.py:363
  5.3 0.0 copy-start.5
  5.3 0.0 copy-start
  5.3 0.0 copy-start.1
  5.3 0.0 copy-start.2
  5.3 0.3 place_kernel.1
  5.7 0.5 %copy-done.5 = bf16[1,128,4,128]{3,2,1,0:T(4,128)(2,1)S(1)} copy-done((bf16[1,128,4,128]{3,2,1,0:T(4,128)(2,1)S(1)}, bf16[1,128,4,128]{3,2,1,0:T(4,128)(2,1)}, u32[]{:S(2)}) %copy-start.5) | copy-done | bytes 131096
  6.2 1.5 %collective-permute-start.2 = (bf16[4,128,128]{2,1,0:T(8,128)(2,1)S(1)}, bf16[4,128,128]{2,1,0:T(8,128)(2,1)S(1)}, u32[]{:S(2)}, u32[]{:S(2)}) collective-permute-start(bf16[4,128,128]{2,1,0:T(8,128)(2,1)S(1)} %bitcast.27), channel_id=1, source_target_pairs={{0,2},{1,3},{2,4},{3,5},{4,6},{5,7},{6,0},{7,1},{8,10},{9,11},{10,... | collective-permute-start | bytes 393224 | tf_op jit(solution)/shard_map/ppermute | solution.py:19
  7.8 0.0 copy-done
  7.8 0.0 copy-done.1
  7.8 0.0 copy-done.2
  7.8 0.0 copy-start.3
  7.8 1.4 %pull_kernel.1 = (bf16[4,1024,128]{2,1,0:T(8,128)(2,1)S(1)}, bf16[4,1024,128]{2,1,0:T(8,128)(2,1)S(1)}, f32[8,1024]{1,0:T(8,128)S(1)}, bf16[512,1024]{1,0:T(8,128)(2,1)S(1)}) custom-call(s32[8,1024]{1,0:T(8,128)S(1)} %get-tuple-element.46.refs_0_.refs_8_, bf16[128,32,128]{2,1,0:T(8,128)(2,1)S(1)} %bitcast.31, bf16[64,32,128]{2,1,0:T(8,128)(2,1)S(1)} %bitcast.33, ...), custom_call_target="tpu_custom_call" | custom-call | flops 1073741824 | bytes 4194304 | tf_op jit(solution)/shard_map/pull_kernel/pallas_call | solution.py:340
  9.2 0.0 collective-permute-done.refs_1_.refs_4_
  9.2 0.1 collective-permute-start.1
  9.3 0.0 copy-done.3
  9.3 0.8 %hidden_grad_kernel.1 = (bf16[4,1024,128]{2,1,0:T(8,128)(2,1)S(1)}, bf16[4,512,128]{2,1,0:T(8,128)(2,1)S(1)}) custom-call(s32[8,1024]{1,0:T(8,128)S(1)} %get-tuple-element.46.refs_0_.refs_8_, f32[8,1024]{1,0:T(8,128)S(1)} %get-tuple-element.52.refs_1_, bf16[4,1024,128]{2,1,0:T(8,128)(2,1)S(1)} %get-tuple-element.53.refs_2_.refs_6_, ...), custom_call_target="tpu_custom_call" | custom-call | flops 2147483648 | bytes 4194304 | tf_op jit(solution)/shard_map/hidden_grad_kernel/pallas_call | solution.py:340
  10.1 0.5 %collective-permute-done.1.refs_2_.refs_5_ = bf16[4,128,128]{2,1,0:T(8,128)(2,1)S(1)} collective-permute-done((bf16[4,128,128]{2,1,0:T(8,128)(2,1)S(1)}, bf16[4,128,128]{2,1,0:T(8,128)(2,1)S(1)}, u32[]{:S(2)}, u32[]{:S(2)}) %collective-permute-start.1) | collective-permute-done | bytes 131104 | tf_op jit(solution)/shard_map/ppermute | solution.py:29
  10.7 1.2 %score_kernel.2.refs_1_.refs_2_ = bf16[2,384,1024]{2,1,0:T(8,128)(2,1)S(1)} custom-call(bf16[4,1024,128]{2,1,0:T(8,128)(2,1)S(1)} %get-tuple-element.47.refs_0_, bf16[4,128,128]{2,1,0:T(8,128)(2,1)S(1)} %collective-permute-done.refs_1_.refs_4_, bf16[4,128,128]{2,1,0:T(8,128)(2,1)S(1)} %collective-permute-done.1.refs_2_.refs_5_, ...), custom_call_target="tpu_custom_call" | custom-call | flops 2147483648 | bytes 4194304 | tf_op jit(solution)/shard_map/score_kernel/pallas_call | solution.py:340
  11.8 0.3 collective-permute-done.2.refs_3_.refs_7_
  12.1 0.0 copy-start.4
  12.2 0.1 collective-permute-start.3
  12.2 1.2 %score_kernel.3.refs_2_.refs_3_ = bf16[2,384,1024]{2,1,0:T(8,128)(2,1)S(1)} custom-call(bf16[4,1024,128]{2,1,0:T(8,128)(2,1)S(1)} %get-tuple-element.47.refs_0_, bf16[4,128,128]{2,1,0:T(8,128)(2,1)S(1)} %collective-permute-done.refs_1_.refs_4_, bf16[4,128,128]{2,1,0:T(8,128)(2,1)S(1)} %collective-permute-done.1.refs_2_.refs_5_, ...), custom_call_target="tpu_custom_call" | custom-call | flops 2147483648 | bytes 4194304 | tf_op jit(solution)/shard_map/score_kernel/pallas_call | solution.py:340
  13.4 0.2 collective-permute-done.3.refs_4_.refs_8_
  13.6 0.0 copy-done.4
  13.6 2.7 %forward_kernel.1 = (bf16[16,128,128]{2,1,0:T(8,128)(2,1)S(1)}, bf16[16,128,128]{2,1,0:T(8,128)(2,1)S(1)}) custom-call(f32[4,16]{1,0:T(4,128)S(1)} %bitcast.36, bf16[2,384,1024]{2,1,0:T(8,128)(2,1)S(1)} %score_kernel.2.refs_1_.refs_2_, bf16[2,384,1024]{2,1,0:T(8,128)(2,1)S(1)} %score_kernel.3.refs_2_.refs_3_, ...), custom_call_target="tpu_custom_call" | custom-call | flops 4294967296 | bytes 10485760 | tf_op jit(solution)/shard_map/forward_kernel/pallas_call | solution.py:340
  16.3 0.4 %collective-permute-start.4 = (bf16[16,128,128]{2,1,0:T(8,128)(2,1)S(1)}, bf16[16,128,128]{2,1,0:T(8,128)(2,1)S(1)}, u32[]{:S(2)}, u32[]{:S(2)}) collective-permute-start(bf16[16,128,128]{2,1,0:T(8,128)(2,1)S(1)} %get-tuple-element.66), channel_id=1, source_target_pairs={{0,1},{1,0},{2,3},{3,2},{4,5},{5,4},{6,7},{7,6},{8,9},{9,8},{10,11... | collective-permute-start | bytes 1572872 | tf_op jit(solution)/shard_map/ppermute | solution.py:29
  16.7 1.6 %collective-permute-done.4 = bf16[16,128,128]{2,1,0:T(8,128)(2,1)S(1)} collective-permute-done((bf16[16,128,128]{2,1,0:T(8,128)(2,1)S(1)}, bf16[16,128,128]{2,1,0:T(8,128)(2,1)S(1)}, u32[]{:S(2)}, u32[]{:S(2)}) %collective-permute-start.4) | collective-permute-done | bytes 524320 | tf_op jit(solution)/shard_map/ppermute | solution.py:29
  18.3 0.1 add_convert_fusion
  18.5 2.4 %collective-permute-start.8 = (bf16[4,128,128]{2,1,0:T(8,128)(2,1)S(1)}, bf16[4,128,128]{2,1,0:T(8,128)(2,1)S(1)}, u32[]{:S(2)}, u32[]{:S(2)}) collective-permute-start(bf16[4,128,128]{2,1,0:T(8,128)(2,1)S(1)} %get-tuple-element.85), channel_id=1, source_target_pairs={{0,6},{1,7},{2,4},{3,5},{4,2},{5,3},{6,0},{7,1},{8,14},{9,15},{10,... | collective-permute-start | bytes 393224 | tf_op jit(solution)/shard_map/ppermute | solution.py:29
  20.9 0.3 collective-permute-start.7
  21.2 0.8 %collective-permute-start.6 = (bf16[4,128,128]{2,1,0:T(8,128)(2,1)S(1)}, bf16[4,128,128]{2,1,0:T(8,128)(2,1)S(1)}, u32[]{:S(2)}, u32[]{:S(2)}) collective-permute-start(bf16[4,128,128]{2,1,0:T(8,128)(2,1)S(1)} %get-tuple-element.87), channel_id=1, source_target_pairs={{0,2},{1,3},{2,0},{3,1},{4,6},{5,7},{6,4},{7,5},{8,10},{9,11},{10,... | collective-permute-start | bytes 393224 | tf_op jit(solution)/shard_map/ppermute | solution.py:29
  22.0 4.7 %backward_kernel.1 = (bf16[128,32,128]{2,1,0:T(8,128)(2,1)}, bf16[8,128,128]{2,1,0:T(8,128)(2,1)S(1)}, bf16[8,128,128]{2,1,0:T(8,128)(2,1)S(1)}, f32[8,128,128]{2,1,0:T(8,128)S(1)}) custom-call(bf16[4,1024,128]{2,1,0:T(8,128)(2,1)S(1)} %get-tuple-element.47.refs_0_, bf16[4,1024,128]{2,1,0:T(8,128)(2,1)S(1)} %get-tuple-element.55.refs_1_, ...), custom_call_target="tpu_custom_call" | custom-call | flops 4294967296 | bytes 10485760 | tf_op jit(solution)/shard_map/backward_kernel/pallas_call | solution.py:340
  26.7 0.1 collective-permute-start.5
  26.8 0.0 collective-permute-done.8
  26.8 1.2 %collective-permute-done.7 = bf16[4,128,128]{2,1,0:T(8,128)(2,1)S(1)} collective-permute-done((bf16[4,128,128]{2,1,0:T(8,128)(2,1)S(1)}, bf16[4,128,128]{2,1,0:T(8,128)(2,1)S(1)}, u32[]{:S(2)}, u32[]{:S(2)}) %collective-permute-start.7) | collective-permute-done | bytes 131104 | tf_op jit(solution)/shard_map/ppermute | solution.py:29
  28.0 0.1 collective-permute-done.6
  28.1 0.1 add_convert_fusion.2
  28.2 0.1 collective-permute-done.5.refs_1_
  28.3 0.1 add_convert_fusion.1
  28.4 2.4 %collective-permute-start.9 = (bf16[8,128,128]{2,1,0:T(8,128)(2,1)S(1)}, bf16[8,128,128]{2,1,0:T(8,128)(2,1)S(1)}, u32[]{:S(2)}, u32[]{:S(2)}) collective-permute-start(bf16[8,128,128]{2,1,0:T(8,128)(2,1)S(1)} %add_convert_fusion.1), channel_id=1, source_target_pairs={{0,6},{1,7},{2,0},{3,1},{4,2},{5,3},{6,4},{7,5},{8,14},{9,15},{10,... | collective-permute-start | bytes 786440 | tf_op jit(solution)/shard_map/ppermute | solution.py:19
  30.8 3.5 %collective-permute-start.12 = (bf16[1,128,128]{2,1,0:T(8,128)(2,1)S(1)}, bf16[1,128,128]{2,1,0:T(8,128)(2,1)S(1)}, u32[]{:S(2)}, u32[]{:S(2)}) collective-permute-start(bf16[1,128,128]{2,1,0:T(8,128)(2,1)S(1)} %get-tuple-element.88), channel_id=1, source_target_pairs={{0,24},{8,16},{16,8},{24,0},{1,25},{9,17},{17,9},{25,1},{2,26},{10... | collective-permute-start | bytes 98312 | tf_op jit(solution)/shard_map/ppermute | solution.py:29
  34.3 0.0 collective-permute-start.11
  34.3 0.9 %collective-permute-start.10 = (bf16[1,128,128]{2,1,0:T(8,128)(2,1)S(1)}, bf16[1,128,128]{2,1,0:T(8,128)(2,1)S(1)}, u32[]{:S(2)}, u32[]{:S(2)}) collective-permute-start(bf16[1,128,128]{2,1,0:T(8,128)(2,1)S(1)} %get-tuple-element.90), channel_id=1, source_target_pairs={{0,16},{8,24},{16,0},{24,8},{1,17},{9,25},{17,1},{25,9},{2,18},{10... | collective-permute-start | bytes 98312 | tf_op jit(solution)/shard_map/ppermute | solution.py:29
  35.3 1.3 %collective-permute-done.12.refs_6_ = bf16[1,128,128]{2,1,0:T(8,128)(2,1)S(1)} collective-permute-done((bf16[1,128,128]{2,1,0:T(8,128)(2,1)S(1)}, bf16[1,128,128]{2,1,0:T(8,128)(2,1)S(1)}, u32[]{:S(2)}, u32[]{:S(2)}) %collective-permute-start.12) | collective-permute-done | bytes 32800 | tf_op jit(solution)/shard_map/ppermute | solution.py:29
  36.6 1.7 %collective-permute-done.11.refs_5_ = bf16[1,128,128]{2,1,0:T(8,128)(2,1)S(1)} collective-permute-done((bf16[1,128,128]{2,1,0:T(8,128)(2,1)S(1)}, bf16[1,128,128]{2,1,0:T(8,128)(2,1)S(1)}, u32[]{:S(2)}, u32[]{:S(2)}) %collective-permute-start.11) | collective-permute-done | bytes 32800 | tf_op jit(solution)/shard_map/ppermute | solution.py:29
  38.3 1.0 %collective-permute-done.10.refs_4_ = bf16[1,128,128]{2,1,0:T(8,128)(2,1)S(1)} collective-permute-done((bf16[1,128,128]{2,1,0:T(8,128)(2,1)S(1)}, bf16[1,128,128]{2,1,0:T(8,128)(2,1)S(1)}, u32[]{:S(2)}, u32[]{:S(2)}) %collective-permute-start.10) | collective-permute-done | bytes 32800 | tf_op jit(solution)/shard_map/ppermute | solution.py:29
  39.3 0.0 collective-permute-done.9.refs_2_
  39.3 0.8 %finish_kernel.1 = (bf16[512,128]{1,0:T(8,128)(2,1)}, bf16[512,128]{1,0:T(8,128)(2,1)}, f32[16,4,128]{2,1,0:T(4,128)}, f32[16,4,128]{2,1,0:T(4,128)}) custom-call(f32[8,128,128]{2,1,0:T(8,128)S(1)} %get-tuple-element.69.refs_0_, bf16[8,128,128]{2,1,0:T(8,128)(2,1)S(1)} %collective-permute-done.5.refs_1_, ...), custom_call_target="tpu_custom_call" | custom-call | flops 1048576 | bytes 1048576 | tf_op jit(solution)/shard_map/finish_kernel/pallas_call | solution.py:340
  (5 shorter events, 0.1 us)
Async XLA Ops:
  1.6 7.6 %collective-permute-start = (bf16[4,128,128]{2,1,0:T(8,128)(2,1)S(1)}, bf16[4,128,128]{2,1,0:T(8,128)(2,1)S(1)}, u32[]{:S(2)}, u32[]{:S(2)}) collective-permute-start(bf16[4,128,128]{2,1,0:T(8,128)(2,1)S(1)} %bitcast.22), channel_id=1, source_target_pairs={{0,2},{1,3},{2,4},{3,5},{4,6},{5,7},{6,0},{7,1},{8,10},{9,11},{10,... | collective-permute-start | bytes 393224 | tf_op jit(solution)/shard_map/ppermute | solution.py:19
  5.3 0.9 %copy-start.5 = (bf16[1,128,4,128]{3,2,1,0:T(4,128)(2,1)S(1)}, bf16[1,128,4,128]{3,2,1,0:T(4,128)(2,1)}, u32[]{:S(2)}) copy-start(bf16[1,128,4,128]{3,2,1,0:T(4,128)(2,1)} %param.11) | copy-start | bytes 393220
  5.3 2.5 %copy-start = (bf16[1,128,32,128]{3,2,1,0:T(8,128)(2,1)S(1)}, bf16[1,128,32,128]{3,2,1,0:T(8,128)(2,1)}, u32[]{:S(2)}) copy-start(bf16[1,128,32,128]{3,2,1,0:T(8,128)(2,1)} %param.12) | copy-start | bytes 3145732
  5.3 2.5 %copy-start.1 = (bf16[1,128,32,128]{3,2,1,0:T(8,128)(2,1)S(1)}, bf16[1,128,32,128]{3,2,1,0:T(8,128)(2,1)}, u32[]{:S(2)}) copy-start(bf16[1,128,32,128]{3,2,1,0:T(8,128)(2,1)} %param.9) | copy-start | bytes 3145732
  5.3 2.4 %copy-start.2 = (bf16[16,4,32,128]{3,2,1,0:T(8,128)(2,1)S(1)}, bf16[16,4,32,128]{3,2,1,0:T(8,128)(2,1)}, u32[]{:S(2)}) copy-start(bf16[16,4,32,128]{3,2,1,0:T(8,128)(2,1)} %param.13) | copy-start | bytes 1572868
  6.2 5.9 %collective-permute-start.2 = (bf16[4,128,128]{2,1,0:T(8,128)(2,1)S(1)}, bf16[4,128,128]{2,1,0:T(8,128)(2,1)S(1)}, u32[]{:S(2)}, u32[]{:S(2)}) collective-permute-start(bf16[4,128,128]{2,1,0:T(8,128)(2,1)S(1)} %bitcast.27), channel_id=1, source_target_pairs={{0,2},{1,3},{2,4},{3,5},{4,6},{5,7},{6,0},{7,1},{8,10},{9,11},{10,... | collective-permute-start | bytes 393224 | tf_op jit(solution)/shard_map/ppermute | solution.py:19
  7.8 1.6 %copy-start.3 = (bf16[16,4,32,128]{3,2,1,0:T(8,128)(2,1)S(1)}, bf16[16,4,32,128]{3,2,1,0:T(8,128)(2,1)}, u32[]{:S(2)}) copy-start(bf16[16,4,32,128]{3,2,1,0:T(8,128)(2,1)} %param.14) | copy-start | bytes 1572868
  9.2 1.4 %collective-permute-start.1 = (bf16[4,128,128]{2,1,0:T(8,128)(2,1)S(1)}, bf16[4,128,128]{2,1,0:T(8,128)(2,1)S(1)}, u32[]{:S(2)}, u32[]{:S(2)}) collective-permute-start(bf16[4,128,128]{2,1,0:T(8,128)(2,1)S(1)} %broadcast_select_fusion.1), channel_id=1, source_target_pairs={{0,1},{1,0},{2,3},{3,2},{4,5},{5,4},{6,7},{7,6},{8,9},{9,8},{10,11... | collective-permute-start | bytes 393224 | tf_op jit(solution)/shard_map/ppermute | solution.py:29
  12.1 1.4 %copy-start.4 = (f32[16,4]{0,1:T(4,128)S(1)}, f32[16,4]{0,1:T(4,128)}, u32[]{:S(2)}) copy-start(f32[16,4]{0,1:T(4,128)} %param.15) | copy-start | bytes 772
  12.2 1.4 %collective-permute-start.3 = (bf16[4,128,128]{2,1,0:T(8,128)(2,1)S(1)}, bf16[4,128,128]{2,1,0:T(8,128)(2,1)S(1)}, u32[]{:S(2)}, u32[]{:S(2)}) collective-permute-start(bf16[4,128,128]{2,1,0:T(8,128)(2,1)S(1)} %broadcast_select_fusion), channel_id=1, source_target_pairs={{0,1},{1,0},{2,3},{3,2},{4,5},{5,4},{6,7},{7,6},{8,9},{9,8},{10,11... | collective-permute-start | bytes 393224 | tf_op jit(solution)/shard_map/ppermute | solution.py:29
  16.3 2.0 %collective-permute-start.4 = (bf16[16,128,128]{2,1,0:T(8,128)(2,1)S(1)}, bf16[16,128,128]{2,1,0:T(8,128)(2,1)S(1)}, u32[]{:S(2)}, u32[]{:S(2)}) collective-permute-start(bf16[16,128,128]{2,1,0:T(8,128)(2,1)S(1)} %get-tuple-element.66), channel_id=1, source_target_pairs={{0,1},{1,0},{2,3},{3,2},{4,5},{5,4},{6,7},{7,6},{8,9},{9,8},{10,11... | collective-permute-start | bytes 1572872 | tf_op jit(solution)/shard_map/ppermute | solution.py:29
  18.5 8.3 %collective-permute-start.8 = (bf16[4,128,128]{2,1,0:T(8,128)(2,1)S(1)}, bf16[4,128,128]{2,1,0:T(8,128)(2,1)S(1)}, u32[]{:S(2)}, u32[]{:S(2)}) collective-permute-start(bf16[4,128,128]{2,1,0:T(8,128)(2,1)S(1)} %get-tuple-element.85), channel_id=1, source_target_pairs={{0,6},{1,7},{2,4},{3,5},{4,2},{5,3},{6,0},{7,1},{8,14},{9,15},{10,... | collective-permute-start | bytes 393224 | tf_op jit(solution)/shard_map/ppermute | solution.py:29
  20.9 7.1 %collective-permute-start.7 = (bf16[4,128,128]{2,1,0:T(8,128)(2,1)S(1)}, bf16[4,128,128]{2,1,0:T(8,128)(2,1)S(1)}, u32[]{:S(2)}, u32[]{:S(2)}) collective-permute-start(bf16[4,128,128]{2,1,0:T(8,128)(2,1)S(1)} %get-tuple-element.86), channel_id=1, source_target_pairs={{0,4},{1,5},{2,6},{3,7},{4,0},{5,1},{6,2},{7,3},{8,12},{9,13},{10,... | collective-permute-start | bytes 393224 | tf_op jit(solution)/shard_map/ppermute | solution.py:29
  21.2 6.9 %collective-permute-start.6 = (bf16[4,128,128]{2,1,0:T(8,128)(2,1)S(1)}, bf16[4,128,128]{2,1,0:T(8,128)(2,1)S(1)}, u32[]{:S(2)}, u32[]{:S(2)}) collective-permute-start(bf16[4,128,128]{2,1,0:T(8,128)(2,1)S(1)} %get-tuple-element.87), channel_id=1, source_target_pairs={{0,2},{1,3},{2,0},{3,1},{4,6},{5,7},{6,4},{7,5},{8,10},{9,11},{10,... | collective-permute-start | bytes 393224 | tf_op jit(solution)/shard_map/ppermute | solution.py:29
  26.7 1.6 %collective-permute-start.5 = (bf16[8,128,128]{2,1,0:T(8,128)(2,1)S(1)}, bf16[8,128,128]{2,1,0:T(8,128)(2,1)S(1)}, u32[]{:S(2)}, u32[]{:S(2)}) collective-permute-start(bf16[8,128,128]{2,1,0:T(8,128)(2,1)S(1)} %get-tuple-element.70), channel_id=1, source_target_pairs={{0,1},{1,0},{2,3},{3,2},{4,5},{5,4},{6,7},{7,6},{8,9},{9,8},{10,11... | collective-permute-start | bytes 786440 | tf_op jit(solution)/shard_map/ppermute | solution.py:29
  28.4 10.9 %collective-permute-start.9 = (bf16[8,128,128]{2,1,0:T(8,128)(2,1)S(1)}, bf16[8,128,128]{2,1,0:T(8,128)(2,1)S(1)}, u32[]{:S(2)}, u32[]{:S(2)}) collective-permute-start(bf16[8,128,128]{2,1,0:T(8,128)(2,1)S(1)} %add_convert_fusion.1), channel_id=1, source_target_pairs={{0,6},{1,7},{2,0},{3,1},{4,2},{5,3},{6,4},{7,5},{8,14},{9,15},{10,... | collective-permute-start | bytes 786440 | tf_op jit(solution)/shard_map/ppermute | solution.py:19
  30.8 5.8 %collective-permute-start.12 = (bf16[1,128,128]{2,1,0:T(8,128)(2,1)S(1)}, bf16[1,128,128]{2,1,0:T(8,128)(2,1)S(1)}, u32[]{:S(2)}, u32[]{:S(2)}) collective-permute-start(bf16[1,128,128]{2,1,0:T(8,128)(2,1)S(1)} %get-tuple-element.88), channel_id=1, source_target_pairs={{0,24},{8,16},{16,8},{24,0},{1,25},{9,17},{17,9},{25,1},{2,26},{10... | collective-permute-start | bytes 98312 | tf_op jit(solution)/shard_map/ppermute | solution.py:29
  34.3 3.9 %collective-permute-start.11 = (bf16[1,128,128]{2,1,0:T(8,128)(2,1)S(1)}, bf16[1,128,128]{2,1,0:T(8,128)(2,1)S(1)}, u32[]{:S(2)}, u32[]{:S(2)}) collective-permute-start(bf16[1,128,128]{2,1,0:T(8,128)(2,1)S(1)} %get-tuple-element.89), channel_id=1, source_target_pairs={{0,8},{8,0},{16,24},{24,16},{1,9},{9,1},{17,25},{25,17},{2,10},{10... | collective-permute-start | bytes 98312 | tf_op jit(solution)/shard_map/ppermute | solution.py:29
  34.3 5.0 %collective-permute-start.10 = (bf16[1,128,128]{2,1,0:T(8,128)(2,1)S(1)}, bf16[1,128,128]{2,1,0:T(8,128)(2,1)S(1)}, u32[]{:S(2)}, u32[]{:S(2)}) collective-permute-start(bf16[1,128,128]{2,1,0:T(8,128)(2,1)S(1)} %get-tuple-element.90), channel_id=1, source_target_pairs={{0,16},{8,24},{16,0},{24,8},{1,17},{9,25},{17,1},{25,9},{2,18},{10... | collective-permute-start | bytes 98312 | tf_op jit(solution)/shard_map/ppermute | solution.py:29

commit v13 on v12

--- a/solution.py
+++ b/solution.py
@@ -258,15 +258,14 @@
 
 
 def backward_kernel(
-    queries_ref, gh_ref, near_ref, far_ref, two_keys, one_keys, own_keys, two_values, one_values, own_values,
-    dq_hbm, back_two_ref, back_one_ref, back_own_ref, dq_ref, sems, *, kv, group, scaling,
-):
-    tokens, dim = own_keys.shape[1:]
+    queries_ref, gh_ref, near_ref, far_ref, two_ref, one_ref, own_ref,
+    back_two_ref, back_one_ref, back_own_ref, grad_ref, *, kv, scaling,
+):
+    tokens = own_ref.shape[1]
 
     def weight_grad_of(g):
-        return dot(window_of(two_values, one_values, own_values, g), gh_ref[g], 1, 1)
-
-    copies = []
+        return dot(window_of(two_ref, one_ref, own_ref, g), gh_ref[g], 1, 1)
+
     weight_grad = weight_grad_of(0)
     for g in range(kv):
         ahead = weight_grad_of(g + 1) if g + 1 < kv else None
@@ -274,13 +273,7 @@
         weights = low.astype(WIDE)
         delta = jnp.sum(weights * weight_grad, axis=0, keepdims=True)
         score_grad = (weights * (weight_grad - delta)).astype(LOW)
-        query_grad = (dot(window_of(two_keys, one_keys, own_keys, g), score_grad, 0, 0) * scaling).T.reshape(tokens, group, dim)
-        if g % 2 == 1:
-            heads = slice((g - 1) * group, (g + 1) * group)
-            dq_ref[:, heads, :] = jnp.concatenate([before, query_grad], axis=1).astype(LOW)
-            copies.append(pltpu.make_async_copy(dq_ref.at[:, heads], dq_hbm.at[:, heads], sems.at[g // 2]))
-            copies[-1].start()
-        before = query_grad
+        grad_ref[g] = score_grad
         key_grad = dot(score_grad, queries_ref[g], 1, 0) * scaling
         value_grad = dot(low, gh_ref[g], 1, 0)
         for place, grad in ((g, key_grad), (kv + g, value_grad)):
@@ -288,6 +281,22 @@
             back_one_ref[place] = grad[tokens : 2 * tokens].astype(LOW)
             back_own_ref[place] = grad[2 * tokens :]
         weight_grad = ahead
+
+
+def query_kernel(
+    grad_ref, two_ref, one_ref, own_ref, dq_hbm, dq_ref, sems, *, kv, group, scaling,
+):
+    tokens, dim = own_ref.shape[1:]
+    copies = []
+    for g in range(kv):
+        query_grad = dot(window_of(two_ref, one_ref, own_ref, g), grad_ref[g], 0, 0) * scaling
+        query_grad = query_grad.T.reshape(tokens, group, dim)
+        if g % 2 == 1:
+            heads = slice((g - 1) * group, (g + 1) * group)
+            dq_ref[:, heads, :] = jnp.concatenate([before, query_grad], axis=1).astype(LOW)
+            copies.append(pltpu.make_async_copy(dq_ref.at[:, heads], dq_hbm.at[:, heads], sems.at[g // 2]))
+            copies[-1].start()
+        before = query_grad
     for copy in copies:
         copy.wait()
 
@@ -394,17 +403,15 @@
     part = (keep.astype(WIDE) + exchanged(send, {"ctx": 1}).astype(WIDE)).astype(LOW)
     near, part = lax.optimization_barrier((near, part))
     window = (2 * kv, tokens, dim)
-    d_queries, back_two, back_one, back_own = call(
-        backward_kernel,
-        [((tokens, heads, dim), LOW), (window, LOW), (window, LOW), (window, WIDE)],
-        4 * 2**30, 10 * 2**20,
-        scratch=[
-            pltpu.VMEM((tokens, heads, dim), LOW), pltpu.SemaphoreType.DMA((kv // 2,)),
-        ],
-        out_specs=[pl.BlockSpec(memory_space=pltpu.HBM), vmem, vmem, vmem], scaling=scaling, **sizes,
-    )(
-        queries, grad_hidden, near, far, two_keys, one_keys, own_keys, two_values, one_values, own_values,
-    )
+    back_two, back_one, back_own, score_grad = call(
+        backward_kernel, [(window, LOW), (window, LOW), (window, WIDE), ((kv, 3 * tokens, lanes), LOW)],
+        4 * 2**30, 10 * 2**20, kv=kv, scaling=scaling,
+    )(queries, grad_hidden, near, far, two_values, one_values, own_values)
+    d_queries, = call(
+        query_kernel, [((tokens, heads, dim), LOW)], 2 * 2**30, 5 * 2**20,
+        scratch=[pltpu.VMEM((tokens, heads, dim), LOW), pltpu.SemaphoreType.DMA((kv // 2,))],
+        out_specs=[pl.BlockSpec(memory_space=pltpu.HBM)], scaling=scaling, **sizes,
+    )(score_grad, two_keys, one_keys, own_keys)
     from_mate = exchanged(back_one, {"ctx": 1})
     onward = back_two.astype(WIDE) + jnp.where(even, 0.0, from_mate.astype(WIDE))
     onward = onward.astype(LOW)

time: 40.4 us -> 39.5 us (0.978)
  starting transfers between devices: 15.6 us -> 14.9 us
    ppermute x3, starting transfers between devices: 6.92 us -> 6.24 us  [shifted(): lax.ppermute(value, axis, [(source, (source + steps) % count) for source...]
    pallas_call x8 -> x9, Pallas kernels: 13.1 us -> 13.4 us  [run(): pl.pallas_call(lambda *refs: body(*refs, **fixed), out_shape=[jax.ShapeDt...]
  transfers between devices with their start and end apart: 13 -> 13, of which waited for: 10 -> 9; matrix products, arithmetic and copies ran while one was open for 2% -> 2% of each run, Pallas kernels for 24% -> 25%
where the time goes in v13:
time: 39.5 us; the launch traced here: 39.3 us
  starting transfers between devices  14.9 us (38%)
  Pallas kernels  13.4 us (34%)
  waiting for transfers between devices  7.67 us (19%)
  local copies, waits for them, and re-layouts  1.52 us (4%)
  other arithmetic  1.05 us (3%)
  between operations  0.87 us (2%)
    pallas_call x9, Pallas kernels, run(): pl.pallas_call(lambda *refs: body(*refs, **fixed), out_shape=[jax.ShapeDt...  13.4 us
    ppermute x10, starting transfers between devices, exchanged(): lax.ppermute(value, axes, [(int(source), int(target)) for source, target...  8.63 us
    ppermute x10, waiting for transfers between devices, exchanged(): lax.ppermute(value, axes, [(int(source), int(target)) for source, target...  7.34 us
    ppermute x3, starting transfers between devices, shifted(): lax.ppermute(value, axis, [(source, (source + steps) % count) for source...  6.24 us
    optimization_barrier x1, local copies, waits for them, and re-layouts, on_device(): key_rows, even = lax.optimization_barrier((key_rows, even))  0.92 us
  transfers between devices with their start and end apart: 13, of which 9 were waited for; matrix products, arithmetic and copies ran while one was open for 2% of the time, Pallas kernels for 25%

profile of v13, /device:TPU:0, one launch (start us, length us, event | category | flops | bytes accessed | tf_op | source)
XLA Modules:
  0.0 39.3 jit_solution(3625028263743696215)
XLA Ops:
  0.6 0.9 %copy.18 = bf16[1,128,4,128]{3,1,2,0:T(8,128)(2,1)S(1)} copy(bf16[1,128,4,128]{3,2,1,0:T(4,128)(2,1)} %param.10) | data formatting | bytes 262144 | tf_op jit(solution)/shard_map/optimization_barrier | solution.py:366
  1.6 3.0 %collective-permute-start = (bf16[4,128,128]{2,1,0:T(8,128)(2,1)S(1)}, bf16[4,128,128]{2,1,0:T(8,128)(2,1)S(1)}, u32[]{:S(2)}, u32[]{:S(2)}) collective-permute-start(bf16[4,128,128]{2,1,0:T(8,128)(2,1)S(1)} %bitcast.22), channel_id=1, source_target_pairs={{0,2},{1,3},{2,4},{3,5},{4,6},{5,7},{6,0},{7,1},{8,10},{9,11},{10,... | collective-permute-start | bytes 393224 | tf_op jit(solution)/shard_map/ppermute | solution.py:19
  4.6 0.7 %pad_add_fusion.refs_0_ = s32[2,1024]{1,0:T(2,128)S(1)} fusion(s32[1,1024]{1,0:T(1,128)} %param.17, s32[1,1024]{1,0:T(1,128)} %param.16), kind=kLoop, calls=%fused_computation.7 | loop fusion | flops 2048 | bytes 16384 | tf_op jit(solution)/shard_map/concatenate | solution.py:372
  5.3 0.0 copy-start.5
  5.3 0.0 copy-start
  5.3 0.0 copy-start.1
  5.3 0.0 copy-start.2
  5.3 0.3 place_kernel.1
  5.7 0.5 %copy-done.5 = bf16[1,128,4,128]{3,2,1,0:T(4,128)(2,1)S(1)} copy-done((bf16[1,128,4,128]{3,2,1,0:T(4,128)(2,1)S(1)}, bf16[1,128,4,128]{3,2,1,0:T(4,128)(2,1)}, u32[]{:S(2)}) %copy-start.5) | copy-done | bytes 131096
  6.2 1.5 %collective-permute-start.2 = (bf16[4,128,128]{2,1,0:T(8,128)(2,1)S(1)}, bf16[4,128,128]{2,1,0:T(8,128)(2,1)S(1)}, u32[]{:S(2)}, u32[]{:S(2)}) collective-permute-start(bf16[4,128,128]{2,1,0:T(8,128)(2,1)S(1)} %bitcast.27), channel_id=1, source_target_pairs={{0,2},{1,3},{2,4},{3,5},{4,6},{5,7},{6,0},{7,1},{8,10},{9,11},{10,... | collective-permute-start | bytes 393224 | tf_op jit(solution)/shard_map/ppermute | solution.py:19
  7.8 0.0 copy-done
  7.8 0.0 copy-done.1
  7.8 0.0 copy-done.2
  7.8 0.0 copy-start.3
  7.8 1.4 %pull_kernel.1 = (bf16[4,1024,128]{2,1,0:T(8,128)(2,1)S(1)}, bf16[4,1024,128]{2,1,0:T(8,128)(2,1)S(1)}, f32[8,1024]{1,0:T(8,128)S(1)}, bf16[512,1024]{1,0:T(8,128)(2,1)S(1)}) custom-call(s32[8,1024]{1,0:T(8,128)S(1)} %get-tuple-element.46.refs_0_.refs_8_, bf16[128,32,128]{2,1,0:T(8,128)(2,1)S(1)} %bitcast.31, bf16[64,32,128]{2,1,0:T(8,128)(2,1)S(1)} %bitcast.33, ...), custom_call_target="tpu_custom_call" | custom-call | flops 1073741824 | bytes 4194304 | tf_op jit(solution)/shard_map/pull_kernel/pallas_call | solution.py:349
  9.2 0.0 collective-permute-done.refs_1_
  9.2 0.1 collective-permute-start.1
  9.3 0.0 copy-done.3
  9.3 0.8 %hidden_grad_kernel.1 = (bf16[4,1024,128]{2,1,0:T(8,128)(2,1)S(1)}, bf16[4,512,128]{2,1,0:T(8,128)(2,1)S(1)}) custom-call(s32[8,1024]{1,0:T(8,128)S(1)} %get-tuple-element.46.refs_0_.refs_8_, f32[8,1024]{1,0:T(8,128)S(1)} %get-tuple-element.52.refs_1_, bf16[4,1024,128]{2,1,0:T(8,128)(2,1)S(1)} %get-tuple-element.53.refs_2_.refs_6_, ...), custom_call_target="tpu_custom_call" | custom-call | flops 2147483648 | bytes 4194304 | tf_op jit(solution)/shard_map/hidden_grad_kernel/pallas_call | solution.py:349
  10.1 0.5 %collective-permute-done.1.refs_2_ = bf16[4,128,128]{2,1,0:T(8,128)(2,1)S(1)} collective-permute-done((bf16[4,128,128]{2,1,0:T(8,128)(2,1)S(1)}, bf16[4,128,128]{2,1,0:T(8,128)(2,1)S(1)}, u32[]{:S(2)}, u32[]{:S(2)}) %collective-permute-start.1) | collective-permute-done | bytes 131104 | tf_op jit(solution)/shard_map/ppermute | solution.py:29
  10.6 1.2 %score_kernel.2.refs_1_.refs_2_ = bf16[2,384,1024]{2,1,0:T(8,128)(2,1)S(1)} custom-call(bf16[4,1024,128]{2,1,0:T(8,128)(2,1)S(1)} %get-tuple-element.47.refs_0_, bf16[4,128,128]{2,1,0:T(8,128)(2,1)S(1)} %collective-permute-done.refs_1_, bf16[4,128,128]{2,1,0:T(8,128)(2,1)S(1)} %collective-permute-done.1.refs_2_, bf16[4,128,128]{2,1,0:T(8,128)(2,1)S(1)} %bitcast.24, ...), custom_call_target="tpu_custom_call" | custom-call | flops 2147483648 | bytes 4194304 | tf_op jit(solution)/shard_map/score_kernel/pallas_call | solution.py:349
  11.8 0.3 collective-permute-done.2.refs_3_.refs_4_
  12.1 0.0 copy-start.4
  12.2 0.1 collective-permute-start.3
  12.2 1.2 %score_kernel.3.refs_2_.refs_3_ = bf16[2,384,1024]{2,1,0:T(8,128)(2,1)S(1)} custom-call(bf16[4,1024,128]{2,1,0:T(8,128)(2,1)S(1)} %get-tuple-element.47.refs_0_, bf16[4,128,128]{2,1,0:T(8,128)(2,1)S(1)} %collective-permute-done.refs_1_, bf16[4,128,128]{2,1,0:T(8,128)(2,1)S(1)} %collective-permute-done.1.refs_2_, bf16[4,128,128]{2,1,0:T(8,128)(2,1)S(1)} %bitcast.25, ...), custom_call_target="tpu_custom_call" | custom-call | flops 2147483648 | bytes 4194304 | tf_op jit(solution)/shard_map/score_kernel/pallas_call | solution.py:349
  13.4 0.2 collective-permute-done.3.refs_4_.refs_5_
  13.6 0.0 copy-done.4
  13.6 2.7 %forward_kernel.1 = (bf16[16,128,128]{2,1,0:T(8,128)(2,1)S(1)}, bf16[16,128,128]{2,1,0:T(8,128)(2,1)S(1)}) custom-call(f32[4,16]{1,0:T(4,128)S(1)} %bitcast.36, bf16[2,384,1024]{2,1,0:T(8,128)(2,1)S(1)} %score_kernel.2.refs_1_.refs_2_, bf16[2,384,1024]{2,1,0:T(8,128)(2,1)S(1)} %score_kernel.3.refs_2_.refs_3_, ...), custom_call_target="tpu_custom_call" | custom-call | flops 4294967296 | bytes 10485760 | tf_op jit(solution)/shard_map/forward_kernel/pallas_call | solution.py:349
  16.3 0.4 %collective-permute-start.4 = (bf16[16,128,128]{2,1,0:T(8,128)(2,1)S(1)}, bf16[16,128,128]{2,1,0:T(8,128)(2,1)S(1)}, u32[]{:S(2)}, u32[]{:S(2)}) collective-permute-start(bf16[16,128,128]{2,1,0:T(8,128)(2,1)S(1)} %get-tuple-element.66), channel_id=1, source_target_pairs={{0,1},{1,0},{2,3},{3,2},{4,5},{5,4},{6,7},{7,6},{8,9},{9,8},{10,11... | collective-permute-start | bytes 1572872 | tf_op jit(solution)/shard_map/ppermute | solution.py:29
  16.7 1.6 %collective-permute-done.4 = bf16[16,128,128]{2,1,0:T(8,128)(2,1)S(1)} collective-permute-done((bf16[16,128,128]{2,1,0:T(8,128)(2,1)S(1)}, bf16[16,128,128]{2,1,0:T(8,128)(2,1)S(1)}, u32[]{:S(2)}, u32[]{:S(2)}) %collective-permute-start.4) | collective-permute-done | bytes 524320 | tf_op jit(solution)/shard_map/ppermute | solution.py:29
  18.3 0.1 add_convert_fusion
  18.5 2.4 %collective-permute-start.8 = (bf16[4,128,128]{2,1,0:T(8,128)(2,1)S(1)}, bf16[4,128,128]{2,1,0:T(8,128)(2,1)S(1)}, u32[]{:S(2)}, u32[]{:S(2)}) collective-permute-start(bf16[4,128,128]{2,1,0:T(8,128)(2,1)S(1)} %get-tuple-element.85), channel_id=1, source_target_pairs={{0,6},{1,7},{2,4},{3,5},{4,2},{5,3},{6,0},{7,1},{8,14},{9,15},{10,... | collective-permute-start | bytes 393224 | tf_op jit(solution)/shard_map/ppermute | solution.py:29
  20.9 0.3 collective-permute-start.7
  21.2 0.8 %collective-permute-start.6 = (bf16[4,128,128]{2,1,0:T(8,128)(2,1)S(1)}, bf16[4,128,128]{2,1,0:T(8,128)(2,1)S(1)}, u32[]{:S(2)}, u32[]{:S(2)}) collective-permute-start(bf16[4,128,128]{2,1,0:T(8,128)(2,1)S(1)} %get-tuple-element.87), channel_id=1, source_target_pairs={{0,2},{1,3},{2,0},{3,1},{4,6},{5,7},{6,4},{7,5},{8,10},{9,11},{10,... | collective-permute-start | bytes 393224 | tf_op jit(solution)/shard_map/ppermute | solution.py:29
  22.0 3.3 %backward_kernel.1 = (bf16[8,128,128]{2,1,0:T(8,128)(2,1)S(1)}, bf16[8,128,128]{2,1,0:T(8,128)(2,1)S(1)}, f32[8,128,128]{2,1,0:T(8,128)S(1)}, bf16[4,384,1024]{2,1,0:T(8,128)(2,1)S(1)}) custom-call(bf16[4,1024,128]{2,1,0:T(8,128)(2,1)S(1)} %get-tuple-element.47.refs_0_, bf16[4,1024,128]{2,1,0:T(8,128)(2,1)S(1)} %get-tuple-element.55.refs_1_, ...), custom_call_target="tpu_custom_call" | custom-call | flops 4294967296 | bytes 10485760 | tf_op jit(solution)/shard_map/backward_kernel/pallas_call | solution.py:349
  25.4 0.1 collective-permute-start.5
  25.4 0.2 collective-permute-done.8
  25.6 2.4 %collective-permute-done.7 = bf16[4,128,128]{2,1,0:T(8,128)(2,1)S(1)} collective-permute-done((bf16[4,128,128]{2,1,0:T(8,128)(2,1)S(1)}, bf16[4,128,128]{2,1,0:T(8,128)(2,1)S(1)}, u32[]{:S(2)}, u32[]{:S(2)}) %collective-permute-start.7) | collective-permute-done | bytes 131104 | tf_op jit(solution)/shard_map/ppermute | solution.py:29
  28.0 0.1 collective-permute-done.6
  28.1 0.1 add_convert_fusion.2
  28.2 0.0 collective-permute-done.5.refs_1_
  28.2 0.1 add_convert_fusion.1
  28.3 1.7 %collective-permute-start.9 = (bf16[8,128,128]{2,1,0:T(8,128)(2,1)S(1)}, bf16[8,128,128]{2,1,0:T(8,128)(2,1)S(1)}, u32[]{:S(2)}, u32[]{:S(2)}) collective-permute-start(bf16[8,128,128]{2,1,0:T(8,128)(2,1)S(1)} %add_convert_fusion.1), channel_id=1, source_target_pairs={{0,6},{1,7},{2,0},{3,1},{4,2},{5,3},{6,4},{7,5},{8,14},{9,15},{10,... | collective-permute-start | bytes 786440 | tf_op jit(solution)/shard_map/ppermute | solution.py:19
  30.0 3.7 %collective-permute-start.12 = (bf16[1,128,128]{2,1,0:T(8,128)(2,1)S(1)}, bf16[1,128,128]{2,1,0:T(8,128)(2,1)S(1)}, u32[]{:S(2)}, u32[]{:S(2)}) collective-permute-start(bf16[1,128,128]{2,1,0:T(8,128)(2,1)S(1)} %get-tuple-element.88), channel_id=1, source_target_pairs={{0,24},{8,16},{16,8},{24,0},{1,25},{9,17},{17,9},{25,1},{2,26},{10... | collective-permute-start | bytes 98312 | tf_op jit(solution)/shard_map/ppermute | solution.py:29
  33.7 0.0 collective-permute-start.11
  33.7 0.8 %collective-permute-start.10 = (bf16[1,128,128]{2,1,0:T(8,128)(2,1)S(1)}, bf16[1,128,128]{2,1,0:T(8,128)(2,1)S(1)}, u32[]{:S(2)}, u32[]{:S(2)}) collective-permute-start(bf16[1,128,128]{2,1,0:T(8,128)(2,1)S(1)} %get-tuple-element.90), channel_id=1, source_target_pairs={{0,16},{8,24},{16,0},{24,8},{1,17},{9,25},{17,1},{25,9},{2,18},{10... | collective-permute-start | bytes 98312 | tf_op jit(solution)/shard_map/ppermute | solution.py:29
  34.5 1.6 %query_kernel.1 = bf16[128,32,128]{2,1,0:T(8,128)(2,1)} custom-call(bf16[4,384,1024]{2,1,0:T(8,128)(2,1)S(1)} %get-tuple-element.68.refs_0_, bf16[4,128,128]{2,1,0:T(8,128)(2,1)S(1)} %collective-permute-done.refs_1_, bf16[4,128,128]{2,1,0:T(8,128)(2,1)S(1)} %collective-permute-done.1.refs_2_, bf16[4,128,128]{2,1,0:T(8,128)(2,1)S(1)} %bitcast.26), custom_call_target="tpu_custom_call" | custom-call | flops 2147483648 | bytes 5242880 | tf_op jit(solution)/shard_map/query_kernel/pallas_call | solution.py:349
  36.1 0.0 collective-permute-done.12.refs_6_
  36.1 1.5 %collective-permute-done.11.refs_5_ = bf16[1,128,128]{2,1,0:T(8,128)(2,1)S(1)} collective-permute-done((bf16[1,128,128]{2,1,0:T(8,128)(2,1)S(1)}, bf16[1,128,128]{2,1,0:T(8,128)(2,1)S(1)}, u32[]{:S(2)}, u32[]{:S(2)}) %collective-permute-start.11) | collective-permute-done | bytes 32800 | tf_op jit(solution)/shard_map/ppermute | solution.py:29
  37.6 0.9 %collective-permute-done.10.refs_4_ = bf16[1,128,128]{2,1,0:T(8,128)(2,1)S(1)} collective-permute-done((bf16[1,128,128]{2,1,0:T(8,128)(2,1)S(1)}, bf16[1,128,128]{2,1,0:T(8,128)(2,1)S(1)}, u32[]{:S(2)}, u32[]{:S(2)}) %collective-permute-start.10) | collective-permute-done | bytes 32800 | tf_op jit(solution)/shard_map/ppermute | solution.py:29
  38.5 0.0 collective-permute-done.9.refs_2_
  38.5 0.8 %finish_kernel.1 = (bf16[512,128]{1,0:T(8,128)(2,1)}, bf16[512,128]{1,0:T(8,128)(2,1)}, f32[16,4,128]{2,1,0:T(4,128)}, f32[16,4,128]{2,1,0:T(4,128)}) custom-call(f32[8,128,128]{2,1,0:T(8,128)S(1)} %get-tuple-element.69.refs_0_, bf16[8,128,128]{2,1,0:T(8,128)(2,1)S(1)} %collective-permute-done.5.refs_1_, ...), custom_call_target="tpu_custom_call" | custom-call | flops 1048576 | bytes 1048576 | tf_op jit(solution)/shard_map/finish_kernel/pallas_call | solution.py:349
  (5 shorter events, 0.1 us)
Async XLA Ops:
  1.6 7.6 %collective-permute-start = (bf16[4,128,128]{2,1,0:T(8,128)(2,1)S(1)}, bf16[4,128,128]{2,1,0:T(8,128)(2,1)S(1)}, u32[]{:S(2)}, u32[]{:S(2)}) collective-permute-start(bf16[4,128,128]{2,1,0:T(8,128)(2,1)S(1)} %bitcast.22), channel_id=1, source_target_pairs={{0,2},{1,3},{2,4},{3,5},{4,6},{5,7},{6,0},{7,1},{8,10},{9,11},{10,... | collective-permute-start | bytes 393224 | tf_op jit(solution)/shard_map/ppermute | solution.py:19
  5.3 0.9 %copy-start.5 = (bf16[1,128,4,128]{3,2,1,0:T(4,128)(2,1)S(1)}, bf16[1,128,4,128]{3,2,1,0:T(4,128)(2,1)}, u32[]{:S(2)}) copy-start(bf16[1,128,4,128]{3,2,1,0:T(4,128)(2,1)} %param.11) | copy-start | bytes 393220
  5.3 2.5 %copy-start = (bf16[1,128,32,128]{3,2,1,0:T(8,128)(2,1)S(1)}, bf16[1,128,32,128]{3,2,1,0:T(8,128)(2,1)}, u32[]{:S(2)}) copy-start(bf16[1,128,32,128]{3,2,1,0:T(8,128)(2,1)} %param.12) | copy-start | bytes 3145732
  5.3 2.5 %copy-start.1 = (bf16[1,128,32,128]{3,2,1,0:T(8,128)(2,1)S(1)}, bf16[1,128,32,128]{3,2,1,0:T(8,128)(2,1)}, u32[]{:S(2)}) copy-start(bf16[1,128,32,128]{3,2,1,0:T(8,128)(2,1)} %param.9) | copy-start | bytes 3145732
  5.3 2.4 %copy-start.2 = (bf16[16,4,32,128]{3,2,1,0:T(8,128)(2,1)S(1)}, bf16[16,4,32,128]{3,2,1,0:T(8,128)(2,1)}, u32[]{:S(2)}) copy-start(bf16[16,4,32,128]{3,2,1,0:T(8,128)(2,1)} %param.13) | copy-start | bytes 1572868
  6.2 5.9 %collective-permute-start.2 = (bf16[4,128,128]{2,1,0:T(8,128)(2,1)S(1)}, bf16[4,128,128]{2,1,0:T(8,128)(2,1)S(1)}, u32[]{:S(2)}, u32[]{:S(2)}) collective-permute-start(bf16[4,128,128]{2,1,0:T(8,128)(2,1)S(1)} %bitcast.27), channel_id=1, source_target_pairs={{0,2},{1,3},{2,4},{3,5},{4,6},{5,7},{6,0},{7,1},{8,10},{9,11},{10,... | collective-permute-start | bytes 393224 | tf_op jit(solution)/shard_map/ppermute | solution.py:19
  7.8 1.5 %copy-start.3 = (bf16[16,4,32,128]{3,2,1,0:T(8,128)(2,1)S(1)}, bf16[16,4,32,128]{3,2,1,0:T(8,128)(2,1)}, u32[]{:S(2)}) copy-start(bf16[16,4,32,128]{3,2,1,0:T(8,128)(2,1)} %param.14) | copy-start | bytes 1572868
  9.2 1.4 %collective-permute-start.1 = (bf16[4,128,128]{2,1,0:T(8,128)(2,1)S(1)}, bf16[4,128,128]{2,1,0:T(8,128)(2,1)S(1)}, u32[]{:S(2)}, u32[]{:S(2)}) collective-permute-start(bf16[4,128,128]{2,1,0:T(8,128)(2,1)S(1)} %broadcast_select_fusion.1), channel_id=1, source_target_pairs={{0,1},{1,0},{2,3},{3,2},{4,5},{5,4},{6,7},{7,6},{8,9},{9,8},{10,11... | collective-permute-start | bytes 393224 | tf_op jit(solution)/shard_map/ppermute | solution.py:29
  12.1 1.4 %copy-start.4 = (f32[16,4]{0,1:T(4,128)S(1)}, f32[16,4]{0,1:T(4,128)}, u32[]{:S(2)}) copy-start(f32[16,4]{0,1:T(4,128)} %param.15) | copy-start | bytes 772
  12.2 1.4 %collective-permute-start.3 = (bf16[4,128,128]{2,1,0:T(8,128)(2,1)S(1)}, bf16[4,128,128]{2,1,0:T(8,128)(2,1)S(1)}, u32[]{:S(2)}, u32[]{:S(2)}) collective-permute-start(bf16[4,128,128]{2,1,0:T(8,128)(2,1)S(1)} %broadcast_select_fusion), channel_id=1, source_target_pairs={{0,1},{1,0},{2,3},{3,2},{4,5},{5,4},{6,7},{7,6},{8,9},{9,8},{10,11... | collective-permute-start | bytes 393224 | tf_op jit(solution)/shard_map/ppermute | solution.py:29
  16.3 2.0 %collective-permute-start.4 = (bf16[16,128,128]{2,1,0:T(8,128)(2,1)S(1)}, bf16[16,128,128]{2,1,0:T(8,128)(2,1)S(1)}, u32[]{:S(2)}, u32[]{:S(2)}) collective-permute-start(bf16[16,128,128]{2,1,0:T(8,128)(2,1)S(1)} %get-tuple-element.66), channel_id=1, source_target_pairs={{0,1},{1,0},{2,3},{3,2},{4,5},{5,4},{6,7},{7,6},{8,9},{9,8},{10,11... | collective-permute-start | bytes 1572872 | tf_op jit(solution)/shard_map/ppermute | solution.py:29
  18.5 7.1 %collective-permute-start.8 = (bf16[4,128,128]{2,1,0:T(8,128)(2,1)S(1)}, bf16[4,128,128]{2,1,0:T(8,128)(2,1)S(1)}, u32[]{:S(2)}, u32[]{:S(2)}) collective-permute-start(bf16[4,128,128]{2,1,0:T(8,128)(2,1)S(1)} %get-tuple-element.85), channel_id=1, source_target_pairs={{0,6},{1,7},{2,4},{3,5},{4,2},{5,3},{6,0},{7,1},{8,14},{9,15},{10,... | collective-permute-start | bytes 393224 | tf_op jit(solution)/shard_map/ppermute | solution.py:29
  20.9 7.1 %collective-permute-start.7 = (bf16[4,128,128]{2,1,0:T(8,128)(2,1)S(1)}, bf16[4,128,128]{2,1,0:T(8,128)(2,1)S(1)}, u32[]{:S(2)}, u32[]{:S(2)}) collective-permute-start(bf16[4,128,128]{2,1,0:T(8,128)(2,1)S(1)} %get-tuple-element.86), channel_id=1, source_target_pairs={{0,4},{1,5},{2,6},{3,7},{4,0},{5,1},{6,2},{7,3},{8,12},{9,13},{10,... | collective-permute-start | bytes 393224 | tf_op jit(solution)/shard_map/ppermute | solution.py:29
  21.2 6.9 %collective-permute-start.6 = (bf16[4,128,128]{2,1,0:T(8,128)(2,1)S(1)}, bf16[4,128,128]{2,1,0:T(8,128)(2,1)S(1)}, u32[]{:S(2)}, u32[]{:S(2)}) collective-permute-start(bf16[4,128,128]{2,1,0:T(8,128)(2,1)S(1)} %get-tuple-element.87), channel_id=1, source_target_pairs={{0,2},{1,3},{2,0},{3,1},{4,6},{5,7},{6,4},{7,5},{8,10},{9,11},{10,... | collective-permute-start | bytes 393224 | tf_op jit(solution)/shard_map/ppermute | solution.py:29
  25.4 2.8 %collective-permute-start.5 = (bf16[8,128,128]{2,1,0:T(8,128)(2,1)S(1)}, bf16[8,128,128]{2,1,0:T(8,128)(2,1)S(1)}, u32[]{:S(2)}, u32[]{:S(2)}) collective-permute-start(bf16[8,128,128]{2,1,0:T(8,128)(2,1)S(1)} %get-tuple-element.70), channel_id=1, source_target_pairs={{0,1},{1,0},{2,3},{3,2},{4,5},{5,4},{6,7},{7,6},{8,9},{9,8},{10,11... | collective-permute-start | bytes 786440 | tf_op jit(solution)/shard_map/ppermute | solution.py:29
  28.3 10.2 %collective-permute-start.9 = (bf16[8,128,128]{2,1,0:T(8,128)(2,1)S(1)}, bf16[8,128,128]{2,1,0:T(8,128)(2,1)S(1)}, u32[]{:S(2)}, u32[]{:S(2)}) collective-permute-start(bf16[8,128,128]{2,1,0:T(8,128)(2,1)S(1)} %add_convert_fusion.1), channel_id=1, source_target_pairs={{0,6},{1,7},{2,0},{3,1},{4,2},{5,3},{6,4},{7,5},{8,14},{9,15},{10,... | collective-permute-start | bytes 786440 | tf_op jit(solution)/shard_map/ppermute | solution.py:19
  30.0 6.1 %collective-permute-start.12 = (bf16[1,128,128]{2,1,0:T(8,128)(2,1)S(1)}, bf16[1,128,128]{2,1,0:T(8,128)(2,1)S(1)}, u32[]{:S(2)}, u32[]{:S(2)}) collective-permute-start(bf16[1,128,128]{2,1,0:T(8,128)(2,1)S(1)} %get-tuple-element.88), channel_id=1, source_target_pairs={{0,24},{8,16},{16,8},{24,0},{1,25},{9,17},{17,9},{25,1},{2,26},{10... | collective-permute-start | bytes 98312 | tf_op jit(solution)/shard_map/ppermute | solution.py:29
  33.7 3.9 %collective-permute-start.11 = (bf16[1,128,128]{2,1,0:T(8,128)(2,1)S(1)}, bf16[1,128,128]{2,1,0:T(8,128)(2,1)S(1)}, u32[]{:S(2)}, u32[]{:S(2)}) collective-permute-start(bf16[1,128,128]{2,1,0:T(8,128)(2,1)S(1)} %get-tuple-element.89), channel_id=1, source_target_pairs={{0,8},{8,0},{16,24},{24,16},{1,9},{9,1},{17,25},{25,17},{2,10},{10... | collective-permute-start | bytes 98312 | tf_op jit(solution)/shard_map/ppermute | solution.py:29
  33.7 4.8 %collective-permute-start.10 = (bf16[1,128,128]{2,1,0:T(8,128)(2,1)S(1)}, bf16[1,128,128]{2,1,0:T(8,128)(2,1)S(1)}, u32[]{:S(2)}, u32[]{:S(2)}) collective-permute-start(bf16[1,128,128]{2,1,0:T(8,128)(2,1)S(1)} %get-tuple-element.90), channel_id=1, source_target_pairs={{0,16},{8,24},{16,0},{24,8},{1,17},{9,25},{17,1},{25,9},{2,18},{10... | collective-permute-start | bytes 98312 | tf_op jit(solution)/shard_map/ppermute | solution.py:29

commit v14 on v13

--- a/solution.py
+++ b/solution.py
@@ -194,17 +194,13 @@
     return jnp.concatenate([two_ref[head], one_ref[head], own_ref[head]], axis=0)
 
 
-def score_kernel(queries_ref, two_ref, one_ref, own_ref, bias_ref, low_ref, *, group, scaling, first):
-    tokens = own_ref.shape[1]
+def weigh(windows_ref, queries_ref, bias_ref, low_ref, group, scaling, first):
+    tokens = windows_ref.shape[1] // 3
     _, here = places(queries_ref.shape[1], tokens, group)
     count = low_ref.shape[0]
-
-    def scores_of(at):
-        return dot(window_of(two_ref, one_ref, own_ref, first + at), queries_ref[first + at], 1, 1)
-
-    scores = scores_of(0)
+    scores = dot(windows_ref[first], queries_ref[first], 1, 1)
     for at in range(count):
-        ahead = scores_of(at + 1) if at + 1 < count else None
+        ahead = dot(windows_ref[first + at + 1], queries_ref[first + at + 1], 1, 1) if at + 1 < count else None
         fold = jnp.where(here, scores[2 * tokens :], scores[0:tokens]) * scaling + bias_ref[0]
         mid = scores[tokens : 2 * tokens] * scaling + bias_ref[1]
         top = jnp.max(jnp.maximum(fold, mid), axis=0, keepdims=True)
@@ -215,6 +211,22 @@
         pieces = [jnp.where(here, 0.0, fold), mid * share, jnp.where(here, fold, 0.0)]
         low_ref[at] = jnp.concatenate([piece.astype(LOW) for piece in pieces], axis=0)
         scores = ahead
+
+
+def near_kernel(
+    queries_ref, two_ref, one_ref, own_ref, bias_ref, low_ref, windows_ref, wide_ref, *, kv, group, scaling,
+):
+    tokens = own_ref.shape[0] // kv
+    for at, ref in enumerate((two_ref, one_ref, own_ref)):
+        wide_ref[at] = ref[...].astype(WIDE)
+        for m in range(kv):
+            rows = wide_ref[at, pl.ds(m, tokens, stride=kv), :]
+            windows_ref[m, at * tokens : (at + 1) * tokens, :] = rows.astype(LOW)
+    weigh(windows_ref, queries_ref, bias_ref, low_ref, group, scaling, 0)
+
+
+def far_kernel(queries_ref, windows_ref, bias_ref, low_ref, *, group, scaling, first):
+    weigh(windows_ref, queries_ref, bias_ref, low_ref, group, scaling, first)
 
 
 def forward_kernel(
@@ -284,12 +296,12 @@
 
 
 def query_kernel(
-    grad_ref, two_ref, one_ref, own_ref, dq_hbm, dq_ref, sems, *, kv, group, scaling,
-):
-    tokens, dim = own_ref.shape[1:]
+    grad_ref, windows_ref, dq_hbm, dq_ref, sems, *, kv, group, scaling,
+):
+    tokens, _, dim = dq_ref.shape
     copies = []
     for g in range(kv):
-        query_grad = dot(window_of(two_ref, one_ref, own_ref, g), grad_ref[g], 0, 0) * scaling
+        query_grad = dot(windows_ref[g], grad_ref[g], 0, 0) * scaling
         query_grad = query_grad.T.reshape(tokens, group, dim)
         if g % 2 == 1:
             heads = slice((g - 1) * group, (g + 1) * group)
@@ -364,7 +376,7 @@
     rows = here * 2 * span // rep
     even = jnp.reshape(lax.axis_index("ctx") % 2 == 0, (1, 1, 1))
     key_rows, even = lax.optimization_barrier((key_rows, even))
-    own_keys = lax.optimization_barrier(jnp.moveaxis(key_rows[0], 1, 0))
+    own_keys = key_rows[0]
     two_keys = shifted(own_keys, "ctx", 2)
     meta, biases = call(
         place_kernel, [((8, lanes), jnp.int32), ((2, tokens, lanes), WIDE)], 8 * 2**30, 2**20,
@@ -385,16 +397,17 @@
     )(meta, pulled, cots, rot, proj)
     one_keys, grad_hidden = lax.optimization_barrier((one_keys, grad_hidden))
 
-    def weights_of(first):
-        return call(
-            score_kernel, [((kv // 2, 3 * tokens, lanes), LOW)], 2 * 2**30, 4 * 2**20,
-            group=group, scaling=scaling, first=first,
-        )(queries, two_keys, one_keys, own_keys, biases)[0]
-
-    near = weights_of(0)
+    flat = (tokens * kv, dim)
+    near, windows = call(
+        near_kernel, [((kv // 2, 3 * tokens, lanes), LOW), ((kv, 3 * tokens, dim), LOW)], 2 * 2**30, 4 * 2**20,
+        scratch=[pltpu.VMEM((3, *flat), WIDE)], scaling=scaling, **sizes,
+    )(queries, two_keys.reshape(flat), one_keys.reshape(flat), own_keys.reshape(flat), biases)
     two_values, near = lax.optimization_barrier((two_values, near))
     one_values = exchanged(jnp.where(even, own_values, two_values), {"ctx": 1})
-    far = weights_of(kv // 2)
+    far, = call(
+        far_kernel, [((kv // 2, 3 * tokens, lanes), LOW)], 2 * 2**30, 4 * 2**20,
+        group=group, scaling=scaling, first=kv // 2,
+    )(queries, windows, biases)
     one_values, far = lax.optimization_barrier((one_values, far))
     send, keep = call(
         forward_kernel, [((ctx * rep // 2, rows, dim), LOW)] * 2, 4 * 2**30, 10 * 2**20,
@@ -411,7 +424,7 @@
         query_kernel, [((tokens, heads, dim), LOW)], 2 * 2**30, 5 * 2**20,
         scratch=[pltpu.VMEM((tokens, heads, dim), LOW), pltpu.SemaphoreType.DMA((kv // 2,))],
         out_specs=[pl.BlockSpec(memory_space=pltpu.HBM)], scaling=scaling, **sizes,
-    )(score_grad, two_keys, one_keys, own_keys)
+    )(score_grad, windows)
     from_mate = exchanged(back_one, {"ctx": 1})
     onward = back_two.astype(WIDE) + jnp.where(even, 0.0, from_mate.astype(WIDE))
     onward = onward.astype(LOW)

time: 39.5 us -> 38.7 us (0.980)
  local copies, waits for them, and re-layouts: 1.52 us -> 0.6 us
    optimization_barrier x1 -> x0, local copies, waits for them, and re-layouts: 0.92 us -> none  [on_device(): key_rows, even = lax.optimization_barrier((key_rows, even))]
  transfers between devices with their start and end apart: 13 -> 13, of which waited for: 9 -> 8; matrix products, arithmetic and copies ran while one was open for 2% -> 2% of each run, Pallas kernels for 25% -> 25%
where the time goes in v14:
time: 38.7 us; the launch traced here: 38.5 us
  starting transfers between devices  14.9 us (39%)
  Pallas kernels  13.4 us (35%)
  waiting for transfers between devices  7.63 us (20%)
  other arithmetic  1.11 us (3%)
  between operations  0.87 us (2%)
  local copies, waits for them, and re-layouts  0.6 us (2%)
    pallas_call x9, Pallas kernels, run(): pl.pallas_call(lambda *refs: body(*refs, **fixed), out_shape=[jax.ShapeDt...  13.4 us
    ppermute x10, starting transfers between devices, exchanged(): lax.ppermute(value, axes, [(int(source), int(target)) for source, target...  8.63 us
    ppermute x10, waiting for transfers between devices, exchanged(): lax.ppermute(value, axes, [(int(source), int(target)) for source, target...  7.4 us
    ppermute x3, starting transfers between devices, shifted(): lax.ppermute(value, axis, [(source, (source + steps) % count) for source...  6.27 us
  transfers between devices with their start and end apart: 13, of which 8 were waited for; matrix products, arithmetic and copies ran while one was open for 2% of the time, Pallas kernels for 25%

profile of v14, /device:TPU:0, one launch (start us, length us, event | category | flops | bytes accessed | tf_op | source)
XLA Modules:
  0.0 38.5 jit_solution(7242315141620098274)
XLA Ops:
  0.6 3.0 %collective-permute-start = (bf16[128,4,128]{2,1,0:T(4,128)(2,1)}, bf16[128,4,128]{2,1,0:T(4,128)(2,1)S(1)}, u32[]{:S(2)}, u32[]{:S(2)}) collective-permute-start(bf16[128,4,128]{2,1,0:T(4,128)(2,1)} %bitcast.26), channel_id=1, source_target_pairs={{0,2},{1,3},{2,4},{3,5},{4,6},{5,7},{6,0},{7,1},{8,10},{9,11},{10,... | collective-permute-start | bytes 393224 | tf_op jit(solution)/shard_map/ppermute | solution.py:19
  3.6 0.7 %pad_add_fusion.refs_0_ = s32[2,1024]{1,0:T(2,128)S(1)} fusion(s32[1,1024]{1,0:T(1,128)} %param.17, s32[1,1024]{1,0:T(1,128)} %param.16), kind=kLoop, calls=%fused_computation.6 | loop fusion | flops 2048 | bytes 16384 | tf_op jit(solution)/shard_map/concatenate | solution.py:384
  4.4 0.0 copy-start.6
  4.4 0.0 copy-start.1
  4.4 0.0 copy-start.2
  4.4 0.0 copy-start.3
  4.4 0.3 place_kernel.1
  4.8 0.5 %copy-done.6 = bf16[1,128,4,128]{3,2,1,0:T(4,128)(2,1)S(1)} copy-done((bf16[1,128,4,128]{3,2,1,0:T(4,128)(2,1)S(1)}, bf16[1,128,4,128]{3,2,1,0:T(4,128)(2,1)}, u32[]{:S(2)}) %copy-start.6) | copy-done | bytes 131096
  5.3 1.5 %collective-permute-start.2 = (bf16[4,128,128]{2,1,0:T(8,128)(2,1)S(1)}, bf16[4,128,128]{2,1,0:T(8,128)(2,1)S(1)}, u32[]{:S(2)}, u32[]{:S(2)}) collective-permute-start(bf16[4,128,128]{2,1,0:T(8,128)(2,1)S(1)} %bitcast.22), channel_id=1, source_target_pairs={{0,2},{1,3},{2,4},{3,5},{4,6},{5,7},{6,0},{7,1},{8,10},{9,11},{10,... | collective-permute-start | bytes 393224 | tf_op jit(solution)/shard_map/ppermute | solution.py:19
  6.8 0.0 copy-done.1
  6.8 0.0 copy-done.2
  6.8 0.0 copy-done.3
  6.8 0.0 copy-start
  6.8 0.0 copy-start.4
  6.9 1.4 %pull_kernel.1 = (bf16[4,1024,128]{2,1,0:T(8,128)(2,1)S(1)}, bf16[4,1024,128]{2,1,0:T(8,128)(2,1)S(1)}, f32[8,1024]{1,0:T(8,128)S(1)}, bf16[512,1024]{1,0:T(8,128)(2,1)S(1)}) custom-call(s32[8,1024]{1,0:T(8,128)S(1)} %get-tuple-element.48.refs_0_.refs_8_, bf16[128,32,128]{2,1,0:T(8,128)(2,1)S(1)} %bitcast.29, bf16[64,32,128]{2,1,0:T(8,128)(2,1)S(1)} %bitcast.31, ...), custom_call_target="tpu_custom_call" | custom-call | flops 1073741824 | bytes 4194304 | tf_op jit(solution)/shard_map/pull_kernel/pallas_call | solution.py:361
  8.3 0.0 collective-permute-done
  8.3 0.0 copy-done
  8.3 0.1 broadcast_select_fusion.1
  8.4 0.1 collective-permute-start.1
  8.5 0.0 copy-done.4
  8.5 0.8 %hidden_grad_kernel.1 = (bf16[4,1024,128]{2,1,0:T(8,128)(2,1)S(1)}, bf16[4,512,128]{2,1,0:T(8,128)(2,1)S(1)}) custom-call(s32[8,1024]{1,0:T(8,128)S(1)} %get-tuple-element.48.refs_0_.refs_8_, f32[8,1024]{1,0:T(8,128)S(1)} %get-tuple-element.54.refs_1_, bf16[4,1024,128]{2,1,0:T(8,128)(2,1)S(1)} %get-tuple-element.55.refs_2_.refs_6_, ...), custom_call_target="tpu_custom_call" | custom-call | flops 2147483648 | bytes 4194304 | tf_op jit(solution)/shard_map/hidden_grad_kernel/pallas_call | solution.py:361
  9.2 0.5 %collective-permute-done.1 = bf16[128,4,128]{2,1,0:T(4,128)(2,1)S(1)} collective-permute-done((bf16[128,4,128]{2,1,0:T(4,128)(2,1)S(1)}, bf16[128,4,128]{2,1,0:T(4,128)(2,1)S(1)}, u32[]{:S(2)}, u32[]{:S(2)}) %collective-permute-start.1) | collective-permute-done | bytes 131104 | tf_op jit(solution)/shard_map/ppermute | solution.py:29
  9.8 1.2 %near_kernel.1 = (bf16[2,384,1024]{2,1,0:T(8,128)(2,1)S(1)}, bf16[4,384,128]{2,1,0:T(8,128)(2,1)S(1)}) custom-call(bf16[4,1024,128]{2,1,0:T(8,128)(2,1)S(1)} %get-tuple-element.49.refs_0_, bf16[512,128]{1,0:T(8,128)(2,1)S(1)} %bitcast.28, bf16[512,128]{1,0:T(8,128)(2,1)S(1)} %bitcast.34, bf16[512,128]{1,0:T(8,128)(2,1)S(1)} %bitcast.27, ...), custom_call_target="tpu_custom_call" | custom-call | flops 2147483648 | bytes 4194304 | tf_op jit(solution)/shard_map/near_kernel/pallas_call | solution.py:361
  11.0 0.2 collective-permute-done.2.refs_3_.refs_4_
  11.2 0.1 collective-permute-start.3
  11.3 0.0 copy-start.5
  11.3 1.2 %far_kernel.1.refs_2_.refs_3_ = bf16[2,384,1024]{2,1,0:T(8,128)(2,1)S(1)} custom-call(bf16[4,1024,128]{2,1,0:T(8,128)(2,1)S(1)} %get-tuple-element.49.refs_0_, bf16[4,384,128]{2,1,0:T(8,128)(2,1)S(1)} %get-tuple-element.64.refs_1_, f32[2,128,1024]{2,1,0:T(8,128)S(1)} %get-tuple-element.60.refs_4_.refs_2_), custom_call_target="tpu_custom_call" | custom-call | flops 2147483648 | bytes 4194304 | tf_op jit(solution)/shard_map/far_kernel/pallas_call | solution.py:361
  12.5 0.2 collective-permute-done.3.refs_4_.refs_5_
  12.6 0.0 copy-done.5
  12.6 2.7 %forward_kernel.1 = (bf16[16,128,128]{2,1,0:T(8,128)(2,1)S(1)}, bf16[16,128,128]{2,1,0:T(8,128)(2,1)S(1)}) custom-call(f32[4,16]{1,0:T(4,128)S(1)} %bitcast.35, bf16[2,384,1024]{2,1,0:T(8,128)(2,1)S(1)} %get-tuple-element.71.refs_1_.refs_2_, bf16[2,384,1024]{2,1,0:T(8,128)(2,1)S(1)} %far_kernel.1.refs_2_.refs_3_, ...), custom_call_target="tpu_custom_call" | custom-call | flops 4294967296 | bytes 10485760 | tf_op jit(solution)/shard_map/forward_kernel/pallas_call | solution.py:361
  15.4 0.4 %collective-permute-start.4 = (bf16[16,128,128]{2,1,0:T(8,128)(2,1)S(1)}, bf16[16,128,128]{2,1,0:T(8,128)(2,1)S(1)}, u32[]{:S(2)}, u32[]{:S(2)}) collective-permute-start(bf16[16,128,128]{2,1,0:T(8,128)(2,1)S(1)} %get-tuple-element.70), channel_id=1, source_target_pairs={{0,1},{1,0},{2,3},{3,2},{4,5},{5,4},{6,7},{7,6},{8,9},{9,8},{10,11... | collective-permute-start | bytes 1572872 | tf_op jit(solution)/shard_map/ppermute | solution.py:29
  15.8 1.6 %collective-permute-done.4 = bf16[16,128,128]{2,1,0:T(8,128)(2,1)S(1)} collective-permute-done((bf16[16,128,128]{2,1,0:T(8,128)(2,1)S(1)}, bf16[16,128,128]{2,1,0:T(8,128)(2,1)S(1)}, u32[]{:S(2)}, u32[]{:S(2)}) %collective-permute-start.4) | collective-permute-done | bytes 524320 | tf_op jit(solution)/shard_map/ppermute | solution.py:29
  17.4 0.1 add_convert_fusion
  17.5 2.8 %collective-permute-start.8 = (bf16[4,128,128]{2,1,0:T(8,128)(2,1)S(1)}, bf16[4,128,128]{2,1,0:T(8,128)(2,1)S(1)}, u32[]{:S(2)}, u32[]{:S(2)}) collective-permute-start(bf16[4,128,128]{2,1,0:T(8,128)(2,1)S(1)} %get-tuple-element.89), channel_id=1, source_target_pairs={{0,6},{1,7},{2,4},{3,5},{4,2},{5,3},{6,0},{7,1},{8,14},{9,15},{10,... | collective-permute-start | bytes 393224 | tf_op jit(solution)/shard_map/ppermute | solution.py:29
  20.3 0.1 collective-permute-start.7
  20.4 0.7 %collective-permute-start.6 = (bf16[4,128,128]{2,1,0:T(8,128)(2,1)S(1)}, bf16[4,128,128]{2,1,0:T(8,128)(2,1)S(1)}, u32[]{:S(2)}, u32[]{:S(2)}) collective-permute-start(bf16[4,128,128]{2,1,0:T(8,128)(2,1)S(1)} %get-tuple-element.91), channel_id=1, source_target_pairs={{0,2},{1,3},{2,0},{3,1},{4,6},{5,7},{6,4},{7,5},{8,10},{9,11},{10,... | collective-permute-start | bytes 393224 | tf_op jit(solution)/shard_map/ppermute | solution.py:29
  21.1 3.3 %backward_kernel.1 = (bf16[8,128,128]{2,1,0:T(8,128)(2,1)S(1)}, bf16[8,128,128]{2,1,0:T(8,128)(2,1)S(1)}, f32[8,128,128]{2,1,0:T(8,128)S(1)}, bf16[4,384,1024]{2,1,0:T(8,128)(2,1)S(1)}) custom-call(bf16[4,1024,128]{2,1,0:T(8,128)(2,1)S(1)} %get-tuple-element.49.refs_0_, bf16[4,1024,128]{2,1,0:T(8,128)(2,1)S(1)} %get-tuple-element.57.refs_1_, ...), custom_call_target="tpu_custom_call" | custom-call | flops 4294967296 | bytes 10485760 | tf_op jit(solution)/shard_map/backward_kernel/pallas_call | solution.py:361
  24.4 0.1 collective-permute-start.5
  24.5 0.0 collective-permute-done.8
  24.5 2.6 %collective-permute-done.7 = bf16[4,128,128]{2,1,0:T(8,128)(2,1)S(1)} collective-permute-done((bf16[4,128,128]{2,1,0:T(8,128)(2,1)S(1)}, bf16[4,128,128]{2,1,0:T(8,128)(2,1)S(1)}, u32[]{:S(2)}, u32[]{:S(2)}) %collective-permute-start.7) | collective-permute-done | bytes 131104 | tf_op jit(solution)/shard_map/ppermute | solution.py:29
  27.1 0.1 collective-permute-done.6
  27.3 0.1 add_convert_fusion.2
  27.3 0.0 collective-permute-done.5.refs_1_
  27.3 0.1 add_convert_fusion.1
  27.4 1.7 %collective-permute-start.9 = (bf16[8,128,128]{2,1,0:T(8,128)(2,1)S(1)}, bf16[8,128,128]{2,1,0:T(8,128)(2,1)S(1)}, u32[]{:S(2)}, u32[]{:S(2)}) collective-permute-start(bf16[8,128,128]{2,1,0:T(8,128)(2,1)S(1)} %add_convert_fusion.1), channel_id=1, source_target_pairs={{0,6},{1,7},{2,0},{3,1},{4,2},{5,3},{6,4},{7,5},{8,14},{9,15},{10,... | collective-permute-start | bytes 786440 | tf_op jit(solution)/shard_map/ppermute | solution.py:19
  29.2 3.6 %collective-permute-start.12 = (bf16[1,128,128]{2,1,0:T(8,128)(2,1)S(1)}, bf16[1,128,128]{2,1,0:T(8,128)(2,1)S(1)}, u32[]{:S(2)}, u32[]{:S(2)}) collective-permute-start(bf16[1,128,128]{2,1,0:T(8,128)(2,1)S(1)} %get-tuple-element.92), channel_id=1, source_target_pairs={{0,24},{8,16},{16,8},{24,0},{1,25},{9,17},{17,9},{25,1},{2,26},{10... | collective-permute-start | bytes 98312 | tf_op jit(solution)/shard_map/ppermute | solution.py:29
  32.8 0.0 collective-permute-start.11
  32.8 0.8 %collective-permute-start.10 = (bf16[1,128,128]{2,1,0:T(8,128)(2,1)S(1)}, bf16[1,128,128]{2,1,0:T(8,128)(2,1)S(1)}, u32[]{:S(2)}, u32[]{:S(2)}) collective-permute-start(bf16[1,128,128]{2,1,0:T(8,128)(2,1)S(1)} %get-tuple-element.94), channel_id=1, source_target_pairs={{0,16},{8,24},{16,0},{24,8},{1,17},{9,25},{17,1},{25,9},{2,18},{10... | collective-permute-start | bytes 98312 | tf_op jit(solution)/shard_map/ppermute | solution.py:29
  33.6 1.6 %query_kernel.1 = bf16[128,32,128]{2,1,0:T(8,128)(2,1)} custom-call(bf16[4,384,1024]{2,1,0:T(8,128)(2,1)S(1)} %get-tuple-element.72.refs_0_, bf16[4,384,128]{2,1,0:T(8,128)(2,1)S(1)} %get-tuple-element.64.refs_1_), custom_call_target="tpu_custom_call" | custom-call | flops 2147483648 | bytes 5242880 | tf_op jit(solution)/shard_map/query_kernel/pallas_call | solution.py:361
  35.3 0.0 collective-permute-done.12.refs_6_
  35.3 1.5 %collective-permute-done.11.refs_5_ = bf16[1,128,128]{2,1,0:T(8,128)(2,1)S(1)} collective-permute-done((bf16[1,128,128]{2,1,0:T(8,128)(2,1)S(1)}, bf16[1,128,128]{2,1,0:T(8,128)(2,1)S(1)}, u32[]{:S(2)}, u32[]{:S(2)}) %collective-permute-start.11) | collective-permute-done | bytes 32800 | tf_op jit(solution)/shard_map/ppermute | solution.py:29
  36.8 0.9 %collective-permute-done.10.refs_4_ = bf16[1,128,128]{2,1,0:T(8,128)(2,1)S(1)} collective-permute-done((bf16[1,128,128]{2,1,0:T(8,128)(2,1)S(1)}, bf16[1,128,128]{2,1,0:T(8,128)(2,1)S(1)}, u32[]{:S(2)}, u32[]{:S(2)}) %collective-permute-start.10) | collective-permute-done | bytes 32800 | tf_op jit(solution)/shard_map/ppermute | solution.py:29
  37.7 0.0 collective-permute-done.9.refs_2_
  37.7 0.8 %finish_kernel.1 = (bf16[512,128]{1,0:T(8,128)(2,1)}, bf16[512,128]{1,0:T(8,128)(2,1)}, f32[16,4,128]{2,1,0:T(4,128)}, f32[16,4,128]{2,1,0:T(4,128)}) custom-call(f32[8,128,128]{2,1,0:T(8,128)S(1)} %get-tuple-element.73.refs_0_, bf16[8,128,128]{2,1,0:T(8,128)(2,1)S(1)} %collective-permute-done.5.refs_1_, ...), custom_call_target="tpu_custom_call" | custom-call | flops 1048576 | bytes 1048576 | tf_op jit(solution)/shard_map/finish_kernel/pallas_call | solution.py:361
  (4 shorter events, 0.1 us)
Async XLA Ops:
  0.6 7.7 %collective-permute-start = (bf16[128,4,128]{2,1,0:T(4,128)(2,1)}, bf16[128,4,128]{2,1,0:T(4,128)(2,1)S(1)}, u32[]{:S(2)}, u32[]{:S(2)}) collective-permute-start(bf16[128,4,128]{2,1,0:T(4,128)(2,1)} %bitcast.26), channel_id=1, source_target_pairs={{0,2},{1,3},{2,4},{3,5},{4,6},{5,7},{6,0},{7,1},{8,10},{9,11},{10,... | collective-permute-start | bytes 393224 | tf_op jit(solution)/shard_map/ppermute | solution.py:19
  4.4 0.9 %copy-start.6 = (bf16[1,128,4,128]{3,2,1,0:T(4,128)(2,1)S(1)}, bf16[1,128,4,128]{3,2,1,0:T(4,128)(2,1)}, u32[]{:S(2)}) copy-start(bf16[1,128,4,128]{3,2,1,0:T(4,128)(2,1)} %param.11) | copy-start | bytes 393220
  4.4 2.5 %copy-start.1 = (bf16[1,128,32,128]{3,2,1,0:T(8,128)(2,1)S(1)}, bf16[1,128,32,128]{3,2,1,0:T(8,128)(2,1)}, u32[]{:S(2)}) copy-start(bf16[1,128,32,128]{3,2,1,0:T(8,128)(2,1)} %param.12) | copy-start | bytes 3145732
  4.4 2.5 %copy-start.2 = (bf16[1,128,32,128]{3,2,1,0:T(8,128)(2,1)S(1)}, bf16[1,128,32,128]{3,2,1,0:T(8,128)(2,1)}, u32[]{:S(2)}) copy-start(bf16[1,128,32,128]{3,2,1,0:T(8,128)(2,1)} %param.9) | copy-start | bytes 3145732
  4.4 2.4 %copy-start.3 = (bf16[16,4,32,128]{3,2,1,0:T(8,128)(2,1)S(1)}, bf16[16,4,32,128]{3,2,1,0:T(8,128)(2,1)}, u32[]{:S(2)}) copy-start(bf16[16,4,32,128]{3,2,1,0:T(8,128)(2,1)} %param.13) | copy-start | bytes 1572868
  5.3 5.9 %collective-permute-start.2 = (bf16[4,128,128]{2,1,0:T(8,128)(2,1)S(1)}, bf16[4,128,128]{2,1,0:T(8,128)(2,1)S(1)}, u32[]{:S(2)}, u32[]{:S(2)}) collective-permute-start(bf16[4,128,128]{2,1,0:T(8,128)(2,1)S(1)} %bitcast.22), channel_id=1, source_target_pairs={{0,2},{1,3},{2,4},{3,5},{4,6},{5,7},{6,0},{7,1},{8,10},{9,11},{10,... | collective-permute-start | bytes 393224 | tf_op jit(solution)/shard_map/ppermute | solution.py:19
  6.8 1.5 %copy-start = (bf16[1,128,4,128]{3,2,1,0:T(4,128)(2,1)S(1)}, bf16[1,128,4,128]{3,2,1,0:T(4,128)(2,1)}, u32[]{:S(2)}) copy-start(bf16[1,128,4,128]{3,2,1,0:T(4,128)(2,1)} %param.10) | copy-start | bytes 393220
  6.8 1.6 %copy-start.4 = (bf16[16,4,32,128]{3,2,1,0:T(8,128)(2,1)S(1)}, bf16[16,4,32,128]{3,2,1,0:T(8,128)(2,1)}, u32[]{:S(2)}) copy-start(bf16[16,4,32,128]{3,2,1,0:T(8,128)(2,1)} %param.14) | copy-start | bytes 1572868
  8.4 1.4 %collective-permute-start.1 = (bf16[128,4,128]{2,1,0:T(4,128)(2,1)S(1)}, bf16[128,4,128]{2,1,0:T(4,128)(2,1)S(1)}, u32[]{:S(2)}, u32[]{:S(2)}) collective-permute-start(bf16[128,4,128]{2,1,0:T(4,128)(2,1)S(1)} %broadcast_select_fusion.1), channel_id=1, source_target_pairs={{0,1},{1,0},{2,3},{3,2},{4,5},{5,4},{6,7},{7,6},{8,9},{9,8},{10,11... | collective-permute-start | bytes 393224 | tf_op jit(solution)/shard_map/ppermute | solution.py:29
  11.2 1.4 %collective-permute-start.3 = (bf16[4,128,128]{2,1,0:T(8,128)(2,1)S(1)}, bf16[4,128,128]{2,1,0:T(8,128)(2,1)S(1)}, u32[]{:S(2)}, u32[]{:S(2)}) collective-permute-start(bf16[4,128,128]{2,1,0:T(8,128)(2,1)S(1)} %broadcast_select_fusion), channel_id=1, source_target_pairs={{0,1},{1,0},{2,3},{3,2},{4,5},{5,4},{6,7},{7,6},{8,9},{9,8},{10,11... | collective-permute-start | bytes 393224 | tf_op jit(solution)/shard_map/ppermute | solution.py:29
  11.3 1.3 %copy-start.5 = (f32[16,4]{0,1:T(4,128)S(1)}, f32[16,4]{0,1:T(4,128)}, u32[]{:S(2)}) copy-start(f32[16,4]{0,1:T(4,128)} %param.15) | copy-start | bytes 772
  15.4 2.0 %collective-permute-start.4 = (bf16[16,128,128]{2,1,0:T(8,128)(2,1)S(1)}, bf16[16,128,128]{2,1,0:T(8,128)(2,1)S(1)}, u32[]{:S(2)}, u32[]{:S(2)}) collective-permute-start(bf16[16,128,128]{2,1,0:T(8,128)(2,1)S(1)} %get-tuple-element.70), channel_id=1, source_target_pairs={{0,1},{1,0},{2,3},{3,2},{4,5},{5,4},{6,7},{7,6},{8,9},{9,8},{10,11... | collective-permute-start | bytes 1572872 | tf_op jit(solution)/shard_map/ppermute | solution.py:29
  17.5 7.0 %collective-permute-start.8 = (bf16[4,128,128]{2,1,0:T(8,128)(2,1)S(1)}, bf16[4,128,128]{2,1,0:T(8,128)(2,1)S(1)}, u32[]{:S(2)}, u32[]{:S(2)}) collective-permute-start(bf16[4,128,128]{2,1,0:T(8,128)(2,1)S(1)} %get-tuple-element.89), channel_id=1, source_target_pairs={{0,6},{1,7},{2,4},{3,5},{4,2},{5,3},{6,0},{7,1},{8,14},{9,15},{10,... | collective-permute-start | bytes 393224 | tf_op jit(solution)/shard_map/ppermute | solution.py:29
  20.3 6.8 %collective-permute-start.7 = (bf16[4,128,128]{2,1,0:T(8,128)(2,1)S(1)}, bf16[4,128,128]{2,1,0:T(8,128)(2,1)S(1)}, u32[]{:S(2)}, u32[]{:S(2)}) collective-permute-start(bf16[4,128,128]{2,1,0:T(8,128)(2,1)S(1)} %get-tuple-element.90), channel_id=1, source_target_pairs={{0,4},{1,5},{2,6},{3,7},{4,0},{5,1},{6,2},{7,3},{8,12},{9,13},{10,... | collective-permute-start | bytes 393224 | tf_op jit(solution)/shard_map/ppermute | solution.py:29
  20.4 6.9 %collective-permute-start.6 = (bf16[4,128,128]{2,1,0:T(8,128)(2,1)S(1)}, bf16[4,128,128]{2,1,0:T(8,128)(2,1)S(1)}, u32[]{:S(2)}, u32[]{:S(2)}) collective-permute-start(bf16[4,128,128]{2,1,0:T(8,128)(2,1)S(1)} %get-tuple-element.91), channel_id=1, source_target_pairs={{0,2},{1,3},{2,0},{3,1},{4,6},{5,7},{6,4},{7,5},{8,10},{9,11},{10,... | collective-permute-start | bytes 393224 | tf_op jit(solution)/shard_map/ppermute | solution.py:29
  24.4 2.9 %collective-permute-start.5 = (bf16[8,128,128]{2,1,0:T(8,128)(2,1)S(1)}, bf16[8,128,128]{2,1,0:T(8,128)(2,1)S(1)}, u32[]{:S(2)}, u32[]{:S(2)}) collective-permute-start(bf16[8,128,128]{2,1,0:T(8,128)(2,1)S(1)} %get-tuple-element.74), channel_id=1, source_target_pairs={{0,1},{1,0},{2,3},{3,2},{4,5},{5,4},{6,7},{7,6},{8,9},{9,8},{10,11... | collective-permute-start | bytes 786440 | tf_op jit(solution)/shard_map/ppermute | solution.py:29
  27.4 10.2 %collective-permute-start.9 = (bf16[8,128,128]{2,1,0:T(8,128)(2,1)S(1)}, bf16[8,128,128]{2,1,0:T(8,128)(2,1)S(1)}, u32[]{:S(2)}, u32[]{:S(2)}) collective-permute-start(bf16[8,128,128]{2,1,0:T(8,128)(2,1)S(1)} %add_convert_fusion.1), channel_id=1, source_target_pairs={{0,6},{1,7},{2,0},{3,1},{4,2},{5,3},{6,4},{7,5},{8,14},{9,15},{10,... | collective-permute-start | bytes 786440 | tf_op jit(solution)/shard_map/ppermute | solution.py:19
  29.2 6.1 %collective-permute-start.12 = (bf16[1,128,128]{2,1,0:T(8,128)(2,1)S(1)}, bf16[1,128,128]{2,1,0:T(8,128)(2,1)S(1)}, u32[]{:S(2)}, u32[]{:S(2)}) collective-permute-start(bf16[1,128,128]{2,1,0:T(8,128)(2,1)S(1)} %get-tuple-element.92), channel_id=1, source_target_pairs={{0,24},{8,16},{16,8},{24,0},{1,25},{9,17},{17,9},{25,1},{2,26},{10... | collective-permute-start | bytes 98312 | tf_op jit(solution)/shard_map/ppermute | solution.py:29
  32.8 3.9 %collective-permute-start.11 = (bf16[1,128,128]{2,1,0:T(8,128)(2,1)S(1)}, bf16[1,128,128]{2,1,0:T(8,128)(2,1)S(1)}, u32[]{:S(2)}, u32[]{:S(2)}) collective-permute-start(bf16[1,128,128]{2,1,0:T(8,128)(2,1)S(1)} %get-tuple-element.93), channel_id=1, source_target_pairs={{0,8},{8,0},{16,24},{24,16},{1,9},{9,1},{17,25},{25,17},{2,10},{10... | collective-permute-start | bytes 98312 | tf_op jit(solution)/shard_map/ppermute | solution.py:29
  32.8 4.8 %collective-permute-start.10 = (bf16[1,128,128]{2,1,0:T(8,128)(2,1)S(1)}, bf16[1,128,128]{2,1,0:T(8,128)(2,1)S(1)}, u32[]{:S(2)}, u32[]{:S(2)}) collective-permute-start(bf16[1,128,128]{2,1,0:T(8,128)(2,1)S(1)} %get-tuple-element.94), channel_id=1, source_target_pairs={{0,16},{8,24},{16,0},{24,8},{1,17},{9,25},{17,1},{25,9},{2,18},{10... | collective-permute-start | bytes 98312 | tf_op jit(solution)/shard_map/ppermute | solution.py:29

commit v15 on v13

--- a/solution.py
+++ b/solution.py
@@ -194,40 +194,77 @@
     return jnp.concatenate([two_ref[head], one_ref[head], own_ref[head]], axis=0)
 
 
-def score_kernel(queries_ref, two_ref, one_ref, own_ref, bias_ref, low_ref, *, group, scaling, first):
-    tokens = own_ref.shape[1]
+def head_major(ref, wide_ref, outs):
+    count = len(outs)
+    wide_ref[...] = ref[...].astype(WIDE)
+    for m, out in enumerate(outs):
+        out[...] = wide_ref[pl.ds(m, out.shape[0], stride=count), :].astype(LOW)
+
+
+def fold_kernel(
+    queries_ref, two_ref, own_ref, bias_ref, fold_ref, stats_ref, two_keys_ref, own_keys_ref, wide_ref,
+    *, kv, group, scaling,
+):
+    tokens = two_keys_ref.shape[1]
     _, here = places(queries_ref.shape[1], tokens, group)
-    count = low_ref.shape[0]
-
-    def scores_of(at):
-        return dot(window_of(two_ref, one_ref, own_ref, first + at), queries_ref[first + at], 1, 1)
+    for at, (ref, keys_ref) in enumerate(((two_ref, two_keys_ref), (own_ref, own_keys_ref))):
+        head_major(ref, wide_ref.at[at], [keys_ref.at[m] for m in range(kv)])
+
+    def scores_of(g):
+        return dot(jnp.concatenate([two_keys_ref[g], own_keys_ref[g]], axis=0), queries_ref[g], 1, 1)
 
     scores = scores_of(0)
-    for at in range(count):
-        ahead = scores_of(at + 1) if at + 1 < count else None
-        fold = jnp.where(here, scores[2 * tokens :], scores[0:tokens]) * scaling + bias_ref[0]
-        mid = scores[tokens : 2 * tokens] * scaling + bias_ref[1]
-        top = jnp.max(jnp.maximum(fold, mid), axis=0, keepdims=True)
+    for g in range(kv):
+        ahead = scores_of(g + 1) if g + 1 < kv else None
+        fold = jnp.where(here, scores[tokens:], scores[0:tokens]) * scaling + bias_ref[0]
+        top = jnp.max(fold, axis=0, keepdims=True)
         fold = jnp.exp(fold - top)
+        fold_ref[g] = fold
+        stats_ref[g, 0:1, :] = top
+        stats_ref[g, 1:2, :] = jnp.sum(fold, axis=0, keepdims=True)
+        scores = ahead
+
+
+def middle_kernel(
+    queries_ref, one_ref, bias_ref, fold_ref, stats_ref, low_ref, one_keys_ref, wide_ref, *, kv, group, scaling,
+):
+    tokens = one_keys_ref.shape[1]
+    _, here = places(queries_ref.shape[1], tokens, group)
+    head_major(one_ref, wide_ref, [one_keys_ref.at[m] for m in range(kv)])
+
+    def scores_of(g):
+        return dot(one_keys_ref[g], queries_ref[g], 1, 1)
+
+    scores = scores_of(0)
+    for g in range(kv):
+        ahead = scores_of(g + 1) if g + 1 < kv else None
+        mid = scores * scaling + bias_ref[1]
+        fold_top = stats_ref[g, 0:1, :]
+        top = jnp.maximum(fold_top, jnp.max(mid, axis=0, keepdims=True))
         mid = jnp.exp(mid - top)
-        share = 1.0 / jnp.sum(fold + mid, axis=0, keepdims=True)
-        fold = fold * share
-        pieces = [jnp.where(here, 0.0, fold), mid * share, jnp.where(here, fold, 0.0)]
-        low_ref[at] = jnp.concatenate([piece.astype(LOW) for piece in pieces], axis=0)
+        fade = jnp.exp(fold_top - top)
+        share = 1.0 / (stats_ref[g, 1:2, :] * fade + jnp.sum(mid, axis=0, keepdims=True))
+        fold = fold_ref[g] * (fade * share)
+        low_ref[g, 0:tokens, :] = jnp.where(here, 0.0, fold).astype(LOW)
+        low_ref[g, tokens : 2 * tokens, :] = (mid * share).astype(LOW)
+        low_ref[g, 2 * tokens :, :] = jnp.where(here, fold, 0.0).astype(LOW)
         scores = ahead
 
 
 def forward_kernel(
-    shift_ref, near_ref, far_ref, two_ref, one_ref, own_ref, cots_ref, diff_ref, meta_ref, pull_ref,
-    send_ref, keep_ref, *, kv, group, tenants, rank, owned,
-):
-    dim = own_ref.shape[2]
+    shift_ref, low_ref, two_ref, one_ref, own_ref, cots_ref, diff_ref, meta_ref, pull_ref,
+    send_ref, keep_ref, values_ref, wide_ref, *, kv, group, tenants, rank, owned,
+):
+    dim = own_ref.shape[1]
+    tokens = own_ref.shape[0] // kv
+    for at, ref in enumerate((two_ref, one_ref, own_ref)):
+        rows = slice(at * tokens, (at + 1) * tokens)
+        head_major(ref, wide_ref.at[at], [values_ref.at[m, rows] for m in range(kv)])
     owner = meta_ref[1:2, :]
     lanes = owner.shape[1]
     hidden = []
     for g in range(kv):
-        low = (near_ref if g < kv // 2 else far_ref)[g % (kv // 2)]
-        hidden.append(dot(window_of(two_ref, one_ref, own_ref, g), low, 0, 0).astype(LOW))
+        hidden.append(dot(values_ref[g], low_ref[g], 0, 0).astype(LOW))
     hidden = jnp.concatenate(hidden, axis=0)
     on_diff = dot(jnp.concatenate([diff_ref[g] for g in range(kv)], axis=1), hidden, 1, 0)
     lifted = own_terms(on_diff, owner, tenants, rank, group)
@@ -258,18 +295,17 @@
 
 
 def backward_kernel(
-    queries_ref, gh_ref, near_ref, far_ref, two_ref, one_ref, own_ref,
-    back_two_ref, back_one_ref, back_own_ref, grad_ref, *, kv, scaling,
-):
-    tokens = own_ref.shape[1]
+    queries_ref, gh_ref, low_ref, values_ref, back_two_ref, back_one_ref, back_own_ref, grad_ref, *, kv, scaling,
+):
+    tokens = back_own_ref.shape[1]
 
     def weight_grad_of(g):
-        return dot(window_of(two_ref, one_ref, own_ref, g), gh_ref[g], 1, 1)
+        return dot(values_ref[g], gh_ref[g], 1, 1)
 
     weight_grad = weight_grad_of(0)
     for g in range(kv):
         ahead = weight_grad_of(g + 1) if g + 1 < kv else None
-        low = (near_ref if g < kv // 2 else far_ref)[g % (kv // 2)]
+        low = low_ref[g]
         weights = low.astype(WIDE)
         delta = jnp.sum(weights * weight_grad, axis=0, keepdims=True)
         score_grad = (weights * (weight_grad - delta)).astype(LOW)
@@ -286,7 +322,7 @@
 def query_kernel(
     grad_ref, two_ref, one_ref, own_ref, dq_hbm, dq_ref, sems, *, kv, group, scaling,
 ):
-    tokens, dim = own_ref.shape[1:]
+    tokens, _, dim = dq_ref.shape
     copies = []
     for g in range(kv):
         query_grad = dot(window_of(two_ref, one_ref, own_ref, g), grad_ref[g], 0, 0) * scaling
@@ -364,54 +400,57 @@
     rows = here * 2 * span // rep
     even = jnp.reshape(lax.axis_index("ctx") % 2 == 0, (1, 1, 1))
     key_rows, even = lax.optimization_barrier((key_rows, even))
-    own_keys = lax.optimization_barrier(jnp.moveaxis(key_rows[0], 1, 0))
+    own_keys = key_rows[0]
     two_keys = shifted(own_keys, "ctx", 2)
     meta, biases = call(
         place_kernel, [((8, lanes), jnp.int32), ((2, tokens, lanes), WIDE)], 8 * 2**30, 2**20,
         group=group,
     )(jnp.concatenate([doc_starts, tenant_ids], axis=0))
-    own_values, meta = lax.optimization_barrier((jnp.moveaxis(value_matrix[0], 1, 0), meta))
+    own_values, meta = lax.optimization_barrier((value_matrix[0], meta))
     two_values = shifted(own_values, "ctx", 2)
     cots, queries, pulled, pull = call(
         pull_kernel,
         [((kv, lanes, dim), LOW), ((kv, lanes, dim), LOW), ((8, lanes), WIDE), ((span * group, lanes), LOW)],
         2**30, 4 * 2**20, tenants=tenants, rank=rank, owned=here, **sizes,
     )(meta, upstream, rot, queries)
-    two_keys, pulled = lax.optimization_barrier((two_keys, pulled))
-    one_keys = exchanged(jnp.where(even, own_keys, two_keys), {"ctx": 1})
     grad_hidden, diff = call(
         hidden_grad_kernel, [((kv, lanes, dim), LOW), ((kv, span * group, dim), LOW)],
         2 * 2**30, 4 * 2**20, tenants=tenants, rank=rank, **sizes,
     )(meta, pulled, cots, rot, proj)
-    one_keys, grad_hidden = lax.optimization_barrier((one_keys, grad_hidden))
-
-    def weights_of(first):
-        return call(
-            score_kernel, [((kv // 2, 3 * tokens, lanes), LOW)], 2 * 2**30, 4 * 2**20,
-            group=group, scaling=scaling, first=first,
-        )(queries, two_keys, one_keys, own_keys, biases)[0]
-
-    near = weights_of(0)
-    two_values, near = lax.optimization_barrier((two_values, near))
+    two_keys, grad_hidden = lax.optimization_barrier((two_keys, grad_hidden))
+    one_keys = exchanged(jnp.where(even, own_keys, two_keys), {"ctx": 1})
+    flat, heads_first = (tokens * kv, dim), ((kv, tokens, dim), LOW)
+    fold, stats, two_heads, own_heads = call(
+        fold_kernel, [((kv, tokens, lanes), WIDE), ((kv, 2, lanes), WIDE), heads_first, heads_first],
+        2 * 2**30, 4 * 2**20, scratch=[pltpu.VMEM((2, *flat), WIDE)], scaling=scaling, **sizes,
+    )(queries, two_keys.reshape(flat), own_keys.reshape(flat), biases)
+    one_keys, two_values, fold = lax.optimization_barrier((one_keys, two_values, fold))
     one_values = exchanged(jnp.where(even, own_values, two_values), {"ctx": 1})
-    far = weights_of(kv // 2)
-    one_values, far = lax.optimization_barrier((one_values, far))
-    send, keep = call(
-        forward_kernel, [((ctx * rep // 2, rows, dim), LOW)] * 2, 4 * 2**30, 10 * 2**20,
+    low, one_heads = call(
+        middle_kernel, [((kv, 3 * tokens, lanes), LOW), heads_first], 2 * 2**30, 4 * 2**20,
+        scratch=[pltpu.VMEM(flat, WIDE)], scaling=scaling, **sizes,
+    )(queries, one_keys.reshape(flat), biases, fold, stats)
+    one_values, low = lax.optimization_barrier((one_values, low))
+    send, keep, values = call(
+        forward_kernel, [((ctx * rep // 2, rows, dim), LOW)] * 2 + [((kv, 3 * tokens, dim), LOW)],
+        4 * 2**30, 10 * 2**20, scratch=[pltpu.VMEM((3, *flat), WIDE)],
         tenants=tenants, rank=rank, owned=here, **sizes,
-    )(shift_bias.T, near, far, two_values, one_values, own_values, cots, diff, meta, pull)
+    )(
+        shift_bias.T, low, two_values.reshape(flat), one_values.reshape(flat), own_values.reshape(flat),
+        cots, diff, meta, pull,
+    )
     part = (keep.astype(WIDE) + exchanged(send, {"ctx": 1}).astype(WIDE)).astype(LOW)
-    near, part = lax.optimization_barrier((near, part))
+    low, part = lax.optimization_barrier((low, part))
     window = (2 * kv, tokens, dim)
     back_two, back_one, back_own, score_grad = call(
         backward_kernel, [(window, LOW), (window, LOW), (window, WIDE), ((kv, 3 * tokens, lanes), LOW)],
         4 * 2**30, 10 * 2**20, kv=kv, scaling=scaling,
-    )(queries, grad_hidden, near, far, two_values, one_values, own_values)
+    )(queries, grad_hidden, low, values)
     d_queries, = call(
         query_kernel, [((tokens, heads, dim), LOW)], 2 * 2**30, 5 * 2**20,
         scratch=[pltpu.VMEM((tokens, heads, dim), LOW), pltpu.SemaphoreType.DMA((kv // 2,))],
         out_specs=[pl.BlockSpec(memory_space=pltpu.HBM)], scaling=scaling, **sizes,
-    )(score_grad, two_keys, one_keys, own_keys)
+    )(score_grad, two_heads, one_heads, own_heads)
     from_mate = exchanged(back_one, {"ctx": 1})
     onward = back_two.astype(WIDE) + jnp.where(even, 0.0, from_mate.astype(WIDE))
     onward = onward.astype(LOW)

time: 39.5 us -> 39 us (0.987)
  local copies, waits for them, and re-layouts: 1.52 us -> 0.68 us
    optimization_barrier x1 -> x0, local copies, waits for them, and re-layouts: 0.92 us -> none  [on_device(): key_rows, even = lax.optimization_barrier((key_rows, even))]
    ppermute x3, waiting for transfers between devices: 0.33 us -> 0.98 us  [shifted(): lax.ppermute(value, axis, [(source, (source + steps) % count) for source...]
    ppermute x10, waiting for transfers between devices: 7.34 us -> 6.81 us  [exchanged(): lax.ppermute(value, axes, [(int(source), int(target)) for source, target...]
  transfers between devices with their start and end apart: 13 -> 13, of which waited for: 9 -> 7; matrix products, arithmetic and copies ran while one was open for 2% -> 2% of each run, Pallas kernels for 25% -> 25%
where the time goes in v15:
time: 39 us; the launch traced here: 38.7 us
  starting transfers between devices  14.8 us (38%)
  Pallas kernels  13.5 us (35%)
  waiting for transfers between devices  7.79 us (20%)
  other arithmetic  1.11 us (3%)
  between operations  0.87 us (2%)
  local copies, waits for them, and re-layouts  0.68 us (2%)
    pallas_call x9, Pallas kernels, run(): pl.pallas_call(lambda *refs: body(*refs, **fixed), out_shape=[jax.ShapeDt...  13.5 us
    ppermute x10, starting transfers between devices, exchanged(): lax.ppermute(value, axes, [(int(source), int(target)) for source, target...  8.78 us
    ppermute x10, waiting for transfers between devices, exchanged(): lax.ppermute(value, axes, [(int(source), int(target)) for source, target...  6.81 us
    ppermute x3, starting transfers between devices, shifted(): lax.ppermute(value, axis, [(source, (source + steps) % count) for source...  5.98 us
    ppermute x3, waiting for transfers between devices, shifted(): lax.ppermute(value, axis, [(source, (source + steps) % count) for source...  0.98 us
  transfers between devices with their start and end apart: 13, of which 7 were waited for; matrix products, arithmetic and copies ran while one was open for 2% of the time, Pallas kernels for 25%

profile of v15, /device:TPU:0, one launch (start us, length us, event | category | flops | bytes accessed | tf_op | source)
XLA Modules:
  0.0 38.7 jit_solution(5388891279636775569)
XLA Ops:
  0.6 3.0 %collective-permute-start = (bf16[128,4,128]{2,1,0:T(4,128)(2,1)}, bf16[128,4,128]{2,1,0:T(4,128)(2,1)S(1)}, u32[]{:S(2)}, u32[]{:S(2)}) collective-permute-start(bf16[128,4,128]{2,1,0:T(4,128)(2,1)} %bitcast.24), channel_id=1, source_target_pairs={{0,2},{1,3},{2,4},{3,5},{4,6},{5,7},{6,0},{7,1},{8,10},{9,11},{10,... | collective-permute-start | bytes 393224 | tf_op jit(solution)/shard_map/ppermute | solution.py:19
  3.6 0.7 %pad_add_fusion.refs_0_ = s32[2,1024]{1,0:T(2,128)S(1)} fusion(s32[1,1024]{1,0:T(1,128)} %param.17, s32[1,1024]{1,0:T(1,128)} %param.16), kind=kLoop, calls=%fused_computation.5 | loop fusion | flops 2048 | bytes 16384 | tf_op jit(solution)/shard_map/concatenate | solution.py:408
  4.4 0.0 copy-start.1
  4.4 0.0 copy-start.2
  4.4 0.0 copy-start.3
  4.4 0.0 copy-start.4
  4.4 0.3 place_kernel.1
  4.8 0.0 copy-start.5
  4.8 0.5 %copy-done.1 = bf16[1,128,4,128]{3,2,1,0:T(4,128)(2,1)S(1)} copy-done((bf16[1,128,4,128]{3,2,1,0:T(4,128)(2,1)S(1)}, bf16[1,128,4,128]{3,2,1,0:T(4,128)(2,1)}, u32[]{:S(2)}) %copy-start.1) | copy-done | bytes 131096
  5.3 1.5 %collective-permute-start.2 = (bf16[128,4,128]{2,1,0:T(4,128)(2,1)S(1)}, bf16[128,4,128]{2,1,0:T(4,128)(2,1)S(1)}, u32[]{:S(2)}, u32[]{:S(2)}) collective-permute-start(bf16[128,4,128]{2,1,0:T(4,128)(2,1)S(1)} %bitcast.26), channel_id=1, source_target_pairs={{0,2},{1,3},{2,4},{3,5},{4,6},{5,7},{6,0},{7,1},{8,10},{9,11},{10,... | collective-permute-start | bytes 393224 | tf_op jit(solution)/shard_map/ppermute | solution.py:19
  6.8 0.0 copy-done.2
  6.8 0.0 copy-done.3
  6.8 0.0 copy-done.4
  6.8 1.4 %pull_kernel.1 = (bf16[4,1024,128]{2,1,0:T(8,128)(2,1)S(1)}, bf16[4,1024,128]{2,1,0:T(8,128)(2,1)S(1)}, f32[8,1024]{1,0:T(8,128)S(1)}, bf16[512,1024]{1,0:T(8,128)(2,1)S(1)}) custom-call(s32[8,1024]{1,0:T(8,128)S(1)} %get-tuple-element.52.refs_0_.refs_7_, bf16[128,32,128]{2,1,0:T(8,128)(2,1)S(1)} %bitcast.32, bf16[64,32,128]{2,1,0:T(8,128)(2,1)S(1)} %bitcast.34, ...), custom_call_target="tpu_custom_call" | custom-call | flops 1073741824 | bytes 4194304 | tf_op jit(solution)/shard_map/pull_kernel/pallas_call | solution.py:385
  8.2 0.0 copy-done.5
  8.2 0.0 copy-start
  8.2 0.8 %hidden_grad_kernel.1 = (bf16[4,1024,128]{2,1,0:T(8,128)(2,1)S(1)}, bf16[4,512,128]{2,1,0:T(8,128)(2,1)S(1)}) custom-call(s32[8,1024]{1,0:T(8,128)S(1)} %get-tuple-element.52.refs_0_.refs_7_, f32[8,1024]{1,0:T(8,128)S(1)} %get-tuple-element.55.refs_1_, bf16[4,1024,128]{2,1,0:T(8,128)(2,1)S(1)} %get-tuple-element.56.refs_2_.refs_5_, ...), custom_call_target="tpu_custom_call" | custom-call | flops 2147483648 | bytes 4194304 | tf_op jit(solution)/shard_map/hidden_grad_kernel/pallas_call | solution.py:385
  9.0 0.0 collective-permute-done
  9.0 0.1 copy-done
  9.1 0.1 broadcast_select_fusion.1
  9.2 0.1 collective-permute-start.1
  9.2 0.9 %fold_kernel.1 = (f32[4,128,1024]{2,1,0:T(8,128)S(1)}, f32[4,2,1024]{2,1,0:T(2,128)S(1)}, bf16[4,128,128]{2,1,0:T(8,128)(2,1)S(1)}, bf16[4,128,128]{2,1,0:T(8,128)(2,1)S(1)}) custom-call(bf16[4,1024,128]{2,1,0:T(8,128)(2,1)S(1)} %get-tuple-element.53.refs_0_, bf16[512,128]{1,0:T(8,128)(2,1)S(1)} %bitcast.31, bf16[512,128]{1,0:T(8,128)(2,1)S(1)} %bitcast.25, ...), custom_call_target="tpu_custom_call" | custom-call | flops 2147483648 | bytes 4194304 | tf_op jit(solution)/shard_map/fold_kernel/pallas_call | solution.py:385
  10.2 1.0 %collective-permute-done.2 = bf16[128,4,128]{2,1,0:T(4,128)(2,1)S(1)} collective-permute-done((bf16[128,4,128]{2,1,0:T(4,128)(2,1)S(1)}, bf16[128,4,128]{2,1,0:T(4,128)(2,1)S(1)}, u32[]{:S(2)}, u32[]{:S(2)}) %collective-permute-start.2) | collective-permute-done | bytes 131104 | tf_op jit(solution)/shard_map/ppermute | solution.py:19
  11.1 0.0 collective-permute-done.1
  11.1 0.1 collective-permute-start.3
  11.2 0.0 copy-start.6
  11.2 1.5 %middle_kernel.1 = (bf16[4,384,1024]{2,1,0:T(8,128)(2,1)S(1)}, bf16[4,128,128]{2,1,0:T(8,128)(2,1)S(1)}) custom-call(bf16[4,1024,128]{2,1,0:T(8,128)(2,1)S(1)} %get-tuple-element.53.refs_0_, bf16[512,128]{1,0:T(8,128)(2,1)S(1)} %bitcast.37, f32[2,128,1024]{2,1,0:T(8,128)S(1)} %get-tuple-element.62.refs_3_.refs_2_, ...), custom_call_target="tpu_custom_call" | custom-call | flops 2147483648 | bytes 4194304 | tf_op jit(solution)/shard_map/middle_kernel/pallas_call | solution.py:385
  12.7 0.0 collective-permute-done.3
  12.7 0.0 copy-done.6
  12.7 2.8 %forward_kernel.1 = (bf16[16,128,128]{2,1,0:T(8,128)(2,1)S(1)}, bf16[16,128,128]{2,1,0:T(8,128)(2,1)S(1)}, bf16[4,384,128]{2,1,0:T(8,128)(2,1)S(1)}) custom-call(f32[4,16]{1,0:T(4,128)S(1)} %bitcast.39, bf16[4,384,1024]{2,1,0:T(8,128)(2,1)S(1)} %get-tuple-element.75.refs_1_.refs_2_, bf16[512,128]{1,0:T(8,128)(2,1)S(1)} %bitcast.30, ...), custom_call_target="tpu_custom_call" | custom-call | flops 4294967296 | bytes 10485760 | tf_op jit(solution)/shard_map/forward_kernel/pallas_call | solution.py:385
  15.6 0.6 %collective-permute-start.4 = (bf16[16,128,128]{2,1,0:T(8,128)(2,1)S(1)}, bf16[16,128,128]{2,1,0:T(8,128)(2,1)S(1)}, u32[]{:S(2)}, u32[]{:S(2)}) collective-permute-start(bf16[16,128,128]{2,1,0:T(8,128)(2,1)S(1)} %get-tuple-element.74), channel_id=1, source_target_pairs={{0,1},{1,0},{2,3},{3,2},{4,5},{5,4},{6,7},{7,6},{8,9},{9,8},{10,11... | collective-permute-start | bytes 1572872 | tf_op jit(solution)/shard_map/ppermute | solution.py:29
  16.1 1.5 %collective-permute-done.4 = bf16[16,128,128]{2,1,0:T(8,128)(2,1)S(1)} collective-permute-done((bf16[16,128,128]{2,1,0:T(8,128)(2,1)S(1)}, bf16[16,128,128]{2,1,0:T(8,128)(2,1)S(1)}, u32[]{:S(2)}, u32[]{:S(2)}) %collective-permute-start.4) | collective-permute-done | bytes 524320 | tf_op jit(solution)/shard_map/ppermute | solution.py:29
  17.7 0.1 add_convert_fusion
  17.9 1.8 %collective-permute-start.8 = (bf16[4,128,128]{2,1,0:T(8,128)(2,1)S(1)}, bf16[4,128,128]{2,1,0:T(8,128)(2,1)S(1)}, u32[]{:S(2)}, u32[]{:S(2)}) collective-permute-start(bf16[4,128,128]{2,1,0:T(8,128)(2,1)S(1)} %get-tuple-element.97), channel_id=1, source_target_pairs={{0,6},{1,7},{2,4},{3,5},{4,2},{5,3},{6,0},{7,1},{8,14},{9,15},{10,... | collective-permute-start | bytes 393224 | tf_op jit(solution)/shard_map/ppermute | solution.py:29
  19.7 0.7 %collective-permute-start.7 = (bf16[4,128,128]{2,1,0:T(8,128)(2,1)S(1)}, bf16[4,128,128]{2,1,0:T(8,128)(2,1)S(1)}, u32[]{:S(2)}, u32[]{:S(2)}) collective-permute-start(bf16[4,128,128]{2,1,0:T(8,128)(2,1)S(1)} %get-tuple-element.98), channel_id=1, source_target_pairs={{0,4},{1,5},{2,6},{3,7},{4,0},{5,1},{6,2},{7,3},{8,12},{9,13},{10,... | collective-permute-start | bytes 393224 | tf_op jit(solution)/shard_map/ppermute | solution.py:29
  20.4 1.1 %collective-permute-start.6 = (bf16[4,128,128]{2,1,0:T(8,128)(2,1)S(1)}, bf16[4,128,128]{2,1,0:T(8,128)(2,1)S(1)}, u32[]{:S(2)}, u32[]{:S(2)}) collective-permute-start(bf16[4,128,128]{2,1,0:T(8,128)(2,1)S(1)} %get-tuple-element.99), channel_id=1, source_target_pairs={{0,2},{1,3},{2,0},{3,1},{4,6},{5,7},{6,4},{7,5},{8,10},{9,11},{10,... | collective-permute-start | bytes 393224 | tf_op jit(solution)/shard_map/ppermute | solution.py:29
  21.4 3.3 %backward_kernel.1 = (bf16[8,128,128]{2,1,0:T(8,128)(2,1)S(1)}, bf16[8,128,128]{2,1,0:T(8,128)(2,1)S(1)}, f32[8,128,128]{2,1,0:T(8,128)S(1)}, bf16[4,384,1024]{2,1,0:T(8,128)(2,1)S(1)}) custom-call(bf16[4,1024,128]{2,1,0:T(8,128)(2,1)S(1)} %get-tuple-element.53.refs_0_, bf16[4,1024,128]{2,1,0:T(8,128)(2,1)S(1)} %get-tuple-element.58.refs_1_, ...), custom_call_target="tpu_custom_call" | custom-call | flops 4294967296 | bytes 10485760 | tf_op jit(solution)/shard_map/backward_kernel/pallas_call | solution.py:385
  24.7 0.1 collective-permute-start.5
  24.8 0.4 collective-permute-done.8
  25.2 2.2 %collective-permute-done.7 = bf16[4,128,128]{2,1,0:T(8,128)(2,1)S(1)} collective-permute-done((bf16[4,128,128]{2,1,0:T(8,128)(2,1)S(1)}, bf16[4,128,128]{2,1,0:T(8,128)(2,1)S(1)}, u32[]{:S(2)}, u32[]{:S(2)}) %collective-permute-start.7) | collective-permute-done | bytes 131104 | tf_op jit(solution)/shard_map/ppermute | solution.py:29
  27.4 0.3 collective-permute-done.6
  27.7 0.1 add_convert_fusion.2
  27.8 0.0 collective-permute-done.5.refs_1_
  27.8 0.1 add_convert_fusion.1
  27.9 1.5 %collective-permute-start.9 = (bf16[8,128,128]{2,1,0:T(8,128)(2,1)S(1)}, bf16[8,128,128]{2,1,0:T(8,128)(2,1)S(1)}, u32[]{:S(2)}, u32[]{:S(2)}) collective-permute-start(bf16[8,128,128]{2,1,0:T(8,128)(2,1)S(1)} %add_convert_fusion.1), channel_id=1, source_target_pairs={{0,6},{1,7},{2,0},{3,1},{4,2},{5,3},{6,4},{7,5},{8,14},{9,15},{10,... | collective-permute-start | bytes 786440 | tf_op jit(solution)/shard_map/ppermute | solution.py:19
  29.4 3.7 %collective-permute-start.12 = (bf16[1,128,128]{2,1,0:T(8,128)(2,1)S(1)}, bf16[1,128,128]{2,1,0:T(8,128)(2,1)S(1)}, u32[]{:S(2)}, u32[]{:S(2)}) collective-permute-start(bf16[1,128,128]{2,1,0:T(8,128)(2,1)S(1)} %get-tuple-element.100), channel_id=1, source_target_pairs={{0,24},{8,16},{16,8},{24,0},{1,25},{9,17},{17,9},{25,1},{2,26},{10... | collective-permute-start | bytes 98312 | tf_op jit(solution)/shard_map/ppermute | solution.py:29
  33.0 0.0 collective-permute-start.11
  33.0 0.8 %collective-permute-start.10 = (bf16[1,128,128]{2,1,0:T(8,128)(2,1)S(1)}, bf16[1,128,128]{2,1,0:T(8,128)(2,1)S(1)}, u32[]{:S(2)}, u32[]{:S(2)}) collective-permute-start(bf16[1,128,128]{2,1,0:T(8,128)(2,1)S(1)} %get-tuple-element.102), channel_id=1, source_target_pairs={{0,16},{8,24},{16,0},{24,8},{1,17},{9,25},{17,1},{25,9},{2,18},{10... | collective-permute-start | bytes 98312 | tf_op jit(solution)/shard_map/ppermute | solution.py:29
  33.8 1.6 %query_kernel.1 = bf16[128,32,128]{2,1,0:T(8,128)(2,1)} custom-call(bf16[4,384,1024]{2,1,0:T(8,128)(2,1)S(1)} %get-tuple-element.77.refs_0_, bf16[4,128,128]{2,1,0:T(8,128)(2,1)S(1)} %get-tuple-element.78.refs_1_, bf16[4,128,128]{2,1,0:T(8,128)(2,1)S(1)} %get-tuple-element.79.refs_2_, bf16[4,128,128]{2,1,0:T(8,128)(2,1)S(1)} %get-tuple-element.80.refs_3_), custom_call_target="tpu_custom_call" | custom-call | flops 2147483648 | bytes 5242880 | tf_op jit(solution)/shard_map/query_kernel/pallas_call | solution.py:385
  35.5 0.0 collective-permute-done.12.refs_6_
  35.5 1.5 %collective-permute-done.11.refs_5_ = bf16[1,128,128]{2,1,0:T(8,128)(2,1)S(1)} collective-permute-done((bf16[1,128,128]{2,1,0:T(8,128)(2,1)S(1)}, bf16[1,128,128]{2,1,0:T(8,128)(2,1)S(1)}, u32[]{:S(2)}, u32[]{:S(2)}) %collective-permute-start.11) | collective-permute-done | bytes 32800 | tf_op jit(solution)/shard_map/ppermute | solution.py:29
  37.0 0.9 %collective-permute-done.10.refs_4_ = bf16[1,128,128]{2,1,0:T(8,128)(2,1)S(1)} collective-permute-done((bf16[1,128,128]{2,1,0:T(8,128)(2,1)S(1)}, bf16[1,128,128]{2,1,0:T(8,128)(2,1)S(1)}, u32[]{:S(2)}, u32[]{:S(2)}) %collective-permute-start.10) | collective-permute-done | bytes 32800 | tf_op jit(solution)/shard_map/ppermute | solution.py:29
  37.9 0.0 collective-permute-done.9.refs_2_
  37.9 0.8 %finish_kernel.1 = (bf16[512,128]{1,0:T(8,128)(2,1)}, bf16[512,128]{1,0:T(8,128)(2,1)}, f32[16,4,128]{2,1,0:T(4,128)}, f32[16,4,128]{2,1,0:T(4,128)}) custom-call(f32[8,128,128]{2,1,0:T(8,128)S(1)} %get-tuple-element.81.refs_0_, bf16[8,128,128]{2,1,0:T(8,128)(2,1)S(1)} %collective-permute-done.5.refs_1_, ...), custom_call_target="tpu_custom_call" | custom-call | flops 1048576 | bytes 1048576 | tf_op jit(solution)/shard_map/finish_kernel/pallas_call | solution.py:385
  (3 shorter events, 0.1 us)
Async XLA Ops:
  0.6 8.3 %collective-permute-start = (bf16[128,4,128]{2,1,0:T(4,128)(2,1)}, bf16[128,4,128]{2,1,0:T(4,128)(2,1)S(1)}, u32[]{:S(2)}, u32[]{:S(2)}) collective-permute-start(bf16[128,4,128]{2,1,0:T(4,128)(2,1)} %bitcast.24), channel_id=1, source_target_pairs={{0,2},{1,3},{2,4},{3,5},{4,6},{5,7},{6,0},{7,1},{8,10},{9,11},{10,... | collective-permute-start | bytes 393224 | tf_op jit(solution)/shard_map/ppermute | solution.py:19
  4.4 0.9 %copy-start.1 = (bf16[1,128,4,128]{3,2,1,0:T(4,128)(2,1)S(1)}, bf16[1,128,4,128]{3,2,1,0:T(4,128)(2,1)}, u32[]{:S(2)}) copy-start(bf16[1,128,4,128]{3,2,1,0:T(4,128)(2,1)} %param.11) | copy-start | bytes 393220
  4.4 2.4 %copy-start.2 = (bf16[1,128,32,128]{3,2,1,0:T(8,128)(2,1)S(1)}, bf16[1,128,32,128]{3,2,1,0:T(8,128)(2,1)}, u32[]{:S(2)}) copy-start(bf16[1,128,32,128]{3,2,1,0:T(8,128)(2,1)} %param.12) | copy-start | bytes 3145732
  4.4 2.4 %copy-start.3 = (bf16[1,128,32,128]{3,2,1,0:T(8,128)(2,1)S(1)}, bf16[1,128,32,128]{3,2,1,0:T(8,128)(2,1)}, u32[]{:S(2)}) copy-start(bf16[1,128,32,128]{3,2,1,0:T(8,128)(2,1)} %param.9) | copy-start | bytes 3145732
  4.4 2.4 %copy-start.4 = (bf16[16,4,32,128]{3,2,1,0:T(8,128)(2,1)S(1)}, bf16[16,4,32,128]{3,2,1,0:T(8,128)(2,1)}, u32[]{:S(2)}) copy-start(bf16[16,4,32,128]{3,2,1,0:T(8,128)(2,1)} %param.13) | copy-start | bytes 1572868
  4.8 3.4 %copy-start.5 = (bf16[16,4,32,128]{3,2,1,0:T(8,128)(2,1)S(1)}, bf16[16,4,32,128]{3,2,1,0:T(8,128)(2,1)}, u32[]{:S(2)}) copy-start(bf16[16,4,32,128]{3,2,1,0:T(8,128)(2,1)} %param.14) | copy-start | bytes 1572868
  5.3 5.9 %collective-permute-start.2 = (bf16[128,4,128]{2,1,0:T(4,128)(2,1)S(1)}, bf16[128,4,128]{2,1,0:T(4,128)(2,1)S(1)}, u32[]{:S(2)}, u32[]{:S(2)}) collective-permute-start(bf16[128,4,128]{2,1,0:T(4,128)(2,1)S(1)} %bitcast.26), channel_id=1, source_target_pairs={{0,2},{1,3},{2,4},{3,5},{4,6},{5,7},{6,0},{7,1},{8,10},{9,11},{10,... | collective-permute-start | bytes 393224 | tf_op jit(solution)/shard_map/ppermute | solution.py:19
  8.2 0.9 %copy-start = (bf16[1,128,4,128]{3,2,1,0:T(4,128)(2,1)S(1)}, bf16[1,128,4,128]{3,2,1,0:T(4,128)(2,1)}, u32[]{:S(2)}) copy-start(bf16[1,128,4,128]{3,2,1,0:T(4,128)(2,1)} %param.10) | copy-start | bytes 393220
  9.2 2.0 %collective-permute-start.1 = (bf16[128,4,128]{2,1,0:T(4,128)(2,1)S(1)}, bf16[128,4,128]{2,1,0:T(4,128)(2,1)S(1)}, u32[]{:S(2)}, u32[]{:S(2)}) collective-permute-start(bf16[128,4,128]{2,1,0:T(4,128)(2,1)S(1)} %broadcast_select_fusion.1), channel_id=1, source_target_pairs={{0,1},{1,0},{2,3},{3,2},{4,5},{5,4},{6,7},{7,6},{8,9},{9,8},{10,11... | collective-permute-start | bytes 393224 | tf_op jit(solution)/shard_map/ppermute | solution.py:29
  11.1 1.6 %collective-permute-start.3 = (bf16[128,4,128]{2,1,0:T(4,128)(2,1)S(1)}, bf16[128,4,128]{2,1,0:T(4,128)(2,1)S(1)}, u32[]{:S(2)}, u32[]{:S(2)}) collective-permute-start(bf16[128,4,128]{2,1,0:T(4,128)(2,1)S(1)} %bitcast.40), channel_id=1, source_target_pairs={{0,1},{1,0},{2,3},{3,2},{4,5},{5,4},{6,7},{7,6},{8,9},{9,8},{10,11... | collective-permute-start | bytes 393224 | tf_op jit(solution)/shard_map/ppermute | solution.py:29
  11.2 1.5 %copy-start.6 = (f32[16,4]{0,1:T(4,128)S(1)}, f32[16,4]{0,1:T(4,128)}, u32[]{:S(2)}) copy-start(f32[16,4]{0,1:T(4,128)} %param.15) | copy-start | bytes 772
  15.6 2.1 %collective-permute-start.4 = (bf16[16,128,128]{2,1,0:T(8,128)(2,1)S(1)}, bf16[16,128,128]{2,1,0:T(8,128)(2,1)S(1)}, u32[]{:S(2)}, u32[]{:S(2)}) collective-permute-start(bf16[16,128,128]{2,1,0:T(8,128)(2,1)S(1)} %get-tuple-element.74), channel_id=1, source_target_pairs={{0,1},{1,0},{2,3},{3,2},{4,5},{5,4},{6,7},{7,6},{8,9},{9,8},{10,11... | collective-permute-start | bytes 1572872 | tf_op jit(solution)/shard_map/ppermute | solution.py:29
  17.9 7.3 %collective-permute-start.8 = (bf16[4,128,128]{2,1,0:T(8,128)(2,1)S(1)}, bf16[4,128,128]{2,1,0:T(8,128)(2,1)S(1)}, u32[]{:S(2)}, u32[]{:S(2)}) collective-permute-start(bf16[4,128,128]{2,1,0:T(8,128)(2,1)S(1)} %get-tuple-element.97), channel_id=1, source_target_pairs={{0,6},{1,7},{2,4},{3,5},{4,2},{5,3},{6,0},{7,1},{8,14},{9,15},{10,... | collective-permute-start | bytes 393224 | tf_op jit(solution)/shard_map/ppermute | solution.py:29
  19.7 7.7 %collective-permute-start.7 = (bf16[4,128,128]{2,1,0:T(8,128)(2,1)S(1)}, bf16[4,128,128]{2,1,0:T(8,128)(2,1)S(1)}, u32[]{:S(2)}, u32[]{:S(2)}) collective-permute-start(bf16[4,128,128]{2,1,0:T(8,128)(2,1)S(1)} %get-tuple-element.98), channel_id=1, source_target_pairs={{0,4},{1,5},{2,6},{3,7},{4,0},{5,1},{6,2},{7,3},{8,12},{9,13},{10,... | collective-permute-start | bytes 393224 | tf_op jit(solution)/shard_map/ppermute | solution.py:29
  20.4 7.3 %collective-permute-start.6 = (bf16[4,128,128]{2,1,0:T(8,128)(2,1)S(1)}, bf16[4,128,128]{2,1,0:T(8,128)(2,1)S(1)}, u32[]{:S(2)}, u32[]{:S(2)}) collective-permute-start(bf16[4,128,128]{2,1,0:T(8,128)(2,1)S(1)} %get-tuple-element.99), channel_id=1, source_target_pairs={{0,2},{1,3},{2,0},{3,1},{4,6},{5,7},{6,4},{7,5},{8,10},{9,11},{10,... | collective-permute-start | bytes 393224 | tf_op jit(solution)/shard_map/ppermute | solution.py:29
  24.7 3.0 %collective-permute-start.5 = (bf16[8,128,128]{2,1,0:T(8,128)(2,1)S(1)}, bf16[8,128,128]{2,1,0:T(8,128)(2,1)S(1)}, u32[]{:S(2)}, u32[]{:S(2)}) collective-permute-start(bf16[8,128,128]{2,1,0:T(8,128)(2,1)S(1)} %get-tuple-element.82), channel_id=1, source_target_pairs={{0,1},{1,0},{2,3},{3,2},{4,5},{5,4},{6,7},{7,6},{8,9},{9,8},{10,11... | collective-permute-start | bytes 786440 | tf_op jit(solution)/shard_map/ppermute | solution.py:29
  27.9 10.0 %collective-permute-start.9 = (bf16[8,128,128]{2,1,0:T(8,128)(2,1)S(1)}, bf16[8,128,128]{2,1,0:T(8,128)(2,1)S(1)}, u32[]{:S(2)}, u32[]{:S(2)}) collective-permute-start(bf16[8,128,128]{2,1,0:T(8,128)(2,1)S(1)} %add_convert_fusion.1), channel_id=1, source_target_pairs={{0,6},{1,7},{2,0},{3,1},{4,2},{5,3},{6,4},{7,5},{8,14},{9,15},{10,... | collective-permute-start | bytes 786440 | tf_op jit(solution)/shard_map/ppermute | solution.py:19
  29.4 6.1 %collective-permute-start.12 = (bf16[1,128,128]{2,1,0:T(8,128)(2,1)S(1)}, bf16[1,128,128]{2,1,0:T(8,128)(2,1)S(1)}, u32[]{:S(2)}, u32[]{:S(2)}) collective-permute-start(bf16[1,128,128]{2,1,0:T(8,128)(2,1)S(1)} %get-tuple-element.100), channel_id=1, source_target_pairs={{0,24},{8,16},{16,8},{24,0},{1,25},{9,17},{17,9},{25,1},{2,26},{10... | collective-permute-start | bytes 98312 | tf_op jit(solution)/shard_map/ppermute | solution.py:29
  33.0 3.9 %collective-permute-start.11 = (bf16[1,128,128]{2,1,0:T(8,128)(2,1)S(1)}, bf16[1,128,128]{2,1,0:T(8,128)(2,1)S(1)}, u32[]{:S(2)}, u32[]{:S(2)}) collective-permute-start(bf16[1,128,128]{2,1,0:T(8,128)(2,1)S(1)} %get-tuple-element.101), channel_id=1, source_target_pairs={{0,8},{8,0},{16,24},{24,16},{1,9},{9,1},{17,25},{25,17},{2,10},{10... | collective-permute-start | bytes 98312 | tf_op jit(solution)/shard_map/ppermute | solution.py:29
  33.0 4.8 %collective-permute-start.10 = (bf16[1,128,128]{2,1,0:T(8,128)(2,1)S(1)}, bf16[1,128,128]{2,1,0:T(8,128)(2,1)S(1)}, u32[]{:S(2)}, u32[]{:S(2)}) collective-permute-start(bf16[1,128,128]{2,1,0:T(8,128)(2,1)S(1)} %get-tuple-element.102), channel_id=1, source_target_pairs={{0,16},{8,24},{16,0},{24,8},{1,17},{9,25},{17,1},{25,9},{2,18},{10... | collective-permute-start | bytes 98312 | tf_op jit(solution)/shard_map/ppermute | solution.py:29

commit v16 on v15

--- a/solution.py
+++ b/solution.py
@@ -226,18 +226,21 @@
 
 
 def middle_kernel(
-    queries_ref, one_ref, bias_ref, fold_ref, stats_ref, low_ref, one_keys_ref, wide_ref, *, kv, group, scaling,
+    queries_ref, one_ref, bias_ref, fold_ref, stats_ref, low_ref, one_keys_ref, wide_ref,
+    *, kv, group, scaling, first,
 ):
     tokens = one_keys_ref.shape[1]
     _, here = places(queries_ref.shape[1], tokens, group)
     head_major(one_ref, wide_ref, [one_keys_ref.at[m] for m in range(kv)])
+    count = low_ref.shape[0]
 
     def scores_of(g):
         return dot(one_keys_ref[g], queries_ref[g], 1, 1)
 
-    scores = scores_of(0)
-    for g in range(kv):
-        ahead = scores_of(g + 1) if g + 1 < kv else None
+    scores = scores_of(first)
+    for at in range(count):
+        g = first + at
+        ahead = scores_of(g + 1) if at + 1 < count else None
         mid = scores * scaling + bias_ref[1]
         fold_top = stats_ref[g, 0:1, :]
         top = jnp.maximum(fold_top, jnp.max(mid, axis=0, keepdims=True))
@@ -245,67 +248,104 @@
         fade = jnp.exp(fold_top - top)
         share = 1.0 / (stats_ref[g, 1:2, :] * fade + jnp.sum(mid, axis=0, keepdims=True))
         fold = fold_ref[g] * (fade * share)
-        low_ref[g, 0:tokens, :] = jnp.where(here, 0.0, fold).astype(LOW)
-        low_ref[g, tokens : 2 * tokens, :] = (mid * share).astype(LOW)
-        low_ref[g, 2 * tokens :, :] = jnp.where(here, fold, 0.0).astype(LOW)
+        low_ref[at, 0:tokens, :] = jnp.where(here, 0.0, fold).astype(LOW)
+        low_ref[at, tokens : 2 * tokens, :] = (mid * share).astype(LOW)
+        low_ref[at, 2 * tokens :, :] = jnp.where(here, fold, 0.0).astype(LOW)
         scores = ahead
 
 
+def half_of(refs, g):
+    return refs[g // refs[0].shape[0]].at[g % refs[0].shape[0]]
+
+
+def hidden_kernel(near_ref, far_ref, two_ref, own_ref, part_ref, two_values_ref, own_values_ref, wide_ref, *, kv):
+    tokens, dim = two_values_ref.shape[1:]
+    for at, (ref, values_ref) in enumerate(((two_ref, two_values_ref), (own_ref, own_values_ref))):
+        head_major(ref, wide_ref.at[at], [values_ref.at[m] for m in range(kv)])
+    for g in range(kv):
+        low_ref = half_of((near_ref, far_ref), g)
+        part_ref[g * dim : (g + 1) * dim, :] = dot(two_values_ref[g], low_ref[0:tokens, :], 0, 0) + dot(
+            own_values_ref[g], low_ref[2 * tokens :, :], 0, 0
+        )
+
+
+def sent_slots(group, owned, odd):
+    return [slot for slot in range(group) if (slot // owned) % 2 == odd]
+
+
+def write_parts(into, slots, on_rot, on_proj, kv, group, owned, span, dim):
+    rep, me = lax.axis_size("rep"), lax.axis_index("ctx")
+    per_group = group // owned
+    here_rows = span // rep
+    for g in range(kv):
+        columns = slice(g * dim, (g + 1) * dim)
+        for low in sorted({slot // owned for slot in slots}):
+            device = (g ^ (me // per_group)) * per_group + low
+            for r in range(rep):
+                pieces = []
+                for slot in range(low * owned, (low + 1) * owned):
+                    first = slots.index(slot) * span + r * here_rows
+                    rows = slice(first, first + here_rows)
+                    pieces += [on_rot[rows, columns], on_proj[rows, columns]]
+                into[reduce_place(dict(ctx=device, rep=r))] = jnp.concatenate(pieces, axis=0).astype(LOW)
+
+
 def forward_kernel(
-    shift_ref, low_ref, two_ref, one_ref, own_ref, cots_ref, diff_ref, meta_ref, pull_ref,
-    send_ref, keep_ref, values_ref, wide_ref, *, kv, group, tenants, rank, owned,
-):
-    dim = own_ref.shape[1]
-    tokens = own_ref.shape[0] // kv
-    for at, ref in enumerate((two_ref, one_ref, own_ref)):
-        rows = slice(at * tokens, (at + 1) * tokens)
-        head_major(ref, wide_ref.at[at], [values_ref.at[m, rows] for m in range(kv)])
+    shift_ref, near_ref, far_ref, part_ref, one_ref, cots_ref, diff_ref, meta_ref, pull_ref,
+    send_ref, hidden_ref, lift_ref, one_values_ref, wide_ref, *, kv, group, tenants, rank, owned,
+):
+    tokens, dim = one_values_ref.shape[1:]
+    head_major(one_ref, wide_ref, [one_values_ref.at[m] for m in range(kv)])
     owner = meta_ref[1:2, :]
     lanes = owner.shape[1]
     hidden = []
     for g in range(kv):
-        hidden.append(dot(values_ref[g], low_ref[g], 0, 0).astype(LOW))
+        low_ref = half_of((near_ref, far_ref), g)
+        middle = dot(one_values_ref[g], low_ref[tokens : 2 * tokens, :], 0, 0)
+        hidden.append((part_ref[g * dim : (g + 1) * dim, :] + middle).astype(LOW))
     hidden = jnp.concatenate(hidden, axis=0)
+    hidden_ref[...] = hidden
     on_diff = dot(jnp.concatenate([diff_ref[g] for g in range(kv)], axis=1), hidden, 1, 0)
     lifted = own_terms(on_diff, owner, tenants, rank, group)
     one_hot = (owner == lax.broadcasted_iota(jnp.int32, (tenants, lanes), 0)).astype(WIDE)
     bias = jnp.concatenate([shift_ref[...]] * (8 // rank), axis=0)
     shift = dot(bias, one_hot, 1, 0, lax.Precision.HIGHEST)
     lifted = (lifted + shift).astype(LOW).astype(WIDE)
-    rep = lax.axis_size("rep")
-    me = lax.axis_index("ctx")
-    per_group = group // owned
     span = tenants * rank
-    slots = slots_of(lanes, group, owned)
-    lift_all = jnp.concatenate(picked_rows(lifted, owner, slots, tenants, rank, group), axis=0)
-    on_proj = dot(pull_ref[...], hidden, 1, 1)
-    on_rot = dot(lift_all, jnp.concatenate([cots_ref[g] for g in range(kv)], axis=1), 1, 0) - on_proj
-    here_rows = span // rep
-    for g in range(kv):
-        columns = slice(g * dim, (g + 1) * dim)
-        for low in range(per_group):
-            device = (g ^ (me // per_group)) * per_group + low
-            into = send_ref if low % 2 else keep_ref
-            for r in range(rep):
-                pieces = []
-                for h in range(low * owned, (low + 1) * owned):
-                    rows = slice(h * span + r * here_rows, h * span + (r + 1) * here_rows)
-                    pieces += [on_rot[rows, columns], on_proj[rows, columns]]
-                into[reduce_place(dict(ctx=device, rep=r))] = jnp.concatenate(pieces, axis=0).astype(LOW)
+    lifts = picked_rows(lifted, owner, slots_of(lanes, group, owned), tenants, rank, group)
+    for at, slot in enumerate(sent_slots(group, owned, 0)):
+        lift_ref[at * span : (at + 1) * span, :] = lifts[slot]
+    slots = sent_slots(group, owned, 1)
+    pulls = [pull_ref[slot * span : (slot + 1) * span, :] for slot in slots]
+    on_proj = dot(jnp.concatenate(pulls, axis=0), hidden, 1, 1)
+    cots = jnp.concatenate([cots_ref[g] for g in range(kv)], axis=1)
+    on_rot = dot(jnp.concatenate([lifts[slot] for slot in slots], axis=0), cots, 1, 0) - on_proj
+    write_parts(send_ref, slots, on_rot, on_proj, kv, group, owned, span, dim)
+
+
+def keep_kernel(hidden_ref, lift_ref, cots_ref, pull_ref, keep_ref, *, kv, group, span, owned):
+    dim = cots_ref.shape[2]
+    slots = sent_slots(group, owned, 0)
+    pulls = [pull_ref[slot * span : (slot + 1) * span, :] for slot in slots]
+    on_proj = dot(jnp.concatenate(pulls, axis=0), hidden_ref[...], 1, 1)
+    cots = jnp.concatenate([cots_ref[g] for g in range(kv)], axis=1)
+    on_rot = dot(lift_ref[...], cots, 1, 0) - on_proj
+    write_parts(keep_ref, slots, on_rot, on_proj, kv, group, owned, span, dim)
 
 
 def backward_kernel(
-    queries_ref, gh_ref, low_ref, values_ref, back_two_ref, back_one_ref, back_own_ref, grad_ref, *, kv, scaling,
+    queries_ref, gh_ref, near_ref, far_ref, two_ref, one_ref, own_ref, back_two_ref, back_one_ref, back_own_ref, grad_ref,
+    *, kv, scaling,
 ):
     tokens = back_own_ref.shape[1]
 
     def weight_grad_of(g):
-        return dot(values_ref[g], gh_ref[g], 1, 1)
+        return dot(window_of(two_ref, one_ref, own_ref, g), gh_ref[g], 1, 1)
 
     weight_grad = weight_grad_of(0)
     for g in range(kv):
         ahead = weight_grad_of(g + 1) if g + 1 < kv else None
-        low = low_ref[g]
+        low = half_of((near_ref, far_ref), g)[...]
         weights = low.astype(WIDE)
         delta = jnp.sum(weights * weight_grad, axis=0, keepdims=True)
         score_grad = (weights * (weight_grad - delta)).astype(LOW)
@@ -424,28 +464,40 @@
         fold_kernel, [((kv, tokens, lanes), WIDE), ((kv, 2, lanes), WIDE), heads_first, heads_first],
         2 * 2**30, 4 * 2**20, scratch=[pltpu.VMEM((2, *flat), WIDE)], scaling=scaling, **sizes,
     )(queries, two_keys.reshape(flat), own_keys.reshape(flat), biases)
-    one_keys, two_values, fold = lax.optimization_barrier((one_keys, two_values, fold))
+    one_keys, fold = lax.optimization_barrier((one_keys, fold))
+
+    def weights_of(first):
+        return call(
+            middle_kernel, [((kv // 2, 3 * tokens, lanes), LOW), heads_first], 2**30, 4 * 2**20,
+            scratch=[pltpu.VMEM(flat, WIDE)], scaling=scaling, first=first, **sizes,
+        )(queries, one_keys.reshape(flat), biases, fold, stats)
+
+    near, one_heads = weights_of(0)
+    two_values, near = lax.optimization_barrier((two_values, near))
     one_values = exchanged(jnp.where(even, own_values, two_values), {"ctx": 1})
-    low, one_heads = call(
-        middle_kernel, [((kv, 3 * tokens, lanes), LOW), heads_first], 2 * 2**30, 4 * 2**20,
-        scratch=[pltpu.VMEM(flat, WIDE)], scaling=scaling, **sizes,
-    )(queries, one_keys.reshape(flat), biases, fold, stats)
-    one_values, low = lax.optimization_barrier((one_values, low))
-    send, keep, values = call(
-        forward_kernel, [((ctx * rep // 2, rows, dim), LOW)] * 2 + [((kv, 3 * tokens, dim), LOW)],
-        4 * 2**30, 10 * 2**20, scratch=[pltpu.VMEM((3, *flat), WIDE)],
+    far, _ = weights_of(kv // 2)
+    part_hidden, two_sides, own_sides = call(
+        hidden_kernel, [((heads // group * dim, lanes), WIDE), heads_first, heads_first], 2**30, 4 * 2**20,
+        scratch=[pltpu.VMEM((2, *flat), WIDE)], kv=kv,
+    )(near, far, two_values.reshape(flat), own_values.reshape(flat))
+    one_values, part_hidden = lax.optimization_barrier((one_values, part_hidden))
+    kept = (span * group // 2, lanes)
+    send, hidden, lift, one_sides = call(
+        forward_kernel,
+        [((ctx * rep // 2, rows, dim), LOW), (part_hidden.shape, LOW), (kept, LOW), heads_first],
+        3 * 2**30, 10 * 2**20, scratch=[pltpu.VMEM(flat, WIDE)],
         tenants=tenants, rank=rank, owned=here, **sizes,
-    )(
-        shift_bias.T, low, two_values.reshape(flat), one_values.reshape(flat), own_values.reshape(flat),
-        cots, diff, meta, pull,
-    )
+    )(shift_bias.T, near, far, part_hidden, one_values.reshape(flat), cots, diff, meta, pull)
+    keep, = call(
+        keep_kernel, [((ctx * rep // 2, rows, dim), LOW)], 2**30, 5 * 2**20, span=span, owned=here, **sizes,
+    )(hidden, lift, cots, pull)
     part = (keep.astype(WIDE) + exchanged(send, {"ctx": 1}).astype(WIDE)).astype(LOW)
-    low, part = lax.optimization_barrier((low, part))
+    near, part = lax.optimization_barrier((near, part))
     window = (2 * kv, tokens, dim)
     back_two, back_one, back_own, score_grad = call(
         backward_kernel, [(window, LOW), (window, LOW), (window, WIDE), ((kv, 3 * tokens, lanes), LOW)],
         4 * 2**30, 10 * 2**20, kv=kv, scaling=scaling,
-    )(queries, grad_hidden, low, values)
+    )(queries, grad_hidden, near, far, two_sides, one_sides, own_sides)
     d_queries, = call(
         query_kernel, [((tokens, heads, dim), LOW)], 2 * 2**30, 5 * 2**20,
         scratch=[pltpu.VMEM((tokens, heads, dim), LOW), pltpu.SemaphoreType.DMA((kv // 2,))],

time: 39 us -> 38.5 us (0.987)
  waiting for transfers between devices: 7.79 us -> 6 us
  Pallas kernels: 13.5 us -> 14.5 us
    pallas_call x9 -> x12, Pallas kernels: 13.5 us -> 14.5 us  [run(): pl.pallas_call(lambda *refs: body(*refs, **fixed), out_shape=[jax.ShapeDt...]
    ppermute x3, waiting for transfers between devices: 0.98 us -> 0.01 us  [shifted(): lax.ppermute(value, axis, [(source, (source + steps) % count) for source...]
    ppermute x10, waiting for transfers between devices: 6.81 us -> 5.99 us  [exchanged(): lax.ppermute(value, axes, [(int(source), int(target)) for source, target...]
  transfers between devices with their start and end apart: 13 -> 13, of which waited for: 7 -> 6; matrix products, arithmetic and copies ran while one was open for 2% -> 2% of each run, Pallas kernels for 25% -> 31%
where the time goes in v16:
time: 38.5 us; the launch traced here: 38.3 us
  starting transfers between devices  15.1 us (39%)
  Pallas kernels  14.5 us (38%)
  waiting for transfers between devices  6 us (16%)
  other arithmetic  1.11 us (3%)
  between operations  0.89 us (2%)
  local copies, waits for them, and re-layouts  0.68 us (2%)
    pallas_call x12, Pallas kernels, run(): pl.pallas_call(lambda *refs: body(*refs, **fixed), out_shape=[jax.ShapeDt...  14.5 us
    ppermute x10, starting transfers between devices, exchanged(): lax.ppermute(value, axes, [(int(source), int(target)) for source, target...  8.81 us
    ppermute x3, starting transfers between devices, shifted(): lax.ppermute(value, axis, [(source, (source + steps) % count) for source...  6.28 us
    ppermute x10, waiting for transfers between devices, exchanged(): lax.ppermute(value, axes, [(int(source), int(target)) for source, target...  5.99 us
  transfers between devices with their start and end apart: 13, of which 6 were waited for; matrix products, arithmetic and copies ran while one was open for 2% of the time, Pallas kernels for 31%

profile of v16, /device:TPU:0, one launch (start us, length us, event | category | flops | bytes accessed | tf_op | source)
XLA Modules:
  0.0 38.3 jit_solution(15523996690858668686)
XLA Ops:
  0.6 3.0 %collective-permute-start = (bf16[128,4,128]{2,1,0:T(4,128)(2,1)}, bf16[128,4,128]{2,1,0:T(4,128)(2,1)S(1)}, u32[]{:S(2)}, u32[]{:S(2)}) collective-permute-start(bf16[128,4,128]{2,1,0:T(4,128)(2,1)} %bitcast.26), channel_id=1, source_target_pairs={{0,2},{1,3},{2,4},{3,5},{4,6},{5,7},{6,0},{7,1},{8,10},{9,11},{10,... | collective-permute-start | bytes 393224 | tf_op jit(solution)/shard_map/ppermute | solution.py:19
  3.6 0.7 %pad_add_fusion.refs_0_ = s32[2,1024]{1,0:T(2,128)S(1)} fusion(s32[1,1024]{1,0:T(1,128)} %param.17, s32[1,1024]{1,0:T(1,128)} %param.16), kind=kLoop, calls=%fused_computation.5 | loop fusion | flops 2048 | bytes 16384 | tf_op jit(solution)/shard_map/concatenate | solution.py:448
  4.4 0.0 copy-start.1
  4.4 0.0 copy-start.2
  4.4 0.0 copy-start.3
  4.4 0.0 copy-start.4
  4.4 0.3 place_kernel.1
  4.8 0.0 copy-start.5
  4.8 0.5 %copy-done.1 = bf16[1,128,4,128]{3,2,1,0:T(4,128)(2,1)S(1)} copy-done((bf16[1,128,4,128]{3,2,1,0:T(4,128)(2,1)S(1)}, bf16[1,128,4,128]{3,2,1,0:T(4,128)(2,1)}, u32[]{:S(2)}) %copy-start.1) | copy-done | bytes 131096
  5.3 1.5 %collective-permute-start.1 = (bf16[128,4,128]{2,1,0:T(4,128)(2,1)S(1)}, bf16[128,4,128]{2,1,0:T(4,128)(2,1)S(1)}, u32[]{:S(2)}, u32[]{:S(2)}) collective-permute-start(bf16[128,4,128]{2,1,0:T(4,128)(2,1)S(1)} %bitcast.28), channel_id=1, source_target_pairs={{0,2},{1,3},{2,4},{3,5},{4,6},{5,7},{6,0},{7,1},{8,10},{9,11},{10,... | collective-permute-start | bytes 393224 | tf_op jit(solution)/shard_map/ppermute | solution.py:19
  6.8 0.0 copy-done.2
  6.8 0.0 copy-done.3
  6.8 0.0 copy-done.4
  6.8 1.4 %pull_kernel.1 = (bf16[4,1024,128]{2,1,0:T(8,128)(2,1)S(1)}, bf16[4,1024,128]{2,1,0:T(8,128)(2,1)S(1)}, f32[8,1024]{1,0:T(8,128)S(1)}, bf16[512,1024]{1,0:T(8,128)(2,1)S(1)}) custom-call(s32[8,1024]{1,0:T(8,128)S(1)} %get-tuple-element.58.refs_0_.refs_7_, bf16[128,32,128]{2,1,0:T(8,128)(2,1)S(1)} %bitcast.34, bf16[64,32,128]{2,1,0:T(8,128)(2,1)S(1)} %bitcast.36, ...), custom_call_target="tpu_custom_call" | custom-call | flops 1073741824 | bytes 4194304 | tf_op jit(solution)/shard_map/pull_kernel/pallas_call | solution.py:425
  8.2 0.0 copy-done.5
  8.2 0.0 copy-start
  8.2 0.8 %hidden_grad_kernel.1 = (bf16[4,1024,128]{2,1,0:T(8,128)(2,1)S(1)}, bf16[4,512,128]{2,1,0:T(8,128)(2,1)S(1)}) custom-call(s32[8,1024]{1,0:T(8,128)S(1)} %get-tuple-element.58.refs_0_.refs_7_, f32[8,1024]{1,0:T(8,128)S(1)} %get-tuple-element.61.refs_1_, bf16[4,1024,128]{2,1,0:T(8,128)(2,1)S(1)} %get-tuple-element.62.refs_2_.refs_5_, ...), custom_call_target="tpu_custom_call" | custom-call | flops 2147483648 | bytes 4194304 | tf_op jit(solution)/shard_map/hidden_grad_kernel/pallas_call | solution.py:425
  9.0 0.0 collective-permute-done
  9.0 0.1 copy-done
  9.1 0.1 broadcast_select_fusion.1
  9.2 0.1 collective-permute-start.2
  9.2 0.9 %fold_kernel.1 = (f32[4,128,1024]{2,1,0:T(8,128)S(1)}, f32[4,2,1024]{2,1,0:T(2,128)S(1)}, bf16[4,128,128]{2,1,0:T(8,128)(2,1)S(1)}, bf16[4,128,128]{2,1,0:T(8,128)(2,1)S(1)}) custom-call(bf16[4,1024,128]{2,1,0:T(8,128)(2,1)S(1)} %get-tuple-element.59.refs_0_, bf16[512,128]{1,0:T(8,128)(2,1)S(1)} %bitcast.33, bf16[512,128]{1,0:T(8,128)(2,1)S(1)} %bitcast.27, ...), custom_call_target="tpu_custom_call" | custom-call | flops 2147483648 | bytes 4194304 | tf_op jit(solution)/shard_map/fold_kernel/pallas_call | solution.py:425
  10.2 0.4 %collective-permute-done.2 = bf16[128,4,128]{2,1,0:T(4,128)(2,1)S(1)} collective-permute-done((bf16[128,4,128]{2,1,0:T(4,128)(2,1)S(1)}, bf16[128,4,128]{2,1,0:T(4,128)(2,1)S(1)}, u32[]{:S(2)}, u32[]{:S(2)}) %collective-permute-start.2) | collective-permute-done | bytes 131104 | tf_op jit(solution)/shard_map/ppermute | solution.py:29
  10.6 0.8 %middle_kernel.2 = (bf16[2,384,1024]{2,1,0:T(8,128)(2,1)S(1)}, bf16[4,128,128]{2,1,0:T(8,128)(2,1)S(1)}) custom-call(bf16[4,1024,128]{2,1,0:T(8,128)(2,1)S(1)} %get-tuple-element.59.refs_0_, bf16[512,128]{1,0:T(8,128)(2,1)S(1)} %bitcast.24, f32[2,128,1024]{2,1,0:T(8,128)S(1)} %get-tuple-element.68.refs_3_.refs_2_, ...), custom_call_target="tpu_custom_call" | custom-call | flops 1073741824 | bytes 4194304 | tf_op jit(solution)/shard_map/middle_kernel/pallas_call | solution.py:425
  11.4 0.0 collective-permute-done.1
  11.4 0.2 collective-permute-start.3
  11.6 0.8 %middle_kernel.3 = (bf16[2,384,1024]{2,1,0:T(8,128)(2,1)S(1)}, bf16[4,128,128]{2,1,0:T(8,128)(2,1)}) custom-call(bf16[4,1024,128]{2,1,0:T(8,128)(2,1)S(1)} %get-tuple-element.59.refs_0_, bf16[512,128]{1,0:T(8,128)(2,1)S(1)} %bitcast.25, f32[2,128,1024]{2,1,0:T(8,128)S(1)} %get-tuple-element.68.refs_3_.refs_2_, ...), custom_call_target="tpu_custom_call" | custom-call | flops 1073741824 | bytes 4194304 | tf_op jit(solution)/shard_map/middle_kernel/pallas_call | solution.py:425
  12.4 0.0 copy-start.6
  12.5 0.8 %hidden_kernel.1 = (f32[512,1024]{1,0:T(8,128)S(1)}, bf16[4,128,128]{2,1,0:T(8,128)(2,1)S(1)}, bf16[4,128,128]{2,1,0:T(8,128)(2,1)S(1)}) custom-call(bf16[2,384,1024]{2,1,0:T(8,128)(2,1)S(1)} %get-tuple-element.85.refs_0_.refs_1_.refs_2_, bf16[2,384,1024]{2,1,0:T(8,128)(2,1)S(1)} %get-tuple-element.75.refs_1_.refs_2_.refs_3_, bf16[512,128]{1,0:T(8,128)(2,1)S(1)} %bitcast.32, ...), custom_call_target="tpu_custom_call" | custom-call | flops 1073741824 | bytes 4194304 | tf_op jit(solution)/shard_map/hidden_kernel/pallas_call | solution.py:425
  13.2 0.0 collective-permute-done.3
  13.3 0.0 copy-done.6
  13.3 2.0 %forward_kernel.1 = (bf16[16,128,128]{2,1,0:T(8,128)(2,1)S(1)}, bf16[512,1024]{1,0:T(8,128)(2,1)S(1)}, bf16[256,1024]{1,0:T(8,128)(2,1)S(1)}, bf16[4,128,128]{2,1,0:T(8,128)(2,1)S(1)}) custom-call(f32[4,16]{1,0:T(4,128)S(1)} %bitcast.40, bf16[2,384,1024]{2,1,0:T(8,128)(2,1)S(1)} %get-tuple-element.85.refs_0_.refs_1_.refs_2_, ...), custom_call_target="tpu_custom_call" | custom-call | flops 3221225472 | bytes 10485760 | tf_op jit(solution)/shard_map/forward_kernel/pallas_call | solution.py:425
  15.3 0.4 %collective-permute-start.4 = (bf16[16,128,128]{2,1,0:T(8,128)(2,1)S(1)}, bf16[16,128,128]{2,1,0:T(8,128)(2,1)S(1)}, u32[]{:S(2)}, u32[]{:S(2)}) collective-permute-start(bf16[16,128,128]{2,1,0:T(8,128)(2,1)S(1)} %get-tuple-element.84), channel_id=1, source_target_pairs={{0,1},{1,0},{2,3},{3,2},{4,5},{5,4},{6,7},{7,6},{8,9},{9,8},{10,11... | collective-permute-start | bytes 1572872 | tf_op jit(solution)/shard_map/ppermute | solution.py:29
  15.7 0.8 %keep_kernel.1 = bf16[16,128,128]{2,1,0:T(8,128)(2,1)S(1)} custom-call(bf16[512,1024]{1,0:T(8,128)(2,1)S(1)} %get-tuple-element.82.refs_0_, bf16[256,1024]{1,0:T(8,128)(2,1)S(1)} %get-tuple-element.83.refs_1_, bf16[4,1024,128]{2,1,0:T(8,128)(2,1)S(1)} %get-tuple-element.62.refs_2_.refs_5_, bf16[512,1024]{1,0:T(8,128)(2,1)S(1)} %get-tuple-element.81.refs_8_.refs_3_), custom_call_target="tpu_custom_call" | custom-call | flops 1073741824 | bytes 5242880 | tf_op jit(solution)/shard_map/keep_kernel/pallas_call | solution.py:425
  16.5 0.8 %collective-permute-done.4 = bf16[16,128,128]{2,1,0:T(8,128)(2,1)S(1)} collective-permute-done((bf16[16,128,128]{2,1,0:T(8,128)(2,1)S(1)}, bf16[16,128,128]{2,1,0:T(8,128)(2,1)S(1)}, u32[]{:S(2)}, u32[]{:S(2)}) %collective-permute-start.4) | collective-permute-done | bytes 524320 | tf_op jit(solution)/shard_map/ppermute | solution.py:29
  17.3 0.1 add_convert_fusion
  17.5 2.2 %collective-permute-start.8 = (bf16[4,128,128]{2,1,0:T(8,128)(2,1)S(1)}, bf16[4,128,128]{2,1,0:T(8,128)(2,1)S(1)}, u32[]{:S(2)}, u32[]{:S(2)}) collective-permute-start(bf16[4,128,128]{2,1,0:T(8,128)(2,1)S(1)} %get-tuple-element.109), channel_id=1, source_target_pairs={{0,6},{1,7},{2,4},{3,5},{4,2},{5,3},{6,0},{7,1},{8,14},{9,15},{10,... | collective-permute-start | bytes 393224 | tf_op jit(solution)/shard_map/ppermute | solution.py:29
  19.6 0.9 %collective-permute-start.7 = (bf16[4,128,128]{2,1,0:T(8,128)(2,1)S(1)}, bf16[4,128,128]{2,1,0:T(8,128)(2,1)S(1)}, u32[]{:S(2)}, u32[]{:S(2)}) collective-permute-start(bf16[4,128,128]{2,1,0:T(8,128)(2,1)S(1)} %get-tuple-element.110), channel_id=1, source_target_pairs={{0,4},{1,5},{2,6},{3,7},{4,0},{5,1},{6,2},{7,3},{8,12},{9,13},{10,... | collective-permute-start | bytes 393224 | tf_op jit(solution)/shard_map/ppermute | solution.py:29
  20.5 0.5 %collective-permute-start.6 = (bf16[4,128,128]{2,1,0:T(8,128)(2,1)S(1)}, bf16[4,128,128]{2,1,0:T(8,128)(2,1)S(1)}, u32[]{:S(2)}, u32[]{:S(2)}) collective-permute-start(bf16[4,128,128]{2,1,0:T(8,128)(2,1)S(1)} %get-tuple-element.111), channel_id=1, source_target_pairs={{0,2},{1,3},{2,0},{3,1},{4,6},{5,7},{6,4},{7,5},{8,10},{9,11},{10,... | collective-permute-start | bytes 393224 | tf_op jit(solution)/shard_map/ppermute | solution.py:29
  21.0 3.4 %backward_kernel.1 = (bf16[8,128,128]{2,1,0:T(8,128)(2,1)S(1)}, bf16[8,128,128]{2,1,0:T(8,128)(2,1)S(1)}, f32[8,128,128]{2,1,0:T(8,128)S(1)}, bf16[4,384,1024]{2,1,0:T(8,128)(2,1)S(1)}) custom-call(bf16[4,1024,128]{2,1,0:T(8,128)(2,1)S(1)} %get-tuple-element.59.refs_0_, bf16[4,1024,128]{2,1,0:T(8,128)(2,1)S(1)} %get-tuple-element.64.refs_1_, ...), custom_call_target="tpu_custom_call" | custom-call | flops 4294967296 | bytes 10485760 | tf_op jit(solution)/shard_map/backward_kernel/pallas_call | solution.py:425
  24.5 0.1 collective-permute-start.5
  24.6 0.2 collective-permute-done.8
  24.7 2.2 %collective-permute-done.7 = bf16[4,128,128]{2,1,0:T(8,128)(2,1)S(1)} collective-permute-done((bf16[4,128,128]{2,1,0:T(8,128)(2,1)S(1)}, bf16[4,128,128]{2,1,0:T(8,128)(2,1)S(1)}, u32[]{:S(2)}, u32[]{:S(2)}) %collective-permute-start.7) | collective-permute-done | bytes 131104 | tf_op jit(solution)/shard_map/ppermute | solution.py:29
  27.0 0.0 collective-permute-done.6
  27.0 0.1 add_convert_fusion.2
  27.1 0.0 collective-permute-done.5.refs_1_
  27.1 0.1 add_convert_fusion.1
  27.2 1.8 %collective-permute-start.9 = (bf16[8,128,128]{2,1,0:T(8,128)(2,1)S(1)}, bf16[8,128,128]{2,1,0:T(8,128)(2,1)S(1)}, u32[]{:S(2)}, u32[]{:S(2)}) collective-permute-start(bf16[8,128,128]{2,1,0:T(8,128)(2,1)S(1)} %add_convert_fusion.1), channel_id=1, source_target_pairs={{0,6},{1,7},{2,0},{3,1},{4,2},{5,3},{6,4},{7,5},{8,14},{9,15},{10,... | collective-permute-start | bytes 786440 | tf_op jit(solution)/shard_map/ppermute | solution.py:19
  29.0 3.7 %collective-permute-start.12 = (bf16[1,128,128]{2,1,0:T(8,128)(2,1)S(1)}, bf16[1,128,128]{2,1,0:T(8,128)(2,1)S(1)}, u32[]{:S(2)}, u32[]{:S(2)}) collective-permute-start(bf16[1,128,128]{2,1,0:T(8,128)(2,1)S(1)} %get-tuple-element.112), channel_id=1, source_target_pairs={{0,24},{8,16},{16,8},{24,0},{1,25},{9,17},{17,9},{25,1},{2,26},{10... | collective-permute-start | bytes 98312 | tf_op jit(solution)/shard_map/ppermute | solution.py:29
  32.7 0.0 collective-permute-start.11
  32.7 0.8 %collective-permute-start.10 = (bf16[1,128,128]{2,1,0:T(8,128)(2,1)S(1)}, bf16[1,128,128]{2,1,0:T(8,128)(2,1)S(1)}, u32[]{:S(2)}, u32[]{:S(2)}) collective-permute-start(bf16[1,128,128]{2,1,0:T(8,128)(2,1)S(1)} %get-tuple-element.114), channel_id=1, source_target_pairs={{0,16},{8,24},{16,0},{24,8},{1,17},{9,25},{17,1},{25,9},{2,18},{10... | collective-permute-start | bytes 98312 | tf_op jit(solution)/shard_map/ppermute | solution.py:29
  33.5 1.6 %query_kernel.1 = bf16[128,32,128]{2,1,0:T(8,128)(2,1)} custom-call(bf16[4,384,1024]{2,1,0:T(8,128)(2,1)S(1)} %get-tuple-element.89.refs_0_, bf16[4,128,128]{2,1,0:T(8,128)(2,1)S(1)} %get-tuple-element.90.refs_1_, bf16[4,128,128]{2,1,0:T(8,128)(2,1)S(1)} %get-tuple-element.91.refs_2_, bf16[4,128,128]{2,1,0:T(8,128)(2,1)S(1)} %get-tuple-element.92.refs_3_), custom_call_target="tpu_custom_call" | custom-call | flops 2147483648 | bytes 5242880 | tf_op jit(solution)/shard_map/query_kernel/pallas_call | solution.py:425
  35.1 0.0 collective-permute-done.12.refs_6_
  35.1 1.5 %collective-permute-done.11.refs_5_ = bf16[1,128,128]{2,1,0:T(8,128)(2,1)S(1)} collective-permute-done((bf16[1,128,128]{2,1,0:T(8,128)(2,1)S(1)}, bf16[1,128,128]{2,1,0:T(8,128)(2,1)S(1)}, u32[]{:S(2)}, u32[]{:S(2)}) %collective-permute-start.11) | collective-permute-done | bytes 32800 | tf_op jit(solution)/shard_map/ppermute | solution.py:29
  36.6 0.9 %collective-permute-done.10.refs_4_ = bf16[1,128,128]{2,1,0:T(8,128)(2,1)S(1)} collective-permute-done((bf16[1,128,128]{2,1,0:T(8,128)(2,1)S(1)}, bf16[1,128,128]{2,1,0:T(8,128)(2,1)S(1)}, u32[]{:S(2)}, u32[]{:S(2)}) %collective-permute-start.10) | collective-permute-done | bytes 32800 | tf_op jit(solution)/shard_map/ppermute | solution.py:29
  37.5 0.0 collective-permute-done.9.refs_2_
  37.5 0.8 %finish_kernel.1 = (bf16[512,128]{1,0:T(8,128)(2,1)}, bf16[512,128]{1,0:T(8,128)(2,1)}, f32[16,4,128]{2,1,0:T(4,128)}, f32[16,4,128]{2,1,0:T(4,128)}) custom-call(f32[8,128,128]{2,1,0:T(8,128)S(1)} %get-tuple-element.93.refs_0_, bf16[8,128,128]{2,1,0:T(8,128)(2,1)S(1)} %collective-permute-done.5.refs_1_, ...), custom_call_target="tpu_custom_call" | custom-call | flops 1048576 | bytes 1048576 | tf_op jit(solution)/shard_map/finish_kernel/pallas_call | solution.py:425
  (3 shorter events, 0.1 us)
Async XLA Ops:
  0.6 8.3 %collective-permute-start = (bf16[128,4,128]{2,1,0:T(4,128)(2,1)}, bf16[128,4,128]{2,1,0:T(4,128)(2,1)S(1)}, u32[]{:S(2)}, u32[]{:S(2)}) collective-permute-start(bf16[128,4,128]{2,1,0:T(4,128)(2,1)} %bitcast.26), channel_id=1, source_target_pairs={{0,2},{1,3},{2,4},{3,5},{4,6},{5,7},{6,0},{7,1},{8,10},{9,11},{10,... | collective-permute-start | bytes 393224 | tf_op jit(solution)/shard_map/ppermute | solution.py:19
  4.4 0.9 %copy-start.1 = (bf16[1,128,4,128]{3,2,1,0:T(4,128)(2,1)S(1)}, bf16[1,128,4,128]{3,2,1,0:T(4,128)(2,1)}, u32[]{:S(2)}) copy-start(bf16[1,128,4,128]{3,2,1,0:T(4,128)(2,1)} %param.11) | copy-start | bytes 393220
  4.4 2.4 %copy-start.2 = (bf16[1,128,32,128]{3,2,1,0:T(8,128)(2,1)S(1)}, bf16[1,128,32,128]{3,2,1,0:T(8,128)(2,1)}, u32[]{:S(2)}) copy-start(bf16[1,128,32,128]{3,2,1,0:T(8,128)(2,1)} %param.12) | copy-start | bytes 3145732
  4.4 2.4 %copy-start.3 = (bf16[1,128,32,128]{3,2,1,0:T(8,128)(2,1)S(1)}, bf16[1,128,32,128]{3,2,1,0:T(8,128)(2,1)}, u32[]{:S(2)}) copy-start(bf16[1,128,32,128]{3,2,1,0:T(8,128)(2,1)} %param.9) | copy-start | bytes 3145732
  4.4 2.4 %copy-start.4 = (bf16[16,4,32,128]{3,2,1,0:T(8,128)(2,1)S(1)}, bf16[16,4,32,128]{3,2,1,0:T(8,128)(2,1)}, u32[]{:S(2)}) copy-start(bf16[16,4,32,128]{3,2,1,0:T(8,128)(2,1)} %param.13) | copy-start | bytes 1572868
  4.8 3.4 %copy-start.5 = (bf16[16,4,32,128]{3,2,1,0:T(8,128)(2,1)S(1)}, bf16[16,4,32,128]{3,2,1,0:T(8,128)(2,1)}, u32[]{:S(2)}) copy-start(bf16[16,4,32,128]{3,2,1,0:T(8,128)(2,1)} %param.14) | copy-start | bytes 1572868
  5.3 6.1 %collective-permute-start.1 = (bf16[128,4,128]{2,1,0:T(4,128)(2,1)S(1)}, bf16[128,4,128]{2,1,0:T(4,128)(2,1)S(1)}, u32[]{:S(2)}, u32[]{:S(2)}) collective-permute-start(bf16[128,4,128]{2,1,0:T(4,128)(2,1)S(1)} %bitcast.28), channel_id=1, source_target_pairs={{0,2},{1,3},{2,4},{3,5},{4,6},{5,7},{6,0},{7,1},{8,10},{9,11},{10,... | collective-permute-start | bytes 393224 | tf_op jit(solution)/shard_map/ppermute | solution.py:19
  8.2 0.9 %copy-start = (bf16[1,128,4,128]{3,2,1,0:T(4,128)(2,1)S(1)}, bf16[1,128,4,128]{3,2,1,0:T(4,128)(2,1)}, u32[]{:S(2)}) copy-start(bf16[1,128,4,128]{3,2,1,0:T(4,128)(2,1)} %param.10) | copy-start | bytes 393220
  9.2 1.4 %collective-permute-start.2 = (bf16[128,4,128]{2,1,0:T(4,128)(2,1)S(1)}, bf16[128,4,128]{2,1,0:T(4,128)(2,1)S(1)}, u32[]{:S(2)}, u32[]{:S(2)}) collective-permute-start(bf16[128,4,128]{2,1,0:T(4,128)(2,1)S(1)} %broadcast_select_fusion.1), channel_id=1, source_target_pairs={{0,1},{1,0},{2,3},{3,2},{4,5},{5,4},{6,7},{7,6},{8,9},{9,8},{10,11... | collective-permute-start | bytes 393224 | tf_op jit(solution)/shard_map/ppermute | solution.py:29
  11.4 1.8 %collective-permute-start.3 = (bf16[128,4,128]{2,1,0:T(4,128)(2,1)S(1)}, bf16[128,4,128]{2,1,0:T(4,128)(2,1)S(1)}, u32[]{:S(2)}, u32[]{:S(2)}) collective-permute-start(bf16[128,4,128]{2,1,0:T(4,128)(2,1)S(1)} %bitcast.41), channel_id=1, source_target_pairs={{0,1},{1,0},{2,3},{3,2},{4,5},{5,4},{6,7},{7,6},{8,9},{9,8},{10,11... | collective-permute-start | bytes 393224 | tf_op jit(solution)/shard_map/ppermute | solution.py:29
  12.4 0.8 %copy-start.6 = (f32[16,4]{0,1:T(4,128)S(1)}, f32[16,4]{0,1:T(4,128)}, u32[]{:S(2)}) copy-start(f32[16,4]{0,1:T(4,128)} %param.15) | copy-start | bytes 772
  15.3 2.0 %collective-permute-start.4 = (bf16[16,128,128]{2,1,0:T(8,128)(2,1)S(1)}, bf16[16,128,128]{2,1,0:T(8,128)(2,1)S(1)}, u32[]{:S(2)}, u32[]{:S(2)}) collective-permute-start(bf16[16,128,128]{2,1,0:T(8,128)(2,1)S(1)} %get-tuple-element.84), channel_id=1, source_target_pairs={{0,1},{1,0},{2,3},{3,2},{4,5},{5,4},{6,7},{7,6},{8,9},{9,8},{10,11... | collective-permute-start | bytes 1572872 | tf_op jit(solution)/shard_map/ppermute | solution.py:29
  17.5 7.3 %collective-permute-start.8 = (bf16[4,128,128]{2,1,0:T(8,128)(2,1)S(1)}, bf16[4,128,128]{2,1,0:T(8,128)(2,1)S(1)}, u32[]{:S(2)}, u32[]{:S(2)}) collective-permute-start(bf16[4,128,128]{2,1,0:T(8,128)(2,1)S(1)} %get-tuple-element.109), channel_id=1, source_target_pairs={{0,6},{1,7},{2,4},{3,5},{4,2},{5,3},{6,0},{7,1},{8,14},{9,15},{10,... | collective-permute-start | bytes 393224 | tf_op jit(solution)/shard_map/ppermute | solution.py:29
  19.6 7.4 %collective-permute-start.7 = (bf16[4,128,128]{2,1,0:T(8,128)(2,1)S(1)}, bf16[4,128,128]{2,1,0:T(8,128)(2,1)S(1)}, u32[]{:S(2)}, u32[]{:S(2)}) collective-permute-start(bf16[4,128,128]{2,1,0:T(8,128)(2,1)S(1)} %get-tuple-element.110), channel_id=1, source_target_pairs={{0,4},{1,5},{2,6},{3,7},{4,0},{5,1},{6,2},{7,3},{8,12},{9,13},{10,... | collective-permute-start | bytes 393224 | tf_op jit(solution)/shard_map/ppermute | solution.py:29
  20.5 6.5 %collective-permute-start.6 = (bf16[4,128,128]{2,1,0:T(8,128)(2,1)S(1)}, bf16[4,128,128]{2,1,0:T(8,128)(2,1)S(1)}, u32[]{:S(2)}, u32[]{:S(2)}) collective-permute-start(bf16[4,128,128]{2,1,0:T(8,128)(2,1)S(1)} %get-tuple-element.111), channel_id=1, source_target_pairs={{0,2},{1,3},{2,0},{3,1},{4,6},{5,7},{6,4},{7,5},{8,10},{9,11},{10,... | collective-permute-start | bytes 393224 | tf_op jit(solution)/shard_map/ppermute | solution.py:29
  24.5 2.6 %collective-permute-start.5 = (bf16[8,128,128]{2,1,0:T(8,128)(2,1)S(1)}, bf16[8,128,128]{2,1,0:T(8,128)(2,1)S(1)}, u32[]{:S(2)}, u32[]{:S(2)}) collective-permute-start(bf16[8,128,128]{2,1,0:T(8,128)(2,1)S(1)} %get-tuple-element.94), channel_id=1, source_target_pairs={{0,1},{1,0},{2,3},{3,2},{4,5},{5,4},{6,7},{7,6},{8,9},{9,8},{10,11... | collective-permute-start | bytes 786440 | tf_op jit(solution)/shard_map/ppermute | solution.py:29
  27.2 10.3 %collective-permute-start.9 = (bf16[8,128,128]{2,1,0:T(8,128)(2,1)S(1)}, bf16[8,128,128]{2,1,0:T(8,128)(2,1)S(1)}, u32[]{:S(2)}, u32[]{:S(2)}) collective-permute-start(bf16[8,128,128]{2,1,0:T(8,128)(2,1)S(1)} %add_convert_fusion.1), channel_id=1, source_target_pairs={{0,6},{1,7},{2,0},{3,1},{4,2},{5,3},{6,4},{7,5},{8,14},{9,15},{10,... | collective-permute-start | bytes 786440 | tf_op jit(solution)/shard_map/ppermute | solution.py:19
  29.0 6.1 %collective-permute-start.12 = (bf16[1,128,128]{2,1,0:T(8,128)(2,1)S(1)}, bf16[1,128,128]{2,1,0:T(8,128)(2,1)S(1)}, u32[]{:S(2)}, u32[]{:S(2)}) collective-permute-start(bf16[1,128,128]{2,1,0:T(8,128)(2,1)S(1)} %get-tuple-element.112), channel_id=1, source_target_pairs={{0,24},{8,16},{16,8},{24,0},{1,25},{9,17},{17,9},{25,1},{2,26},{10... | collective-permute-start | bytes 98312 | tf_op jit(solution)/shard_map/ppermute | solution.py:29
  32.7 3.9 %collective-permute-start.11 = (bf16[1,128,128]{2,1,0:T(8,128)(2,1)S(1)}, bf16[1,128,128]{2,1,0:T(8,128)(2,1)S(1)}, u32[]{:S(2)}, u32[]{:S(2)}) collective-permute-start(bf16[1,128,128]{2,1,0:T(8,128)(2,1)S(1)} %get-tuple-element.113), channel_id=1, source_target_pairs={{0,8},{8,0},{16,24},{24,16},{1,9},{9,1},{17,25},{25,17},{2,10},{10... | collective-permute-start | bytes 98312 | tf_op jit(solution)/shard_map/ppermute | solution.py:29
  32.7 4.8 %collective-permute-start.10 = (bf16[1,128,128]{2,1,0:T(8,128)(2,1)S(1)}, bf16[1,128,128]{2,1,0:T(8,128)(2,1)S(1)}, u32[]{:S(2)}, u32[]{:S(2)}) collective-permute-start(bf16[1,128,128]{2,1,0:T(8,128)(2,1)S(1)} %get-tuple-element.114), channel_id=1, source_target_pairs={{0,16},{8,24},{16,0},{24,8},{1,17},{9,25},{17,1},{25,9},{2,18},{10... | collective-permute-start | bytes 98312 | tf_op jit(solution)/shard_map/ppermute | solution.py:29

commit v17 on v16

--- a/solution.py
+++ b/solution.py
@@ -190,8 +190,8 @@
     return key, key <= query
 
 
-def window_of(two_ref, one_ref, own_ref, head):
-    return jnp.concatenate([two_ref[head], one_ref[head], own_ref[head]], axis=0)
+def window_of(two_ref, own_ref, one_ref, head):
+    return jnp.concatenate([two_ref[head], own_ref[head], one_ref[head]], axis=0)
 
 
 def head_major(ref, wide_ref, outs):
@@ -225,13 +225,22 @@
         scores = ahead
 
 
-def middle_kernel(
-    queries_ref, one_ref, bias_ref, fold_ref, stats_ref, low_ref, one_keys_ref, wide_ref,
-    *, kv, group, scaling, first,
-):
+def near_kernel(
+    queries_ref, one_ref, bias_ref, fold_ref, stats_ref, low_ref, one_keys_ref, wide_ref, *, kv, group, scaling,
+):
+    head_major(one_ref, wide_ref, [one_keys_ref.at[m] for m in range(kv)])
+    weigh(queries_ref, one_keys_ref, bias_ref, fold_ref, stats_ref, low_ref, group, scaling, 0)
+
+
+def far_kernel(
+    queries_ref, one_keys_ref, bias_ref, fold_ref, stats_ref, low_ref, *, group, scaling, first,
+):
+    weigh(queries_ref, one_keys_ref, bias_ref, fold_ref, stats_ref, low_ref, group, scaling, first)
+
+
+def weigh(queries_ref, one_keys_ref, bias_ref, fold_ref, stats_ref, low_ref, group, scaling, first):
     tokens = one_keys_ref.shape[1]
     _, here = places(queries_ref.shape[1], tokens, group)
-    head_major(one_ref, wide_ref, [one_keys_ref.at[m] for m in range(kv)])
     count = low_ref.shape[0]
 
     def scores_of(g):
@@ -249,8 +258,8 @@
         share = 1.0 / (stats_ref[g, 1:2, :] * fade + jnp.sum(mid, axis=0, keepdims=True))
         fold = fold_ref[g] * (fade * share)
         low_ref[at, 0:tokens, :] = jnp.where(here, 0.0, fold).astype(LOW)
-        low_ref[at, tokens : 2 * tokens, :] = (mid * share).astype(LOW)
-        low_ref[at, 2 * tokens :, :] = jnp.where(here, fold, 0.0).astype(LOW)
+        low_ref[at, tokens : 2 * tokens, :] = jnp.where(here, fold, 0.0).astype(LOW)
+        low_ref[at, 2 * tokens :, :] = (mid * share).astype(LOW)
         scores = ahead
 
 
@@ -264,9 +273,8 @@
         head_major(ref, wide_ref.at[at], [values_ref.at[m] for m in range(kv)])
     for g in range(kv):
         low_ref = half_of((near_ref, far_ref), g)
-        part_ref[g * dim : (g + 1) * dim, :] = dot(two_values_ref[g], low_ref[0:tokens, :], 0, 0) + dot(
-            own_values_ref[g], low_ref[2 * tokens :, :], 0, 0
-        )
+        values = jnp.concatenate([two_values_ref[g], own_values_ref[g]], axis=0)
+        part_ref[g * dim : (g + 1) * dim, :] = dot(values, low_ref[0 : 2 * tokens, :], 0, 0)
 
 
 def sent_slots(group, owned, odd):
@@ -301,7 +309,7 @@
     hidden = []
     for g in range(kv):
         low_ref = half_of((near_ref, far_ref), g)
-        middle = dot(one_values_ref[g], low_ref[tokens : 2 * tokens, :], 0, 0)
+        middle = dot(one_values_ref[g], low_ref[2 * tokens :, :], 0, 0)
         hidden.append((part_ref[g * dim : (g + 1) * dim, :] + middle).astype(LOW))
     hidden = jnp.concatenate(hidden, axis=0)
     hidden_ref[...] = hidden
@@ -340,7 +348,7 @@
     tokens = back_own_ref.shape[1]
 
     def weight_grad_of(g):
-        return dot(window_of(two_ref, one_ref, own_ref, g), gh_ref[g], 1, 1)
+        return dot(window_of(two_ref, own_ref, one_ref, g), gh_ref[g], 1, 1)
 
     weight_grad = weight_grad_of(0)
     for g in range(kv):
@@ -354,8 +362,8 @@
         value_grad = dot(low, gh_ref[g], 1, 0)
         for place, grad in ((g, key_grad), (kv + g, value_grad)):
             back_two_ref[place] = grad[0:tokens].astype(LOW)
-            back_one_ref[place] = grad[tokens : 2 * tokens].astype(LOW)
-            back_own_ref[place] = grad[2 * tokens :]
+            back_own_ref[place] = grad[tokens : 2 * tokens]
+            back_one_ref[place] = grad[2 * tokens :].astype(LOW)
         weight_grad = ahead
 
 
@@ -365,7 +373,7 @@
     tokens, _, dim = dq_ref.shape
     copies = []
     for g in range(kv):
-        query_grad = dot(window_of(two_ref, one_ref, own_ref, g), grad_ref[g], 0, 0) * scaling
+        query_grad = dot(window_of(two_ref, own_ref, one_ref, g), grad_ref[g], 0, 0) * scaling
         query_grad = query_grad.T.reshape(tokens, group, dim)
         if g % 2 == 1:
             heads = slice((g - 1) * group, (g + 1) * group)
@@ -446,8 +454,9 @@
         place_kernel, [((8, lanes), jnp.int32), ((2, tokens, lanes), WIDE)], 8 * 2**30, 2**20,
         group=group,
     )(jnp.concatenate([doc_starts, tenant_ids], axis=0))
-    own_values, meta = lax.optimization_barrier((value_matrix[0], meta))
-    two_values = shifted(own_values, "ctx", 2)
+    own_values = value_matrix[0]
+    leaving, meta = lax.optimization_barrier((own_values, meta))
+    two_values = shifted(leaving, "ctx", 2)
     cots, queries, pulled, pull = call(
         pull_kernel,
         [((kv, lanes, dim), LOW), ((kv, lanes, dim), LOW), ((8, lanes), WIDE), ((span * group, lanes), LOW)],
@@ -466,16 +475,16 @@
     )(queries, two_keys.reshape(flat), own_keys.reshape(flat), biases)
     one_keys, fold = lax.optimization_barrier((one_keys, fold))
 
-    def weights_of(first):
-        return call(
-            middle_kernel, [((kv // 2, 3 * tokens, lanes), LOW), heads_first], 2**30, 4 * 2**20,
-            scratch=[pltpu.VMEM(flat, WIDE)], scaling=scaling, first=first, **sizes,
-        )(queries, one_keys.reshape(flat), biases, fold, stats)
-
-    near, one_heads = weights_of(0)
+    halves = ((kv // 2, 3 * tokens, lanes), LOW)
+    near, one_heads = call(
+        near_kernel, [halves, heads_first], 2**30, 4 * 2**20,
+        scratch=[pltpu.VMEM(flat, WIDE)], scaling=scaling, **sizes,
+    )(queries, one_keys.reshape(flat), biases, fold, stats)
     two_values, near = lax.optimization_barrier((two_values, near))
     one_values = exchanged(jnp.where(even, own_values, two_values), {"ctx": 1})
-    far, _ = weights_of(kv // 2)
+    far, = call(
+        far_kernel, [halves], 2**30, 4 * 2**20, group=group, scaling=scaling, first=kv // 2,
+    )(queries, one_heads, biases, fold, stats)
     part_hidden, two_sides, own_sides = call(
         hidden_kernel, [((heads // group * dim, lanes), WIDE), heads_first, heads_first], 2**30, 4 * 2**20,
         scratch=[pltpu.VMEM((2, *flat), WIDE)], kv=kv,

time: 38.5 us -> 38.4 us (level)
  transfers between devices with their start and end apart: 13 -> 13, of which waited for: 6 -> 6; matrix products, arithmetic and copies ran while one was open for 2% -> 2% of each run, Pallas kernels for 31% -> 30%
where the time goes in v17:
time: 38.4 us; the launch traced here: 38.2 us
  starting transfers between devices  15.1 us (39%)
  Pallas kernels  14.3 us (37%)
  waiting for transfers between devices  6.01 us (16%)
  other arithmetic  1.16 us (3%)
  between operations  0.88 us (2%)
  local copies, waits for them, and re-layouts  0.78 us (2%)
    pallas_call x12, Pallas kernels, run(): pl.pallas_call(lambda *refs: body(*refs, **fixed), out_shape=[jax.ShapeDt...  14.3 us
    ppermute x10, starting transfers between devices, exchanged(): lax.ppermute(value, axes, [(int(source), int(target)) for source, target...  8.8 us
    ppermute x3, starting transfers between devices, shifted(): lax.ppermute(value, axis, [(source, (source + steps) % count) for source...  6.28 us
    ppermute x10, waiting for transfers between devices, exchanged(): lax.ppermute(value, axes, [(int(source), int(target)) for source, target...  6 us
  transfers between devices with their start and end apart: 13, of which 6 were waited for; matrix products, arithmetic and copies ran while one was open for 2% of the time, Pallas kernels for 30%

profile of v17, /device:TPU:0, one launch (start us, length us, event | category | flops | bytes accessed | tf_op | source)
XLA Modules:
  0.0 38.2 jit_solution(16240064390924926803)
XLA Ops:
  0.6 3.0 %collective-permute-start = (bf16[128,4,128]{2,1,0:T(4,128)(2,1)}, bf16[128,4,128]{2,1,0:T(4,128)(2,1)S(1)}, u32[]{:S(2)}, u32[]{:S(2)}) collective-permute-start(bf16[128,4,128]{2,1,0:T(4,128)(2,1)} %bitcast.23), channel_id=1, source_target_pairs={{0,2},{1,3},{2,4},{3,5},{4,6},{5,7},{6,0},{7,1},{8,10},{9,11},{10,... | collective-permute-start | bytes 393224 | tf_op jit(solution)/shard_map/ppermute | solution.py:19
  3.6 0.7 %pad_add_fusion.refs_0_ = s32[2,1024]{1,0:T(2,128)S(1)} fusion(s32[1,1024]{1,0:T(1,128)} %param.17, s32[1,1024]{1,0:T(1,128)} %param.16), kind=kLoop, calls=%fused_computation.5 | loop fusion | flops 2048 | bytes 16384 | tf_op jit(solution)/shard_map/concatenate | solution.py:456
  4.4 0.0 copy-start.1
  4.4 0.0 copy-start.2
  4.4 0.0 copy-start.3
  4.4 0.0 copy-start.4
  4.4 0.3 place_kernel.1
  4.8 0.0 copy-start.5
  4.8 0.5 %copy-done.1 = bf16[1,128,4,128]{3,2,1,0:T(4,128)(2,1)S(1)} copy-done((bf16[1,128,4,128]{3,2,1,0:T(4,128)(2,1)S(1)}, bf16[1,128,4,128]{3,2,1,0:T(4,128)(2,1)}, u32[]{:S(2)}) %copy-start.1) | copy-done | bytes 131096
  5.3 1.5 %collective-permute-start.1 = (bf16[128,4,128]{2,1,0:T(4,128)(2,1)S(1)}, bf16[128,4,128]{2,1,0:T(4,128)(2,1)S(1)}, u32[]{:S(2)}, u32[]{:S(2)}) collective-permute-start(bf16[128,4,128]{2,1,0:T(4,128)(2,1)S(1)} %bitcast.25), channel_id=1, source_target_pairs={{0,2},{1,3},{2,4},{3,5},{4,6},{5,7},{6,0},{7,1},{8,10},{9,11},{10,... | collective-permute-start | bytes 393224 | tf_op jit(solution)/shard_map/ppermute | solution.py:19
  6.8 0.0 copy-done.2
  6.8 0.0 copy-done.3
  6.8 0.0 copy-done.4
  6.8 1.4 %pull_kernel.1 = (bf16[4,1024,128]{2,1,0:T(8,128)(2,1)S(1)}, bf16[4,1024,128]{2,1,0:T(8,128)(2,1)S(1)}, f32[8,1024]{1,0:T(8,128)S(1)}, bf16[512,1024]{1,0:T(8,128)(2,1)S(1)}) custom-call(s32[8,1024]{1,0:T(8,128)S(1)} %get-tuple-element.57.refs_0_.refs_7_, bf16[128,32,128]{2,1,0:T(8,128)(2,1)S(1)} %bitcast.29, bf16[64,32,128]{2,1,0:T(8,128)(2,1)S(1)} %bitcast.31, ...), custom_call_target="tpu_custom_call" | custom-call | flops 1073741824 | bytes 4194304 | tf_op jit(solution)/shard_map/pull_kernel/pallas_call | solution.py:433
  8.2 0.0 copy-done.5
  8.2 0.0 copy-start
  8.2 0.8 %hidden_grad_kernel.1 = (bf16[4,1024,128]{2,1,0:T(8,128)(2,1)S(1)}, bf16[4,512,128]{2,1,0:T(8,128)(2,1)S(1)}) custom-call(s32[8,1024]{1,0:T(8,128)S(1)} %get-tuple-element.57.refs_0_.refs_7_, f32[8,1024]{1,0:T(8,128)S(1)} %get-tuple-element.60.refs_1_, bf16[4,1024,128]{2,1,0:T(8,128)(2,1)S(1)} %get-tuple-element.61.refs_2_.refs_5_, ...), custom_call_target="tpu_custom_call" | custom-call | flops 2147483648 | bytes 4194304 | tf_op jit(solution)/shard_map/hidden_grad_kernel/pallas_call | solution.py:433
  9.0 0.0 collective-permute-done
  9.0 0.1 copy-done
  9.1 0.1 broadcast_select_fusion.1
  9.2 0.1 collective-permute-start.2
  9.2 0.9 %fold_kernel.1 = (f32[4,128,1024]{2,1,0:T(8,128)S(1)}, f32[4,2,1024]{2,1,0:T(2,128)S(1)}, bf16[4,128,128]{2,1,0:T(8,128)(2,1)S(1)}, bf16[4,128,128]{2,1,0:T(8,128)(2,1)S(1)}) custom-call(bf16[4,1024,128]{2,1,0:T(8,128)(2,1)S(1)} %get-tuple-element.58.refs_0_, bf16[512,128]{1,0:T(8,128)(2,1)S(1)} %bitcast.28, bf16[512,128]{1,0:T(8,128)(2,1)S(1)} %bitcast.24, ...), custom_call_target="tpu_custom_call" | custom-call | flops 2147483648 | bytes 4194304 | tf_op jit(solution)/shard_map/fold_kernel/pallas_call | solution.py:433
  10.2 0.4 %collective-permute-done.2 = bf16[128,4,128]{2,1,0:T(4,128)(2,1)S(1)} collective-permute-done((bf16[128,4,128]{2,1,0:T(4,128)(2,1)S(1)}, bf16[128,4,128]{2,1,0:T(4,128)(2,1)S(1)}, u32[]{:S(2)}, u32[]{:S(2)}) %collective-permute-start.2) | collective-permute-done | bytes 131104 | tf_op jit(solution)/shard_map/ppermute | solution.py:29
  10.6 0.8 %near_kernel.1 = (bf16[2,384,1024]{2,1,0:T(8,128)(2,1)S(1)}, bf16[4,128,128]{2,1,0:T(8,128)(2,1)S(1)}) custom-call(bf16[4,1024,128]{2,1,0:T(8,128)(2,1)S(1)} %get-tuple-element.58.refs_0_, bf16[512,128]{1,0:T(8,128)(2,1)S(1)} %bitcast.22, f32[2,128,1024]{2,1,0:T(8,128)S(1)} %get-tuple-element.67.refs_3_.refs_2_, ...), custom_call_target="tpu_custom_call" | custom-call | flops 1073741824 | bytes 4194304 | tf_op jit(solution)/shard_map/near_kernel/pallas_call | solution.py:433
  11.4 0.0 collective-permute-done.1
  11.4 0.1 broadcast_select_fusion
  11.5 0.2 collective-permute-start.3
  11.7 0.8 %far_kernel.1.refs_1_.refs_2_.refs_3_ = bf16[2,384,1024]{2,1,0:T(8,128)(2,1)S(1)} custom-call(bf16[4,1024,128]{2,1,0:T(8,128)(2,1)S(1)} %get-tuple-element.58.refs_0_, bf16[4,128,128]{2,1,0:T(8,128)(2,1)S(1)} %get-tuple-element.74.refs_1_.refs_2_, f32[2,128,1024]{2,1,0:T(8,128)S(1)} %get-tuple-element.67.refs_3_.refs_2_, ...), custom_call_target="tpu_custom_call" | custom-call | flops 1073741824 | bytes 4194304 | tf_op jit(solution)/shard_map/far_kernel/pallas_call | solution.py:433
  12.5 0.0 copy-start.6
  12.5 0.6 %hidden_kernel.1 = (f32[512,1024]{1,0:T(8,128)S(1)}, bf16[4,128,128]{2,1,0:T(8,128)(2,1)S(1)}, bf16[4,128,128]{2,1,0:T(8,128)(2,1)S(1)}) custom-call(bf16[2,384,1024]{2,1,0:T(8,128)(2,1)S(1)} %get-tuple-element.84.refs_0_.refs_1_.refs_2_, bf16[2,384,1024]{2,1,0:T(8,128)(2,1)S(1)} %far_kernel.1.refs_1_.refs_2_.refs_3_, bf16[512,128]{1,0:T(8,128)(2,1)S(1)} %bitcast.27, ...), custom_call_target="tpu_custom_call" | custom-call | flops 1073741824 | bytes 4194304 | tf_op jit(solution)/shard_map/hidden_kernel/pallas_call | solution.py:433
  13.0 0.0 collective-permute-done.3
  13.0 0.1 copy-done.6
  13.1 2.0 %forward_kernel.1 = (bf16[16,128,128]{2,1,0:T(8,128)(2,1)S(1)}, bf16[512,1024]{1,0:T(8,128)(2,1)S(1)}, bf16[256,1024]{1,0:T(8,128)(2,1)S(1)}, bf16[4,128,128]{2,1,0:T(8,128)(2,1)S(1)}) custom-call(f32[4,16]{1,0:T(4,128)S(1)} %bitcast.35, bf16[2,384,1024]{2,1,0:T(8,128)(2,1)S(1)} %get-tuple-element.84.refs_0_.refs_1_.refs_2_, ...), custom_call_target="tpu_custom_call" | custom-call | flops 3221225472 | bytes 10485760 | tf_op jit(solution)/shard_map/forward_kernel/pallas_call | solution.py:433
  15.2 0.4 %collective-permute-start.4 = (bf16[16,128,128]{2,1,0:T(8,128)(2,1)S(1)}, bf16[16,128,128]{2,1,0:T(8,128)(2,1)S(1)}, u32[]{:S(2)}, u32[]{:S(2)}) collective-permute-start(bf16[16,128,128]{2,1,0:T(8,128)(2,1)S(1)} %get-tuple-element.83), channel_id=1, source_target_pairs={{0,1},{1,0},{2,3},{3,2},{4,5},{5,4},{6,7},{7,6},{8,9},{9,8},{10,11... | collective-permute-start | bytes 1572872 | tf_op jit(solution)/shard_map/ppermute | solution.py:29
  15.6 0.8 %keep_kernel.1 = bf16[16,128,128]{2,1,0:T(8,128)(2,1)S(1)} custom-call(bf16[512,1024]{1,0:T(8,128)(2,1)S(1)} %get-tuple-element.81.refs_0_, bf16[256,1024]{1,0:T(8,128)(2,1)S(1)} %get-tuple-element.82.refs_1_, bf16[4,1024,128]{2,1,0:T(8,128)(2,1)S(1)} %get-tuple-element.61.refs_2_.refs_5_, bf16[512,1024]{1,0:T(8,128)(2,1)S(1)} %get-tuple-element.80.refs_8_.refs_3_), custom_call_target="tpu_custom_call" | custom-call | flops 1073741824 | bytes 5242880 | tf_op jit(solution)/shard_map/keep_kernel/pallas_call | solution.py:433
  16.4 0.8 %collective-permute-done.4 = bf16[16,128,128]{2,1,0:T(8,128)(2,1)S(1)} collective-permute-done((bf16[16,128,128]{2,1,0:T(8,128)(2,1)S(1)}, bf16[16,128,128]{2,1,0:T(8,128)(2,1)S(1)}, u32[]{:S(2)}, u32[]{:S(2)}) %collective-permute-start.4) | collective-permute-done | bytes 524320 | tf_op jit(solution)/shard_map/ppermute | solution.py:29
  17.1 0.1 add_convert_fusion
  17.3 2.2 %collective-permute-start.8 = (bf16[4,128,128]{2,1,0:T(8,128)(2,1)S(1)}, bf16[4,128,128]{2,1,0:T(8,128)(2,1)S(1)}, u32[]{:S(2)}, u32[]{:S(2)}) collective-permute-start(bf16[4,128,128]{2,1,0:T(8,128)(2,1)S(1)} %get-tuple-element.107), channel_id=1, source_target_pairs={{0,6},{1,7},{2,4},{3,5},{4,2},{5,3},{6,0},{7,1},{8,14},{9,15},{10,... | collective-permute-start | bytes 393224 | tf_op jit(solution)/shard_map/ppermute | solution.py:29
  19.5 0.9 %collective-permute-start.7 = (bf16[4,128,128]{2,1,0:T(8,128)(2,1)S(1)}, bf16[4,128,128]{2,1,0:T(8,128)(2,1)S(1)}, u32[]{:S(2)}, u32[]{:S(2)}) collective-permute-start(bf16[4,128,128]{2,1,0:T(8,128)(2,1)S(1)} %get-tuple-element.108), channel_id=1, source_target_pairs={{0,4},{1,5},{2,6},{3,7},{4,0},{5,1},{6,2},{7,3},{8,12},{9,13},{10,... | collective-permute-start | bytes 393224 | tf_op jit(solution)/shard_map/ppermute | solution.py:29
  20.4 0.5 %collective-permute-start.6 = (bf16[4,128,128]{2,1,0:T(8,128)(2,1)S(1)}, bf16[4,128,128]{2,1,0:T(8,128)(2,1)S(1)}, u32[]{:S(2)}, u32[]{:S(2)}) collective-permute-start(bf16[4,128,128]{2,1,0:T(8,128)(2,1)S(1)} %get-tuple-element.109), channel_id=1, source_target_pairs={{0,2},{1,3},{2,0},{3,1},{4,6},{5,7},{6,4},{7,5},{8,10},{9,11},{10,... | collective-permute-start | bytes 393224 | tf_op jit(solution)/shard_map/ppermute | solution.py:29
  20.9 3.5 %backward_kernel.1 = (bf16[8,128,128]{2,1,0:T(8,128)(2,1)S(1)}, bf16[8,128,128]{2,1,0:T(8,128)(2,1)S(1)}, f32[8,128,128]{2,1,0:T(8,128)S(1)}, bf16[4,384,1024]{2,1,0:T(8,128)(2,1)S(1)}) custom-call(bf16[4,1024,128]{2,1,0:T(8,128)(2,1)S(1)} %get-tuple-element.58.refs_0_, bf16[4,1024,128]{2,1,0:T(8,128)(2,1)S(1)} %get-tuple-element.63.refs_1_, ...), custom_call_target="tpu_custom_call" | custom-call | flops 4294967296 | bytes 10485760 | tf_op jit(solution)/shard_map/backward_kernel/pallas_call | solution.py:433
  24.4 0.1 collective-permute-start.5
  24.4 0.2 collective-permute-done.8
  24.6 2.2 %collective-permute-done.7 = bf16[4,128,128]{2,1,0:T(8,128)(2,1)S(1)} collective-permute-done((bf16[4,128,128]{2,1,0:T(8,128)(2,1)S(1)}, bf16[4,128,128]{2,1,0:T(8,128)(2,1)S(1)}, u32[]{:S(2)}, u32[]{:S(2)}) %collective-permute-start.7) | collective-permute-done | bytes 131104 | tf_op jit(solution)/shard_map/ppermute | solution.py:29
  26.9 0.0 collective-permute-done.6
  26.9 0.1 add_convert_fusion.2
  26.9 0.0 collective-permute-done.5.refs_1_
  27.0 0.1 add_convert_fusion.1
  27.1 1.8 %collective-permute-start.9 = (bf16[8,128,128]{2,1,0:T(8,128)(2,1)S(1)}, bf16[8,128,128]{2,1,0:T(8,128)(2,1)S(1)}, u32[]{:S(2)}, u32[]{:S(2)}) collective-permute-start(bf16[8,128,128]{2,1,0:T(8,128)(2,1)S(1)} %add_convert_fusion.1), channel_id=1, source_target_pairs={{0,6},{1,7},{2,0},{3,1},{4,2},{5,3},{6,4},{7,5},{8,14},{9,15},{10,... | collective-permute-start | bytes 786440 | tf_op jit(solution)/shard_map/ppermute | solution.py:19
  28.9 3.7 %collective-permute-start.12 = (bf16[1,128,128]{2,1,0:T(8,128)(2,1)S(1)}, bf16[1,128,128]{2,1,0:T(8,128)(2,1)S(1)}, u32[]{:S(2)}, u32[]{:S(2)}) collective-permute-start(bf16[1,128,128]{2,1,0:T(8,128)(2,1)S(1)} %get-tuple-element.110), channel_id=1, source_target_pairs={{0,24},{8,16},{16,8},{24,0},{1,25},{9,17},{17,9},{25,1},{2,26},{10... | collective-permute-start | bytes 98312 | tf_op jit(solution)/shard_map/ppermute | solution.py:29
  32.5 0.0 collective-permute-start.11
  32.5 0.8 %collective-permute-start.10 = (bf16[1,128,128]{2,1,0:T(8,128)(2,1)S(1)}, bf16[1,128,128]{2,1,0:T(8,128)(2,1)S(1)}, u32[]{:S(2)}, u32[]{:S(2)}) collective-permute-start(bf16[1,128,128]{2,1,0:T(8,128)(2,1)S(1)} %get-tuple-element.112), channel_id=1, source_target_pairs={{0,16},{8,24},{16,0},{24,8},{1,17},{9,25},{17,1},{25,9},{2,18},{10... | collective-permute-start | bytes 98312 | tf_op jit(solution)/shard_map/ppermute | solution.py:29
  33.3 1.6 %query_kernel.1 = bf16[128,32,128]{2,1,0:T(8,128)(2,1)} custom-call(bf16[4,384,1024]{2,1,0:T(8,128)(2,1)S(1)} %get-tuple-element.88.refs_0_, bf16[4,128,128]{2,1,0:T(8,128)(2,1)S(1)} %get-tuple-element.89.refs_1_, bf16[4,128,128]{2,1,0:T(8,128)(2,1)S(1)} %get-tuple-element.74.refs_1_.refs_2_, bf16[4,128,128]{2,1,0:T(8,128)(2,1)S(1)} %get-tuple-element.90.refs_3_), custom_call_target="tpu_custom_call" | custom-call | flops 2147483648 | bytes 5242880 | tf_op jit(solution)/shard_map/query_kernel/pallas_call | solution.py:433
  35.0 0.0 collective-permute-done.12.refs_6_
  35.0 1.5 %collective-permute-done.11.refs_5_ = bf16[1,128,128]{2,1,0:T(8,128)(2,1)S(1)} collective-permute-done((bf16[1,128,128]{2,1,0:T(8,128)(2,1)S(1)}, bf16[1,128,128]{2,1,0:T(8,128)(2,1)S(1)}, u32[]{:S(2)}, u32[]{:S(2)}) %collective-permute-start.11) | collective-permute-done | bytes 32800 | tf_op jit(solution)/shard_map/ppermute | solution.py:29
  36.4 0.9 %collective-permute-done.10.refs_4_ = bf16[1,128,128]{2,1,0:T(8,128)(2,1)S(1)} collective-permute-done((bf16[1,128,128]{2,1,0:T(8,128)(2,1)S(1)}, bf16[1,128,128]{2,1,0:T(8,128)(2,1)S(1)}, u32[]{:S(2)}, u32[]{:S(2)}) %collective-permute-start.10) | collective-permute-done | bytes 32800 | tf_op jit(solution)/shard_map/ppermute | solution.py:29
  37.4 0.0 collective-permute-done.9.refs_2_
  37.4 0.8 %finish_kernel.1 = (bf16[512,128]{1,0:T(8,128)(2,1)}, bf16[512,128]{1,0:T(8,128)(2,1)}, f32[16,4,128]{2,1,0:T(4,128)}, f32[16,4,128]{2,1,0:T(4,128)}) custom-call(f32[8,128,128]{2,1,0:T(8,128)S(1)} %get-tuple-element.91.refs_0_, bf16[8,128,128]{2,1,0:T(8,128)(2,1)S(1)} %collective-permute-done.5.refs_1_, ...), custom_call_target="tpu_custom_call" | custom-call | flops 1048576 | bytes 1048576 | tf_op jit(solution)/shard_map/finish_kernel/pallas_call | solution.py:433
  (2 shorter events, 0.0 us)
Async XLA Ops:
  0.6 8.3 %collective-permute-start = (bf16[128,4,128]{2,1,0:T(4,128)(2,1)}, bf16[128,4,128]{2,1,0:T(4,128)(2,1)S(1)}, u32[]{:S(2)}, u32[]{:S(2)}) collective-permute-start(bf16[128,4,128]{2,1,0:T(4,128)(2,1)} %bitcast.23), channel_id=1, source_target_pairs={{0,2},{1,3},{2,4},{3,5},{4,6},{5,7},{6,0},{7,1},{8,10},{9,11},{10,... | collective-permute-start | bytes 393224 | tf_op jit(solution)/shard_map/ppermute | solution.py:19
  4.4 0.9 %copy-start.1 = (bf16[1,128,4,128]{3,2,1,0:T(4,128)(2,1)S(1)}, bf16[1,128,4,128]{3,2,1,0:T(4,128)(2,1)}, u32[]{:S(2)}) copy-start(bf16[1,128,4,128]{3,2,1,0:T(4,128)(2,1)} %param.11) | copy-start | bytes 393220
  4.4 2.4 %copy-start.2 = (bf16[1,128,32,128]{3,2,1,0:T(8,128)(2,1)S(1)}, bf16[1,128,32,128]{3,2,1,0:T(8,128)(2,1)}, u32[]{:S(2)}) copy-start(bf16[1,128,32,128]{3,2,1,0:T(8,128)(2,1)} %param.12) | copy-start | bytes 3145732
  4.4 2.4 %copy-start.3 = (bf16[1,128,32,128]{3,2,1,0:T(8,128)(2,1)S(1)}, bf16[1,128,32,128]{3,2,1,0:T(8,128)(2,1)}, u32[]{:S(2)}) copy-start(bf16[1,128,32,128]{3,2,1,0:T(8,128)(2,1)} %param.9) | copy-start | bytes 3145732
  4.4 2.4 %copy-start.4 = (bf16[16,4,32,128]{3,2,1,0:T(8,128)(2,1)S(1)}, bf16[16,4,32,128]{3,2,1,0:T(8,128)(2,1)}, u32[]{:S(2)}) copy-start(bf16[16,4,32,128]{3,2,1,0:T(8,128)(2,1)} %param.13) | copy-start | bytes 1572868
  4.8 3.4 %copy-start.5 = (bf16[16,4,32,128]{3,2,1,0:T(8,128)(2,1)S(1)}, bf16[16,4,32,128]{3,2,1,0:T(8,128)(2,1)}, u32[]{:S(2)}) copy-start(bf16[16,4,32,128]{3,2,1,0:T(8,128)(2,1)} %param.14) | copy-start | bytes 1572868
  5.3 6.1 %collective-permute-start.1 = (bf16[128,4,128]{2,1,0:T(4,128)(2,1)S(1)}, bf16[128,4,128]{2,1,0:T(4,128)(2,1)S(1)}, u32[]{:S(2)}, u32[]{:S(2)}) collective-permute-start(bf16[128,4,128]{2,1,0:T(4,128)(2,1)S(1)} %bitcast.25), channel_id=1, source_target_pairs={{0,2},{1,3},{2,4},{3,5},{4,6},{5,7},{6,0},{7,1},{8,10},{9,11},{10,... | collective-permute-start | bytes 393224 | tf_op jit(solution)/shard_map/ppermute | solution.py:19
  8.2 0.9 %copy-start = (bf16[1,128,4,128]{3,2,1,0:T(4,128)(2,1)S(1)}, bf16[1,128,4,128]{3,2,1,0:T(4,128)(2,1)}, u32[]{:S(2)}) copy-start(bf16[1,128,4,128]{3,2,1,0:T(4,128)(2,1)} %param.10) | copy-start | bytes 393220
  9.2 1.4 %collective-permute-start.2 = (bf16[128,4,128]{2,1,0:T(4,128)(2,1)S(1)}, bf16[128,4,128]{2,1,0:T(4,128)(2,1)S(1)}, u32[]{:S(2)}, u32[]{:S(2)}) collective-permute-start(bf16[128,4,128]{2,1,0:T(4,128)(2,1)S(1)} %broadcast_select_fusion.1), channel_id=1, source_target_pairs={{0,1},{1,0},{2,3},{3,2},{4,5},{5,4},{6,7},{7,6},{8,9},{9,8},{10,11... | collective-permute-start | bytes 393224 | tf_op jit(solution)/shard_map/ppermute | solution.py:29
  11.5 1.6 %collective-permute-start.3 = (bf16[128,4,128]{2,1,0:T(4,128)(2,1)S(1)}, bf16[128,4,128]{2,1,0:T(4,128)(2,1)S(1)}, u32[]{:S(2)}, u32[]{:S(2)}) collective-permute-start(bf16[128,4,128]{2,1,0:T(4,128)(2,1)S(1)} %broadcast_select_fusion), channel_id=1, source_target_pairs={{0,1},{1,0},{2,3},{3,2},{4,5},{5,4},{6,7},{7,6},{8,9},{9,8},{10,11... | collective-permute-start | bytes 393224 | tf_op jit(solution)/shard_map/ppermute | solution.py:29
  12.5 0.7 %copy-start.6 = (f32[16,4]{0,1:T(4,128)S(1)}, f32[16,4]{0,1:T(4,128)}, u32[]{:S(2)}) copy-start(f32[16,4]{0,1:T(4,128)} %param.15) | copy-start | bytes 772
  15.2 2.0 %collective-permute-start.4 = (bf16[16,128,128]{2,1,0:T(8,128)(2,1)S(1)}, bf16[16,128,128]{2,1,0:T(8,128)(2,1)S(1)}, u32[]{:S(2)}, u32[]{:S(2)}) collective-permute-start(bf16[16,128,128]{2,1,0:T(8,128)(2,1)S(1)} %get-tuple-element.83), channel_id=1, source_target_pairs={{0,1},{1,0},{2,3},{3,2},{4,5},{5,4},{6,7},{7,6},{8,9},{9,8},{10,11... | collective-permute-start | bytes 1572872 | tf_op jit(solution)/shard_map/ppermute | solution.py:29
  17.3 7.3 %collective-permute-start.8 = (bf16[4,128,128]{2,1,0:T(8,128)(2,1)S(1)}, bf16[4,128,128]{2,1,0:T(8,128)(2,1)S(1)}, u32[]{:S(2)}, u32[]{:S(2)}) collective-permute-start(bf16[4,128,128]{2,1,0:T(8,128)(2,1)S(1)} %get-tuple-element.107), channel_id=1, source_target_pairs={{0,6},{1,7},{2,4},{3,5},{4,2},{5,3},{6,0},{7,1},{8,14},{9,15},{10,... | collective-permute-start | bytes 393224 | tf_op jit(solution)/shard_map/ppermute | solution.py:29
  19.5 7.4 %collective-permute-start.7 = (bf16[4,128,128]{2,1,0:T(8,128)(2,1)S(1)}, bf16[4,128,128]{2,1,0:T(8,128)(2,1)S(1)}, u32[]{:S(2)}, u32[]{:S(2)}) collective-permute-start(bf16[4,128,128]{2,1,0:T(8,128)(2,1)S(1)} %get-tuple-element.108), channel_id=1, source_target_pairs={{0,4},{1,5},{2,6},{3,7},{4,0},{5,1},{6,2},{7,3},{8,12},{9,13},{10,... | collective-permute-start | bytes 393224 | tf_op jit(solution)/shard_map/ppermute | solution.py:29
  20.4 6.5 %collective-permute-start.6 = (bf16[4,128,128]{2,1,0:T(8,128)(2,1)S(1)}, bf16[4,128,128]{2,1,0:T(8,128)(2,1)S(1)}, u32[]{:S(2)}, u32[]{:S(2)}) collective-permute-start(bf16[4,128,128]{2,1,0:T(8,128)(2,1)S(1)} %get-tuple-element.109), channel_id=1, source_target_pairs={{0,2},{1,3},{2,0},{3,1},{4,6},{5,7},{6,4},{7,5},{8,10},{9,11},{10,... | collective-permute-start | bytes 393224 | tf_op jit(solution)/shard_map/ppermute | solution.py:29
  24.4 2.6 %collective-permute-start.5 = (bf16[8,128,128]{2,1,0:T(8,128)(2,1)S(1)}, bf16[8,128,128]{2,1,0:T(8,128)(2,1)S(1)}, u32[]{:S(2)}, u32[]{:S(2)}) collective-permute-start(bf16[8,128,128]{2,1,0:T(8,128)(2,1)S(1)} %get-tuple-element.92), channel_id=1, source_target_pairs={{0,1},{1,0},{2,3},{3,2},{4,5},{5,4},{6,7},{7,6},{8,9},{9,8},{10,11... | collective-permute-start | bytes 786440 | tf_op jit(solution)/shard_map/ppermute | solution.py:29
  27.1 10.3 %collective-permute-start.9 = (bf16[8,128,128]{2,1,0:T(8,128)(2,1)S(1)}, bf16[8,128,128]{2,1,0:T(8,128)(2,1)S(1)}, u32[]{:S(2)}, u32[]{:S(2)}) collective-permute-start(bf16[8,128,128]{2,1,0:T(8,128)(2,1)S(1)} %add_convert_fusion.1), channel_id=1, source_target_pairs={{0,6},{1,7},{2,0},{3,1},{4,2},{5,3},{6,4},{7,5},{8,14},{9,15},{10,... | collective-permute-start | bytes 786440 | tf_op jit(solution)/shard_map/ppermute | solution.py:19
  28.9 6.1 %collective-permute-start.12 = (bf16[1,128,128]{2,1,0:T(8,128)(2,1)S(1)}, bf16[1,128,128]{2,1,0:T(8,128)(2,1)S(1)}, u32[]{:S(2)}, u32[]{:S(2)}) collective-permute-start(bf16[1,128,128]{2,1,0:T(8,128)(2,1)S(1)} %get-tuple-element.110), channel_id=1, source_target_pairs={{0,24},{8,16},{16,8},{24,0},{1,25},{9,17},{17,9},{25,1},{2,26},{10... | collective-permute-start | bytes 98312 | tf_op jit(solution)/shard_map/ppermute | solution.py:29
  32.5 3.9 %collective-permute-start.11 = (bf16[1,128,128]{2,1,0:T(8,128)(2,1)S(1)}, bf16[1,128,128]{2,1,0:T(8,128)(2,1)S(1)}, u32[]{:S(2)}, u32[]{:S(2)}) collective-permute-start(bf16[1,128,128]{2,1,0:T(8,128)(2,1)S(1)} %get-tuple-element.111), channel_id=1, source_target_pairs={{0,8},{8,0},{16,24},{24,16},{1,9},{9,1},{17,25},{25,17},{2,10},{10... | collective-permute-start | bytes 98312 | tf_op jit(solution)/shard_map/ppermute | solution.py:29
  32.5 4.8 %collective-permute-start.10 = (bf16[1,128,128]{2,1,0:T(8,128)(2,1)S(1)}, bf16[1,128,128]{2,1,0:T(8,128)(2,1)S(1)}, u32[]{:S(2)}, u32[]{:S(2)}) collective-permute-start(bf16[1,128,128]{2,1,0:T(8,128)(2,1)S(1)} %get-tuple-element.112), channel_id=1, source_target_pairs={{0,16},{8,24},{16,0},{24,8},{1,17},{9,25},{17,1},{25,9},{2,18},{10... | collective-permute-start | bytes 98312 | tf_op jit(solution)/shard_map/ppermute | solution.py:29

commit v18 on v17

--- a/solution.py
+++ b/solution.py
@@ -385,26 +385,37 @@
         copy.wait()
 
 
-def finish_kernel(
-    own_ref, mate_ref, two_ref, part_ref, *refs, kv, owned,
-):
-    *other_refs, keys_ref, values_ref, rot_ref, proj_ref, wide_ref = refs
+def finish_kernel(own_ref, mate_ref, two_ref, part_ref, *refs, kv, owned):
+    *other_refs, keys_hbm, values_hbm, rot_hbm, proj_hbm, wide_ref, low_ref, grads_ref, sems = refs
+    copies = [
+        pltpu.make_async_copy(source, target, sems.at[at])
+        for at, (source, target) in enumerate(
+            (
+                (grads_ref.at[0], rot_hbm), (grads_ref.at[1], proj_hbm),
+                (low_ref.at[0], keys_hbm), (low_ref.at[1], values_hbm),
+            )
+        )
+    ]
     total = part_ref[0].astype(WIDE)
     for other_ref in other_refs:
         total = total + other_ref[0].astype(WIDE)
-    size = rot_ref.shape[0]
-    for place in range(owned):
-        for at, out in enumerate((rot_ref, proj_ref)):
+    size = grads_ref.shape[1]
+    for at in range(2):
+        for place in range(owned):
             row = (2 * place + at) * size
-            out[:, place, :] = total[row : row + size]
+            grads_ref[at, :, place, :] = total[row : row + size]
+        copies[at].start()
     tokens = own_ref.shape[1]
     even = (lax.axis_index("ctx") % 2 == 0).astype(WIDE)
-    for at, out in enumerate((keys_ref, values_ref)):
+    for at in range(2):
         for m in range(kv):
             place = at * kv + m
             total = own_ref[place] + two_ref[place].astype(WIDE) + even * mate_ref[place].astype(WIDE)
             wide_ref[at, pl.ds(m, tokens, stride=kv), :] = total
-        out[...] = wide_ref[at].astype(LOW)
+        low_ref[at] = wide_ref[at].astype(LOW)
+        copies[2 + at].start()
+    for copy in copies:
+        copy.wait()
 
 
 def on_device(
@@ -529,7 +540,11 @@
             part = part.astype(LOW)
     d_keys, d_values, *grads = call(
         finish_kernel, [((tokens * kv, dim), LOW)] * 2 + [((span // rep, here, dim), WIDE)] * 2, 2**20, 2**20,
-        scratch=[pltpu.VMEM((2, tokens * kv, dim), WIDE)], kv=kv, owned=here,
+        scratch=[
+            pltpu.VMEM((2, tokens * kv, dim), WIDE), pltpu.VMEM((2, tokens * kv, dim), LOW),
+            pltpu.VMEM((2, span // rep, here, dim), WIDE), pltpu.SemaphoreType.DMA((4,)),
+        ],
+        out_specs=[pl.BlockSpec(memory_space=pltpu.HBM)] * 4, kv=kv, owned=here,
     )(back_own, from_mate, from_two, part, *others)
     grads = [grad.reshape(tenants // rep, rank, here, dim) for grad in grads]
     d_keys, d_values = (grad.reshape(key_rows.shape) for grad in (d_keys, d_values))

time: 38.4 us -> 38.5 us (level)
  no operation moved by 1% of the time
where the time goes in v18:
time: 38.5 us; the launch traced here: 38.2 us
  starting transfers between devices  15.1 us (39%)
  Pallas kernels  14.3 us (37%)
  waiting for transfers between devices  6.01 us (16%)
  other arithmetic  1.16 us (3%)
  between operations  0.88 us (2%)
  local copies, waits for them, and re-layouts  0.78 us (2%)
    pallas_call x12, Pallas kernels, run(): pl.pallas_call(lambda *refs: body(*refs, **fixed), out_shape=[jax.ShapeDt...  14.3 us
    ppermute x10, starting transfers between devices, exchanged(): lax.ppermute(value, axes, [(int(source), int(target)) for source, target...  8.8 us
    ppermute x3, starting transfers between devices, shifted(): lax.ppermute(value, axis, [(source, (source + steps) % count) for source...  6.28 us
    ppermute x10, waiting for transfers between devices, exchanged(): lax.ppermute(value, axes, [(int(source), int(target)) for source, target...  6 us
  transfers between devices with their start and end apart: 13, of which 6 were waited for; matrix products, arithmetic and copies ran while one was open for 2% of the time, Pallas kernels for 30%

profile of v18, /device:TPU:0, one launch (start us, length us, event | category | flops | bytes accessed | tf_op | source)
XLA Modules:
  0.0 38.2 jit_solution(1447084441913465416)
XLA Ops:
  0.6 3.0 %collective-permute-start = (bf16[128,4,128]{2,1,0:T(4,128)(2,1)}, bf16[128,4,128]{2,1,0:T(4,128)(2,1)S(1)}, u32[]{:S(2)}, u32[]{:S(2)}) collective-permute-start(bf16[128,4,128]{2,1,0:T(4,128)(2,1)} %bitcast.23), channel_id=1, source_target_pairs={{0,2},{1,3},{2,4},{3,5},{4,6},{5,7},{6,0},{7,1},{8,10},{9,11},{10,... | collective-permute-start | bytes 393224 | tf_op jit(solution)/shard_map/ppermute | solution.py:19
  3.6 0.7 %pad_add_fusion.refs_0_ = s32[2,1024]{1,0:T(2,128)S(1)} fusion(s32[1,1024]{1,0:T(1,128)} %param.17, s32[1,1024]{1,0:T(1,128)} %param.16), kind=kLoop, calls=%fused_computation.5 | loop fusion | flops 2048 | bytes 16384 | tf_op jit(solution)/shard_map/concatenate | solution.py:467
  4.4 0.0 copy-start.1
  4.4 0.0 copy-start.2
  4.4 0.0 copy-start.3
  4.4 0.0 copy-start.4
  4.4 0.3 place_kernel.1
  4.8 0.0 copy-start.5
  4.8 0.5 %copy-done.1 = bf16[1,128,4,128]{3,2,1,0:T(4,128)(2,1)S(1)} copy-done((bf16[1,128,4,128]{3,2,1,0:T(4,128)(2,1)S(1)}, bf16[1,128,4,128]{3,2,1,0:T(4,128)(2,1)}, u32[]{:S(2)}) %copy-start.1) | copy-done | bytes 131096
  5.3 1.5 %collective-permute-start.1 = (bf16[128,4,128]{2,1,0:T(4,128)(2,1)S(1)}, bf16[128,4,128]{2,1,0:T(4,128)(2,1)S(1)}, u32[]{:S(2)}, u32[]{:S(2)}) collective-permute-start(bf16[128,4,128]{2,1,0:T(4,128)(2,1)S(1)} %bitcast.25), channel_id=1, source_target_pairs={{0,2},{1,3},{2,4},{3,5},{4,6},{5,7},{6,0},{7,1},{8,10},{9,11},{10,... | collective-permute-start | bytes 393224 | tf_op jit(solution)/shard_map/ppermute | solution.py:19
  6.8 0.0 copy-done.2
  6.8 0.0 copy-done.3
  6.8 0.0 copy-done.4
  6.8 1.4 %pull_kernel.1 = (bf16[4,1024,128]{2,1,0:T(8,128)(2,1)S(1)}, bf16[4,1024,128]{2,1,0:T(8,128)(2,1)S(1)}, f32[8,1024]{1,0:T(8,128)S(1)}, bf16[512,1024]{1,0:T(8,128)(2,1)S(1)}) custom-call(s32[8,1024]{1,0:T(8,128)S(1)} %get-tuple-element.57.refs_0_.refs_7_, bf16[128,32,128]{2,1,0:T(8,128)(2,1)S(1)} %bitcast.29, bf16[64,32,128]{2,1,0:T(8,128)(2,1)S(1)} %bitcast.31, ...), custom_call_target="tpu_custom_call" | custom-call | flops 1073741824 | bytes 4194304 | tf_op jit(solution)/shard_map/pull_kernel/pallas_call | solution.py:444
  8.2 0.0 copy-done.5
  8.2 0.0 copy-start
  8.2 0.8 %hidden_grad_kernel.1 = (bf16[4,1024,128]{2,1,0:T(8,128)(2,1)S(1)}, bf16[4,512,128]{2,1,0:T(8,128)(2,1)S(1)}) custom-call(s32[8,1024]{1,0:T(8,128)S(1)} %get-tuple-element.57.refs_0_.refs_7_, f32[8,1024]{1,0:T(8,128)S(1)} %get-tuple-element.60.refs_1_, bf16[4,1024,128]{2,1,0:T(8,128)(2,1)S(1)} %get-tuple-element.61.refs_2_.refs_5_, ...), custom_call_target="tpu_custom_call" | custom-call | flops 2147483648 | bytes 4194304 | tf_op jit(solution)/shard_map/hidden_grad_kernel/pallas_call | solution.py:444
  9.0 0.0 collective-permute-done
  9.0 0.1 copy-done
  9.1 0.1 broadcast_select_fusion.1
  9.2 0.1 collective-permute-start.2
  9.2 0.9 %fold_kernel.1 = (f32[4,128,1024]{2,1,0:T(8,128)S(1)}, f32[4,2,1024]{2,1,0:T(2,128)S(1)}, bf16[4,128,128]{2,1,0:T(8,128)(2,1)S(1)}, bf16[4,128,128]{2,1,0:T(8,128)(2,1)S(1)}) custom-call(bf16[4,1024,128]{2,1,0:T(8,128)(2,1)S(1)} %get-tuple-element.58.refs_0_, bf16[512,128]{1,0:T(8,128)(2,1)S(1)} %bitcast.28, bf16[512,128]{1,0:T(8,128)(2,1)S(1)} %bitcast.24, ...), custom_call_target="tpu_custom_call" | custom-call | flops 2147483648 | bytes 4194304 | tf_op jit(solution)/shard_map/fold_kernel/pallas_call | solution.py:444
  10.2 0.4 %collective-permute-done.2 = bf16[128,4,128]{2,1,0:T(4,128)(2,1)S(1)} collective-permute-done((bf16[128,4,128]{2,1,0:T(4,128)(2,1)S(1)}, bf16[128,4,128]{2,1,0:T(4,128)(2,1)S(1)}, u32[]{:S(2)}, u32[]{:S(2)}) %collective-permute-start.2) | collective-permute-done | bytes 131104 | tf_op jit(solution)/shard_map/ppermute | solution.py:29
  10.6 0.8 %near_kernel.1 = (bf16[2,384,1024]{2,1,0:T(8,128)(2,1)S(1)}, bf16[4,128,128]{2,1,0:T(8,128)(2,1)S(1)}) custom-call(bf16[4,1024,128]{2,1,0:T(8,128)(2,1)S(1)} %get-tuple-element.58.refs_0_, bf16[512,128]{1,0:T(8,128)(2,1)S(1)} %bitcast.22, f32[2,128,1024]{2,1,0:T(8,128)S(1)} %get-tuple-element.67.refs_3_.refs_2_, ...), custom_call_target="tpu_custom_call" | custom-call | flops 1073741824 | bytes 4194304 | tf_op jit(solution)/shard_map/near_kernel/pallas_call | solution.py:444
  11.4 0.0 collective-permute-done.1
  11.4 0.1 broadcast_select_fusion
  11.5 0.2 collective-permute-start.3
  11.7 0.8 %far_kernel.1.refs_1_.refs_2_.refs_3_ = bf16[2,384,1024]{2,1,0:T(8,128)(2,1)S(1)} custom-call(bf16[4,1024,128]{2,1,0:T(8,128)(2,1)S(1)} %get-tuple-element.58.refs_0_, bf16[4,128,128]{2,1,0:T(8,128)(2,1)S(1)} %get-tuple-element.74.refs_1_.refs_2_, f32[2,128,1024]{2,1,0:T(8,128)S(1)} %get-tuple-element.67.refs_3_.refs_2_, ...), custom_call_target="tpu_custom_call" | custom-call | flops 1073741824 | bytes 4194304 | tf_op jit(solution)/shard_map/far_kernel/pallas_call | solution.py:444
  12.5 0.0 copy-start.6
  12.5 0.6 %hidden_kernel.1 = (f32[512,1024]{1,0:T(8,128)S(1)}, bf16[4,128,128]{2,1,0:T(8,128)(2,1)S(1)}, bf16[4,128,128]{2,1,0:T(8,128)(2,1)S(1)}) custom-call(bf16[2,384,1024]{2,1,0:T(8,128)(2,1)S(1)} %get-tuple-element.84.refs_0_.refs_1_.refs_2_, bf16[2,384,1024]{2,1,0:T(8,128)(2,1)S(1)} %far_kernel.1.refs_1_.refs_2_.refs_3_, bf16[512,128]{1,0:T(8,128)(2,1)S(1)} %bitcast.27, ...), custom_call_target="tpu_custom_call" | custom-call | flops 1073741824 | bytes 4194304 | tf_op jit(solution)/shard_map/hidden_kernel/pallas_call | solution.py:444
  13.0 0.0 collective-permute-done.3
  13.0 0.1 copy-done.6
  13.1 2.0 %forward_kernel.1 = (bf16[16,128,128]{2,1,0:T(8,128)(2,1)S(1)}, bf16[512,1024]{1,0:T(8,128)(2,1)S(1)}, bf16[256,1024]{1,0:T(8,128)(2,1)S(1)}, bf16[4,128,128]{2,1,0:T(8,128)(2,1)S(1)}) custom-call(f32[4,16]{1,0:T(4,128)S(1)} %bitcast.35, bf16[2,384,1024]{2,1,0:T(8,128)(2,1)S(1)} %get-tuple-element.84.refs_0_.refs_1_.refs_2_, ...), custom_call_target="tpu_custom_call" | custom-call | flops 3221225472 | bytes 10485760 | tf_op jit(solution)/shard_map/forward_kernel/pallas_call | solution.py:444
  15.2 0.4 %collective-permute-start.4 = (bf16[16,128,128]{2,1,0:T(8,128)(2,1)S(1)}, bf16[16,128,128]{2,1,0:T(8,128)(2,1)S(1)}, u32[]{:S(2)}, u32[]{:S(2)}) collective-permute-start(bf16[16,128,128]{2,1,0:T(8,128)(2,1)S(1)} %get-tuple-element.83), channel_id=1, source_target_pairs={{0,1},{1,0},{2,3},{3,2},{4,5},{5,4},{6,7},{7,6},{8,9},{9,8},{10,11... | collective-permute-start | bytes 1572872 | tf_op jit(solution)/shard_map/ppermute | solution.py:29
  15.6 0.8 %keep_kernel.1 = bf16[16,128,128]{2,1,0:T(8,128)(2,1)S(1)} custom-call(bf16[512,1024]{1,0:T(8,128)(2,1)S(1)} %get-tuple-element.81.refs_0_, bf16[256,1024]{1,0:T(8,128)(2,1)S(1)} %get-tuple-element.82.refs_1_, bf16[4,1024,128]{2,1,0:T(8,128)(2,1)S(1)} %get-tuple-element.61.refs_2_.refs_5_, bf16[512,1024]{1,0:T(8,128)(2,1)S(1)} %get-tuple-element.80.refs_8_.refs_3_), custom_call_target="tpu_custom_call" | custom-call | flops 1073741824 | bytes 5242880 | tf_op jit(solution)/shard_map/keep_kernel/pallas_call | solution.py:444
  16.4 0.8 %collective-permute-done.4 = bf16[16,128,128]{2,1,0:T(8,128)(2,1)S(1)} collective-permute-done((bf16[16,128,128]{2,1,0:T(8,128)(2,1)S(1)}, bf16[16,128,128]{2,1,0:T(8,128)(2,1)S(1)}, u32[]{:S(2)}, u32[]{:S(2)}) %collective-permute-start.4) | collective-permute-done | bytes 524320 | tf_op jit(solution)/shard_map/ppermute | solution.py:29
  17.1 0.1 add_convert_fusion
  17.3 2.2 %collective-permute-start.8 = (bf16[4,128,128]{2,1,0:T(8,128)(2,1)S(1)}, bf16[4,128,128]{2,1,0:T(8,128)(2,1)S(1)}, u32[]{:S(2)}, u32[]{:S(2)}) collective-permute-start(bf16[4,128,128]{2,1,0:T(8,128)(2,1)S(1)} %get-tuple-element.107), channel_id=1, source_target_pairs={{0,6},{1,7},{2,4},{3,5},{4,2},{5,3},{6,0},{7,1},{8,14},{9,15},{10,... | collective-permute-start | bytes 393224 | tf_op jit(solution)/shard_map/ppermute | solution.py:29
  19.5 0.9 %collective-permute-start.7 = (bf16[4,128,128]{2,1,0:T(8,128)(2,1)S(1)}, bf16[4,128,128]{2,1,0:T(8,128)(2,1)S(1)}, u32[]{:S(2)}, u32[]{:S(2)}) collective-permute-start(bf16[4,128,128]{2,1,0:T(8,128)(2,1)S(1)} %get-tuple-element.108), channel_id=1, source_target_pairs={{0,4},{1,5},{2,6},{3,7},{4,0},{5,1},{6,2},{7,3},{8,12},{9,13},{10,... | collective-permute-start | bytes 393224 | tf_op jit(solution)/shard_map/ppermute | solution.py:29
  20.4 0.5 %collective-permute-start.6 = (bf16[4,128,128]{2,1,0:T(8,128)(2,1)S(1)}, bf16[4,128,128]{2,1,0:T(8,128)(2,1)S(1)}, u32[]{:S(2)}, u32[]{:S(2)}) collective-permute-start(bf16[4,128,128]{2,1,0:T(8,128)(2,1)S(1)} %get-tuple-element.109), channel_id=1, source_target_pairs={{0,2},{1,3},{2,0},{3,1},{4,6},{5,7},{6,4},{7,5},{8,10},{9,11},{10,... | collective-permute-start | bytes 393224 | tf_op jit(solution)/shard_map/ppermute | solution.py:29
  20.9 3.5 %backward_kernel.1 = (bf16[8,128,128]{2,1,0:T(8,128)(2,1)S(1)}, bf16[8,128,128]{2,1,0:T(8,128)(2,1)S(1)}, f32[8,128,128]{2,1,0:T(8,128)S(1)}, bf16[4,384,1024]{2,1,0:T(8,128)(2,1)S(1)}) custom-call(bf16[4,1024,128]{2,1,0:T(8,128)(2,1)S(1)} %get-tuple-element.58.refs_0_, bf16[4,1024,128]{2,1,0:T(8,128)(2,1)S(1)} %get-tuple-element.63.refs_1_, ...), custom_call_target="tpu_custom_call" | custom-call | flops 4294967296 | bytes 10485760 | tf_op jit(solution)/shard_map/backward_kernel/pallas_call | solution.py:444
  24.4 0.1 collective-permute-start.5
  24.4 0.2 collective-permute-done.8
  24.6 2.2 %collective-permute-done.7 = bf16[4,128,128]{2,1,0:T(8,128)(2,1)S(1)} collective-permute-done((bf16[4,128,128]{2,1,0:T(8,128)(2,1)S(1)}, bf16[4,128,128]{2,1,0:T(8,128)(2,1)S(1)}, u32[]{:S(2)}, u32[]{:S(2)}) %collective-permute-start.7) | collective-permute-done | bytes 131104 | tf_op jit(solution)/shard_map/ppermute | solution.py:29
  26.9 0.0 collective-permute-done.6
  26.9 0.1 add_convert_fusion.2
  26.9 0.0 collective-permute-done.5.refs_1_
  27.0 0.1 add_convert_fusion.1
  27.1 1.8 %collective-permute-start.9 = (bf16[8,128,128]{2,1,0:T(8,128)(2,1)S(1)}, bf16[8,128,128]{2,1,0:T(8,128)(2,1)S(1)}, u32[]{:S(2)}, u32[]{:S(2)}) collective-permute-start(bf16[8,128,128]{2,1,0:T(8,128)(2,1)S(1)} %add_convert_fusion.1), channel_id=1, source_target_pairs={{0,6},{1,7},{2,0},{3,1},{4,2},{5,3},{6,4},{7,5},{8,14},{9,15},{10,... | collective-permute-start | bytes 786440 | tf_op jit(solution)/shard_map/ppermute | solution.py:19
  28.9 3.7 %collective-permute-start.12 = (bf16[1,128,128]{2,1,0:T(8,128)(2,1)S(1)}, bf16[1,128,128]{2,1,0:T(8,128)(2,1)S(1)}, u32[]{:S(2)}, u32[]{:S(2)}) collective-permute-start(bf16[1,128,128]{2,1,0:T(8,128)(2,1)S(1)} %get-tuple-element.110), channel_id=1, source_target_pairs={{0,24},{8,16},{16,8},{24,0},{1,25},{9,17},{17,9},{25,1},{2,26},{10... | collective-permute-start | bytes 98312 | tf_op jit(solution)/shard_map/ppermute | solution.py:29
  32.5 0.0 collective-permute-start.11
  32.5 0.8 %collective-permute-start.10 = (bf16[1,128,128]{2,1,0:T(8,128)(2,1)S(1)}, bf16[1,128,128]{2,1,0:T(8,128)(2,1)S(1)}, u32[]{:S(2)}, u32[]{:S(2)}) collective-permute-start(bf16[1,128,128]{2,1,0:T(8,128)(2,1)S(1)} %get-tuple-element.112), channel_id=1, source_target_pairs={{0,16},{8,24},{16,0},{24,8},{1,17},{9,25},{17,1},{25,9},{2,18},{10... | collective-permute-start | bytes 98312 | tf_op jit(solution)/shard_map/ppermute | solution.py:29
  33.3 1.6 %query_kernel.1 = bf16[128,32,128]{2,1,0:T(8,128)(2,1)} custom-call(bf16[4,384,1024]{2,1,0:T(8,128)(2,1)S(1)} %get-tuple-element.88.refs_0_, bf16[4,128,128]{2,1,0:T(8,128)(2,1)S(1)} %get-tuple-element.89.refs_1_, bf16[4,128,128]{2,1,0:T(8,128)(2,1)S(1)} %get-tuple-element.74.refs_1_.refs_2_, bf16[4,128,128]{2,1,0:T(8,128)(2,1)S(1)} %get-tuple-element.90.refs_3_), custom_call_target="tpu_custom_call" | custom-call | flops 2147483648 | bytes 5242880 | tf_op jit(solution)/shard_map/query_kernel/pallas_call | solution.py:444
  35.0 0.0 collective-permute-done.12.refs_6_
  35.0 1.5 %collective-permute-done.11.refs_5_ = bf16[1,128,128]{2,1,0:T(8,128)(2,1)S(1)} collective-permute-done((bf16[1,128,128]{2,1,0:T(8,128)(2,1)S(1)}, bf16[1,128,128]{2,1,0:T(8,128)(2,1)S(1)}, u32[]{:S(2)}, u32[]{:S(2)}) %collective-permute-start.11) | collective-permute-done | bytes 32800 | tf_op jit(solution)/shard_map/ppermute | solution.py:29
  36.4 0.9 %collective-permute-done.10.refs_4_ = bf16[1,128,128]{2,1,0:T(8,128)(2,1)S(1)} collective-permute-done((bf16[1,128,128]{2,1,0:T(8,128)(2,1)S(1)}, bf16[1,128,128]{2,1,0:T(8,128)(2,1)S(1)}, u32[]{:S(2)}, u32[]{:S(2)}) %collective-permute-start.10) | collective-permute-done | bytes 32800 | tf_op jit(solution)/shard_map/ppermute | solution.py:29
  37.4 0.0 collective-permute-done.9.refs_2_
  37.4 0.9 %finish_kernel.1 = (bf16[512,128]{1,0:T(8,128)(2,1)}, bf16[512,128]{1,0:T(8,128)(2,1)}, f32[16,4,128]{2,1,0:T(4,128)}, f32[16,4,128]{2,1,0:T(4,128)}) custom-call(f32[8,128,128]{2,1,0:T(8,128)S(1)} %get-tuple-element.91.refs_0_, bf16[8,128,128]{2,1,0:T(8,128)(2,1)S(1)} %collective-permute-done.5.refs_1_, ...), custom_call_target="tpu_custom_call" | custom-call | flops 1048576 | bytes 1048576 | tf_op jit(solution)/shard_map/finish_kernel/pallas_call | solution.py:444
  (2 shorter events, 0.0 us)
Async XLA Ops:
  0.6 8.3 %collective-permute-start = (bf16[128,4,128]{2,1,0:T(4,128)(2,1)}, bf16[128,4,128]{2,1,0:T(4,128)(2,1)S(1)}, u32[]{:S(2)}, u32[]{:S(2)}) collective-permute-start(bf16[128,4,128]{2,1,0:T(4,128)(2,1)} %bitcast.23), channel_id=1, source_target_pairs={{0,2},{1,3},{2,4},{3,5},{4,6},{5,7},{6,0},{7,1},{8,10},{9,11},{10,... | collective-permute-start | bytes 393224 | tf_op jit(solution)/shard_map/ppermute | solution.py:19
  4.4 0.9 %copy-start.1 = (bf16[1,128,4,128]{3,2,1,0:T(4,128)(2,1)S(1)}, bf16[1,128,4,128]{3,2,1,0:T(4,128)(2,1)}, u32[]{:S(2)}) copy-start(bf16[1,128,4,128]{3,2,1,0:T(4,128)(2,1)} %param.11) | copy-start | bytes 393220
  4.4 2.4 %copy-start.2 = (bf16[1,128,32,128]{3,2,1,0:T(8,128)(2,1)S(1)}, bf16[1,128,32,128]{3,2,1,0:T(8,128)(2,1)}, u32[]{:S(2)}) copy-start(bf16[1,128,32,128]{3,2,1,0:T(8,128)(2,1)} %param.12) | copy-start | bytes 3145732
  4.4 2.4 %copy-start.3 = (bf16[1,128,32,128]{3,2,1,0:T(8,128)(2,1)S(1)}, bf16[1,128,32,128]{3,2,1,0:T(8,128)(2,1)}, u32[]{:S(2)}) copy-start(bf16[1,128,32,128]{3,2,1,0:T(8,128)(2,1)} %param.9) | copy-start | bytes 3145732
  4.4 2.4 %copy-start.4 = (bf16[16,4,32,128]{3,2,1,0:T(8,128)(2,1)S(1)}, bf16[16,4,32,128]{3,2,1,0:T(8,128)(2,1)}, u32[]{:S(2)}) copy-start(bf16[16,4,32,128]{3,2,1,0:T(8,128)(2,1)} %param.13) | copy-start | bytes 1572868
  4.8 3.4 %copy-start.5 = (bf16[16,4,32,128]{3,2,1,0:T(8,128)(2,1)S(1)}, bf16[16,4,32,128]{3,2,1,0:T(8,128)(2,1)}, u32[]{:S(2)}) copy-start(bf16[16,4,32,128]{3,2,1,0:T(8,128)(2,1)} %param.14) | copy-start | bytes 1572868
  5.3 6.1 %collective-permute-start.1 = (bf16[128,4,128]{2,1,0:T(4,128)(2,1)S(1)}, bf16[128,4,128]{2,1,0:T(4,128)(2,1)S(1)}, u32[]{:S(2)}, u32[]{:S(2)}) collective-permute-start(bf16[128,4,128]{2,1,0:T(4,128)(2,1)S(1)} %bitcast.25), channel_id=1, source_target_pairs={{0,2},{1,3},{2,4},{3,5},{4,6},{5,7},{6,0},{7,1},{8,10},{9,11},{10,... | collective-permute-start | bytes 393224 | tf_op jit(solution)/shard_map/ppermute | solution.py:19
  8.2 0.9 %copy-start = (bf16[1,128,4,128]{3,2,1,0:T(4,128)(2,1)S(1)}, bf16[1,128,4,128]{3,2,1,0:T(4,128)(2,1)}, u32[]{:S(2)}) copy-start(bf16[1,128,4,128]{3,2,1,0:T(4,128)(2,1)} %param.10) | copy-start | bytes 393220
  9.2 1.4 %collective-permute-start.2 = (bf16[128,4,128]{2,1,0:T(4,128)(2,1)S(1)}, bf16[128,4,128]{2,1,0:T(4,128)(2,1)S(1)}, u32[]{:S(2)}, u32[]{:S(2)}) collective-permute-start(bf16[128,4,128]{2,1,0:T(4,128)(2,1)S(1)} %broadcast_select_fusion.1), channel_id=1, source_target_pairs={{0,1},{1,0},{2,3},{3,2},{4,5},{5,4},{6,7},{7,6},{8,9},{9,8},{10,11... | collective-permute-start | bytes 393224 | tf_op jit(solution)/shard_map/ppermute | solution.py:29
  11.5 1.6 %collective-permute-start.3 = (bf16[128,4,128]{2,1,0:T(4,128)(2,1)S(1)}, bf16[128,4,128]{2,1,0:T(4,128)(2,1)S(1)}, u32[]{:S(2)}, u32[]{:S(2)}) collective-permute-start(bf16[128,4,128]{2,1,0:T(4,128)(2,1)S(1)} %broadcast_select_fusion), channel_id=1, source_target_pairs={{0,1},{1,0},{2,3},{3,2},{4,5},{5,4},{6,7},{7,6},{8,9},{9,8},{10,11... | collective-permute-start | bytes 393224 | tf_op jit(solution)/shard_map/ppermute | solution.py:29
  12.5 0.7 %copy-start.6 = (f32[16,4]{0,1:T(4,128)S(1)}, f32[16,4]{0,1:T(4,128)}, u32[]{:S(2)}) copy-start(f32[16,4]{0,1:T(4,128)} %param.15) | copy-start | bytes 772
  15.2 2.0 %collective-permute-start.4 = (bf16[16,128,128]{2,1,0:T(8,128)(2,1)S(1)}, bf16[16,128,128]{2,1,0:T(8,128)(2,1)S(1)}, u32[]{:S(2)}, u32[]{:S(2)}) collective-permute-start(bf16[16,128,128]{2,1,0:T(8,128)(2,1)S(1)} %get-tuple-element.83), channel_id=1, source_target_pairs={{0,1},{1,0},{2,3},{3,2},{4,5},{5,4},{6,7},{7,6},{8,9},{9,8},{10,11... | collective-permute-start | bytes 1572872 | tf_op jit(solution)/shard_map/ppermute | solution.py:29
  17.3 7.3 %collective-permute-start.8 = (bf16[4,128,128]{2,1,0:T(8,128)(2,1)S(1)}, bf16[4,128,128]{2,1,0:T(8,128)(2,1)S(1)}, u32[]{:S(2)}, u32[]{:S(2)}) collective-permute-start(bf16[4,128,128]{2,1,0:T(8,128)(2,1)S(1)} %get-tuple-element.107), channel_id=1, source_target_pairs={{0,6},{1,7},{2,4},{3,5},{4,2},{5,3},{6,0},{7,1},{8,14},{9,15},{10,... | collective-permute-start | bytes 393224 | tf_op jit(solution)/shard_map/ppermute | solution.py:29
  19.5 7.4 %collective-permute-start.7 = (bf16[4,128,128]{2,1,0:T(8,128)(2,1)S(1)}, bf16[4,128,128]{2,1,0:T(8,128)(2,1)S(1)}, u32[]{:S(2)}, u32[]{:S(2)}) collective-permute-start(bf16[4,128,128]{2,1,0:T(8,128)(2,1)S(1)} %get-tuple-element.108), channel_id=1, source_target_pairs={{0,4},{1,5},{2,6},{3,7},{4,0},{5,1},{6,2},{7,3},{8,12},{9,13},{10,... | collective-permute-start | bytes 393224 | tf_op jit(solution)/shard_map/ppermute | solution.py:29
  20.4 6.5 %collective-permute-start.6 = (bf16[4,128,128]{2,1,0:T(8,128)(2,1)S(1)}, bf16[4,128,128]{2,1,0:T(8,128)(2,1)S(1)}, u32[]{:S(2)}, u32[]{:S(2)}) collective-permute-start(bf16[4,128,128]{2,1,0:T(8,128)(2,1)S(1)} %get-tuple-element.109), channel_id=1, source_target_pairs={{0,2},{1,3},{2,0},{3,1},{4,6},{5,7},{6,4},{7,5},{8,10},{9,11},{10,... | collective-permute-start | bytes 393224 | tf_op jit(solution)/shard_map/ppermute | solution.py:29
  24.4 2.6 %collective-permute-start.5 = (bf16[8,128,128]{2,1,0:T(8,128)(2,1)S(1)}, bf16[8,128,128]{2,1,0:T(8,128)(2,1)S(1)}, u32[]{:S(2)}, u32[]{:S(2)}) collective-permute-start(bf16[8,128,128]{2,1,0:T(8,128)(2,1)S(1)} %get-tuple-element.92), channel_id=1, source_target_pairs={{0,1},{1,0},{2,3},{3,2},{4,5},{5,4},{6,7},{7,6},{8,9},{9,8},{10,11... | collective-permute-start | bytes 786440 | tf_op jit(solution)/shard_map/ppermute | solution.py:29
  27.1 10.3 %collective-permute-start.9 = (bf16[8,128,128]{2,1,0:T(8,128)(2,1)S(1)}, bf16[8,128,128]{2,1,0:T(8,128)(2,1)S(1)}, u32[]{:S(2)}, u32[]{:S(2)}) collective-permute-start(bf16[8,128,128]{2,1,0:T(8,128)(2,1)S(1)} %add_convert_fusion.1), channel_id=1, source_target_pairs={{0,6},{1,7},{2,0},{3,1},{4,2},{5,3},{6,4},{7,5},{8,14},{9,15},{10,... | collective-permute-start | bytes 786440 | tf_op jit(solution)/shard_map/ppermute | solution.py:19
  28.9 6.1 %collective-permute-start.12 = (bf16[1,128,128]{2,1,0:T(8,128)(2,1)S(1)}, bf16[1,128,128]{2,1,0:T(8,128)(2,1)S(1)}, u32[]{:S(2)}, u32[]{:S(2)}) collective-permute-start(bf16[1,128,128]{2,1,0:T(8,128)(2,1)S(1)} %get-tuple-element.110), channel_id=1, source_target_pairs={{0,24},{8,16},{16,8},{24,0},{1,25},{9,17},{17,9},{25,1},{2,26},{10... | collective-permute-start | bytes 98312 | tf_op jit(solution)/shard_map/ppermute | solution.py:29
  32.5 3.9 %collective-permute-start.11 = (bf16[1,128,128]{2,1,0:T(8,128)(2,1)S(1)}, bf16[1,128,128]{2,1,0:T(8,128)(2,1)S(1)}, u32[]{:S(2)}, u32[]{:S(2)}) collective-permute-start(bf16[1,128,128]{2,1,0:T(8,128)(2,1)S(1)} %get-tuple-element.111), channel_id=1, source_target_pairs={{0,8},{8,0},{16,24},{24,16},{1,9},{9,1},{17,25},{25,17},{2,10},{10... | collective-permute-start | bytes 98312 | tf_op jit(solution)/shard_map/ppermute | solution.py:29
  32.5 4.8 %collective-permute-start.10 = (bf16[1,128,128]{2,1,0:T(8,128)(2,1)S(1)}, bf16[1,128,128]{2,1,0:T(8,128)(2,1)S(1)}, u32[]{:S(2)}, u32[]{:S(2)}) collective-permute-start(bf16[1,128,128]{2,1,0:T(8,128)(2,1)S(1)} %get-tuple-element.112), channel_id=1, source_target_pairs={{0,16},{8,24},{16,0},{24,8},{1,17},{9,25},{17,1},{25,9},{2,18},{10... | collective-permute-start | bytes 98312 | tf_op jit(solution)/shard_map/ppermute | solution.py:29

commit v19 on v17

--- a/solution.py
+++ b/solution.py
@@ -33,7 +33,8 @@
     ctx, rep = lax.axis_size("ctx"), lax.axis_size("rep")
     bits = [{"ctx": 1 << at} for at in range(ctx.bit_length() - 2, 0, -1)]
     bits += [{"rep": 1 << at} for at in range(rep.bit_length() - 1)]
-    return [bits[at : at + 2] for at in range(0, len(bits), 2)]
+    over_ctx = ctx.bit_length() - 2
+    return [bits[at : at + 2] for at in range(0, over_ctx, 2)] + [[bit] for bit in bits[over_ctx:]]
 
 
 def reduce_place(index):
@@ -516,13 +517,12 @@
     onward = back_two.astype(WIDE) + jnp.where(even, 0.0, from_mate.astype(WIDE))
     onward = onward.astype(LOW)
 
+    from_two = shifted(onward, "ctx", -2)
     groups = reduce_groups()
     for at, group_bits in enumerate(groups):
-        beside = back_own if at == 0 else None
-        if at == len(groups) - 1:
+        if at == len(groups) - 2:
             part, onward = lax.optimization_barrier((part, onward))
-            from_two = shifted(onward, "ctx", -2)
-            beside = from_two
+        beside = {0: back_own, len(groups) - 2: onward, len(groups) - 1: from_two}.get(at)
         part, others = scattered(part, group_bits, beside)
         if at < len(groups) - 1:
             part = part.astype(WIDE) + sum(other.astype(WIDE) for other in others)

time: 38.4 us -> 37.7 us (0.982)
  waiting for transfers between devices: 6.01 us -> 5.49 us
    ppermute x10 -> x9, waiting for transfers between devices: 6 us -> 5.13 us  [exchanged(): lax.ppermute(value, axes, [(int(source), int(target)) for source, target...]
    ppermute x10 -> x9, starting transfers between devices: 8.8 us -> 8.65 us  [exchanged(): lax.ppermute(value, axes, [(int(source), int(target)) for source, target...]
  transfers between devices with their start and end apart: 13 -> 12, of which waited for: 6 -> 7; matrix products, arithmetic and copies ran while one was open for 2% -> 2% of each run, Pallas kernels for 30% -> 30%
where the time goes in v19:
time: 37.7 us; the launch traced here: 37.5 us
  starting transfers between devices  14.9 us (40%)
  Pallas kernels  14.3 us (38%)
  waiting for transfers between devices  5.49 us (15%)
  other arithmetic  1.18 us (3%)
  between operations  0.89 us (2%)
  local copies, waits for them, and re-layouts  0.79 us (2%)
    pallas_call x12, Pallas kernels, run(): pl.pallas_call(lambda *refs: body(*refs, **fixed), out_shape=[jax.ShapeDt...  14.3 us
    ppermute x9, starting transfers between devices, exchanged(): lax.ppermute(value, axes, [(int(source), int(target)) for source, target...  8.65 us
    ppermute x3, starting transfers between devices, shifted(): lax.ppermute(value, axis, [(source, (source + steps) % count) for source...  6.23 us
    ppermute x9, waiting for transfers between devices, exchanged(): lax.ppermute(value, axes, [(int(source), int(target)) for source, target...  5.13 us
  transfers between devices with their start and end apart: 12, of which 7 were waited for; matrix products, arithmetic and copies ran while one was open for 2% of the time, Pallas kernels for 30%

profile of v19, /device:TPU:0, one launch (start us, length us, event | category | flops | bytes accessed | tf_op | source)
XLA Modules:
  0.0 37.5 jit_solution(18295575122795996131)
XLA Ops:
  0.6 3.0 %collective-permute-start = (bf16[128,4,128]{2,1,0:T(4,128)(2,1)}, bf16[128,4,128]{2,1,0:T(4,128)(2,1)S(1)}, u32[]{:S(2)}, u32[]{:S(2)}) collective-permute-start(bf16[128,4,128]{2,1,0:T(4,128)(2,1)} %bitcast.23), channel_id=1, source_target_pairs={{0,2},{1,3},{2,4},{3,5},{4,6},{5,7},{6,0},{7,1},{8,10},{9,11},{10,... | collective-permute-start | bytes 393224 | tf_op jit(solution)/shard_map/ppermute | solution.py:19
  3.6 0.7 %pad_add_fusion.refs_0_ = s32[2,1024]{1,0:T(2,128)S(1)} fusion(s32[1,1024]{1,0:T(1,128)} %param.17, s32[1,1024]{1,0:T(1,128)} %param.16), kind=kLoop, calls=%fused_computation.6 | loop fusion | flops 2048 | bytes 16384 | tf_op jit(solution)/shard_map/concatenate | solution.py:457
  4.4 0.0 copy-start.1
  4.4 0.0 copy-start.2
  4.4 0.0 copy-start.3
  4.4 0.0 copy-start.4
  4.4 0.3 place_kernel.1
  4.8 0.0 copy-start.5
  4.8 0.5 %copy-done.1 = bf16[1,128,4,128]{3,2,1,0:T(4,128)(2,1)S(1)} copy-done((bf16[1,128,4,128]{3,2,1,0:T(4,128)(2,1)S(1)}, bf16[1,128,4,128]{3,2,1,0:T(4,128)(2,1)}, u32[]{:S(2)}) %copy-start.1) | copy-done | bytes 131096
  5.3 1.5 %collective-permute-start.1 = (bf16[128,4,128]{2,1,0:T(4,128)(2,1)S(1)}, bf16[128,4,128]{2,1,0:T(4,128)(2,1)S(1)}, u32[]{:S(2)}, u32[]{:S(2)}) collective-permute-start(bf16[128,4,128]{2,1,0:T(4,128)(2,1)S(1)} %bitcast.25), channel_id=1, source_target_pairs={{0,2},{1,3},{2,4},{3,5},{4,6},{5,7},{6,0},{7,1},{8,10},{9,11},{10,... | collective-permute-start | bytes 393224 | tf_op jit(solution)/shard_map/ppermute | solution.py:19
  6.8 0.0 copy-done.2
  6.8 0.0 copy-done.3
  6.8 0.0 copy-done.4
  6.8 1.4 %pull_kernel.1 = (bf16[4,1024,128]{2,1,0:T(8,128)(2,1)S(1)}, bf16[4,1024,128]{2,1,0:T(8,128)(2,1)S(1)}, f32[8,1024]{1,0:T(8,128)S(1)}, bf16[512,1024]{1,0:T(8,128)(2,1)S(1)}) custom-call(s32[8,1024]{1,0:T(8,128)S(1)} %get-tuple-element.54.refs_0_.refs_7_, bf16[128,32,128]{2,1,0:T(8,128)(2,1)S(1)} %bitcast.29, bf16[64,32,128]{2,1,0:T(8,128)(2,1)S(1)} %bitcast.31, ...), custom_call_target="tpu_custom_call" | custom-call | flops 1073741824 | bytes 4194304 | tf_op jit(solution)/shard_map/pull_kernel/pallas_call | solution.py:434
  8.2 0.0 copy-done.5
  8.2 0.0 copy-start
  8.2 0.8 %hidden_grad_kernel.1 = (bf16[4,1024,128]{2,1,0:T(8,128)(2,1)S(1)}, bf16[4,512,128]{2,1,0:T(8,128)(2,1)S(1)}) custom-call(s32[8,1024]{1,0:T(8,128)S(1)} %get-tuple-element.54.refs_0_.refs_7_, f32[8,1024]{1,0:T(8,128)S(1)} %get-tuple-element.57.refs_1_, bf16[4,1024,128]{2,1,0:T(8,128)(2,1)S(1)} %get-tuple-element.58.refs_2_.refs_5_, ...), custom_call_target="tpu_custom_call" | custom-call | flops 2147483648 | bytes 4194304 | tf_op jit(solution)/shard_map/hidden_grad_kernel/pallas_call | solution.py:434
  9.0 0.0 collective-permute-done
  9.0 0.1 copy-done
  9.1 0.1 broadcast_select_fusion.1
  9.2 0.1 collective-permute-start.2
  9.2 0.9 %fold_kernel.1 = (f32[4,128,1024]{2,1,0:T(8,128)S(1)}, f32[4,2,1024]{2,1,0:T(2,128)S(1)}, bf16[4,128,128]{2,1,0:T(8,128)(2,1)S(1)}, bf16[4,128,128]{2,1,0:T(8,128)(2,1)S(1)}) custom-call(bf16[4,1024,128]{2,1,0:T(8,128)(2,1)S(1)} %get-tuple-element.55.refs_0_, bf16[512,128]{1,0:T(8,128)(2,1)S(1)} %bitcast.28, bf16[512,128]{1,0:T(8,128)(2,1)S(1)} %bitcast.24, ...), custom_call_target="tpu_custom_call" | custom-call | flops 2147483648 | bytes 4194304 | tf_op jit(solution)/shard_map/fold_kernel/pallas_call | solution.py:434
  10.2 0.4 %collective-permute-done.2 = bf16[128,4,128]{2,1,0:T(4,128)(2,1)S(1)} collective-permute-done((bf16[128,4,128]{2,1,0:T(4,128)(2,1)S(1)}, bf16[128,4,128]{2,1,0:T(4,128)(2,1)S(1)}, u32[]{:S(2)}, u32[]{:S(2)}) %collective-permute-start.2) | collective-permute-done | bytes 131104 | tf_op jit(solution)/shard_map/ppermute | solution.py:29
  10.6 0.8 %near_kernel.1 = (bf16[2,384,1024]{2,1,0:T(8,128)(2,1)S(1)}, bf16[4,128,128]{2,1,0:T(8,128)(2,1)S(1)}) custom-call(bf16[4,1024,128]{2,1,0:T(8,128)(2,1)S(1)} %get-tuple-element.55.refs_0_, bf16[512,128]{1,0:T(8,128)(2,1)S(1)} %bitcast.22, f32[2,128,1024]{2,1,0:T(8,128)S(1)} %get-tuple-element.64.refs_3_.refs_2_, ...), custom_call_target="tpu_custom_call" | custom-call | flops 1073741824 | bytes 4194304 | tf_op jit(solution)/shard_map/near_kernel/pallas_call | solution.py:434
  11.4 0.0 collective-permute-done.1
  11.4 0.1 broadcast_select_fusion
  11.5 0.2 collective-permute-start.3
  11.7 0.8 %far_kernel.1.refs_1_.refs_2_.refs_3_ = bf16[2,384,1024]{2,1,0:T(8,128)(2,1)S(1)} custom-call(bf16[4,1024,128]{2,1,0:T(8,128)(2,1)S(1)} %get-tuple-element.55.refs_0_, bf16[4,128,128]{2,1,0:T(8,128)(2,1)S(1)} %get-tuple-element.71.refs_1_.refs_2_, f32[2,128,1024]{2,1,0:T(8,128)S(1)} %get-tuple-element.64.refs_3_.refs_2_, ...), custom_call_target="tpu_custom_call" | custom-call | flops 1073741824 | bytes 4194304 | tf_op jit(solution)/shard_map/far_kernel/pallas_call | solution.py:434
  12.5 0.0 copy-start.6
  12.5 0.6 %hidden_kernel.1 = (f32[512,1024]{1,0:T(8,128)S(1)}, bf16[4,128,128]{2,1,0:T(8,128)(2,1)S(1)}, bf16[4,128,128]{2,1,0:T(8,128)(2,1)S(1)}) custom-call(bf16[2,384,1024]{2,1,0:T(8,128)(2,1)S(1)} %get-tuple-element.81.refs_0_.refs_1_.refs_2_, bf16[2,384,1024]{2,1,0:T(8,128)(2,1)S(1)} %far_kernel.1.refs_1_.refs_2_.refs_3_, bf16[512,128]{1,0:T(8,128)(2,1)S(1)} %bitcast.27, ...), custom_call_target="tpu_custom_call" | custom-call | flops 1073741824 | bytes 4194304 | tf_op jit(solution)/shard_map/hidden_kernel/pallas_call | solution.py:434
  13.0 0.0 collective-permute-done.3
  13.0 0.1 copy-done.6
  13.1 2.0 %forward_kernel.1 = (bf16[16,128,128]{2,1,0:T(8,128)(2,1)S(1)}, bf16[512,1024]{1,0:T(8,128)(2,1)S(1)}, bf16[256,1024]{1,0:T(8,128)(2,1)S(1)}, bf16[4,128,128]{2,1,0:T(8,128)(2,1)S(1)}) custom-call(f32[4,16]{1,0:T(4,128)S(1)} %bitcast.35, bf16[2,384,1024]{2,1,0:T(8,128)(2,1)S(1)} %get-tuple-element.81.refs_0_.refs_1_.refs_2_, ...), custom_call_target="tpu_custom_call" | custom-call | flops 3221225472 | bytes 10485760 | tf_op jit(solution)/shard_map/forward_kernel/pallas_call | solution.py:434
  15.2 0.4 %collective-permute-start.4 = (bf16[16,128,128]{2,1,0:T(8,128)(2,1)S(1)}, bf16[16,128,128]{2,1,0:T(8,128)(2,1)S(1)}, u32[]{:S(2)}, u32[]{:S(2)}) collective-permute-start(bf16[16,128,128]{2,1,0:T(8,128)(2,1)S(1)} %get-tuple-element.80), channel_id=1, source_target_pairs={{0,1},{1,0},{2,3},{3,2},{4,5},{5,4},{6,7},{7,6},{8,9},{9,8},{10,11... | collective-permute-start | bytes 1572872 | tf_op jit(solution)/shard_map/ppermute | solution.py:29
  15.6 0.8 %keep_kernel.1 = bf16[16,128,128]{2,1,0:T(8,128)(2,1)S(1)} custom-call(bf16[512,1024]{1,0:T(8,128)(2,1)S(1)} %get-tuple-element.78.refs_0_, bf16[256,1024]{1,0:T(8,128)(2,1)S(1)} %get-tuple-element.79.refs_1_, bf16[4,1024,128]{2,1,0:T(8,128)(2,1)S(1)} %get-tuple-element.58.refs_2_.refs_5_, bf16[512,1024]{1,0:T(8,128)(2,1)S(1)} %get-tuple-element.77.refs_8_.refs_3_), custom_call_target="tpu_custom_call" | custom-call | flops 1073741824 | bytes 5242880 | tf_op jit(solution)/shard_map/keep_kernel/pallas_call | solution.py:434
  16.4 0.8 %collective-permute-done.4 = bf16[16,128,128]{2,1,0:T(8,128)(2,1)S(1)} collective-permute-done((bf16[16,128,128]{2,1,0:T(8,128)(2,1)S(1)}, bf16[16,128,128]{2,1,0:T(8,128)(2,1)S(1)}, u32[]{:S(2)}, u32[]{:S(2)}) %collective-permute-start.4) | collective-permute-done | bytes 524320 | tf_op jit(solution)/shard_map/ppermute | solution.py:29
  17.1 0.1 add_convert_fusion
  17.3 2.2 %collective-permute-start.9 = (bf16[4,128,128]{2,1,0:T(8,128)(2,1)S(1)}, bf16[4,128,128]{2,1,0:T(8,128)(2,1)S(1)}, u32[]{:S(2)}, u32[]{:S(2)}) collective-permute-start(bf16[4,128,128]{2,1,0:T(8,128)(2,1)S(1)} %get-tuple-element.101), channel_id=1, source_target_pairs={{0,6},{1,7},{2,4},{3,5},{4,2},{5,3},{6,0},{7,1},{8,14},{9,15},{10,... | collective-permute-start | bytes 393224 | tf_op jit(solution)/shard_map/ppermute | solution.py:29
  19.5 0.9 %collective-permute-start.8 = (bf16[4,128,128]{2,1,0:T(8,128)(2,1)S(1)}, bf16[4,128,128]{2,1,0:T(8,128)(2,1)S(1)}, u32[]{:S(2)}, u32[]{:S(2)}) collective-permute-start(bf16[4,128,128]{2,1,0:T(8,128)(2,1)S(1)} %get-tuple-element.102), channel_id=1, source_target_pairs={{0,4},{1,5},{2,6},{3,7},{4,0},{5,1},{6,2},{7,3},{8,12},{9,13},{10,... | collective-permute-start | bytes 393224 | tf_op jit(solution)/shard_map/ppermute | solution.py:29
  20.4 0.5 %collective-permute-start.7 = (bf16[4,128,128]{2,1,0:T(8,128)(2,1)S(1)}, bf16[4,128,128]{2,1,0:T(8,128)(2,1)S(1)}, u32[]{:S(2)}, u32[]{:S(2)}) collective-permute-start(bf16[4,128,128]{2,1,0:T(8,128)(2,1)S(1)} %get-tuple-element.103), channel_id=1, source_target_pairs={{0,2},{1,3},{2,0},{3,1},{4,6},{5,7},{6,4},{7,5},{8,10},{9,11},{10,... | collective-permute-start | bytes 393224 | tf_op jit(solution)/shard_map/ppermute | solution.py:29
  20.9 3.5 %backward_kernel.1 = (bf16[8,128,128]{2,1,0:T(8,128)(2,1)S(1)}, bf16[8,128,128]{2,1,0:T(8,128)(2,1)S(1)}, f32[8,128,128]{2,1,0:T(8,128)S(1)}, bf16[4,384,1024]{2,1,0:T(8,128)(2,1)S(1)}) custom-call(bf16[4,1024,128]{2,1,0:T(8,128)(2,1)S(1)} %get-tuple-element.55.refs_0_, bf16[4,1024,128]{2,1,0:T(8,128)(2,1)S(1)} %get-tuple-element.60.refs_1_, ...), custom_call_target="tpu_custom_call" | custom-call | flops 4294967296 | bytes 10485760 | tf_op jit(solution)/shard_map/backward_kernel/pallas_call | solution.py:434
  24.4 0.1 collective-permute-start.5
  24.4 0.2 collective-permute-done.9
  24.6 2.2 %collective-permute-done.8 = bf16[4,128,128]{2,1,0:T(8,128)(2,1)S(1)} collective-permute-done((bf16[4,128,128]{2,1,0:T(8,128)(2,1)S(1)}, bf16[4,128,128]{2,1,0:T(8,128)(2,1)S(1)}, u32[]{:S(2)}, u32[]{:S(2)}) %collective-permute-start.8) | collective-permute-done | bytes 131104 | tf_op jit(solution)/shard_map/ppermute | solution.py:29
  26.9 0.0 collective-permute-done.7
  26.9 0.1 add_convert_fusion.2
  26.9 0.0 collective-permute-done.5.refs_1_
  27.0 0.1 add_convert_fusion.1
  27.1 1.6 %collective-permute-start.10 = (bf16[2,128,128]{2,1,0:T(8,128)(2,1)S(1)}, bf16[2,128,128]{2,1,0:T(8,128)(2,1)S(1)}, u32[]{:S(2)}, u32[]{:S(2)}) collective-permute-start(bf16[2,128,128]{2,1,0:T(8,128)(2,1)S(1)} %slice.29), channel_id=1, source_target_pairs={{0,8},{8,0},{16,24},{24,16},{1,9},{9,1},{17,25},{25,17},{2,10},{10... | collective-permute-start | bytes 196616 | tf_op jit(solution)/shard_map/ppermute | solution.py:29
  28.7 1.7 %collective-permute-start.6 = (bf16[8,128,128]{2,1,0:T(8,128)(2,1)S(1)}, bf16[8,128,128]{2,1,0:T(8,128)(2,1)S(1)}, u32[]{:S(2)}, u32[]{:S(2)}) collective-permute-start(bf16[8,128,128]{2,1,0:T(8,128)(2,1)S(1)} %add_convert_fusion.1), channel_id=1, source_target_pairs={{0,6},{1,7},{2,0},{3,1},{4,2},{5,3},{6,4},{7,5},{8,14},{9,15},{10,... | collective-permute-start | bytes 786440 | tf_op jit(solution)/shard_map/ppermute | solution.py:19
  30.5 0.9 %collective-permute-done.10 = bf16[2,128,128]{2,1,0:T(8,128)(2,1)S(1)} collective-permute-done((bf16[2,128,128]{2,1,0:T(8,128)(2,1)S(1)}, bf16[2,128,128]{2,1,0:T(8,128)(2,1)S(1)}, u32[]{:S(2)}, u32[]{:S(2)}) %collective-permute-start.10) | collective-permute-done | bytes 65568 | tf_op jit(solution)/shard_map/ppermute | solution.py:29
  31.4 2.7 %collective-permute-start.11 = (bf16[1,128,128]{2,1,0:T(8,128)(2,1)S(1)}, bf16[1,128,128]{2,1,0:T(8,128)(2,1)S(1)}, u32[]{:S(2)}, u32[]{:S(2)}) collective-permute-start(bf16[1,128,128]{2,1,0:T(8,128)(2,1)S(1)} %get-tuple-element.104), channel_id=1, source_target_pairs={{0,16},{8,24},{16,0},{24,8},{1,17},{9,25},{17,1},{25,9},{2,18},{10... | collective-permute-start | bytes 98312 | tf_op jit(solution)/shard_map/ppermute | solution.py:29
  34.1 1.6 %query_kernel.1 = bf16[128,32,128]{2,1,0:T(8,128)(2,1)} custom-call(bf16[4,384,1024]{2,1,0:T(8,128)(2,1)S(1)} %get-tuple-element.85.refs_0_, bf16[4,128,128]{2,1,0:T(8,128)(2,1)S(1)} %get-tuple-element.86.refs_1_, bf16[4,128,128]{2,1,0:T(8,128)(2,1)S(1)} %get-tuple-element.71.refs_1_.refs_2_, bf16[4,128,128]{2,1,0:T(8,128)(2,1)S(1)} %get-tuple-element.87.refs_3_), custom_call_target="tpu_custom_call" | custom-call | flops 2147483648 | bytes 5242880 | tf_op jit(solution)/shard_map/query_kernel/pallas_call | solution.py:434
  35.8 0.6 %collective-permute-done.11.refs_4_ = bf16[1,128,128]{2,1,0:T(8,128)(2,1)S(1)} collective-permute-done((bf16[1,128,128]{2,1,0:T(8,128)(2,1)S(1)}, bf16[1,128,128]{2,1,0:T(8,128)(2,1)S(1)}, u32[]{:S(2)}, u32[]{:S(2)}) %collective-permute-start.11) | collective-permute-done | bytes 32800 | tf_op jit(solution)/shard_map/ppermute | solution.py:29
  36.3 0.4 collective-permute-done.6.refs_2_
  36.7 0.8 %finish_kernel.1 = (bf16[512,128]{1,0:T(8,128)(2,1)}, bf16[512,128]{1,0:T(8,128)(2,1)}, f32[16,4,128]{2,1,0:T(4,128)}, f32[16,4,128]{2,1,0:T(4,128)}) custom-call(f32[8,128,128]{2,1,0:T(8,128)S(1)} %get-tuple-element.88.refs_0_, bf16[8,128,128]{2,1,0:T(8,128)(2,1)S(1)} %collective-permute-done.5.refs_1_, ...), custom_call_target="tpu_custom_call" | custom-call | flops 1048576 | bytes 1048576 | tf_op jit(solution)/shard_map/finish_kernel/pallas_call | solution.py:434
  (4 shorter events, 0.1 us)
Async XLA Ops:
  0.6 8.3 %collective-permute-start = (bf16[128,4,128]{2,1,0:T(4,128)(2,1)}, bf16[128,4,128]{2,1,0:T(4,128)(2,1)S(1)}, u32[]{:S(2)}, u32[]{:S(2)}) collective-permute-start(bf16[128,4,128]{2,1,0:T(4,128)(2,1)} %bitcast.23), channel_id=1, source_target_pairs={{0,2},{1,3},{2,4},{3,5},{4,6},{5,7},{6,0},{7,1},{8,10},{9,11},{10,... | collective-permute-start | bytes 393224 | tf_op jit(solution)/shard_map/ppermute | solution.py:19
  4.4 0.9 %copy-start.1 = (bf16[1,128,4,128]{3,2,1,0:T(4,128)(2,1)S(1)}, bf16[1,128,4,128]{3,2,1,0:T(4,128)(2,1)}, u32[]{:S(2)}) copy-start(bf16[1,128,4,128]{3,2,1,0:T(4,128)(2,1)} %param.11) | copy-start | bytes 393220
  4.4 2.4 %copy-start.2 = (bf16[1,128,32,128]{3,2,1,0:T(8,128)(2,1)S(1)}, bf16[1,128,32,128]{3,2,1,0:T(8,128)(2,1)}, u32[]{:S(2)}) copy-start(bf16[1,128,32,128]{3,2,1,0:T(8,128)(2,1)} %param.12) | copy-start | bytes 3145732
  4.4 2.4 %copy-start.3 = (bf16[1,128,32,128]{3,2,1,0:T(8,128)(2,1)S(1)}, bf16[1,128,32,128]{3,2,1,0:T(8,128)(2,1)}, u32[]{:S(2)}) copy-start(bf16[1,128,32,128]{3,2,1,0:T(8,128)(2,1)} %param.9) | copy-start | bytes 3145732
  4.4 2.4 %copy-start.4 = (bf16[16,4,32,128]{3,2,1,0:T(8,128)(2,1)S(1)}, bf16[16,4,32,128]{3,2,1,0:T(8,128)(2,1)}, u32[]{:S(2)}) copy-start(bf16[16,4,32,128]{3,2,1,0:T(8,128)(2,1)} %param.13) | copy-start | bytes 1572868
  4.8 3.4 %copy-start.5 = (bf16[16,4,32,128]{3,2,1,0:T(8,128)(2,1)S(1)}, bf16[16,4,32,128]{3,2,1,0:T(8,128)(2,1)}, u32[]{:S(2)}) copy-start(bf16[16,4,32,128]{3,2,1,0:T(8,128)(2,1)} %param.14) | copy-start | bytes 1572868
  5.3 6.1 %collective-permute-start.1 = (bf16[128,4,128]{2,1,0:T(4,128)(2,1)S(1)}, bf16[128,4,128]{2,1,0:T(4,128)(2,1)S(1)}, u32[]{:S(2)}, u32[]{:S(2)}) collective-permute-start(bf16[128,4,128]{2,1,0:T(4,128)(2,1)S(1)} %bitcast.25), channel_id=1, source_target_pairs={{0,2},{1,3},{2,4},{3,5},{4,6},{5,7},{6,0},{7,1},{8,10},{9,11},{10,... | collective-permute-start | bytes 393224 | tf_op jit(solution)/shard_map/ppermute | solution.py:19
  8.2 0.9 %copy-start = (bf16[1,128,4,128]{3,2,1,0:T(4,128)(2,1)S(1)}, bf16[1,128,4,128]{3,2,1,0:T(4,128)(2,1)}, u32[]{:S(2)}) copy-start(bf16[1,128,4,128]{3,2,1,0:T(4,128)(2,1)} %param.10) | copy-start | bytes 393220
  9.2 1.4 %collective-permute-start.2 = (bf16[128,4,128]{2,1,0:T(4,128)(2,1)S(1)}, bf16[128,4,128]{2,1,0:T(4,128)(2,1)S(1)}, u32[]{:S(2)}, u32[]{:S(2)}) collective-permute-start(bf16[128,4,128]{2,1,0:T(4,128)(2,1)S(1)} %broadcast_select_fusion.1), channel_id=1, source_target_pairs={{0,1},{1,0},{2,3},{3,2},{4,5},{5,4},{6,7},{7,6},{8,9},{9,8},{10,11... | collective-permute-start | bytes 393224 | tf_op jit(solution)/shard_map/ppermute | solution.py:29
  11.5 1.6 %collective-permute-start.3 = (bf16[128,4,128]{2,1,0:T(4,128)(2,1)S(1)}, bf16[128,4,128]{2,1,0:T(4,128)(2,1)S(1)}, u32[]{:S(2)}, u32[]{:S(2)}) collective-permute-start(bf16[128,4,128]{2,1,0:T(4,128)(2,1)S(1)} %broadcast_select_fusion), channel_id=1, source_target_pairs={{0,1},{1,0},{2,3},{3,2},{4,5},{5,4},{6,7},{7,6},{8,9},{9,8},{10,11... | collective-permute-start | bytes 393224 | tf_op jit(solution)/shard_map/ppermute | solution.py:29
  12.5 0.7 %copy-start.6 = (f32[16,4]{0,1:T(4,128)S(1)}, f32[16,4]{0,1:T(4,128)}, u32[]{:S(2)}) copy-start(f32[16,4]{0,1:T(4,128)} %param.15) | copy-start | bytes 772
  15.2 2.0 %collective-permute-start.4 = (bf16[16,128,128]{2,1,0:T(8,128)(2,1)S(1)}, bf16[16,128,128]{2,1,0:T(8,128)(2,1)S(1)}, u32[]{:S(2)}, u32[]{:S(2)}) collective-permute-start(bf16[16,128,128]{2,1,0:T(8,128)(2,1)S(1)} %get-tuple-element.80), channel_id=1, source_target_pairs={{0,1},{1,0},{2,3},{3,2},{4,5},{5,4},{6,7},{7,6},{8,9},{9,8},{10,11... | collective-permute-start | bytes 1572872 | tf_op jit(solution)/shard_map/ppermute | solution.py:29
  17.3 7.3 %collective-permute-start.9 = (bf16[4,128,128]{2,1,0:T(8,128)(2,1)S(1)}, bf16[4,128,128]{2,1,0:T(8,128)(2,1)S(1)}, u32[]{:S(2)}, u32[]{:S(2)}) collective-permute-start(bf16[4,128,128]{2,1,0:T(8,128)(2,1)S(1)} %get-tuple-element.101), channel_id=1, source_target_pairs={{0,6},{1,7},{2,4},{3,5},{4,2},{5,3},{6,0},{7,1},{8,14},{9,15},{10,... | collective-permute-start | bytes 393224 | tf_op jit(solution)/shard_map/ppermute | solution.py:29
  19.5 7.4 %collective-permute-start.8 = (bf16[4,128,128]{2,1,0:T(8,128)(2,1)S(1)}, bf16[4,128,128]{2,1,0:T(8,128)(2,1)S(1)}, u32[]{:S(2)}, u32[]{:S(2)}) collective-permute-start(bf16[4,128,128]{2,1,0:T(8,128)(2,1)S(1)} %get-tuple-element.102), channel_id=1, source_target_pairs={{0,4},{1,5},{2,6},{3,7},{4,0},{5,1},{6,2},{7,3},{8,12},{9,13},{10,... | collective-permute-start | bytes 393224 | tf_op jit(solution)/shard_map/ppermute | solution.py:29
  20.4 6.5 %collective-permute-start.7 = (bf16[4,128,128]{2,1,0:T(8,128)(2,1)S(1)}, bf16[4,128,128]{2,1,0:T(8,128)(2,1)S(1)}, u32[]{:S(2)}, u32[]{:S(2)}) collective-permute-start(bf16[4,128,128]{2,1,0:T(8,128)(2,1)S(1)} %get-tuple-element.103), channel_id=1, source_target_pairs={{0,2},{1,3},{2,0},{3,1},{4,6},{5,7},{6,4},{7,5},{8,10},{9,11},{10,... | collective-permute-start | bytes 393224 | tf_op jit(solution)/shard_map/ppermute | solution.py:29
  24.4 2.6 %collective-permute-start.5 = (bf16[8,128,128]{2,1,0:T(8,128)(2,1)S(1)}, bf16[8,128,128]{2,1,0:T(8,128)(2,1)S(1)}, u32[]{:S(2)}, u32[]{:S(2)}) collective-permute-start(bf16[8,128,128]{2,1,0:T(8,128)(2,1)S(1)} %get-tuple-element.89), channel_id=1, source_target_pairs={{0,1},{1,0},{2,3},{3,2},{4,5},{5,4},{6,7},{7,6},{8,9},{9,8},{10,11... | collective-permute-start | bytes 786440 | tf_op jit(solution)/shard_map/ppermute | solution.py:29
  27.1 4.3 %collective-permute-start.10 = (bf16[2,128,128]{2,1,0:T(8,128)(2,1)S(1)}, bf16[2,128,128]{2,1,0:T(8,128)(2,1)S(1)}, u32[]{:S(2)}, u32[]{:S(2)}) collective-permute-start(bf16[2,128,128]{2,1,0:T(8,128)(2,1)S(1)} %slice.29), channel_id=1, source_target_pairs={{0,8},{8,0},{16,24},{24,16},{1,9},{9,1},{17,25},{25,17},{2,10},{10... | collective-permute-start | bytes 196616 | tf_op jit(solution)/shard_map/ppermute | solution.py:29
  28.7 8.0 %collective-permute-start.6 = (bf16[8,128,128]{2,1,0:T(8,128)(2,1)S(1)}, bf16[8,128,128]{2,1,0:T(8,128)(2,1)S(1)}, u32[]{:S(2)}, u32[]{:S(2)}) collective-permute-start(bf16[8,128,128]{2,1,0:T(8,128)(2,1)S(1)} %add_convert_fusion.1), channel_id=1, source_target_pairs={{0,6},{1,7},{2,0},{3,1},{4,2},{5,3},{6,4},{7,5},{8,14},{9,15},{10,... | collective-permute-start | bytes 786440 | tf_op jit(solution)/shard_map/ppermute | solution.py:19
  31.4 4.9 %collective-permute-start.11 = (bf16[1,128,128]{2,1,0:T(8,128)(2,1)S(1)}, bf16[1,128,128]{2,1,0:T(8,128)(2,1)S(1)}, u32[]{:S(2)}, u32[]{:S(2)}) collective-permute-start(bf16[1,128,128]{2,1,0:T(8,128)(2,1)S(1)} %get-tuple-element.104), channel_id=1, source_target_pairs={{0,16},{8,24},{16,0},{24,8},{1,17},{9,25},{17,1},{25,9},{2,18},{10... | collective-permute-start | bytes 98312 | tf_op jit(solution)/shard_map/ppermute | solution.py:29

commit v20 on v19

--- a/solution.py
+++ b/solution.py
@@ -49,7 +49,7 @@
     count = 1 << len(group)
     size = part.shape[0] // count
     others = []
-    for j in range(1, count):
+    for j in ([1, 3, 2] if count == 4 else [1]):
         bits = {}
         for at, pair in enumerate(reversed(group)):
             if (j >> at) & 1:

time: 37.7 us -> 37.7 us (level)
  no operation moved by 1% of the time
where the time goes in v20:
time: 37.7 us; the launch traced here: 37.5 us
  starting transfers between devices  15.2 us (40%)
  Pallas kernels  14.3 us (38%)
  waiting for transfers between devices  5.13 us (14%)
  other arithmetic  1.18 us (3%)
  between operations  0.89 us (2%)
  local copies, waits for them, and re-layouts  0.79 us (2%)
    pallas_call x12, Pallas kernels, run(): pl.pallas_call(lambda *refs: body(*refs, **fixed), out_shape=[jax.ShapeDt...  14.3 us
    ppermute x9, starting transfers between devices, exchanged(): lax.ppermute(value, axes, [(int(source), int(target)) for source, target...  8.65 us
    ppermute x3, starting transfers between devices, shifted(): lax.ppermute(value, axis, [(source, (source + steps) % count) for source...  6.58 us
    ppermute x9, waiting for transfers between devices, exchanged(): lax.ppermute(value, axes, [(int(source), int(target)) for source, target...  5.12 us
  transfers between devices with their start and end apart: 12, of which 7 were waited for; matrix products, arithmetic and copies ran while one was open for 2% of the time, Pallas kernels for 30%

profile of v20, /device:TPU:0, one launch (start us, length us, event | category | flops | bytes accessed | tf_op | source)
XLA Modules:
  0.0 37.5 jit_solution(16290763181254930830)
XLA Ops:
  0.6 3.0 %collective-permute-start = (bf16[128,4,128]{2,1,0:T(4,128)(2,1)}, bf16[128,4,128]{2,1,0:T(4,128)(2,1)S(1)}, u32[]{:S(2)}, u32[]{:S(2)}) collective-permute-start(bf16[128,4,128]{2,1,0:T(4,128)(2,1)} %bitcast.23), channel_id=1, source_target_pairs={{0,2},{1,3},{2,4},{3,5},{4,6},{5,7},{6,0},{7,1},{8,10},{9,11},{10,... | collective-permute-start | bytes 393224 | tf_op jit(solution)/shard_map/ppermute | solution.py:19
  3.6 0.7 %pad_add_fusion.refs_0_ = s32[2,1024]{1,0:T(2,128)S(1)} fusion(s32[1,1024]{1,0:T(1,128)} %param.17, s32[1,1024]{1,0:T(1,128)} %param.16), kind=kLoop, calls=%fused_computation.6 | loop fusion | flops 2048 | bytes 16384 | tf_op jit(solution)/shard_map/concatenate | solution.py:457
  4.4 0.0 copy-start.1
  4.4 0.0 copy-start.2
  4.4 0.0 copy-start.3
  4.4 0.0 copy-start.4
  4.4 0.3 place_kernel.1
  4.8 0.0 copy-start.5
  4.8 0.5 %copy-done.1 = bf16[1,128,4,128]{3,2,1,0:T(4,128)(2,1)S(1)} copy-done((bf16[1,128,4,128]{3,2,1,0:T(4,128)(2,1)S(1)}, bf16[1,128,4,128]{3,2,1,0:T(4,128)(2,1)}, u32[]{:S(2)}) %copy-start.1) | copy-done | bytes 131096
  5.3 1.5 %collective-permute-start.1 = (bf16[128,4,128]{2,1,0:T(4,128)(2,1)S(1)}, bf16[128,4,128]{2,1,0:T(4,128)(2,1)S(1)}, u32[]{:S(2)}, u32[]{:S(2)}) collective-permute-start(bf16[128,4,128]{2,1,0:T(4,128)(2,1)S(1)} %bitcast.25), channel_id=1, source_target_pairs={{0,2},{1,3},{2,4},{3,5},{4,6},{5,7},{6,0},{7,1},{8,10},{9,11},{10,... | collective-permute-start | bytes 393224 | tf_op jit(solution)/shard_map/ppermute | solution.py:19
  6.8 0.0 copy-done.2
  6.8 0.0 copy-done.3
  6.8 0.0 copy-done.4
  6.8 1.4 %pull_kernel.1 = (bf16[4,1024,128]{2,1,0:T(8,128)(2,1)S(1)}, bf16[4,1024,128]{2,1,0:T(8,128)(2,1)S(1)}, f32[8,1024]{1,0:T(8,128)S(1)}, bf16[512,1024]{1,0:T(8,128)(2,1)S(1)}) custom-call(s32[8,1024]{1,0:T(8,128)S(1)} %get-tuple-element.54.refs_0_.refs_7_, bf16[128,32,128]{2,1,0:T(8,128)(2,1)S(1)} %bitcast.29, bf16[64,32,128]{2,1,0:T(8,128)(2,1)S(1)} %bitcast.31, ...), custom_call_target="tpu_custom_call" | custom-call | flops 1073741824 | bytes 4194304 | tf_op jit(solution)/shard_map/pull_kernel/pallas_call | solution.py:434
  8.2 0.0 copy-done.5
  8.2 0.0 copy-start
  8.2 0.8 %hidden_grad_kernel.1 = (bf16[4,1024,128]{2,1,0:T(8,128)(2,1)S(1)}, bf16[4,512,128]{2,1,0:T(8,128)(2,1)S(1)}) custom-call(s32[8,1024]{1,0:T(8,128)S(1)} %get-tuple-element.54.refs_0_.refs_7_, f32[8,1024]{1,0:T(8,128)S(1)} %get-tuple-element.57.refs_1_, bf16[4,1024,128]{2,1,0:T(8,128)(2,1)S(1)} %get-tuple-element.58.refs_2_.refs_5_, ...), custom_call_target="tpu_custom_call" | custom-call | flops 2147483648 | bytes 4194304 | tf_op jit(solution)/shard_map/hidden_grad_kernel/pallas_call | solution.py:434
  9.0 0.0 collective-permute-done
  9.0 0.1 copy-done
  9.1 0.1 broadcast_select_fusion.1
  9.2 0.1 collective-permute-start.2
  9.2 0.9 %fold_kernel.1 = (f32[4,128,1024]{2,1,0:T(8,128)S(1)}, f32[4,2,1024]{2,1,0:T(2,128)S(1)}, bf16[4,128,128]{2,1,0:T(8,128)(2,1)S(1)}, bf16[4,128,128]{2,1,0:T(8,128)(2,1)S(1)}) custom-call(bf16[4,1024,128]{2,1,0:T(8,128)(2,1)S(1)} %get-tuple-element.55.refs_0_, bf16[512,128]{1,0:T(8,128)(2,1)S(1)} %bitcast.28, bf16[512,128]{1,0:T(8,128)(2,1)S(1)} %bitcast.24, ...), custom_call_target="tpu_custom_call" | custom-call | flops 2147483648 | bytes 4194304 | tf_op jit(solution)/shard_map/fold_kernel/pallas_call | solution.py:434
  10.2 0.4 %collective-permute-done.2 = bf16[128,4,128]{2,1,0:T(4,128)(2,1)S(1)} collective-permute-done((bf16[128,4,128]{2,1,0:T(4,128)(2,1)S(1)}, bf16[128,4,128]{2,1,0:T(4,128)(2,1)S(1)}, u32[]{:S(2)}, u32[]{:S(2)}) %collective-permute-start.2) | collective-permute-done | bytes 131104 | tf_op jit(solution)/shard_map/ppermute | solution.py:29
  10.6 0.8 %near_kernel.1 = (bf16[2,384,1024]{2,1,0:T(8,128)(2,1)S(1)}, bf16[4,128,128]{2,1,0:T(8,128)(2,1)S(1)}) custom-call(bf16[4,1024,128]{2,1,0:T(8,128)(2,1)S(1)} %get-tuple-element.55.refs_0_, bf16[512,128]{1,0:T(8,128)(2,1)S(1)} %bitcast.22, f32[2,128,1024]{2,1,0:T(8,128)S(1)} %get-tuple-element.64.refs_3_.refs_2_, ...), custom_call_target="tpu_custom_call" | custom-call | flops 1073741824 | bytes 4194304 | tf_op jit(solution)/shard_map/near_kernel/pallas_call | solution.py:434
  11.4 0.0 collective-permute-done.1
  11.4 0.1 broadcast_select_fusion
  11.5 0.2 collective-permute-start.3
  11.7 0.8 %far_kernel.1.refs_1_.refs_2_.refs_3_ = bf16[2,384,1024]{2,1,0:T(8,128)(2,1)S(1)} custom-call(bf16[4,1024,128]{2,1,0:T(8,128)(2,1)S(1)} %get-tuple-element.55.refs_0_, bf16[4,128,128]{2,1,0:T(8,128)(2,1)S(1)} %get-tuple-element.71.refs_1_.refs_2_, f32[2,128,1024]{2,1,0:T(8,128)S(1)} %get-tuple-element.64.refs_3_.refs_2_, ...), custom_call_target="tpu_custom_call" | custom-call | flops 1073741824 | bytes 4194304 | tf_op jit(solution)/shard_map/far_kernel/pallas_call | solution.py:434
  12.5 0.0 copy-start.6
  12.5 0.6 %hidden_kernel.1 = (f32[512,1024]{1,0:T(8,128)S(1)}, bf16[4,128,128]{2,1,0:T(8,128)(2,1)S(1)}, bf16[4,128,128]{2,1,0:T(8,128)(2,1)S(1)}) custom-call(bf16[2,384,1024]{2,1,0:T(8,128)(2,1)S(1)} %get-tuple-element.81.refs_0_.refs_1_.refs_2_, bf16[2,384,1024]{2,1,0:T(8,128)(2,1)S(1)} %far_kernel.1.refs_1_.refs_2_.refs_3_, bf16[512,128]{1,0:T(8,128)(2,1)S(1)} %bitcast.27, ...), custom_call_target="tpu_custom_call" | custom-call | flops 1073741824 | bytes 4194304 | tf_op jit(solution)/shard_map/hidden_kernel/pallas_call | solution.py:434
  13.0 0.0 collective-permute-done.3
  13.0 0.1 copy-done.6
  13.1 2.0 %forward_kernel.1 = (bf16[16,128,128]{2,1,0:T(8,128)(2,1)S(1)}, bf16[512,1024]{1,0:T(8,128)(2,1)S(1)}, bf16[256,1024]{1,0:T(8,128)(2,1)S(1)}, bf16[4,128,128]{2,1,0:T(8,128)(2,1)S(1)}) custom-call(f32[4,16]{1,0:T(4,128)S(1)} %bitcast.35, bf16[2,384,1024]{2,1,0:T(8,128)(2,1)S(1)} %get-tuple-element.81.refs_0_.refs_1_.refs_2_, ...), custom_call_target="tpu_custom_call" | custom-call | flops 3221225472 | bytes 10485760 | tf_op jit(solution)/shard_map/forward_kernel/pallas_call | solution.py:434
  15.2 0.4 %collective-permute-start.4 = (bf16[16,128,128]{2,1,0:T(8,128)(2,1)S(1)}, bf16[16,128,128]{2,1,0:T(8,128)(2,1)S(1)}, u32[]{:S(2)}, u32[]{:S(2)}) collective-permute-start(bf16[16,128,128]{2,1,0:T(8,128)(2,1)S(1)} %get-tuple-element.80), channel_id=1, source_target_pairs={{0,1},{1,0},{2,3},{3,2},{4,5},{5,4},{6,7},{7,6},{8,9},{9,8},{10,11... | collective-permute-start | bytes 1572872 | tf_op jit(solution)/shard_map/ppermute | solution.py:29
  15.6 0.8 %keep_kernel.1 = bf16[16,128,128]{2,1,0:T(8,128)(2,1)S(1)} custom-call(bf16[512,1024]{1,0:T(8,128)(2,1)S(1)} %get-tuple-element.78.refs_0_, bf16[256,1024]{1,0:T(8,128)(2,1)S(1)} %get-tuple-element.79.refs_1_, bf16[4,1024,128]{2,1,0:T(8,128)(2,1)S(1)} %get-tuple-element.58.refs_2_.refs_5_, bf16[512,1024]{1,0:T(8,128)(2,1)S(1)} %get-tuple-element.77.refs_8_.refs_3_), custom_call_target="tpu_custom_call" | custom-call | flops 1073741824 | bytes 5242880 | tf_op jit(solution)/shard_map/keep_kernel/pallas_call | solution.py:434
  16.4 0.8 %collective-permute-done.4 = bf16[16,128,128]{2,1,0:T(8,128)(2,1)S(1)} collective-permute-done((bf16[16,128,128]{2,1,0:T(8,128)(2,1)S(1)}, bf16[16,128,128]{2,1,0:T(8,128)(2,1)S(1)}, u32[]{:S(2)}, u32[]{:S(2)}) %collective-permute-start.4) | collective-permute-done | bytes 524320 | tf_op jit(solution)/shard_map/ppermute | solution.py:29
  17.1 0.1 add_convert_fusion
  17.3 1.5 %collective-permute-start.9 = (bf16[4,128,128]{2,1,0:T(8,128)(2,1)S(1)}, bf16[4,128,128]{2,1,0:T(8,128)(2,1)S(1)}, u32[]{:S(2)}, u32[]{:S(2)}) collective-permute-start(bf16[4,128,128]{2,1,0:T(8,128)(2,1)S(1)} %get-tuple-element.101), channel_id=1, source_target_pairs={{0,4},{1,5},{2,6},{3,7},{4,0},{5,1},{6,2},{7,3},{8,12},{9,13},{10,... | collective-permute-start | bytes 393224 | tf_op jit(solution)/shard_map/ppermute | solution.py:29
  18.8 1.5 %collective-permute-start.8 = (bf16[4,128,128]{2,1,0:T(8,128)(2,1)S(1)}, bf16[4,128,128]{2,1,0:T(8,128)(2,1)S(1)}, u32[]{:S(2)}, u32[]{:S(2)}) collective-permute-start(bf16[4,128,128]{2,1,0:T(8,128)(2,1)S(1)} %get-tuple-element.102), channel_id=1, source_target_pairs={{0,6},{1,7},{2,4},{3,5},{4,2},{5,3},{6,0},{7,1},{8,14},{9,15},{10,... | collective-permute-start | bytes 393224 | tf_op jit(solution)/shard_map/ppermute | solution.py:29
  20.4 0.5 %collective-permute-start.7 = (bf16[4,128,128]{2,1,0:T(8,128)(2,1)S(1)}, bf16[4,128,128]{2,1,0:T(8,128)(2,1)S(1)}, u32[]{:S(2)}, u32[]{:S(2)}) collective-permute-start(bf16[4,128,128]{2,1,0:T(8,128)(2,1)S(1)} %get-tuple-element.103), channel_id=1, source_target_pairs={{0,2},{1,3},{2,0},{3,1},{4,6},{5,7},{6,4},{7,5},{8,10},{9,11},{10,... | collective-permute-start | bytes 393224 | tf_op jit(solution)/shard_map/ppermute | solution.py:29
  20.9 3.5 %backward_kernel.1 = (bf16[8,128,128]{2,1,0:T(8,128)(2,1)S(1)}, bf16[8,128,128]{2,1,0:T(8,128)(2,1)S(1)}, f32[8,128,128]{2,1,0:T(8,128)S(1)}, bf16[4,384,1024]{2,1,0:T(8,128)(2,1)S(1)}) custom-call(bf16[4,1024,128]{2,1,0:T(8,128)(2,1)S(1)} %get-tuple-element.55.refs_0_, bf16[4,1024,128]{2,1,0:T(8,128)(2,1)S(1)} %get-tuple-element.60.refs_1_, ...), custom_call_target="tpu_custom_call" | custom-call | flops 4294967296 | bytes 10485760 | tf_op jit(solution)/shard_map/backward_kernel/pallas_call | solution.py:434
  24.4 0.1 collective-permute-start.5
  24.4 1.4 %collective-permute-done.9 = bf16[4,128,128]{2,1,0:T(8,128)(2,1)S(1)} collective-permute-done((bf16[4,128,128]{2,1,0:T(8,128)(2,1)S(1)}, bf16[4,128,128]{2,1,0:T(8,128)(2,1)S(1)}, u32[]{:S(2)}, u32[]{:S(2)}) %collective-permute-start.9) | collective-permute-done | bytes 131104 | tf_op jit(solution)/shard_map/ppermute | solution.py:29
  25.8 0.3 collective-permute-done.8
  26.1 1.1 %collective-permute-done.7 = bf16[4,128,128]{2,1,0:T(8,128)(2,1)S(1)} collective-permute-done((bf16[4,128,128]{2,1,0:T(8,128)(2,1)S(1)}, bf16[4,128,128]{2,1,0:T(8,128)(2,1)S(1)}, u32[]{:S(2)}, u32[]{:S(2)}) %collective-permute-start.7) | collective-permute-done | bytes 131104 | tf_op jit(solution)/shard_map/ppermute | solution.py:29
  27.2 0.1 add_convert_fusion.2
  27.3 0.0 collective-permute-done.5.refs_1_
  27.3 0.1 add_convert_fusion.1
  27.4 1.6 %collective-permute-start.10 = (bf16[2,128,128]{2,1,0:T(8,128)(2,1)S(1)}, bf16[2,128,128]{2,1,0:T(8,128)(2,1)S(1)}, u32[]{:S(2)}, u32[]{:S(2)}) collective-permute-start(bf16[2,128,128]{2,1,0:T(8,128)(2,1)S(1)} %slice.29), channel_id=1, source_target_pairs={{0,8},{8,0},{16,24},{24,16},{1,9},{9,1},{17,25},{25,17},{2,10},{10... | collective-permute-start | bytes 196616 | tf_op jit(solution)/shard_map/ppermute | solution.py:29
  29.0 2.1 %collective-permute-start.6 = (bf16[8,128,128]{2,1,0:T(8,128)(2,1)S(1)}, bf16[8,128,128]{2,1,0:T(8,128)(2,1)S(1)}, u32[]{:S(2)}, u32[]{:S(2)}) collective-permute-start(bf16[8,128,128]{2,1,0:T(8,128)(2,1)S(1)} %add_convert_fusion.1), channel_id=1, source_target_pairs={{0,6},{1,7},{2,0},{3,1},{4,2},{5,3},{6,4},{7,5},{8,14},{9,15},{10,... | collective-permute-start | bytes 786440 | tf_op jit(solution)/shard_map/ppermute | solution.py:19
  31.1 0.6 %collective-permute-done.10 = bf16[2,128,128]{2,1,0:T(8,128)(2,1)S(1)} collective-permute-done((bf16[2,128,128]{2,1,0:T(8,128)(2,1)S(1)}, bf16[2,128,128]{2,1,0:T(8,128)(2,1)S(1)}, u32[]{:S(2)}, u32[]{:S(2)}) %collective-permute-start.10) | collective-permute-done | bytes 65568 | tf_op jit(solution)/shard_map/ppermute | solution.py:29
  31.8 2.7 %collective-permute-start.11 = (bf16[1,128,128]{2,1,0:T(8,128)(2,1)S(1)}, bf16[1,128,128]{2,1,0:T(8,128)(2,1)S(1)}, u32[]{:S(2)}, u32[]{:S(2)}) collective-permute-start(bf16[1,128,128]{2,1,0:T(8,128)(2,1)S(1)} %get-tuple-element.104), channel_id=1, source_target_pairs={{0,16},{8,24},{16,0},{24,8},{1,17},{9,25},{17,1},{25,9},{2,18},{10... | collective-permute-start | bytes 98312 | tf_op jit(solution)/shard_map/ppermute | solution.py:29
  34.4 1.6 %query_kernel.1 = bf16[128,32,128]{2,1,0:T(8,128)(2,1)} custom-call(bf16[4,384,1024]{2,1,0:T(8,128)(2,1)S(1)} %get-tuple-element.85.refs_0_, bf16[4,128,128]{2,1,0:T(8,128)(2,1)S(1)} %get-tuple-element.86.refs_1_, bf16[4,128,128]{2,1,0:T(8,128)(2,1)S(1)} %get-tuple-element.71.refs_1_.refs_2_, bf16[4,128,128]{2,1,0:T(8,128)(2,1)S(1)} %get-tuple-element.87.refs_3_), custom_call_target="tpu_custom_call" | custom-call | flops 2147483648 | bytes 5242880 | tf_op jit(solution)/shard_map/query_kernel/pallas_call | solution.py:434
  36.1 0.6 %collective-permute-done.11.refs_4_ = bf16[1,128,128]{2,1,0:T(8,128)(2,1)S(1)} collective-permute-done((bf16[1,128,128]{2,1,0:T(8,128)(2,1)S(1)}, bf16[1,128,128]{2,1,0:T(8,128)(2,1)S(1)}, u32[]{:S(2)}, u32[]{:S(2)}) %collective-permute-start.11) | collective-permute-done | bytes 32800 | tf_op jit(solution)/shard_map/ppermute | solution.py:29
  36.6 0.0 collective-permute-done.6.refs_2_
  36.6 0.8 %finish_kernel.1 = (bf16[512,128]{1,0:T(8,128)(2,1)}, bf16[512,128]{1,0:T(8,128)(2,1)}, f32[16,4,128]{2,1,0:T(4,128)}, f32[16,4,128]{2,1,0:T(4,128)}) custom-call(f32[8,128,128]{2,1,0:T(8,128)S(1)} %get-tuple-element.88.refs_0_, bf16[8,128,128]{2,1,0:T(8,128)(2,1)S(1)} %collective-permute-done.5.refs_1_, ...), custom_call_target="tpu_custom_call" | custom-call | flops 1048576 | bytes 1048576 | tf_op jit(solution)/shard_map/finish_kernel/pallas_call | solution.py:434
  (4 shorter events, 0.1 us)
Async XLA Ops:
  0.6 8.3 %collective-permute-start = (bf16[128,4,128]{2,1,0:T(4,128)(2,1)}, bf16[128,4,128]{2,1,0:T(4,128)(2,1)S(1)}, u32[]{:S(2)}, u32[]{:S(2)}) collective-permute-start(bf16[128,4,128]{2,1,0:T(4,128)(2,1)} %bitcast.23), channel_id=1, source_target_pairs={{0,2},{1,3},{2,4},{3,5},{4,6},{5,7},{6,0},{7,1},{8,10},{9,11},{10,... | collective-permute-start | bytes 393224 | tf_op jit(solution)/shard_map/ppermute | solution.py:19
  4.4 0.9 %copy-start.1 = (bf16[1,128,4,128]{3,2,1,0:T(4,128)(2,1)S(1)}, bf16[1,128,4,128]{3,2,1,0:T(4,128)(2,1)}, u32[]{:S(2)}) copy-start(bf16[1,128,4,128]{3,2,1,0:T(4,128)(2,1)} %param.11) | copy-start | bytes 393220
  4.4 2.4 %copy-start.2 = (bf16[1,128,32,128]{3,2,1,0:T(8,128)(2,1)S(1)}, bf16[1,128,32,128]{3,2,1,0:T(8,128)(2,1)}, u32[]{:S(2)}) copy-start(bf16[1,128,32,128]{3,2,1,0:T(8,128)(2,1)} %param.12) | copy-start | bytes 3145732
  4.4 2.4 %copy-start.3 = (bf16[1,128,32,128]{3,2,1,0:T(8,128)(2,1)S(1)}, bf16[1,128,32,128]{3,2,1,0:T(8,128)(2,1)}, u32[]{:S(2)}) copy-start(bf16[1,128,32,128]{3,2,1,0:T(8,128)(2,1)} %param.9) | copy-start | bytes 3145732
  4.4 2.4 %copy-start.4 = (bf16[16,4,32,128]{3,2,1,0:T(8,128)(2,1)S(1)}, bf16[16,4,32,128]{3,2,1,0:T(8,128)(2,1)}, u32[]{:S(2)}) copy-start(bf16[16,4,32,128]{3,2,1,0:T(8,128)(2,1)} %param.13) | copy-start | bytes 1572868
  4.8 3.4 %copy-start.5 = (bf16[16,4,32,128]{3,2,1,0:T(8,128)(2,1)S(1)}, bf16[16,4,32,128]{3,2,1,0:T(8,128)(2,1)}, u32[]{:S(2)}) copy-start(bf16[16,4,32,128]{3,2,1,0:T(8,128)(2,1)} %param.14) | copy-start | bytes 1572868
  5.3 6.1 %collective-permute-start.1 = (bf16[128,4,128]{2,1,0:T(4,128)(2,1)S(1)}, bf16[128,4,128]{2,1,0:T(4,128)(2,1)S(1)}, u32[]{:S(2)}, u32[]{:S(2)}) collective-permute-start(bf16[128,4,128]{2,1,0:T(4,128)(2,1)S(1)} %bitcast.25), channel_id=1, source_target_pairs={{0,2},{1,3},{2,4},{3,5},{4,6},{5,7},{6,0},{7,1},{8,10},{9,11},{10,... | collective-permute-start | bytes 393224 | tf_op jit(solution)/shard_map/ppermute | solution.py:19
  8.2 0.9 %copy-start = (bf16[1,128,4,128]{3,2,1,0:T(4,128)(2,1)S(1)}, bf16[1,128,4,128]{3,2,1,0:T(4,128)(2,1)}, u32[]{:S(2)}) copy-start(bf16[1,128,4,128]{3,2,1,0:T(4,128)(2,1)} %param.10) | copy-start | bytes 393220
  9.2 1.4 %collective-permute-start.2 = (bf16[128,4,128]{2,1,0:T(4,128)(2,1)S(1)}, bf16[128,4,128]{2,1,0:T(4,128)(2,1)S(1)}, u32[]{:S(2)}, u32[]{:S(2)}) collective-permute-start(bf16[128,4,128]{2,1,0:T(4,128)(2,1)S(1)} %broadcast_select_fusion.1), channel_id=1, source_target_pairs={{0,1},{1,0},{2,3},{3,2},{4,5},{5,4},{6,7},{7,6},{8,9},{9,8},{10,11... | collective-permute-start | bytes 393224 | tf_op jit(solution)/shard_map/ppermute | solution.py:29
  11.5 1.6 %collective-permute-start.3 = (bf16[128,4,128]{2,1,0:T(4,128)(2,1)S(1)}, bf16[128,4,128]{2,1,0:T(4,128)(2,1)S(1)}, u32[]{:S(2)}, u32[]{:S(2)}) collective-permute-start(bf16[128,4,128]{2,1,0:T(4,128)(2,1)S(1)} %broadcast_select_fusion), channel_id=1, source_target_pairs={{0,1},{1,0},{2,3},{3,2},{4,5},{5,4},{6,7},{7,6},{8,9},{9,8},{10,11... | collective-permute-start | bytes 393224 | tf_op jit(solution)/shard_map/ppermute | solution.py:29
  12.5 0.7 %copy-start.6 = (f32[16,4]{0,1:T(4,128)S(1)}, f32[16,4]{0,1:T(4,128)}, u32[]{:S(2)}) copy-start(f32[16,4]{0,1:T(4,128)} %param.15) | copy-start | bytes 772
  15.2 2.0 %collective-permute-start.4 = (bf16[16,128,128]{2,1,0:T(8,128)(2,1)S(1)}, bf16[16,128,128]{2,1,0:T(8,128)(2,1)S(1)}, u32[]{:S(2)}, u32[]{:S(2)}) collective-permute-start(bf16[16,128,128]{2,1,0:T(8,128)(2,1)S(1)} %get-tuple-element.80), channel_id=1, source_target_pairs={{0,1},{1,0},{2,3},{3,2},{4,5},{5,4},{6,7},{7,6},{8,9},{9,8},{10,11... | collective-permute-start | bytes 1572872 | tf_op jit(solution)/shard_map/ppermute | solution.py:29
  17.3 8.5 %collective-permute-start.9 = (bf16[4,128,128]{2,1,0:T(8,128)(2,1)S(1)}, bf16[4,128,128]{2,1,0:T(8,128)(2,1)S(1)}, u32[]{:S(2)}, u32[]{:S(2)}) collective-permute-start(bf16[4,128,128]{2,1,0:T(8,128)(2,1)S(1)} %get-tuple-element.101), channel_id=1, source_target_pairs={{0,4},{1,5},{2,6},{3,7},{4,0},{5,1},{6,2},{7,3},{8,12},{9,13},{10,... | collective-permute-start | bytes 393224 | tf_op jit(solution)/shard_map/ppermute | solution.py:29
  18.8 7.3 %collective-permute-start.8 = (bf16[4,128,128]{2,1,0:T(8,128)(2,1)S(1)}, bf16[4,128,128]{2,1,0:T(8,128)(2,1)S(1)}, u32[]{:S(2)}, u32[]{:S(2)}) collective-permute-start(bf16[4,128,128]{2,1,0:T(8,128)(2,1)S(1)} %get-tuple-element.102), channel_id=1, source_target_pairs={{0,6},{1,7},{2,4},{3,5},{4,2},{5,3},{6,0},{7,1},{8,14},{9,15},{10,... | collective-permute-start | bytes 393224 | tf_op jit(solution)/shard_map/ppermute | solution.py:29
  20.4 6.8 %collective-permute-start.7 = (bf16[4,128,128]{2,1,0:T(8,128)(2,1)S(1)}, bf16[4,128,128]{2,1,0:T(8,128)(2,1)S(1)}, u32[]{:S(2)}, u32[]{:S(2)}) collective-permute-start(bf16[4,128,128]{2,1,0:T(8,128)(2,1)S(1)} %get-tuple-element.103), channel_id=1, source_target_pairs={{0,2},{1,3},{2,0},{3,1},{4,6},{5,7},{6,4},{7,5},{8,10},{9,11},{10,... | collective-permute-start | bytes 393224 | tf_op jit(solution)/shard_map/ppermute | solution.py:29
  24.4 2.9 %collective-permute-start.5 = (bf16[8,128,128]{2,1,0:T(8,128)(2,1)S(1)}, bf16[8,128,128]{2,1,0:T(8,128)(2,1)S(1)}, u32[]{:S(2)}, u32[]{:S(2)}) collective-permute-start(bf16[8,128,128]{2,1,0:T(8,128)(2,1)S(1)} %get-tuple-element.89), channel_id=1, source_target_pairs={{0,1},{1,0},{2,3},{3,2},{4,5},{5,4},{6,7},{7,6},{8,9},{9,8},{10,11... | collective-permute-start | bytes 786440 | tf_op jit(solution)/shard_map/ppermute | solution.py:29
  27.4 4.3 %collective-permute-start.10 = (bf16[2,128,128]{2,1,0:T(8,128)(2,1)S(1)}, bf16[2,128,128]{2,1,0:T(8,128)(2,1)S(1)}, u32[]{:S(2)}, u32[]{:S(2)}) collective-permute-start(bf16[2,128,128]{2,1,0:T(8,128)(2,1)S(1)} %slice.29), channel_id=1, source_target_pairs={{0,8},{8,0},{16,24},{24,16},{1,9},{9,1},{17,25},{25,17},{2,10},{10... | collective-permute-start | bytes 196616 | tf_op jit(solution)/shard_map/ppermute | solution.py:29
  29.0 7.6 %collective-permute-start.6 = (bf16[8,128,128]{2,1,0:T(8,128)(2,1)S(1)}, bf16[8,128,128]{2,1,0:T(8,128)(2,1)S(1)}, u32[]{:S(2)}, u32[]{:S(2)}) collective-permute-start(bf16[8,128,128]{2,1,0:T(8,128)(2,1)S(1)} %add_convert_fusion.1), channel_id=1, source_target_pairs={{0,6},{1,7},{2,0},{3,1},{4,2},{5,3},{6,4},{7,5},{8,14},{9,15},{10,... | collective-permute-start | bytes 786440 | tf_op jit(solution)/shard_map/ppermute | solution.py:19
  31.8 4.9 %collective-permute-start.11 = (bf16[1,128,128]{2,1,0:T(8,128)(2,1)S(1)}, bf16[1,128,128]{2,1,0:T(8,128)(2,1)S(1)}, u32[]{:S(2)}, u32[]{:S(2)}) collective-permute-start(bf16[1,128,128]{2,1,0:T(8,128)(2,1)S(1)} %get-tuple-element.104), channel_id=1, source_target_pairs={{0,16},{8,24},{16,0},{24,8},{1,17},{9,25},{17,1},{25,9},{2,18},{10... | collective-permute-start | bytes 98312 | tf_op jit(solution)/shard_map/ppermute | solution.py:29
